TPU v7x, 32 devices: a whole 2x2x4 slice. The times are simulated.
32 devices in a mesh: wide: 8 (over y, x, core), narrow: 4 (over z).
Axes of the slice: x: 2, y: 2, z: 4, core: 2. Of those that a mesh axis runs over, the one named last changes fastest.
Arguments:
- x_in: bfloat16 [4096, 2560], P('wide', 'narrow'), may hold values from -6 to 6
- grad_out: bfloat16 [4096, 2560], P('wide', 'narrow'), may hold values from -6 to 6
- w_qa: bfloat16 [2560, 768], P('wide', 'narrow'), may hold values from -0.125 to 0.125
- w_kv: bfloat16 [2560, 256], P('wide', 'narrow'), may hold values from -0.125 to 0.125
- w_kr: bfloat16 [2560, 32], P('wide'), may hold values from -0.125 to 0.125
- w_qb: bfloat16 [768, 3840], P('wide', 'narrow'), may hold values from -0.21875 to 0.21875
- w_kvb: bfloat16 [256, 5120], P('wide', 'narrow'), may hold values from -0.375 to 0.375
- w_o: bfloat16 [2560, 2560], P('wide', 'narrow'), may hold values from -6 to 6
- w_gate: bfloat16 [2560, 6400], P('wide', 'narrow'), may hold values from -0.125 to 0.125
- w_up: bfloat16 [2560, 6400], P('wide', 'narrow'), may hold values from -0.125 to 0.125
- w_down: bfloat16 [2560, 6400], P('wide', 'narrow'), may hold values from -0.75 to 0.75
- norm_gains: float32 [2, 2560], P(None, 'narrow'), may hold values from 0.5 to 1.5
- q_gain: float32 [768], P('narrow'), may hold values from 0.5 to 1.5
- kv_gain: float32 [256], P('narrow'), may hold values from 0.5 to 1.5
- deal: int32 [8, 8], replicated, may hold values from 0 to 7, each once within a row
- lengths: int32 [8, 4], P('wide'), may hold values from 1 to 384, 512 in all within a row
- step_count: int32 [1], replicated, may hold values from 1 to 20
- owner_a: int32 [4, 89], P('narrow'), may hold values from 0 to 135, as said below
- owner_b: int32 [4, 15], P('narrow'), may hold values from 0 to 23, as said below
- owner_c: int32 [4, 20], P('narrow'), may hold values from 0 to 31, as said below
- basis_la: float32 [136, 2560, 512], P('wide', None, 'narrow'), as said below
- basis_ra: float32 [136, 64, 256], P('wide', None, 'narrow'), as said below
- basis_lb: float32 [24, 768, 512], P('wide', None, 'narrow'), as said below
- basis_rb: float32 [24, 64, 256], P('wide', None, 'narrow'), as said below
- basis_lc: float32 [32, 256, 512], P('wide', None, 'narrow'), as said below
- basis_rc: float32 [32, 64, 256], P('wide', None, 'narrow'), as said below
- mom_a: float32 [136, 2560, 256], P('wide', None, 'narrow')
- sq_a: float32 [136, 2560, 256], P('wide', None, 'narrow'), as said below
- mom_b: float32 [24, 768, 256], P('wide', None, 'narrow')
- sq_b: float32 [24, 768, 256], P('wide', None, 'narrow'), as said below
- mom_c: float32 [32, 256, 256], P('wide', None, 'narrow')
- sq_c: float32 [32, 256, 256], P('wide', None, 'narrow'), as said below
- kr_mom: float32 [2560, 32], P('wide')
- kr_sq: float32 [2560, 32], P('wide'), as said below
- gain_mom: float32 [2, 2560], P(None, 'narrow')
- gain_sq: float32 [2, 2560], P(None, 'narrow'), as said below
- qgain_mom: float32 [768], P('narrow')
- qgain_sq: float32 [768], P('narrow'), as said below
- kvgain_mom: float32 [256], P('narrow')
- kvgain_sq: float32 [256], P('narrow'), as said below
Outputs:
- layer_out: float32 [4096, 2560], P('wide', 'narrow')
- grad_in: float32 [4096, 2560], P('wide', 'narrow')
- grad_qa: float32 [2560, 768], P('wide', 'narrow')
- grad_kv: float32 [2560, 256], P('wide', 'narrow')
- grad_qb: float32 [768, 3840], P('wide', 'narrow')
- grad_kvb: float32 [256, 5120], P('wide', 'narrow')
- grad_o: float32 [2560, 2560], P('wide', 'narrow')
- grad_gate: float32 [2560, 6400], P('wide', 'narrow')
- grad_up: float32 [2560, 6400], P('wide', 'narrow')
- grad_down: float32 [2560, 6400], P('wide', 'narrow')
- new_qa: float32 [2560, 768], P('wide', 'narrow')
- new_kv: float32 [2560, 256], P('wide', 'narrow')
- new_qb: float32 [768, 3840], P('wide', 'narrow')
- new_kvb: float32 [256, 5120], P('wide', 'narrow')
- new_o: float32 [2560, 2560], P('wide', 'narrow')
- new_gate: float32 [2560, 6400], P('wide', 'narrow')
- new_up: float32 [2560, 6400], P('wide', 'narrow')
- new_down: float32 [2560, 6400], P('wide', 'narrow')
- grad_kr: float32 [2560, 32], P('wide')
- new_kr: float32 [2560, 32], P('wide')
- new_kr_mom: float32 [2560, 32], P('wide')
- new_kr_sq: float32 [2560, 32], P('wide')
- grad_gains: float32 [2, 2560], P(None, 'narrow')
- new_gains: float32 [2, 2560], P(None, 'narrow')
- new_gain_mom: float32 [2, 2560], P(None, 'narrow')
- new_gain_sq: float32 [2, 2560], P(None, 'narrow')
- grad_qgain: float32 [768], P('narrow')
- new_qgain: float32 [768], P('narrow')
- new_qgain_mom: float32 [768], P('narrow')
- new_qgain_sq: float32 [768], P('narrow')
- grad_kvgain: float32 [256], P('narrow')
- new_kvgain: float32 [256], P('narrow')
- new_kvgain_mom: float32 [256], P('narrow')
- new_kvgain_sq: float32 [256], P('narrow')
- new_mom_a: float32 [136, 2560, 256], P('wide', None, 'narrow')
- new_sq_a: float32 [136, 2560, 256], P('wide', None, 'narrow')
- new_mom_b: float32 [24, 768, 256], P('wide', None, 'narrow')
- new_sq_b: float32 [24, 768, 256], P('wide', None, 'narrow')
- new_mom_c: float32 [32, 256, 256], P('wide', None, 'narrow')
- new_sq_c: float32 [32, 256, 256], P('wide', None, 'narrow')
Inputs may be any that keep to these rules, and one draw needn't show every extreme that they name: Each row of deal is a permutation. `lengths`: each row sums to 512; its largest entry is 384; the last entry counts padding rows. `owner_a`: entries of a row are distinct; slot k belongs to owner k // 17 of wide; in every row some owner holds exactly 17 units. `owner_b`: entries of a row are distinct; slot k belongs to owner k // 3 of wide; in every row some owner holds exactly 3 units. `owner_c`: entries of a row are distinct; slot k belongs to owner k // 4 of wide; in every row some owner holds exactly 4 units. `basis_la`: every block of 128 by 128 is orthogonal. `basis_ra`: every block of 64 by 64 is orthogonal. `basis_lb`: every block of 128 by 128 is orthogonal. `basis_rb`: every block of 64 by 64 is orthogonal. `basis_lc`: every block of 128 by 128 is orthogonal. `basis_rc`: every block of 64 by 64 is orthogonal. `sq_a`: Positive. `sq_b`: Positive. `sq_c`: Positive. `kr_sq`: Positive. `gain_sq`: Positive. `qgain_sq`: Positive. `kvgain_sq`: Positive.
All inputs are finite; a program needn't handle non-finite values.
Results may differ from a plain program's by a relative error of at most 0.015.
Values may be sent and summed in bfloat16 or wider, within the bound.
No kernel may reach another device: no remote copies, remote signals or barrier semaphores. Data moves between devices by JAX's collectives and lax.ppermute only.
A program may use at most 200 MiB of HBM per device.

v0:
```python
import jax
import jax.numpy as jnp
from jax import lax
from jax.sharding import PartitionSpec as P

D = 2560
NOPE = 64
ROPE = 32
VH = 64
QR = 768
KVR = 256
SLAB = 64
BASIS = 128


norm_eps = 1e-05
residual_scale = 1.4 / 62**0.5
beta_one = 0.9
beta_two = 0.95
adam_eps = 1e-08
gain_rate = 0.5
masked_value = -1e30
highest = lax.Precision.HIGHEST


def for_sending(value):
    return jax.tree.map(lambda a: a.astype(jnp.bfloat16) if a.dtype == jnp.float32 else a, value)


def product(left_side, right_side):
    return jnp.dot(left_side, right_side, preferred_element_type=jnp.float32)


def inner_rows(left_side, right_side):
    return lax.dot_general(
        left_side, right_side, (((0,), (0,)), ((), ())), preferred_element_type=jnp.float32
    )


def against_rows(left_side, right_side):
    return lax.dot_general(
        left_side, right_side, (((1,), (1,)), ((), ())), preferred_element_type=jnp.float32
    )


def gather_features(features):
    return jax.tree.map(
        lambda part, own: part.astype(own.dtype),
        lax.all_gather(for_sending(features), "narrow", axis=1, tiled=True),
        features,
    )


def reduce_features(features):
    return lax.psum_scatter(features, "narrow", scatter_dimension=1, tiled=True)


def row_totals(features):
    return lax.psum(features, "narrow")


def rope_tables(positions):
    half_width = ROPE // 2
    frequency = 10000.0 ** (-2.0 * jnp.arange(half_width, dtype=jnp.float32) / ROPE)
    angles = positions.astype(jnp.float32)[:, None] * frequency[None, :]
    return (jnp.cos(angles), jnp.sin(angles))


def rotate(block_in, cosine_table, sine_table, direction_sign):
    half_width = block_in.shape[-1] // 2
    lower_half = block_in[..., :half_width]
    upper_half = block_in[..., half_width:]
    signed_sine = direction_sign * sine_table
    return jnp.concatenate(
        [
            lower_half * cosine_table - upper_half * signed_sine,
            upper_half * cosine_table + lower_half * signed_sine,
        ],
        axis=-1,
    )


def plain_adam(gradient, moment, square, step_rate, tcount):
    new_moment = beta_one * moment + (1.0 - beta_one) * gradient
    new_square = beta_two * square + (1.0 - beta_two) * gradient * gradient
    direction = (
        new_moment
        / (1.0 - beta_one**tcount)
        / (jnp.sqrt(new_square / (1.0 - beta_two**tcount)) + adam_eps)
    )
    return (-step_rate * direction, new_moment, new_square)


def pack_units(blocks):
    joined = jnp.concatenate(blocks, axis=1)
    return joined.reshape(joined.shape[0], -1, SLAB).transpose(1, 0, 2)


def unpack_units(unit_rows, col_widths):
    joined = unit_rows.transpose(1, 0, 2).reshape(unit_rows.shape[1], -1)
    pieces, begin_col = ([], 0)
    for col_width in col_widths:
        pieces.append(joined[:, begin_col : begin_col + col_width])
        begin_col += col_width
    return pieces


def unit_rates(col_widths, rates):
    return jnp.concatenate(
        [
            jnp.full((col_width // SLAB,), step_rate, jnp.float32)
            for col_width, step_rate in zip(col_widths, rates)
        ]
    )


def owner_step(
    gradient, left_basis, right_basis, moment, square, owner_ids, rate_table, wide_index, tcount
):
    capacity, row_count, _ = gradient.shape
    slot_ids = wide_index * capacity + jnp.arange(capacity, dtype=jnp.int32)
    matches = (owner_ids[None, :] == slot_ids[:, None]).astype(jnp.float32)
    occupied = jnp.sum(matches, axis=1) > 0.5
    slot_rate = jnp.sum(matches * rate_table[None, :], axis=1)
    left_pick = left_basis.reshape(capacity, row_count // BASIS, BASIS, BASIS)
    blocks = gradient.reshape(capacity, row_count // BASIS, BASIS, SLAB)
    turned = jnp.einsum("cbik,cbin->cbkn", left_pick, blocks, precision=highest)
    turned = jnp.einsum("cbkn,cnm->cbkm", turned, right_basis, precision=highest).reshape(
        gradient.shape
    )
    new_moment = beta_one * moment + (1.0 - beta_one) * turned
    new_square = beta_two * square + (1.0 - beta_two) * turned * turned
    direction = (
        new_moment
        / (1.0 - beta_one**tcount)
        / (jnp.sqrt(new_square / (1.0 - beta_two**tcount)) + adam_eps)
    )
    rotated_back = jnp.einsum(
        "cbkm,cnm->cbkn", direction.reshape(blocks.shape), right_basis, precision=highest
    )
    rotated_back = jnp.einsum(
        "cbik,cbkn->cbin", left_pick, rotated_back, precision=highest
    ).reshape(gradient.shape)
    occupied_mask = occupied[:, None, None]
    return (
        -slot_rate[:, None, None] * rotated_back,
        jnp.where(occupied_mask, new_moment, moment),
        jnp.where(occupied_mask, new_square, square),
    )


def body(
    x_in,
    grad_out,
    w_qa,
    w_kv,
    w_kr,
    w_qb,
    w_kvb,
    w_o,
    w_gate,
    w_up,
    w_down,
    norm_gains,
    q_gain,
    kv_gain,
    deal,
    lengths,
    step_count,
    owner_a,
    owner_b,
    owner_c,
    basis_la,
    basis_ra,
    basis_lb,
    basis_rb,
    basis_lc,
    basis_rc,
    mom_a,
    sq_a,
    mom_b,
    sq_b,
    mom_c,
    sq_c,
    kr_mom,
    kr_sq,
    gain_mom,
    gain_sq,
    qgain_mom,
    qgain_sq,
    kvgain_mom,
    kvgain_sq,
):
    wide_count = lax.axis_size("wide")
    wide_index = lax.axis_index("wide")
    row_count = x_in.shape[0]
    piece_rows = row_count // wide_count
    deal_row = lax.dynamic_index_in_dim(deal, wide_index, 0, keepdims=False)
    inverse = jnp.argsort(deal_row)

    def outgoing(features):
        return jnp.take(
            features.reshape((wide_count, piece_rows) + features.shape[1:]), inverse, axis=0
        )

    token_in, token_grad = (
        lax.all_to_all(outgoing(x_in), "wide", split_axis=0, concat_axis=0, tiled=True),
        lax.all_to_all(outgoing(grad_out), "wide", split_axis=0, concat_axis=0, tiled=True),
    )
    residual = token_in.reshape(row_count, -1).astype(jnp.float32)
    grad_top = token_grad.reshape(row_count, -1).astype(jnp.float32)
    local_width = residual.shape[1]
    seq_lengths = lengths[0]
    seq_ends = jnp.cumsum(seq_lengths)
    row_ids = jnp.arange(row_count, dtype=jnp.int32)
    segment = jnp.sum((row_ids[:, None] >= seq_ends[None, :-1]).astype(jnp.int32), axis=1)
    pick = jnp.arange(seq_lengths.shape[0], dtype=jnp.int32)[None, :] == segment[:, None]
    seq_start = jnp.sum(jnp.where(pick, (seq_ends - seq_lengths)[None, :], 0), axis=1)
    live_rows = (segment < seq_lengths.shape[0] - 1).astype(jnp.float32)[:, None]
    cosine_table, sine_table = rope_tables(row_ids - seq_start)
    cos_heads = cosine_table[:, None, :]
    sin_heads = sine_table[:, None, :]
    weights = (
        lax.all_gather(w_qa, "wide", axis=0, tiled=True),
        lax.all_gather(w_kv, "wide", axis=0, tiled=True),
        lax.all_gather(w_kr, "wide", axis=0, tiled=True),
        lax.all_gather(w_qb, "wide", axis=0, tiled=True),
        lax.all_gather(w_kvb, "wide", axis=0, tiled=True),
        lax.all_gather(w_o, "wide", axis=0, tiled=True),
        lax.all_gather(w_gate, "wide", axis=0, tiled=True),
        lax.all_gather(w_up, "wide", axis=0, tiled=True),
        lax.all_gather(w_down, "wide", axis=0, tiled=True),
    )
    full_qa, full_kv, full_kr, full_qb, full_kvb, full_o, full_gate, full_up, full_down = weights
    first_sq = row_totals(jnp.sum(residual * residual, axis=1))
    inv_first = lax.rsqrt(first_sq / D + norm_eps)[:, None]
    normed = gather_features((residual * inv_first * norm_gains[0]).astype(jnp.bfloat16))
    q_latent = product(normed, full_qa)
    kv_latent = product(normed, full_kv)
    key_rot = product(normed, full_kr)
    q_sq, kv_sq = row_totals(
        (jnp.sum(q_latent * q_latent, axis=1), jnp.sum(kv_latent * kv_latent, axis=1))
    )
    inv_q = lax.rsqrt(q_sq / QR + norm_eps)[:, None]
    inv_kv = lax.rsqrt(kv_sq / KVR + norm_eps)[:, None]
    q_normed, kv_normed = gather_features(
        (
            (q_latent * inv_q * q_gain).astype(jnp.bfloat16),
            (kv_latent * inv_kv * kv_gain).astype(jnp.bfloat16),
        )
    )
    heads_here = w_o.shape[1] // VH
    q_pre = product(q_normed, full_qb).reshape(row_count, heads_here, NOPE + ROPE)
    kv_pre = product(kv_normed, full_kvb).reshape(row_count, heads_here, NOPE + VH)
    queries = jnp.concatenate(
        [q_pre[..., :NOPE], rotate(q_pre[..., NOPE:], cos_heads, sin_heads, 1.0)], axis=-1
    ).astype(jnp.bfloat16)
    key_turned = rotate(key_rot, cosine_table, sine_table, 1.0)
    key_heads = jnp.concatenate(
        [
            kv_pre[..., :NOPE],
            jnp.broadcast_to(key_turned[:, None, :], (row_count, heads_here, ROPE)),
        ],
        axis=-1,
    ).astype(jnp.bfloat16)
    values = kv_pre[..., NOPE:].astype(jnp.bfloat16)
    block_rows = min(row_count, 512)
    block_starts = jnp.arange(row_count // block_rows, dtype=jnp.int32) * block_rows
    score_scale = (NOPE + ROPE) ** (-0.5)

    def block_scores(first_row):
        query_ids = first_row + jnp.arange(block_rows, dtype=jnp.int32)
        allowed = (segment[:, None] == segment[None, :]) & (row_ids[None, :] <= query_ids[:, None])
        scores = (
            jnp.einsum("qhd,khd->hqk", queries, key_heads, preferred_element_type=jnp.float32)
            * score_scale
        )
        return (queries, jnp.where(allowed[None], scores, masked_value))

    def attend(first_row):
        _, scores = block_scores(first_row)
        row_max = jnp.max(scores, axis=-1, keepdims=True)
        exp_scores = jnp.exp(scores - row_max)
        row_total = jnp.sum(exp_scores, axis=-1, keepdims=True)
        prob_rows = (exp_scores / row_total).astype(jnp.bfloat16)
        mixed_heads = jnp.einsum(
            "hqk,khd->qhd", prob_rows, values, preferred_element_type=jnp.float32
        )
        return (mixed_heads.astype(jnp.bfloat16), (row_max + jnp.log(row_total))[..., 0])

    heads_out, log_totals = lax.map(attend, block_starts)
    heads_out = heads_out.reshape(row_count, heads_here * VH)
    attn_out = reduce_features(against_rows(heads_out, full_o))
    middle = residual + residual_scale * live_rows * attn_out
    second_sq = row_totals(jnp.sum(middle * middle, axis=1))
    inv_second = lax.rsqrt(second_sq / D + norm_eps)[:, None]
    normed_two = gather_features((middle * inv_second * norm_gains[1]).astype(jnp.bfloat16))
    gate_act = product(normed_two, full_gate)
    upward = product(normed_two, full_up)
    silu_gate = jax.nn.silu(gate_act)
    active = (silu_gate * upward).astype(jnp.bfloat16)
    mlp_out = reduce_features(against_rows(active, full_down))
    layer_out = middle + residual_scale * live_rows * mlp_out
    weights = (
        lax.all_gather(w_qa, "wide", axis=0, tiled=True),
        lax.all_gather(w_kv, "wide", axis=0, tiled=True),
        lax.all_gather(w_kr, "wide", axis=0, tiled=True),
        lax.all_gather(w_qb, "wide", axis=0, tiled=True),
        lax.all_gather(w_kvb, "wide", axis=0, tiled=True),
        lax.all_gather(w_o, "wide", axis=0, tiled=True),
        lax.all_gather(w_gate, "wide", axis=0, tiled=True),
        lax.all_gather(w_up, "wide", axis=0, tiled=True),
        lax.all_gather(w_down, "wide", axis=0, tiled=True),
    )
    full_qa, full_kv, full_kr, full_qb, full_kvb, full_o, full_gate, full_up, full_down = weights
    mlp_grad = gather_features((residual_scale * live_rows * grad_top).astype(jnp.bfloat16))
    grad_down = inner_rows(mlp_grad, active)
    active_grad = product(mlp_grad, full_down)
    sigmoid_gate = jax.nn.sigmoid(gate_act)
    gate_grad = (active_grad * upward * (sigmoid_gate + silu_gate * (1.0 - sigmoid_gate))).astype(
        jnp.bfloat16
    )
    up_grad = (active_grad * silu_gate).astype(jnp.bfloat16)
    grad_gate = inner_rows(normed_two, gate_grad)
    grad_up = inner_rows(normed_two, up_grad)
    normed_two_grad = reduce_features(
        against_rows(gate_grad, full_gate) + against_rows(up_grad, full_up)
    )
    post_gain_grad = jnp.sum(normed_two_grad * middle * inv_second, axis=0)
    second_dot = row_totals(jnp.sum(norm_gains[1] * normed_two_grad * middle, axis=1))
    middle_grad = (
        grad_top
        + inv_second * norm_gains[1] * normed_two_grad
        - middle * inv_second**3 * second_dot[:, None] / D
    )
    attn_grad = gather_features((residual_scale * live_rows * middle_grad).astype(jnp.bfloat16))
    grad_o = inner_rows(attn_grad, heads_out)
    heads_grad = product(attn_grad, full_o).astype(jnp.bfloat16).reshape(row_count, heads_here, VH)

    def attend_back(carried, inputs):
        key_grad, value_grad = carried
        first_row, block_lse = inputs
        query_block, scores = block_scores(first_row)
        prob_rows = jnp.exp(scores - block_lse[..., None])
        value_grad = value_grad + jnp.einsum(
            "hqk,qhd->khd",
            prob_rows.astype(jnp.bfloat16),
            heads_grad,
            preferred_element_type=jnp.float32,
        )
        prob_grad = jnp.einsum(
            "qhd,khd->hqk", heads_grad, values, preferred_element_type=jnp.float32
        )
        delta_rows = jnp.sum(prob_rows * prob_grad, axis=-1, keepdims=True)
        score_grad = (prob_rows * (prob_grad - delta_rows)).astype(jnp.bfloat16)
        query_grad = score_scale * jnp.einsum(
            "hqk,khd->qhd", score_grad, key_heads, preferred_element_type=jnp.float32
        )
        key_grad = key_grad + score_scale * jnp.einsum(
            "hqk,qhd->khd", score_grad, query_block, preferred_element_type=jnp.float32
        )
        return ((key_grad, value_grad), query_grad)

    zero_keys = jnp.zeros((row_count, heads_here, NOPE + ROPE), jnp.float32)
    zero_values = jnp.zeros((row_count, heads_here, VH), jnp.float32)
    (key_grad, value_grad), query_grad = lax.scan(
        attend_back, (zero_keys, zero_values), (block_starts, log_totals)
    )
    query_grad = query_grad.reshape(row_count, heads_here, NOPE + ROPE)
    q_pre_grad = jnp.concatenate(
        [query_grad[..., :NOPE], rotate(query_grad[..., NOPE:], cos_heads, sin_heads, -1.0)],
        axis=-1,
    )
    q_pre_grad = q_pre_grad.reshape(row_count, -1).astype(jnp.bfloat16)
    kv_pre_grad = jnp.concatenate([key_grad[..., :NOPE], value_grad], axis=-1)
    kv_pre_grad = kv_pre_grad.reshape(row_count, -1).astype(jnp.bfloat16)
    rot_partial = rotate(jnp.sum(key_grad[..., NOPE:], axis=1), cosine_table, sine_table, -1.0)
    rot_grad = row_totals(rot_partial).astype(jnp.bfloat16)
    grad_qb = inner_rows(q_normed, q_pre_grad)
    grad_kvb = inner_rows(kv_normed, kv_pre_grad)
    q_normed_grad, kv_normed_grad = reduce_features(
        (against_rows(q_pre_grad, full_qb), against_rows(kv_pre_grad, full_kvb))
    )
    q_gain_grad = jnp.sum(q_normed_grad * q_latent * inv_q, axis=0)
    kv_gain_grad = jnp.sum(kv_normed_grad * kv_latent * inv_kv, axis=0)
    q_dot, kv_dot = row_totals(
        (
            jnp.sum(q_gain * q_normed_grad * q_latent, axis=1),
            jnp.sum(kv_gain * kv_normed_grad * kv_latent, axis=1),
        )
    )
    q_latent_grad = (
        inv_q * q_gain * q_normed_grad - q_latent * inv_q**3 * q_dot[:, None] / QR
    ).astype(jnp.bfloat16)
    kv_latent_grad = (
        inv_kv * kv_gain * kv_normed_grad - kv_latent * inv_kv**3 * kv_dot[:, None] / KVR
    ).astype(jnp.bfloat16)
    grad_qa = inner_rows(normed, q_latent_grad)
    grad_kv = inner_rows(normed, kv_latent_grad)
    grad_kr = inner_rows(normed, rot_grad)
    own_kr = lax.dynamic_slice_in_dim(
        full_kr, lax.axis_index("narrow") * local_width, local_width, 0
    )
    normed_grad = reduce_features(
        against_rows(q_latent_grad, full_qa) + against_rows(kv_latent_grad, full_kv)
    ) + against_rows(rot_grad, own_kr)
    in_gain_grad = jnp.sum(normed_grad * residual * inv_first, axis=0)
    first_dot = row_totals(jnp.sum(norm_gains[0] * normed_grad * residual, axis=1))
    input_grad = (
        middle_grad
        + inv_first * norm_gains[0] * normed_grad
        - residual * inv_first**3 * first_dot[:, None] / D
    )
    back_out, back_grad = (
        lax.all_to_all(
            layer_out.reshape(wide_count, piece_rows, -1),
            "wide",
            split_axis=0,
            concat_axis=0,
            tiled=True,
        ),
        lax.all_to_all(
            input_grad.reshape(wide_count, piece_rows, -1),
            "wide",
            split_axis=0,
            concat_axis=0,
            tiled=True,
        ),
    )
    final_out = jnp.take(back_out, deal_row, axis=0).reshape(row_count, -1)
    final_grad = jnp.take(back_grad, deal_row, axis=0).reshape(row_count, -1)
    summed = (
        lax.psum_scatter(grad_qa, "wide", scatter_dimension=0, tiled=True),
        lax.psum_scatter(grad_kv, "wide", scatter_dimension=0, tiled=True),
        lax.psum_scatter(grad_kr, "wide", scatter_dimension=0, tiled=True),
        lax.psum_scatter(grad_qb, "wide", scatter_dimension=0, tiled=True),
        lax.psum_scatter(grad_kvb, "wide", scatter_dimension=0, tiled=True),
        lax.psum_scatter(grad_o, "wide", scatter_dimension=0, tiled=True),
        lax.psum_scatter(grad_gate, "wide", scatter_dimension=0, tiled=True),
        lax.psum_scatter(grad_up, "wide", scatter_dimension=0, tiled=True),
        lax.psum_scatter(grad_down, "wide", scatter_dimension=0, tiled=True),
    )
    block_qa, block_kv, block_kr, block_qb, block_kvb, block_o, block_gate, block_up, block_down = (
        summed
    )
    gains_total, qgain_total, kvgain_total = lax.psum(
        (jnp.stack([in_gain_grad, post_gain_grad]), q_gain_grad, kv_gain_grad), "wide"
    )
    tcount = step_count[0].astype(jnp.float32)
    wide_rate = D ** (-0.5)
    class_a = [block_qa, block_kv, block_o, block_gate, block_up, block_down]
    widths_a = [block.shape[1] for block in class_a]
    rates_a = unit_rates(widths_a, [wide_rate, wide_rate, 1.0, wide_rate, wide_rate, 0.125])
    rates_b = unit_rates([block_qb.shape[1]], [QR ** (-0.5)])
    rates_c = unit_rates([block_kvb.shape[1]], [KVR ** (-0.5)])
    owners_a, owners_b, owners_c = (owner_a[0], owner_b[0], owner_c[0])

    def send_buffer(blocks, owner_ids, capacity):
        unit_rows = pack_units(blocks)
        empty = jnp.zeros((wide_count * capacity,) + unit_rows.shape[1:], jnp.float32)
        return empty.at[owner_ids].set(unit_rows)

    owned_a, owned_b, owned_c = (
        lax.all_to_all(
            send_buffer(class_a, owners_a, mom_a.shape[0]),
            "wide",
            split_axis=0,
            concat_axis=1,
            tiled=True,
        ),
        lax.all_to_all(
            send_buffer([block_qb], owners_b, mom_b.shape[0]),
            "wide",
            split_axis=0,
            concat_axis=1,
            tiled=True,
        ),
        lax.all_to_all(
            send_buffer([block_kvb], owners_c, mom_c.shape[0]),
            "wide",
            split_axis=0,
            concat_axis=1,
            tiled=True,
        ),
    )
    change_a, new_mom_a, new_sq_a = owner_step(
        owned_a, basis_la, basis_ra, mom_a, sq_a, owners_a, rates_a, wide_index, tcount
    )
    change_b, new_mom_b, new_sq_b = owner_step(
        owned_b, basis_lb, basis_rb, mom_b, sq_b, owners_b, rates_b, wide_index, tcount
    )
    change_c, new_mom_c, new_sq_c = owner_step(
        owned_c, basis_lc, basis_rc, mom_c, sq_c, owners_c, rates_c, wide_index, tcount
    )
    back_a, back_b, back_c = (
        lax.all_to_all(
            change_a.astype(jnp.bfloat16), "wide", split_axis=1, concat_axis=0, tiled=True
        ).astype(change_a.dtype),
        lax.all_to_all(
            change_b.astype(jnp.bfloat16), "wide", split_axis=1, concat_axis=0, tiled=True
        ).astype(change_b.dtype),
        lax.all_to_all(
            change_c.astype(jnp.bfloat16), "wide", split_axis=1, concat_axis=0, tiled=True
        ).astype(change_c.dtype),
    )
    updates_a = unpack_units(jnp.take(back_a, owners_a, axis=0), widths_a)
    update_qb = unpack_units(jnp.take(back_b, owners_b, axis=0), [block_qb.shape[1]])[0]
    update_kvb = unpack_units(jnp.take(back_c, owners_c, axis=0), [block_kvb.shape[1]])[0]
    update_kr, new_kr_mom, new_kr_sq = plain_adam(block_kr, kr_mom, kr_sq, wide_rate, tcount)
    update_gains, new_gain_mom, new_gain_sq = plain_adam(
        gains_total, gain_mom, gain_sq, gain_rate, tcount
    )
    update_qgain, new_qgain_mom, new_qgain_sq = plain_adam(
        qgain_total, qgain_mom, qgain_sq, gain_rate, tcount
    )
    update_kvgain, new_kvgain_mom, new_kvgain_sq = plain_adam(
        kvgain_total, kvgain_mom, kvgain_sq, gain_rate, tcount
    )
    return (
        final_out,
        final_grad,
        block_qa,
        block_kv,
        block_qb,
        block_kvb,
        block_o,
        block_gate,
        block_up,
        block_down,
        w_qa.astype(jnp.float32) + updates_a[0],
        w_kv.astype(jnp.float32) + updates_a[1],
        w_qb.astype(jnp.float32) + update_qb,
        w_kvb.astype(jnp.float32) + update_kvb,
        w_o.astype(jnp.float32) + updates_a[2],
        w_gate.astype(jnp.float32) + updates_a[3],
        w_up.astype(jnp.float32) + updates_a[4],
        w_down.astype(jnp.float32) + updates_a[5],
        block_kr,
        w_kr.astype(jnp.float32) + update_kr,
        new_kr_mom,
        new_kr_sq,
        gains_total,
        norm_gains + update_gains,
        new_gain_mom,
        new_gain_sq,
        qgain_total,
        q_gain + update_qgain,
        new_qgain_mom,
        new_qgain_sq,
        kvgain_total,
        kv_gain + update_kvgain,
        new_kvgain_mom,
        new_kvgain_sq,
        new_mom_a,
        new_sq_a,
        new_mom_b,
        new_sq_b,
        new_mom_c,
        new_sq_c,
    )


def solution(mesh):
    return jax.shard_map(
        body,
        mesh=mesh,
        in_specs=(
            P("wide", "narrow"),
            P("wide", "narrow"),
            P("wide", "narrow"),
            P("wide", "narrow"),
            P("wide", None),
            P("wide", "narrow"),
            P("wide", "narrow"),
            P("wide", "narrow"),
            P("wide", "narrow"),
            P("wide", "narrow"),
            P("wide", "narrow"),
            P(None, "narrow"),
            P("narrow"),
            P("narrow"),
            P(),
            P("wide", None),
            P(),
            P("narrow", None),
            P("narrow", None),
            P("narrow", None),
            P("wide", None, "narrow"),
            P("wide", None, "narrow"),
            P("wide", None, "narrow"),
            P("wide", None, "narrow"),
            P("wide", None, "narrow"),
            P("wide", None, "narrow"),
            P("wide", None, "narrow"),
            P("wide", None, "narrow"),
            P("wide", None, "narrow"),
            P("wide", None, "narrow"),
            P("wide", None, "narrow"),
            P("wide", None, "narrow"),
            P("wide", None),
            P("wide", None),
            P(None, "narrow"),
            P(None, "narrow"),
            P("narrow"),
            P("narrow"),
            P("narrow"),
            P("narrow"),
        ),
        out_specs=(
            P("wide", "narrow"),
            P("wide", "narrow"),
            P("wide", "narrow"),
            P("wide", "narrow"),
            P("wide", "narrow"),
            P("wide", "narrow"),
            P("wide", "narrow"),
            P("wide", "narrow"),
            P("wide", "narrow"),
            P("wide", "narrow"),
            P("wide", "narrow"),
            P("wide", "narrow"),
            P("wide", "narrow"),
            P("wide", "narrow"),
            P("wide", "narrow"),
            P("wide", "narrow"),
            P("wide", "narrow"),
            P("wide", "narrow"),
            P("wide", None),
            P("wide", None),
            P("wide", None),
            P("wide", None),
            P(None, "narrow"),
            P(None, "narrow"),
            P(None, "narrow"),
            P(None, "narrow"),
            P("narrow"),
            P("narrow"),
            P("narrow"),
            P("narrow"),
            P("narrow"),
            P("narrow"),
            P("narrow"),
            P("narrow"),
            P("wide", None, "narrow"),
            P("wide", None, "narrow"),
            P("wide", None, "narrow"),
            P("wide", None, "narrow"),
            P("wide", None, "narrow"),
            P("wide", None, "narrow"),
        ),
        check_vma=False,
    )
```

profile of v0, /device:TPU:11, one launch (start us, length us, event | category | flops | bytes accessed | tf_op | source)
XLA Modules:
  0.0 2147.4 jit_solution(8041773173814373825)
XLA Ops:
  19.1 9.6 all-to-all-done
  29.0 7.0 psum.84
  39.4 13.5 all-gather.1
  55.1 8.9 all-gather
  66.4 9.8 all_gather.57
  76.2 8.6 all-gather.2
  97.8 9.6 all-reduce.2
  109.0 9.6 all_gather.56
  125.6 16.2 all_gather.59
  155.9 6.7 fusion.108
  163.2 11.6 all-to-all-start.2
  174.8 9.7 all-to-all-done.2
  185.4 79.4 %reduce-scatter.22.cloned.1.call-done = f32[512,640]{1,0:T(8,128)} async-done(((f32[512,2560]{1,0:T(8,128)}), f32[512,640]{1,0:T(8,128)}) %reduce-scatter.22.cloned.1.call-update) | async-done | bytes 1310736 | tf_op jit(solution)/shard_map/reduce_scatter | solution.py:55
  267.4 7.4 psum.87
  278.6 43.8 %all-gather.21.cloned.1.call-done = bf16[2560,1600]{1,0:T(8,128)(2,1)} async-done(((bf16[320,1600]{1,0:T(8,128)(2,1)}), bf16[2560,1600]{1,0:T(8,128)(2,1)}) %all-gather.21.cloned.1.call-update) | async-done | bytes 8192016 | tf_op jit(solution)/shard_map/all_gather | solution.py:230
  322.3 54.5 %all-gather.19.cloned.1.call-done = bf16[512,2560]{1,0:T(8,128)(2,1)} async-done(((bf16[512,640]{1,0:T(8,128)(2,1)}), bf16[512,2560]{1,0:T(8,128)(2,1)}) %all-gather.19.cloned.1.call-update) | async-done | bytes 2621456 | tf_op jit(solution)/shard_map/all_gather | solution.py:49
  376.8 10.5 fusion.109
  387.3 47.3 %all-gather.23.cloned.1.call-done = bf16[2560,1600]{1,0:T(8,128)(2,1)} async-done(((bf16[320,1600]{1,0:T(8,128)(2,1)}), bf16[2560,1600]{1,0:T(8,128)(2,1)}) %all-gather.23.cloned.1.call-update) | async-done | bytes 8192016 | tf_op jit(solution)/shard_map/all_gather | solution.py:231
  434.6 10.4 fusion.110
  445.0 46.4 %all-gather.25.cloned.1.call-done = bf16[2560,1600]{1,0:T(8,128)(2,1)} async-done(((bf16[320,1600]{1,0:T(8,128)(2,1)}), bf16[2560,1600]{1,0:T(8,128)(2,1)}) %all-gather.25.cloned.1.call-update) | async-done | bytes 8192016 | tf_op jit(solution)/shard_map/all_gather | solution.py:232
  491.5 54.7 %all-gather.27.cloned.1.call-done = bf16[512,2560]{1,0:T(8,128)(2,1)} async-done(((bf16[512,640]{1,0:T(8,128)(2,1)}), bf16[512,2560]{1,0:T(8,128)(2,1)}) %all-gather.27.cloned.1.call-update) | async-done | bytes 2621456 | tf_op jit(solution)/shard_map/all_gather | solution.py:49
  546.1 14.3 multiply_convert_fusion.1
  560.5 8.1 fusion.112
  575.5 11.3 fusion.111
  586.8 83.0 %reduce-scatter.26.cloned.1.call-done = f32[512,640]{1,0:T(8,128)} async-done(((f32[512,2560]{1,0:T(8,128)}), f32[512,640]{1,0:T(8,128)}) %reduce-scatter.26.cloned.1.call-update) | async-done | bytes 1310736 | tf_op jit(solution)/shard_map/reduce_scatter | solution.py:55
  672.2 7.4 psum.88
  679.5 87.0 %reduce-scatter.24.cloned.1.call-done = f32[512,640]{1,0:T(8,128)} async-done(((f32[512,2560]{1,0:T(8,128)}), f32[512,640]{1,0:T(8,128)}) %reduce-scatter.24.cloned.1.call-update) | async-done | bytes 1310736 | tf_op jit(solution)/shard_map/reduce_scatter | solution.py:55
  771.6 52.4 %all-gather.29.cloned.1.call-done = bf16[512,2560]{1,0:T(8,128)(2,1)} async-done(((bf16[512,640]{1,0:T(8,128)(2,1)}), bf16[512,2560]{1,0:T(8,128)(2,1)}) %all-gather.29.cloned.1.call-update) | async-done | bytes 2621456 | tf_op jit(solution)/shard_map/all_gather | solution.py:49
  872.2 36.7 %reduce-scatter.28.cloned.1.call-done = f32[512,192]{0,1:T(8,128)} async-done(((f32[512,768]{0,1:T(8,128)}), f32[512,192]{0,1:T(8,128)}) %reduce-scatter.28.cloned.1.call-update) | async-done | bytes 393232 | tf_op jit(solution)/shard_map/reduce_scatter | solution.py:55
  910.6 13.2 all-reduce.1
  935.1 6.8 fusion.116
  941.9 13.1 fusion.117
  955.3 14.1 fusion.118
  969.4 13.4 fusion.119
  992.6 7.5 all-to-all-start.8
  1010.4 32.2 %reduce-scatter.48.cloned.1.call-done = f32[320,64]{1,0:T(8,128)} async-done(((f32[2560,64]{1,0:T(8,128)}), f32[320,64]{1,0:T(8,128)}) %reduce-scatter.48.cloned.1.call-update) | async-done | bytes 81936 | tf_op jit(solution)/shard_map/reduce_scatter | solution.py:434
  1042.6 47.3 %reduce-scatter.46.cloned.1.call-done = f32[320,192]{1,0:T(8,128)} async-done(((f32[2560,192]{1,0:T(8,128)}), f32[320,192]{1,0:T(8,128)}) %reduce-scatter.46.cloned.1.call-update) | async-done | bytes 245776 | tf_op jit(solution)/shard_map/reduce_scatter | solution.py:433
  1089.9 68.0 %reduce-scatter.38.cloned.1.call-done = f32[320,640]{1,0:T(8,128)} async-done(((f32[2560,640]{1,0:T(8,128)}), f32[320,640]{1,0:T(8,128)}) %reduce-scatter.38.cloned.1.call-update) | async-done | bytes 819216 | tf_op jit(solution)/shard_map/reduce_scatter | solution.py:438
  1157.9 121.5 %reduce-scatter.40.cloned.1.call-done = f32[320,1600]{1,0:T(8,128)} async-done(((f32[2560,1600]{1,0:T(8,128)}), f32[320,1600]{1,0:T(8,128)}) %reduce-scatter.40.cloned.1.call-update) | async-done | bytes 2048016 | tf_op jit(solution)/shard_map/reduce_scatter | solution.py:439
  1279.3 121.7 %reduce-scatter.42.cloned.1.call-done = f32[320,1600]{1,0:T(8,128)} async-done(((f32[2560,1600]{1,0:T(8,128)}), f32[320,1600]{1,0:T(8,128)}) %reduce-scatter.42.cloned.1.call-update) | async-done | bytes 2048016 | tf_op jit(solution)/shard_map/reduce_scatter | solution.py:440
  1401.0 121.7 %reduce-scatter.44.cloned.1.call-done = f32[320,1600]{1,0:T(8,128)} async-done(((f32[2560,1600]{1,0:T(8,128)}), f32[320,1600]{1,0:T(8,128)}) %reduce-scatter.44.cloned.1.call-update) | async-done | bytes 2048016 | tf_op jit(solution)/shard_map/reduce_scatter | solution.py:441
  1522.7 8.7 concatenate.31
  1531.4 9.2 copy.350
  1547.1 20.6 scatter_fusion
  1592.0 26.9 %reduce-scatter.32.cloned.1.call-done = f32[512,640]{1,0:T(8,128)} async-done(((f32[512,2560]{1,0:T(8,128)}), f32[512,640]{1,0:T(8,128)}) %reduce-scatter.32.cloned.1.call-update) | async-done | bytes 1310736 | tf_op jit(solution)/shard_map/reduce_scatter | solution.py:55
  1621.6 7.8 psum.92
  1632.1 87.9 %all-to-all-done.4 = f32[136,320,64]{1,2,0:T(8,128)} async-done(((f32[136,320,64]{1,2,0:T(8,128)}), f32[136,320,64]{1,2,0:T(8,128)}, u32[]{:S(2)}, u32[]{:S(2)}) %all-to-all-start.4) | async-done | bytes 11141152 | tf_op jit(solution)/shard_map/all_to_all | solution.py:464
  1726.0 20.3 copy.474
  1746.3 17.1 reshape.552
  1763.4 29.2 %fusion.8 = f32[17,20,64,128]{3,2,1,0:T(8,128)S(1)} fusion(f32[17,20,128,128]{3,2,1,0:T(8,128)} %bitcast.341, f32[17,20,128,64]{2,1,3,0:T(8,128)} %reshape.552), kind=kOutput, calls=%fused_computation.22 | convolution fusion | flops 4278190080 | bytes 44564480 | tf_op jit(solution)/shard_map/cbik,cbin->cbkn/dot_general | solution.py:127
  1792.6 12.4 fusion.18
  1805.0 22.6 %fusion.13 = (f32[17,2560,64]{1,2,0:T(8,128)}, f32[17,8,20,8,128]{4,3,2,1,0:T(8,128)}, f32[17,2560,64]{1,2,0:T(8,128)}) fusion(f32[17,2560,64]{1,2,0:T(8,128)} %param.71, f32[17,20,8,8,128]{4,3,2,1,0:T(8,128)} %fusion.18, pred[17]{0:T(512)(128)(4,1)S(1)} %broadcast_compare_fusion.2, f32[]{:T(128)} %bitcast.39, f32[]{:T(128)} %bitcast.38, ...), kind=kLoop, calls=%fused_computation.34 | loop fusion | flops 36208640 | bytes 66846744 | tf_op jit(solution)/shard_map/jit(_where)/select_n | solution.py:148
  1832.0 15.5 fusion.3
  1852.3 48.1 %convolution_bitcast_fusion = f32[17,20,8,8,128]{4,3,2,1,0:T(8,128)} fusion(f32[17,20,128,64]{2,3,1,0:T(8,128)} %fusion.3, f32[17,20,128,128]{3,2,1,0:T(8,128)} %bitcast.342), kind=kOutput, calls=%fused_computation.42 | convolution fusion | flops 4278190080 | bytes 44564480 | tf_op jit(solution)/shard_map/cbik,cbkn->cbin/dot_general | solution.py:141
  1905.6 7.7 fusion.1
  1913.3 16.8 copy.357
  1930.1 13.3 reshape.693
  1975.7 41.1 %reduce-scatter.50.cloned.1.call-done = f32[320,32]{1,0:T(8,128)} async-done(((f32[2560,32]{1,0:T(8,128)}), f32[320,32]{1,0:T(8,128)}) %reduce-scatter.50.cloned.1.call-update) | async-done | bytes 40976
  2031.5 11.6 all-reduce
  2052.4 14.8 reshape.694
  2067.2 16.9 copy.358
  2084.1 11.9 reshape.578
  2096.0 12.2 copy.359
  2108.2 9.4 gather_fusion
  (471 shorter events, 292.6 us)
Async XLA Ops:
  7.2 1576.4 %copy-start = (f32[3,768,128]{2,1,0:T(8,128)S(1)}, f32[3,768,128]{2,1,0:T(8,128)}, u32[]{:S(2)}) copy-start(f32[3,768,128]{2,1,0:T(8,128)} %param.66) | copy-start | bytes 3538948
  14.4 24.8 %copy-start.100 = (s32[1,4]{1,0:T(1,128)S(1)}, s32[1,4]{1,0:T(1,128)}, u32[]{:S(2)}) copy-start(s32[1,4]{1,0:T(1,128)} %param.59) | copy-start | bytes 52
  14.4 25.0 %copy-start.46 = (bf16[320,192]{0,1:T(8,128)(2,1)S(1)}, bf16[320,192]{0,1:T(8,128)(2,1)}, u32[]{:S(2)}) copy-start(bf16[320,192]{0,1:T(8,128)(2,1)} %param.46) | copy-start | bytes 368644
  14.4 14.3 all-to-all-start
  19.1 73.5 %all-gather.13.cloned.1.call-start = ((), (), s32[]{:S(2)}) async-start(), calls=%async_computation.25 | async-start | bytes 3276800 | tf_op jit(solution)/shard_map/all_gather | solution.py:49
  19.1 20.3 copy-start.68
  28.7 236.0 %copy-start.5 = (bf16[8,64,640]{2,1,0:T(8,128)(2,1)}, bf16[8,64,640]{2,1,0:T(8,128)(2,1)S(1)}, u32[]{:S(2)}) copy-start(bf16[8,64,640]{2,1,0:T(8,128)(2,1)S(1)} %all-to-all-done) | copy-start | bytes 1966084
  37.6 104.2 %all-gather.15.cloned.1.call-start = ((), (), s32[]{:S(2)}) async-start(), calls=%async_computation.26 | async-start | bytes 1769472 | tf_op jit(solution)/shard_map/all_gather | solution.py:227
  38.4 117.5 %all-gather.17.cloned.1.call-start = ((), (), s32[]{:S(2)}) async-start(), calls=%async_computation.27 | async-start | bytes 3686400 | tf_op jit(solution)/shard_map/all_gather | solution.py:229
  39.1 225.6 %reduce-scatter.22.cloned.1.call-start = ((), (), s32[]{:S(2)}) async-start(), calls=%async_computation.28 | async-start | bytes 6553600 | tf_op jit(solution)/shard_map/reduce_scatter | solution.py:55
  39.4 48.0 %copy-start.84 = (f32[16]{0:T(128)}, f32[16]{0:T(128)S(1)}, u32[]{:S(2)}) copy-start(f32[16]{0:T(128)S(1)} %multiply_power_fusion) | copy-start | bytes 196
  39.4 15.7 copy-start.57
  53.6 22.6 %copy-start.66 = (bf16[320,32]{0,1:T(8,128)(2,1)S(1)}, bf16[320,32]{0,1:T(8,128)(2,1)}, u32[]{:S(2)}) copy-start(bf16[320,32]{0,1:T(8,128)(2,1)} %param.48) | copy-start | bytes 61444
  66.4 29.7 %copy-start.70 = (f32[512]{0:T(512)}, f32[512]{0:T(512)S(1)}, u32[]{:S(2)}) copy-start(f32[512]{0:T(512)S(1)} %subtract_convert_fusion.4) | copy-start | bytes 6148
  76.2 42.4 %copy-start.9 = (bf16[256,1280]{1,0:T(8,128)(2,1)}, bf16[256,1280]{1,0:T(8,128)(2,1)S(1)}, u32[]{:S(2)}) copy-start(bf16[256,1280]{1,0:T(8,128)(2,1)S(1)} %all_gather.57) | copy-start | bytes 1966084
  122.5 27.3 %copy-start.12 = (bf16[512,1280]{0,1:T(8,128)(2,1)}, bf16[512,1280]{0,1:T(8,128)(2,1)S(1)}, u32[]{:S(2)}) copy-start(bf16[512,1280]{0,1:T(8,128)(2,1)S(1)} %copy.340) | copy-start | bytes 3932164
  162.6 159.7 %all-gather.21.cloned.1.call-start = ((), (), s32[]{:S(2)}) async-start(), calls=%async_computation.30 | async-start | bytes 9584640 | tf_op jit(solution)/shard_map/all_gather | solution.py:230
  163.2 21.3 all-to-all-start.2
  174.8 202.0 %all-gather.19.cloned.1.call-start = ((), (), s32[]{:S(2)}) async-start(), calls=%async_computation.29 | async-start | bytes 3276800 | tf_op jit(solution)/shard_map/all_gather | solution.py:49
  275.9 158.7 %all-gather.23.cloned.1.call-start = ((), (), s32[]{:S(2)}) async-start(), calls=%async_computation.31 | async-start | bytes 9584640 | tf_op jit(solution)/shard_map/all_gather | solution.py:231
  276.6 214.8 %all-gather.25.cloned.1.call-start = ((), (), s32[]{:S(2)}) async-start(), calls=%async_computation.32 | async-start | bytes 9584640 | tf_op jit(solution)/shard_map/all_gather | solution.py:232
  277.4 268.8 %all-gather.27.cloned.1.call-start = ((), (), s32[]{:S(2)}) async-start(), calls=%async_computation.34 | async-start | bytes 3276800 | tf_op jit(solution)/shard_map/all_gather | solution.py:49
  278.1 391.8 %reduce-scatter.26.cloned.1.call-start = ((), (), s32[]{:S(2)}) async-start(), calls=%async_computation.35 | async-start | bytes 6553600 | tf_op jit(solution)/shard_map/reduce_scatter | solution.py:55
  546.1 22.5 %slice-start.3 = ((s8[8519680]{0:T(1024)(128)(4,1)}), s8[131072]{0:T(1024)(128)(4,1)S(1)}, s32[]{:S(2)}) async-start(s8[8519680]{0:T(1024)(128)(4,1)} %bitcast.395), calls=%async_computation.52 | async-start | bytes 262144
  546.1 22.5 %slice-start.4 = ((s8[8519680]{0:T(1024)(128)(4,1)}), s8[4194304]{0:T(1024)(128)(4,1)S(1)}, s32[]{:S(2)}) async-start(s8[8519680]{0:T(1024)(128)(4,1)} %bitcast.395), calls=%async_computation.53 | async-start | bytes 8388608
  575.4 191.1 %reduce-scatter.24.cloned.1.call-start = ((), (), s32[]{:S(2)}) async-start(), calls=%async_computation.33 | async-start | bytes 6553600 | tf_op jit(solution)/shard_map/reduce_scatter | solution.py:55
  586.8 179.8 %copy-start.8 = (bf16[8,64,640]{2,1,0:T(8,128)(2,1)S(1)}, bf16[8,64,640]{2,1,0:T(8,128)(2,1)}, u32[]{:S(2)}) copy-start(bf16[8,64,640]{2,1,0:T(8,128)(2,1)} %copy-done.7) | copy-start | bytes 1966084
  586.8 237.3 %all-gather.29.cloned.1.call-start = ((), (), s32[]{:S(2)}) async-start(), calls=%async_computation.36 | async-start | bytes 3276800 | tf_op jit(solution)/shard_map/all_gather | solution.py:49
  770.5 100.0 %reduce-scatter.30.cloned.1.call-start = ((), (), s32[]{:S(2)}) async-start(), calls=%async_computation.38 | async-start | bytes 655360 | tf_op jit(solution)/shard_map/reduce_scatter | solution.py:55
  771.6 59.5 %copy-start.13 = (bf16[512,1280]{0,1:T(8,128)(2,1)S(1)}, bf16[512,1280]{0,1:T(8,128)(2,1)}, u32[]{:S(2)}) copy-start(bf16[512,1280]{0,1:T(8,128)(2,1)} %copy-done.12) | copy-start | bytes 3932164
  852.2 56.7 %reduce-scatter.28.cloned.1.call-start = ((), (), s32[]{:S(2)}) async-start(), calls=%async_computation.37 | async-start | bytes 1966080 | tf_op jit(solution)/shard_map/reduce_scatter | solution.py:55
  859.2 129.5 %reduce-scatter.36.cloned.1.call-start = ((), (), s32[]{:S(2)}) async-start(), calls=%async_computation.41 | async-start | bytes 1474560 | tf_op jit(solution)/shard_map/reduce_scatter | solution.py:437
  861.9 139.5 %reduce-scatter.34.cloned.1.call-start = ((), (), s32[]{:S(2)}) async-start(), calls=%async_computation.40 | async-start | bytes 3538944 | tf_op jit(solution)/shard_map/reduce_scatter | solution.py:436
  865.7 43.2 %copy-start.22 = (f32[512,192]{0,1:T(8,128)S(1)}, f32[512,192]{0,1:T(8,128)}, u32[]{:S(2)}) copy-start(f32[512,192]{0,1:T(8,128)} %get-tuple-element.466) | copy-start | bytes 1179652
  865.8 43.2 %copy-start.76 = (f32[192]{0:T(256)S(1)}, f32[192]{0:T(256)}, u32[]{:S(2)}) copy-start(f32[192]{0:T(256)} %param.56) | copy-start | bytes 2308
  865.8 58.0 %copy-start.81 = (f32[512]{0:T(512)S(1)}, f32[512]{0:T(512)}, u32[]{:S(2)}) copy-start(f32[512]{0:T(512)} %get-tuple-element.452) | copy-start | bytes 6148
  865.8 176.8 %reduce-scatter.48.cloned.1.call-start = ((), (), s32[]{:S(2)}) async-start(), calls=%async_computation.47 | async-start | bytes 1474560 | tf_op jit(solution)/shard_map/reduce_scatter | solution.py:434
  923.8 695.2 %copy-start.60 = (bf16[512,32]{0,1:T(8,128)(2,1)}, bf16[512,32]{0,1:T(8,128)(2,1)S(1)}, u32[]{:S(2)}) copy-start(bf16[512,32]{0,1:T(8,128)(2,1)S(1)} %get-tuple-element.402) | copy-start | bytes 98308
  928.9 161.0 %reduce-scatter.46.cloned.1.call-start = ((), (), s32[]{:S(2)}) async-start(), calls=%async_computation.46 | async-start | bytes 2949120 | tf_op jit(solution)/shard_map/reduce_scatter | solution.py:433
  933.9 224.0 %reduce-scatter.38.cloned.1.call-start = ((), (), s32[]{:S(2)}) async-start(), calls=%async_computation.42 | async-start | bytes 7372800 | tf_op jit(solution)/shard_map/reduce_scatter | solution.py:438
  941.9 337.5 %reduce-scatter.40.cloned.1.call-start = ((), (), s32[]{:S(2)}) async-start(), calls=%async_computation.43 | async-start | bytes 19169280 | tf_op jit(solution)/shard_map/reduce_scatter | solution.py:439
  955.0 446.0 %reduce-scatter.42.cloned.1.call-start = ((), (), s32[]{:S(2)}) async-start(), calls=%async_computation.44 | async-start | bytes 19169280 | tf_op jit(solution)/shard_map/reduce_scatter | solution.py:440
  969.3 553.3 %reduce-scatter.44.cloned.1.call-start = ((), (), s32[]{:S(2)}) async-start(), calls=%async_computation.45 | async-start | bytes 19169280 | tf_op jit(solution)/shard_map/reduce_scatter | solution.py:441
  982.8 636.1 %reduce-scatter.32.cloned.1.call-start = ((), (), s32[]{:S(2)}) async-start(), calls=%async_computation.39 | async-start | bytes 6553600 | tf_op jit(solution)/shard_map/reduce_scatter | solution.py:55
  988.7 14.8 copy-start.87
  992.6 13.5 all-to-all-start.8
  1006.0 561.7 %all-to-all-start.6 = ((f32[24,96,64]{1,2,0:T(8,128)}), f32[24,96,64]{1,2,0:T(8,128)S(1)}, u32[]{:S(2)}, u32[]{:S(2)}) async-start(f32[24,96,64]{1,2,0:T(8,128)} %scatter_fusion.1), calls=%async_computation.18 | async-start | bytes 1572864 | tf_op jit(solution)/shard_map/all_to_all | solution.py:471
  1010.4 536.7 %copy-start.89 = (s32[89]{0:T(128)}, s32[89]{0:T(128)S(1)}, u32[]{:S(2)}) copy-start(s32[89]{0:T(128)S(1)} %fusion.92) | copy-start | bytes 1072
  1567.8 152.3 %all-to-all-start.4 = ((f32[136,320,64]{1,2,0:T(8,128)}), f32[136,320,64]{1,2,0:T(8,128)}, u32[]{:S(2)}, u32[]{:S(2)}) async-start(f32[136,320,64]{1,2,0:T(8,128)} %scatter_fusion), calls=%async_computation.16 | async-start | bytes 26738688 | tf_op jit(solution)/shard_map/all_to_all | solution.py:464
  1587.7 31.3 %copy-start.6 = (bf16[8,64,640]{2,1,0:T(8,128)(2,1)S(1)}, bf16[8,64,640]{2,1,0:T(8,128)(2,1)}, u32[]{:S(2)}) copy-start(bf16[8,64,640]{2,1,0:T(8,128)(2,1)} %copy-done.5) | copy-start | bytes 1966084
  1587.7 31.3 %copy-start.69 = (f32[640]{0:T(1024)S(1)}, f32[640]{0:T(1024)}, u32[]{:S(2)}) copy-start(f32[640]{0:T(1024)} %copy-done.68) | copy-start | bytes 7684
  1587.7 31.3 %copy-start.74 = (f32[512]{0:T(512)S(1)}, f32[512]{0:T(512)}, u32[]{:S(2)}) copy-start(f32[512]{0:T(512)} %copy-done.73) | copy-start | bytes 6148
  1590.2 39.2 %copy-start.79 = (f32[512]{0:T(512)S(1)}, f32[512]{0:T(512)}, u32[]{:S(2)}) copy-start(f32[512]{0:T(512)} %get-tuple-element.450) | copy-start | bytes 6148
  1720.0 107.6 %all-to-all-start.1 = ((f32[8,64,640]{2,1,0:T(8,128)}), f32[8,64,640]{2,1,0:T(8,128)}, u32[]{:S(2)}, u32[]{:S(2)}) async-start(f32[8,64,640]{2,1,0:T(8,128)} %bitcast.14), calls=%async_computation.3 | async-start | bytes 2621440 | tf_op jit(solution)/shard_map/all_to_all | solution.py:415
  1763.4 29.2 %copy-start.30 = (f32[17,64,64]{2,1,0:T(8,128)S(1)}, f32[17,64,64]{2,1,0:T(8,128)}, u32[]{:S(2)}) copy-start(f32[17,64,64]{2,1,0:T(8,128)} %param.65) | copy-start | bytes 835588
  1827.6 19.9 all-to-all-start.9
  1848.1 52.3 %all-to-all-start.7 = ((bf16[8,2,9216]{2,1,0:T(2,128)(2,1)}), bf16[8,2,9216]{2,1,0:T(2,128)(2,1)S(1)}, u32[]{:S(2)}, u32[]{:S(2)}) async-start(bf16[8,2,9216]{2,1,0:T(2,128)(2,1)} %reshape.695), calls=%async_computation.19 | async-start | bytes 589824 | tf_op jit(solution)/shard_map/all_to_all | solution.py:499
  1901.2 42.3 %all-to-all-start.3 = ((f32[8,64,640]{2,1,0:T(8,128)}), f32[8,64,640]{2,1,0:T(8,128)S(1)}, u32[]{:S(2)}, u32[]{:S(2)}) async-start(f32[8,64,640]{2,1,0:T(8,128)} %bitcast.362), calls=%async_computation.9 | async-start | bytes 2621440 | tf_op jit(solution)/shard_map/all_to_all | solution.py:422
  1943.5 108.9 %all-to-all-start.5 = ((bf16[8,2,174080]{2,1,0:T(2,128)(2,1)}), bf16[8,2,174080]{2,1,0:T(2,128)(2,1)}, u32[]{:S(2)}, u32[]{:S(2)}) async-start(bf16[8,2,174080]{2,1,0:T(2,128)(2,1)} %reshape.693), calls=%async_computation.17 | async-start | bytes 11141120 | tf_op jit(solution)/shard_map/all_to_all | solution.py:496
  1948.2 68.5 %reduce-scatter.50.cloned.1.call-start = ((), (), s32[]{:S(2)}) async-start(), calls=%async_computation.48 | async-start | bytes 1474560
  1953.8 14.9 copy-start.50
  1973.6 44.1 %copy-start.67 = (bf16[320,32]{0,1:T(8,128)(2,1)S(1)}, bf16[320,32]{0,1:T(8,128)(2,1)}, u32[]{:S(2)}) copy-start(bf16[320,32]{0,1:T(8,128)(2,1)} %param.48) | copy-start | bytes 61444
  1973.6 45.6 %copy-start.38 = (f32[320,64]{1,0:T(8,128)S(1)}, f32[320,64]{1,0:T(8,128)}, u32[]{:S(2)}) copy-start(f32[320,64]{1,0:T(8,128)} %reduce-scatter.48.cloned.1.call-done) | copy-start | bytes 245764
  2028.3 20.5 copy-start.90
  (78 other events, 342.2 us)
Sparse Core Ops, SparseCore 0:
  37.7 54.7 all-gather.12
  94.4 26.5 all-gather.14
  123.0 32.8 all-gather.16
  162.7 101.9 reduce-scatter.21
  266.4 55.8 all-gather.20
  324.3 52.4 all-gather.18
  378.7 55.8 all-gather.22
  436.5 54.9 all-gather.24
  493.6 52.4 all-gather.26
  575.5 94.2 reduce-scatter.25
  672.2 94.3 reduce-scatter.23
  770.7 53.3 all-gather.28
  852.4 18.1 reduce-scatter.29
  873.3 35.5 reduce-scatter.27
  912.6 38.0 reduce-scatter.35
  955.0 46.2 reduce-scatter.33
  1005.3 37.2 reduce-scatter.47
  1046.1 43.7 reduce-scatter.45
  1094.9 62.9 reduce-scatter.37
  1161.9 117.3 reduce-scatter.39
  1283.5 117.4 reduce-scatter.41
  1405.2 117.4 reduce-scatter.43
  1525.0 93.9 reduce-scatter.31
  1973.8 42.8 reduce-scatter.49
where the time goes:
time: 2160 us; the launch traced here: 2150 us
  waiting for transfers between devices  1290 us (60%)
  matrix products  293 us (14%)
  local copies, waits for them, and re-layouts  256 us (12%)
  blocking collectives  130 us (6%)
  other arithmetic  103 us (5%)
  starting transfers between devices  60.7 us (3%)
    reduce_scatter x6, waiting for transfers between devices, reduce_features(): return lax.psum_scatter(features, 'narrow', scatter_dimension=1, tiled=True)  317 us
    all_gather x4, waiting for transfers between devices, gather_features(): lax.all_gather(for_sending(features), 'narrow', axis=1, tiled=True)  166 us
    reduce_scatter x1, waiting for transfers between devices, body(): lax.psum_scatter(grad_up, 'wide', scatter_dimension=0, tiled=True)  122 us
    reduce_scatter x1, waiting for transfers between devices, body(): lax.psum_scatter(grad_down, 'wide', scatter_dimension=0, tiled=True)  122 us
    reduce_scatter x1, waiting for transfers between devices, body(): lax.psum_scatter(grad_gate, 'wide', scatter_dimension=0, tiled=True)  121 us
    all_to_all x1, waiting for transfers between devices, body(): lax.all_to_all(send_buffer(class_a, owners_a, mom_a.shape[0]), 'wide', sp...  87.9 us
    unnamed x240, local copies, waits for them, and re-layouts  72.5 us
    reduce_scatter x1, waiting for transfers between devices, body(): lax.psum_scatter(grad_o, 'wide', scatter_dimension=0, tiled=True)  68 us
  transfers between devices with their start and end apart: 34, of which 24 were waited for; matrix products, arithmetic and copies ran while one was open for 22% of the time, Pallas kernels for 0%

commit v1 on v0

v1 whole, which is shorter than its diff:
```python
import jax
import jax.numpy as jnp
from jax import lax
from jax.experimental import pallas as pl
from jax.experimental.pallas import tpu as pltpu
from jax.sharding import PartitionSpec as P

D = 2560
NOPE = 64
ROPE = 32
VH = 64
QR = 768
KVR = 256
SLAB = 64
BASIS = 128


norm_eps = 1e-05
residual_scale = 1.4 / 62**0.5
beta_one = 0.9
beta_two = 0.95
adam_eps = 1e-08
gain_rate = 0.5
masked_value = -1e30
bf16 = jnp.bfloat16
f32 = jnp.float32


def product(left_side, right_side):
    return jnp.dot(left_side, right_side, preferred_element_type=jnp.float32)


def inner_rows(left_side, right_side):
    return lax.dot_general(
        left_side, right_side, (((0,), (0,)), ((), ())), preferred_element_type=jnp.float32
    )


def against_rows(left_side, right_side):
    return lax.dot_general(
        left_side, right_side, (((1,), (1,)), ((), ())), preferred_element_type=jnp.float32
    )


def rope_tables(positions):
    half_width = ROPE // 2
    frequency = 10000.0 ** (-2.0 * jnp.arange(half_width, dtype=jnp.float32) / ROPE)
    angles = positions.astype(jnp.float32)[:, None] * frequency[None, :]
    return (jnp.cos(angles), jnp.sin(angles))


def rotate(block_in, cosine_table, sine_table, direction_sign):
    half_width = block_in.shape[-1] // 2
    lower_half = block_in[..., :half_width]
    upper_half = block_in[..., half_width:]
    signed_sine = direction_sign * sine_table
    return jnp.concatenate(
        [
            lower_half * cosine_table - upper_half * signed_sine,
            upper_half * cosine_table + lower_half * signed_sine,
        ],
        axis=-1,
    )


def plain_adam(gradient, moment, square, step_rate, tcount):
    new_moment = beta_one * moment + (1.0 - beta_one) * gradient
    new_square = beta_two * square + (1.0 - beta_two) * gradient * gradient
    direction = (
        new_moment
        / (1.0 - beta_one**tcount)
        / (jnp.sqrt(new_square / (1.0 - beta_two**tcount)) + adam_eps)
    )
    return (-step_rate * direction, new_moment, new_square)


def shifted(value, step):
    count = lax.axis_size("narrow")
    return lax.ppermute(value, "narrow", [(i, (i + step) % count) for i in range(count)])


def flipped(value, bit):
    count = lax.axis_size("wide")
    return lax.ppermute(value, "wide", [(i, i ^ bit) for i in range(count)])


def gather_features(features):
    count = lax.axis_size("narrow")
    index = lax.axis_index("narrow")
    width = features.shape[1]
    parts = [features] + [shifted(features, step) for step in range(1, count)]
    joined = jnp.zeros((features.shape[0], count * width), features.dtype)
    for step, part in enumerate(parts):
        joined = lax.dynamic_update_slice(joined, part, (0, ((index - step) % count) * width))
    return joined


def reduce_features(features):
    count = lax.axis_size("narrow")
    index = lax.axis_index("narrow")
    width = features.shape[1] // count

    def piece(step):
        return lax.dynamic_slice_in_dim(features, ((index + step) % count) * width, width, 1)

    arrived = [shifted(piece(step), step) for step in range(1, count)]
    total = piece(0).astype(f32)
    for part in arrived:
        total = total + part.astype(f32)
    return total


def row_totals(values):
    count = lax.axis_size("narrow")
    return values + sum(shifted(values, step) for step in range(1, count))


def relative_chunks(features):
    count = lax.axis_size("wide")
    order = lax.axis_index("wide") ^ jnp.arange(count, dtype=jnp.int32)
    turned = features.T.reshape(count, features.shape[1] // count, features.shape[0])
    return jnp.take(turned, order, axis=0)


def scatter_rows(left_chunks, right_side):
    count, rows, tokens = left_chunks.shape
    bits = count.bit_length() - 1
    columns = right_side.shape[1]
    near = left_chunks[0::2].reshape(-1, tokens)
    away = left_chunks[1::2].reshape(-1, tokens)
    sent = flipped(product(away, right_side).astype(bf16), 1)
    kept = product(near, right_side).astype(bf16)
    shape = (2,) * (bits - 1) + (rows, columns)
    sent = sent.reshape(shape)
    kept = kept.reshape(shape)
    first_bits = list(range(1, bits))
    middle = (bits - 1) // 2
    half = rows // 2
    results = []
    for begin, order in (
        (0, first_bits),
        (half, first_bits[middle:] + first_bits[:middle]),
    ):
        total = kept[..., begin : begin + half, :].astype(f32) + sent[
            ..., begin : begin + half, :
        ].astype(f32)
        dims = list(range(bits - 1, 0, -1))
        for bit in order:
            at = dims.index(bit)
            dims.pop(at)
            away_part = lax.index_in_dim(total, 1, at, keepdims=False)
            near_part = lax.index_in_dim(total, 0, at, keepdims=False)
            arrived = flipped(away_part.astype(bf16), 1 << bit)
            total = near_part + arrived.astype(f32)
        results.append(total)
    return jnp.concatenate(results, axis=0)


def unit_rates(col_widths, rates):
    return jnp.concatenate(
        [
            jnp.full((col_width // SLAB,), step_rate, jnp.float32)
            for col_width, step_rate in zip(col_widths, rates)
        ]
    )


def slot_kernel(scale_ref, gradient_ref, left_ref, right_ref, moment_ref, square_ref,
                change_ref, new_moment_ref, new_square_ref, whole_ref, turned_ref):
    slot = pl.program_id(0)
    sources, rows = gradient_ref.shape[0], gradient_ref.shape[3]
    blocks = left_ref.shape[1] // BASIS
    right_basis = right_ref[0].astype(bf16)
    for source in range(sources):
        whole_ref[:, source * rows : (source + 1) * rows] = gradient_ref[source, 0].astype(f32)
    rate = scale_ref[slot]
    occupied = scale_ref[pl.num_programs(0) + slot]
    first_scale = scale_ref[2 * pl.num_programs(0)]
    second_scale = scale_ref[2 * pl.num_programs(0) + 1]
    turned_ref[...] = lax.dot_general(
        right_basis, whole_ref[...].astype(bf16), (((0,), (0,)), ((), ())),
        preferred_element_type=f32,
    )

    for block in range(blocks):
        at = slice(block * BASIS, (block + 1) * BASIS)
        left_basis = left_ref[0, at, :].astype(bf16)
        turned = jnp.dot(turned_ref[:, at].astype(bf16), left_basis, preferred_element_type=f32)
        moment = moment_ref[0, :, at]
        square = square_ref[0, :, at]
        new_moment = beta_one * moment + (1.0 - beta_one) * turned
        new_square = beta_two * square + (1.0 - beta_two) * turned * turned
        new_moment_ref[0, :, at] = jnp.where(occupied > 0.5, new_moment, moment)
        new_square_ref[0, :, at] = jnp.where(occupied > 0.5, new_square, square)
        direction = new_moment * first_scale / (jnp.sqrt(new_square * second_scale) + adam_eps)
        turned_ref[:, at] = lax.dot_general(
            direction.astype(bf16), left_basis, (((1,), (1,)), ((), ())),
            preferred_element_type=f32,
        )
    whole_ref[...] = rate * jnp.dot(
        right_basis, turned_ref[...].astype(bf16), preferred_element_type=f32
    )
    for source in range(sources):
        change_ref[source, 0] = whole_ref[:, source * rows : (source + 1) * rows].astype(bf16)


def slot_steps(gradient, left_basis, right_basis, moment, square, scales):
    sources, capacity, _, rows = gradient.shape
    row_count = sources * rows
    moment = moment.transpose(0, 2, 1)
    square = square.transpose(0, 2, 1)
    state = pl.BlockSpec((1, SLAB, row_count), lambda slot: (slot, 0, 0))
    traded = pl.BlockSpec((sources, 1, SLAB, rows), lambda slot: (0, slot, 0, 0))
    change, new_moment, new_square = pl.pallas_call(
        slot_kernel,
        grid=(capacity,),
        in_specs=[
            pl.BlockSpec(memory_space=pltpu.SMEM),
            traded,
            pl.BlockSpec((1, row_count, BASIS), lambda slot: (slot, 0, 0)),
            pl.BlockSpec((1, SLAB, SLAB), lambda slot: (slot, 0, 0)),
            state,
            state,
        ],
        out_specs=[traded, state, state],
        out_shape=[
            jax.ShapeDtypeStruct(gradient.shape, bf16),
            jax.ShapeDtypeStruct(moment.shape, f32),
            jax.ShapeDtypeStruct(square.shape, f32),
        ],
        scratch_shapes=[
            pltpu.VMEM((SLAB, row_count), f32),
            pltpu.VMEM((SLAB, row_count), f32),
        ],
        compiler_params=pltpu.CompilerParams(vmem_limit_bytes=48 * 1024 * 1024),
    )(scales, gradient, left_basis, right_basis, moment, square)
    return change, new_moment.transpose(0, 2, 1), new_square.transpose(0, 2, 1)


def owner_step(
    blocks, owner_ids, left_basis, right_basis, moment, square, rate_table, wide_index, tcount
):
    wide_count = lax.axis_size("wide")
    capacity = moment.shape[0]
    rows = blocks[0].shape[0]
    unit_rows = jnp.concatenate([block.T for block in blocks], axis=0).astype(bf16)
    unit_rows = unit_rows.reshape(-1, SLAB, rows)
    units = unit_rows.shape[0]
    slots = jnp.arange(wide_count * capacity, dtype=jnp.int32)
    matches = slots[:, None] == owner_ids[None, :]
    unit_of = jnp.sum(
        jnp.where(matches, jnp.arange(units, dtype=jnp.int32)[None, :], 0), axis=1
    )
    sending = jnp.take(unit_rows, unit_of, axis=0, mode="clip")
    owned = lax.all_to_all(
        sending.reshape(wide_count, capacity, SLAB, rows), "wide", split_axis=0, concat_axis=0,
        tiled=True,
    )
    slot_ids = wide_index * capacity + jnp.arange(capacity, dtype=jnp.int32)
    own = (owner_ids[None, :] == slot_ids[:, None]).astype(f32)
    slot_rate = -jnp.sum(own * rate_table[None, :], axis=1)
    scales = jnp.concatenate(
        [
            slot_rate,
            jnp.sum(own, axis=1),
            (1.0 / (1.0 - beta_one**tcount))[None],
            (1.0 / (1.0 - beta_two**tcount))[None],
        ]
    )
    change, new_moment, new_square = slot_steps(
        owned, left_basis, right_basis, moment, square, scales
    )
    back = lax.all_to_all(change, "wide", split_axis=0, concat_axis=0, tiled=True)
    back = back.reshape(wide_count * capacity, SLAB, rows)
    steps = jnp.take(back, owner_ids, axis=0, mode="clip").reshape(units * SLAB, rows)
    pieces, begin = ([], 0)
    for block in blocks:
        pieces.append(steps[begin : begin + block.shape[1]].T.astype(f32))
        begin += block.shape[1]
    return pieces, new_moment, new_square


def body(
    x_in,
    grad_out,
    w_qa,
    w_kv,
    w_kr,
    w_qb,
    w_kvb,
    w_o,
    w_gate,
    w_up,
    w_down,
    norm_gains,
    q_gain,
    kv_gain,
    deal,
    lengths,
    step_count,
    owner_a,
    owner_b,
    owner_c,
    basis_la,
    basis_ra,
    basis_lb,
    basis_rb,
    basis_lc,
    basis_rc,
    mom_a,
    sq_a,
    mom_b,
    sq_b,
    mom_c,
    sq_c,
    kr_mom,
    kr_sq,
    gain_mom,
    gain_sq,
    qgain_mom,
    qgain_sq,
    kvgain_mom,
    kvgain_sq,
):
    wide_count = lax.axis_size("wide")
    wide_index = lax.axis_index("wide")
    narrow_index = lax.axis_index("narrow")
    row_count, local_width = x_in.shape
    piece_rows = row_count // wide_count
    deal_row = lax.dynamic_index_in_dim(deal, wide_index, 0, keepdims=False)
    wide_ids = jnp.arange(wide_count, dtype=jnp.int32)
    inverse = jnp.sum(
        jnp.where(deal_row[None, :] == wide_ids[:, None], wide_ids[None, :], 0), axis=1
    )

    def to_working(features):
        outgoing = jnp.take(
            features.reshape((wide_count, piece_rows) + features.shape[1:]), inverse, axis=0,
            mode="clip",
        )
        dealt = lax.all_to_all(outgoing, "wide", split_axis=0, concat_axis=0, tiled=True)
        return dealt.reshape(row_count, -1)

    token_in = to_working(x_in)
    token_grad = to_working(grad_out)
    residual = token_in.astype(f32)
    grad_top = token_grad.astype(f32)
    seq_lengths = lengths[0]
    seq_ends = jnp.cumsum(seq_lengths)
    row_ids = jnp.arange(row_count, dtype=jnp.int32)
    segment = jnp.sum((row_ids[:, None] >= seq_ends[None, :-1]).astype(jnp.int32), axis=1)
    pick = jnp.arange(seq_lengths.shape[0], dtype=jnp.int32)[None, :] == segment[:, None]
    seq_start = jnp.sum(jnp.where(pick, (seq_ends - seq_lengths)[None, :], 0), axis=1)
    live_rows = (segment < seq_lengths.shape[0] - 1).astype(f32)[:, None]
    cosine_table, sine_table = rope_tables(row_ids - seq_start)
    cos_heads = cosine_table[:, None, :]
    sin_heads = sine_table[:, None, :]

    latent_own = jnp.concatenate([w_qa, w_kv, w_kr], axis=1)
    head_rows = jnp.concatenate(
        [jnp.pad(w_qb, ((0, 0), (0, w_kvb.shape[1] - w_qb.shape[1]))), w_kvb], axis=0
    )
    full_latent = lax.all_gather(latent_own, "wide", axis=0, tiled=True)
    full_heads = lax.all_gather(head_rows, "wide", axis=0)
    full_qb = full_heads[:, : w_qb.shape[0], : w_qb.shape[1]].reshape(-1, w_qb.shape[1])
    full_kvb = full_heads[:, w_qb.shape[0] :, :].reshape(-1, w_kvb.shape[1])
    full_o = lax.all_gather(w_o, "wide", axis=0, tiled=True)
    full_gate = lax.all_gather(w_gate, "wide", axis=0, tiled=True)
    full_up = lax.all_gather(w_up, "wide", axis=0, tiled=True)
    full_down = lax.all_gather(w_down, "wide", axis=0, tiled=True)
    gains_all = lax.all_gather(
        jnp.concatenate([norm_gains[0], norm_gains[1], q_gain, kv_gain]), "narrow"
    )
    first_gain = gains_all[:, :local_width].reshape(1, -1)
    second_gain = gains_all[:, local_width : 2 * local_width].reshape(1, -1)
    q_width = q_gain.shape[0]
    kv_width = kv_gain.shape[0]
    q_gain_all = gains_all[:, 2 * local_width : 2 * local_width + q_width].reshape(1, -1)
    kv_gain_all = gains_all[:, 2 * local_width + q_width :].reshape(1, -1)

    def inverse_rms(features, width):
        wide = features.astype(f32)
        return lax.rsqrt(jnp.sum(wide * wide, axis=1, keepdims=True) / width + norm_eps)

    token_all = gather_features(token_in)
    inv_first = inverse_rms(token_all, D)
    normed = (token_all.astype(f32) * inv_first * first_gain).astype(bf16)
    latents = product(normed, full_latent)
    q_latent = latents[:, :q_width]
    kv_latent = latents[:, q_width : q_width + kv_width]
    key_rot = latents[:, q_width + kv_width :]
    narrow_count = lax.axis_size("narrow")
    latents_all = gather_features(latents[:, : q_width + kv_width].astype(bf16))
    latents_all = latents_all.reshape(row_count, narrow_count, q_width + kv_width)
    q_latent_all = latents_all[:, :, :q_width].reshape(row_count, QR).astype(f32)
    kv_latent_all = latents_all[:, :, q_width:].reshape(row_count, KVR).astype(f32)
    inv_q = inverse_rms(q_latent_all, QR)
    inv_kv = inverse_rms(kv_latent_all, KVR)
    q_normed = (q_latent_all * inv_q * q_gain_all).astype(bf16)
    kv_normed = (kv_latent_all * inv_kv * kv_gain_all).astype(bf16)
    heads_here = w_o.shape[1] // VH
    q_pre = product(q_normed, full_qb)
    kv_pre = product(kv_normed, full_kvb)
    q_pre_heads = q_pre.reshape(row_count, heads_here, NOPE + ROPE)
    kv_pre_heads = kv_pre.reshape(row_count, heads_here, NOPE + VH)
    queries = jnp.concatenate(
        [
            q_pre_heads[..., :NOPE],
            rotate(q_pre_heads[..., NOPE:], cos_heads, sin_heads, 1.0),
        ],
        axis=-1,
    ).astype(bf16)
    key_turned = rotate(key_rot, cosine_table, sine_table, 1.0)
    key_heads = jnp.concatenate(
        [
            kv_pre_heads[..., :NOPE],
            jnp.broadcast_to(key_turned[:, None, :], (row_count, heads_here, ROPE)),
        ],
        axis=-1,
    ).astype(bf16)
    values = kv_pre_heads[..., NOPE:].astype(bf16)
    score_scale = (NOPE + ROPE) ** (-0.5)
    allowed = (segment[:, None] == segment[None, :]) & (row_ids[None, :] <= row_ids[:, None])

    def all_scores():
        scores = (
            jnp.einsum("qhd,khd->hqk", queries, key_heads, preferred_element_type=f32)
            * score_scale
        )
        return jnp.where(allowed[None], scores, masked_value)

    scores = all_scores()
    row_max = jnp.max(scores, axis=-1, keepdims=True)
    exp_scores = jnp.exp(scores - row_max)
    row_total = jnp.sum(exp_scores, axis=-1, keepdims=True)
    prob_rows = (exp_scores / row_total).astype(bf16)
    heads_out = jnp.einsum("hqk,khd->qhd", prob_rows, values, preferred_element_type=f32)
    heads_out = heads_out.astype(bf16).reshape(row_count, heads_here * VH)
    log_totals = row_max + jnp.log(row_total)
    attn_out = reduce_features(against_rows(heads_out, full_o).astype(bf16))
    middle = residual + residual_scale * live_rows * attn_out
    middle_all = gather_features(middle.astype(bf16)).astype(f32)
    inv_second = inverse_rms(middle_all, D)
    normed_two = (middle_all * inv_second * second_gain).astype(bf16)
    gate_act = product(normed_two, full_gate)
    upward = product(normed_two, full_up)
    sigmoid_gate = jax.nn.sigmoid(gate_act)
    silu_gate = gate_act * sigmoid_gate
    active = (silu_gate * upward).astype(bf16)
    mlp_out = reduce_features(against_rows(active, full_down).astype(bf16))
    layer_out = middle + residual_scale * live_rows * mlp_out

    mlp_grad = gather_features((residual_scale * live_rows * grad_top).astype(bf16))
    active_grad = product(mlp_grad, full_down)
    gate_grad = (
        active_grad * upward * (sigmoid_gate + silu_gate * (1.0 - sigmoid_gate))
    ).astype(bf16)
    up_grad = (active_grad * silu_gate).astype(bf16)
    normed_two_part = (
        against_rows(gate_grad, full_gate) + against_rows(up_grad, full_up)
    ).astype(bf16)
    second_dot = row_totals(
        jnp.sum(gate_grad.astype(f32) * gate_act + up_grad.astype(f32) * upward, axis=1)
    )[:, None]
    normed_two_grad = reduce_features(normed_two_part)
    block_down = scatter_rows(relative_chunks(mlp_grad), active)
    chunks_two = relative_chunks(normed_two)
    block_gate = scatter_rows(chunks_two, gate_grad)
    block_up = scatter_rows(chunks_two, up_grad)
    post_gain_grad = jnp.sum(normed_two_grad * middle * inv_second, axis=0)
    middle_grad = (
        grad_top
        + inv_second * norm_gains[1] * normed_two_grad
        - middle * inv_second**2 * second_dot / D
    )
    attn_grad = gather_features((residual_scale * live_rows * middle_grad).astype(bf16))
    block_o = scatter_rows(relative_chunks(attn_grad), heads_out)
    heads_grad = product(attn_grad, full_o).astype(bf16).reshape(row_count, heads_here, VH)

    prob_rows = jnp.exp(all_scores() - log_totals)
    value_grad = jnp.einsum(
        "hqk,qhd->khd", prob_rows.astype(bf16), heads_grad, preferred_element_type=f32
    )
    prob_grad = jnp.einsum("qhd,khd->hqk", heads_grad, values, preferred_element_type=f32)
    delta_rows = jnp.sum(prob_rows * prob_grad, axis=-1, keepdims=True)
    score_grad = (prob_rows * (prob_grad - delta_rows)).astype(bf16)
    query_grad = score_scale * jnp.einsum(
        "hqk,khd->qhd", score_grad, key_heads, preferred_element_type=f32
    )
    key_grad = score_scale * jnp.einsum(
        "hqk,qhd->khd", score_grad, queries, preferred_element_type=f32
    )
    q_pre_grad = jnp.concatenate(
        [query_grad[..., :NOPE], rotate(query_grad[..., NOPE:], cos_heads, sin_heads, -1.0)],
        axis=-1,
    )
    q_pre_grad = q_pre_grad.reshape(row_count, -1).astype(bf16)
    kv_pre_grad = jnp.concatenate([key_grad[..., :NOPE], value_grad], axis=-1)
    kv_pre_grad = kv_pre_grad.reshape(row_count, -1).astype(bf16)
    rot_partial = rotate(jnp.sum(key_grad[..., NOPE:], axis=1), cosine_table, sine_table, -1.0)
    rot_grad = row_totals(rot_partial).astype(bf16)
    q_dot = jnp.sum(q_pre_grad.astype(f32) * q_pre, axis=1)
    kv_dot = jnp.sum(kv_pre_grad.astype(f32) * kv_pre, axis=1)
    dots = row_totals(jnp.stack([q_dot, kv_dot]))
    q_dot = dots[0][:, None]
    kv_dot = dots[1][:, None]
    q_part = against_rows(q_pre_grad, full_qb).astype(bf16)
    kv_part = against_rows(kv_pre_grad, full_kvb).astype(bf16)
    both_part = jnp.concatenate(
        [
            q_part.reshape(row_count, narrow_count, q_width),
            kv_part.reshape(row_count, narrow_count, kv_width),
        ],
        axis=-1,
    ).reshape(row_count, -1)
    both_grad = reduce_features(both_part)
    q_normed_grad = both_grad[:, :q_width]
    kv_normed_grad = both_grad[:, q_width:]
    block_qb = scatter_rows(relative_chunks(q_normed), q_pre_grad)
    block_kvb = scatter_rows(relative_chunks(kv_normed), kv_pre_grad)
    q_gain_grad = jnp.sum(q_normed_grad * q_latent * inv_q, axis=0)
    kv_gain_grad = jnp.sum(kv_normed_grad * kv_latent * inv_kv, axis=0)
    q_latent_grad = (
        inv_q * q_gain * q_normed_grad - q_latent * inv_q**2 * q_dot / QR
    ).astype(bf16)
    kv_latent_grad = (
        inv_kv * kv_gain * kv_normed_grad - kv_latent * inv_kv**2 * kv_dot / KVR
    ).astype(bf16)
    share = (narrow_index == 0).astype(f32)
    first_dot = row_totals(
        jnp.sum(q_latent_grad.astype(f32) * q_latent, axis=1)
        + jnp.sum(kv_latent_grad.astype(f32) * kv_latent, axis=1)
        + share * jnp.sum(rot_grad.astype(f32) * key_rot, axis=1)
    )[:, None]
    latent_grad = jnp.concatenate([q_latent_grad, kv_latent_grad, rot_grad], axis=1)
    block_latent = scatter_rows(relative_chunks(normed), latent_grad)
    block_qa = block_latent[:, :q_width]
    block_kv = block_latent[:, q_width : q_width + kv_width]
    block_kr = block_latent[:, q_width + kv_width :]
    full_kr = full_latent[:, q_width + kv_width :]
    own_kr = lax.dynamic_slice_in_dim(full_kr, narrow_index * local_width, local_width, 0)
    normed_part = against_rows(
        latent_grad[:, : q_width + kv_width], full_latent[:, : q_width + kv_width]
    ).astype(bf16)
    normed_grad = reduce_features(normed_part) + against_rows(rot_grad, own_kr)
    in_gain_grad = jnp.sum(normed_grad * residual * inv_first, axis=0)
    input_grad = (
        middle_grad
        + inv_first * norm_gains[0] * normed_grad
        - residual * inv_first**2 * first_dot / D
    )

    def to_input(features):
        returned = lax.all_to_all(
            features.astype(bf16).reshape(wide_count, piece_rows, -1), "wide", split_axis=0,
            concat_axis=0, tiled=True,
        )
        return jnp.take(returned, deal_row, axis=0, mode="clip").astype(f32).reshape(row_count, -1)

    final_out = to_input(layer_out)
    final_grad = to_input(input_grad)
    gain_grads = lax.psum(
        jnp.concatenate([in_gain_grad, post_gain_grad, q_gain_grad, kv_gain_grad]), "wide"
    )
    gains_total = gain_grads[: 2 * local_width].reshape(2, local_width)
    qgain_total = gain_grads[2 * local_width : 2 * local_width + q_width]
    kvgain_total = gain_grads[2 * local_width + q_width :]
    tcount = step_count[0].astype(f32)
    wide_rate = D ** (-0.5)
    class_a = [block_qa, block_kv, block_o, block_gate, block_up, block_down]
    widths_a = [block.shape[1] for block in class_a]
    rates_a = unit_rates(widths_a, [wide_rate, wide_rate, 1.0, wide_rate, wide_rate, 0.125])
    rates_b = unit_rates([block_qb.shape[1]], [QR ** (-0.5)])
    rates_c = unit_rates([block_kvb.shape[1]], [KVR ** (-0.5)])
    updates_a, new_mom_a, new_sq_a = owner_step(
        class_a, owner_a[0], basis_la, basis_ra, mom_a, sq_a, rates_a, wide_index, tcount
    )
    updates_b, new_mom_b, new_sq_b = owner_step(
        [block_qb], owner_b[0], basis_lb, basis_rb, mom_b, sq_b, rates_b, wide_index, tcount
    )
    updates_c, new_mom_c, new_sq_c = owner_step(
        [block_kvb], owner_c[0], basis_lc, basis_rc, mom_c, sq_c, rates_c, wide_index, tcount
    )
    update_qb = updates_b[0]
    update_kvb = updates_c[0]
    update_kr, new_kr_mom, new_kr_sq = plain_adam(block_kr, kr_mom, kr_sq, wide_rate, tcount)
    update_gains, new_gain_mom, new_gain_sq = plain_adam(
        gains_total, gain_mom, gain_sq, gain_rate, tcount
    )
    update_qgain, new_qgain_mom, new_qgain_sq = plain_adam(
        qgain_total, qgain_mom, qgain_sq, gain_rate, tcount
    )
    update_kvgain, new_kvgain_mom, new_kvgain_sq = plain_adam(
        kvgain_total, kvgain_mom, kvgain_sq, gain_rate, tcount
    )
    return (
        final_out,
        final_grad,
        block_qa,
        block_kv,
        block_qb,
        block_kvb,
        block_o,
        block_gate,
        block_up,
        block_down,
        w_qa.astype(f32) + updates_a[0],
        w_kv.astype(f32) + updates_a[1],
        w_qb.astype(f32) + update_qb,
        w_kvb.astype(f32) + update_kvb,
        w_o.astype(f32) + updates_a[2],
        w_gate.astype(f32) + updates_a[3],
        w_up.astype(f32) + updates_a[4],
        w_down.astype(f32) + updates_a[5],
        block_kr,
        w_kr.astype(f32) + update_kr,
        new_kr_mom,
        new_kr_sq,
        gains_total,
        norm_gains + update_gains,
        new_gain_mom,
        new_gain_sq,
        qgain_total,
        q_gain + update_qgain,
        new_qgain_mom,
        new_qgain_sq,
        kvgain_total,
        kv_gain + update_kvgain,
        new_kvgain_mom,
        new_kvgain_sq,
        new_mom_a,
        new_sq_a,
        new_mom_b,
        new_sq_b,
        new_mom_c,
        new_sq_c,
    )


def solution(mesh):
    return jax.shard_map(
        body,
        mesh=mesh,
        in_specs=(
            P("wide", "narrow"),
            P("wide", "narrow"),
            P("wide", "narrow"),
            P("wide", "narrow"),
            P("wide", None),
            P("wide", "narrow"),
            P("wide", "narrow"),
            P("wide", "narrow"),
            P("wide", "narrow"),
            P("wide", "narrow"),
            P("wide", "narrow"),
            P(None, "narrow"),
            P("narrow"),
            P("narrow"),
            P(),
            P("wide", None),
            P(),
            P("narrow", None),
            P("narrow", None),
            P("narrow", None),
            P("wide", None, "narrow"),
            P("wide", None, "narrow"),
            P("wide", None, "narrow"),
            P("wide", None, "narrow"),
            P("wide", None, "narrow"),
            P("wide", None, "narrow"),
            P("wide", None, "narrow"),
            P("wide", None, "narrow"),
            P("wide", None, "narrow"),
            P("wide", None, "narrow"),
            P("wide", None, "narrow"),
            P("wide", None, "narrow"),
            P("wide", None),
            P("wide", None),
            P(None, "narrow"),
            P(None, "narrow"),
            P("narrow"),
            P("narrow"),
            P("narrow"),
            P("narrow"),
        ),
        out_specs=(
            P("wide", "narrow"),
            P("wide", "narrow"),
            P("wide", "narrow"),
            P("wide", "narrow"),
            P("wide", "narrow"),
            P("wide", "narrow"),
            P("wide", "narrow"),
            P("wide", "narrow"),
            P("wide", "narrow"),
            P("wide", "narrow"),
            P("wide", "narrow"),
            P("wide", "narrow"),
            P("wide", "narrow"),
            P("wide", "narrow"),
            P("wide", "narrow"),
            P("wide", "narrow"),
            P("wide", "narrow"),
            P("wide", "narrow"),
            P("wide", None),
            P("wide", None),
            P("wide", None),
            P("wide", None),
            P(None, "narrow"),
            P(None, "narrow"),
            P(None, "narrow"),
            P(None, "narrow"),
            P("narrow"),
            P("narrow"),
            P("narrow"),
            P("narrow"),
            P("narrow"),
            P("narrow"),
            P("narrow"),
            P("narrow"),
            P("wide", None, "narrow"),
            P("wide", None, "narrow"),
            P("wide", None, "narrow"),
            P("wide", None, "narrow"),
            P("wide", None, "narrow"),
            P("wide", None, "narrow"),
        ),
        check_vma=False,
    )
```

time: 2160 us -> 1360 us (0.63)
  waiting for transfers between devices: 1290 us -> 556 us
  matrix products: 293 us -> 143 us
  starting transfers between devices: 60.7 us -> 158 us
  Pallas kernels: 0 us -> 52.3 us
  blocking collectives: 130 us -> 79.8 us
  local copies, waits for them, and re-layouts: 256 us -> 232 us
    reduce_scatter x14 -> x0, waiting for transfers between devices: 831 us -> none  [the longest x6 317 us: reduce_features(): return lax.psum_scatter(features, 'narrow', scatter_dimension=1, tiled=True)]
    ppermute x0 -> x77, waiting for transfers between devices: none -> 479 us  [the longest x42 382 us: shifted(): lax.ppermute(value, 'narrow', [(i, (i + step) % count) for i in range(cou...]
    all_gather x9 -> x6, waiting for transfers between devices: 304 us -> 0.01 us  [the longest x1 0.01 us: body(): full_latent = lax.all_gather(latent_own, 'wide', axis=0, tiled=True)]
    dot_general x24 -> x6, matrix products: 187 us -> 15.4 us  [the longest x1 6.13 us: body(): jnp.einsum('qhd,khd->hqk', heads_grad, values, preferred_element_type=f32)]
    ppermute x0 -> x77, starting transfers between devices: none -> 89.1 us  [the longest x42 48.8 us: shifted(): lax.ppermute(value, 'narrow', [(i, (i + step) % count) for i in range(cou...]
    all_gather x6 -> x1, blocking collectives: 66.6 us -> 10.4 us  [body(): lax.all_gather(jnp.concatenate([norm_gains[0], norm_gains[1], q_gain, kv_...]
    pallas_call x0 -> x3, Pallas kernels: none -> 52.3 us  [slot_steps(): pl.pallas_call(slot_kernel, grid=(capacity,), in_specs=[pl.BlockSpec(memo...]
    unnamed x25 -> x6, waiting for transfers between devices: 45.3 us -> 2.32 us
  transfers between devices with their start and end apart: 34 -> 93, of which waited for: 24 -> 48; matrix products, arithmetic and copies ran while one was open for 22% -> 29% of each run, Pallas kernels for 0% -> 4%
where the time goes in v1:
time: 1360 us; the launch traced here: 1350 us
  waiting for transfers between devices  556 us (41%)
  local copies, waits for them, and re-layouts  232 us (17%)
  starting transfers between devices  158 us (12%)
  matrix products  143 us (11%)
  other arithmetic  105 us (8%)
  blocking collectives  79.8 us (6%)
  Pallas kernels  52.3 us (4%)
  between operations  18.1 us (1%)
    ppermute x42, waiting for transfers between devices, shifted(): lax.ppermute(value, 'narrow', [(i, (i + step) % count) for i in range(cou...  382 us
    ppermute x35, waiting for transfers between devices, flipped(): return lax.ppermute(value, 'wide', [(i, i ^ bit) for i in range(count)])  96.9 us
    dot_general x21, matrix products, product(): return jnp.dot(left_side, right_side, preferred_element_type=jnp.float32)  87 us
    all_to_all x3, waiting for transfers between devices, owner_step(): lax.all_to_all(sending.reshape(wide_count, capacity, SLAB, rows), 'wide',...  73.2 us
    psum x1, blocking collectives, body(): lax.psum(jnp.concatenate([in_gain_grad, post_gain_grad, q_gain_grad, kv_g...  69.3 us
    pallas_call x3, Pallas kernels, slot_steps(): pl.pallas_call(slot_kernel, grid=(capacity,), in_specs=[pl.BlockSpec(memo...  52.3 us
    ppermute x42, starting transfers between devices, shifted(): lax.ppermute(value, 'narrow', [(i, (i + step) % count) for i in range(cou...  48.8 us
    unnamed x351, local copies, waits for them, and re-layouts  43.5 us
  transfers between devices with their start and end apart: 93, of which 48 were waited for; matrix products, arithmetic and copies ran while one was open for 29% of the time, Pallas kernels for 4%

profile of v1, /device:TPU:11, one launch (start us, length us, event | category | flops | bytes accessed | tf_op | source)
XLA Modules:
  0.0 1345.3 jit_solution(9547777974847275533)
XLA Ops:
  15.7 4.9 all-to-all-start
  22.6 10.4 all-gather.2
  34.8 7.1 all-to-all-start.2
  49.9 8.4 collective-permute-done
  60.4 38.1 %collective-permute-done.1 = bf16[512,640]{1,0:T(8,128)(2,1)} collective-permute-done((bf16[512,640]{1,0:T(8,128)(2,1)}, bf16[512,640]{1,0:T(8,128)(2,1)}, u32[]{:S(2)}, u32[]{:S(2)}) %collective-permute-start.1) | collective-permute-done | bytes 655392 | tf_op jit(solution)/shard_map/ppermute | solution.py:79
  126.7 14.8 %collective-permute-done.4 = bf16[512,256]{0,1:T(8,128)(2,1)S(1)} collective-permute-done((bf16[512,256]{0,1:T(8,128)(2,1)S(1)}, bf16[512,256]{0,1:T(8,128)(2,1)S(1)}, u32[]{:S(2)}, u32[]{:S(2)}) %collective-permute-start.4) | collective-permute-done | bytes 262176 | tf_op jit(solution)/shard_map/ppermute | solution.py:79
  141.6 5.0 collective-permute-done.5
  169.8 4.4 convolution_convert_fusion.7
  180.1 13.0 collective-permute-done.6
  193.1 40.4 %collective-permute-done.7 = bf16[512,640]{1,0:T(8,128)(2,1)S(1)} collective-permute-done((bf16[512,640]{1,0:T(8,128)(2,1)}, bf16[512,640]{1,0:T(8,128)(2,1)S(1)}, u32[]{:S(2)}, u32[]{:S(2)}) %collective-permute-start.7) | collective-permute-done | bytes 655392 | tf_op jit(solution)/shard_map/ppermute | solution.py:79
  269.0 25.0 %collective-permute-done.16 = bf16[512,640]{1,0:T(8,128)(2,1)} collective-permute-done((bf16[512,640]{1,0:T(8,128)(2,1)}, bf16[512,640]{1,0:T(8,128)(2,1)}, u32[]{:S(2)}, u32[]{:S(2)}) %collective-permute-start.16) | collective-permute-done | bytes 655392 | tf_op jit(solution)/shard_map/ppermute | solution.py:79
  296.2 30.7 %collective-permute-done.17 = bf16[512,640]{1,0:T(8,128)(2,1)} collective-permute-done((bf16[512,640]{1,0:T(8,128)(2,1)}, bf16[512,640]{1,0:T(8,128)(2,1)}, u32[]{:S(2)}, u32[]{:S(2)}) %collective-permute-start.17) | collective-permute-done | bytes 655392 | tf_op jit(solution)/shard_map/ppermute | solution.py:79
  329.1 7.0 collective-permute-done.9
  338.2 11.9 collective-permute-done.10
  370.0 10.4 fusion.167
  380.3 10.6 fusion.166
  390.9 14.6 %add_reduce_fusion = (f32[512]{0:T(512)S(1)}, bf16[512,1600]{0,1:T(8,128)(2,1)}, bf16[512,1600]{0,1:T(8,128)(2,1)}, bf16[512,1600]{0,1:T(8,128)(2,1)}) fusion(f32[512,1600]{0,1:T(8,128)} %fusion.166, f32[512,1600]{0,1:T(8,128)} %fusion.167, bf16[512,2560]{0,1:T(8,128)(2,1)} %fusion.7, bf16[2560,1600]{1,0:T(8,128)(2,1)} %all-gather.15.cloned.1.call-done), kind=kOutput, calls=%fused_computation.53 | convolution fusion | flops 4210687488 | bytes 22284288 | tf_op jit(solution)/shard_map/dot_general | solution.py:30
  407.6 8.1 fusion.168
  415.8 10.4 add_convert_fusion
  430.1 8.8 convolution_convert_fusion.8
  446.2 35.8 %collective-permute-done.19 = bf16[512,640]{1,0:T(8,128)(2,1)S(1)} collective-permute-done((bf16[512,640]{1,0:T(8,128)(2,1)S(1)}, bf16[512,640]{1,0:T(8,128)(2,1)S(1)}, u32[]{:S(2)}, u32[]{:S(2)}) %collective-permute-start.19) | collective-permute-done | bytes 655392 | tf_op jit(solution)/shard_map/ppermute | solution.py:79
  482.0 31.9 %collective-permute-done.20 = bf16[512,640]{1,0:T(8,128)(2,1)S(1)} collective-permute-done((bf16[512,640]{1,0:T(8,128)(2,1)S(1)}, bf16[512,640]{1,0:T(8,128)(2,1)S(1)}, u32[]{:S(2)}, u32[]{:S(2)}) %collective-permute-start.20) | collective-permute-done | bytes 655392 | tf_op jit(solution)/shard_map/ppermute | solution.py:79
  513.9 10.3 collective-permute-done.12
  524.2 14.0 %collective-permute-done.13 = bf16[512,640]{1,0:T(8,128)(2,1)S(1)} collective-permute-done((bf16[512,640]{1,0:T(8,128)(2,1)S(1)}, bf16[512,640]{1,0:T(8,128)(2,1)S(1)}, u32[]{:S(2)}, u32[]{:S(2)}) %collective-permute-start.13) | collective-permute-done | bytes 655392 | tf_op jit(solution)/shard_map/ppermute | solution.py:79
  560.3 40.0 %collective-permute-done.25 = bf16[512,640]{1,0:T(8,128)(2,1)S(1)} collective-permute-done((bf16[512,640]{1,0:T(8,128)(2,1)S(1)}, bf16[512,640]{1,0:T(8,128)(2,1)S(1)}, u32[]{:S(2)}, u32[]{:S(2)}) %collective-permute-start.25) | collective-permute-done | bytes 655392 | tf_op jit(solution)/shard_map/ppermute | solution.py:79
  603.4 5.1 convolution_convert_fusion.18
  608.8 6.1 multiply_reduce_fusion
  642.5 6.3 broadcast_select_fusion
  650.8 4.3 convolution_convert_fusion.3
  655.1 4.3 convolution_convert_fusion.5
  671.3 6.2 convolution_convert_fusion.1
  677.6 4.7 convolution_convert_fusion
  695.7 6.9 copy.511
  702.6 6.8 copy.507
  709.5 6.9 copy.503
  726.2 7.3 collective-permute-start.52
  734.4 6.5 collective-permute-start.47
  773.1 12.5 all-to-all-start.8
  789.3 5.9 all-to-all-start.1
  795.7 4.4 shard_map.689
  804.4 38.2 %collective-permute-done.34 = bf16[512,640]{1,0:T(8,128)(2,1)} collective-permute-done((bf16[512,640]{1,0:T(8,128)(2,1)}, bf16[512,640]{1,0:T(8,128)(2,1)}, u32[]{:S(2)}, u32[]{:S(2)}) %collective-permute-start.34) | collective-permute-done | bytes 655392 | tf_op jit(solution)/shard_map/ppermute | solution.py:79
  874.1 4.8 collective-permute-done.43
  879.3 6.1 collective-permute-done.45
  913.7 6.9 copy.513
  929.6 6.9 copy.509
  945.3 7.1 copy.505
  971.8 18.2 %collective-permute-done.63 = bf16[2,160,1600]{2,1,0:T(8,128)(2,1)S(1)} collective-permute-done((bf16[2,160,1600]{2,1,0:T(8,128)(2,1)S(1)}, bf16[2,160,1600]{2,1,0:T(8,128)(2,1)S(1)}, u32[]{:S(2)}, u32[]{:S(2)}) %collective-permute-start.63) | collective-permute-done | bytes 1024032 | tf_op jit(solution)/shard_map/ppermute | solution.py:84
  993.2 10.1 collective-permute-done.74
  1005.6 9.1 collective-permute-done.69
  1016.8 9.4 collective-permute-done.64
  1027.3 12.4 all-to-all-start.9
  1043.5 5.2 all-to-all-start.6
  1055.5 5.0 all-to-all-start.3
  1065.7 6.3 concatenate.95
  1072.0 6.2 copy.517
  1078.2 11.6 gather_fusion.6
  1090.7 4.9 all-to-all-start.4
  1096.0 4.7 shard_map.688
  1101.4 68.6 %all-to-all-done.4.gradient_ref = bf16[8,17,64,320]{3,2,1,0:T(8,128)(2,1)} async-done(((bf16[8,17,64,320]{3,2,1,0:T(8,128)(2,1)}), bf16[8,17,64,320]{3,2,1,0:T(8,128)(2,1)}, u32[]{:S(2)}, u32[]{:S(2)}) %all-to-all-start.4) | async-done | bytes 5570592 | tf_op jit(solution)/shard_map/all_to_all | solution.py:255
  1170.0 5.0 all-to-all-start.7
  1175.3 43.2 %shard_map.687 = (bf16[8,17,64,320]{3,2,1,0:T(8,128)(2,1)}, f32[17,64,2560]{2,1,0:T(8,128)}, f32[17,64,2560]{2,1,0:T(8,128)}) custom-call(f32[36]{0:T(128)S(1)} %pad_maximum_fusion.19.scale_ref, bf16[8,17,64,320]{3,2,1,0:T(8,128)(2,1)} %all-to-all-done.4.gradient_ref, f32[17,2560,128]{2,1,0:T(8,128)} %left_ref.3, f32[17,64,64]{2,1,0:T(8,128)S(1)} %copy-done.5, ...), custom_call_target="tpu_custom_call" | custom-call | tf_op jit(solution)/shard_map/pallas_call | solution.py:214
  1219.3 5.2 all-to-all-start.5
  1235.5 69.3 %psum.7 = f32[1536]{0:T(1024)S(1)} all-reduce(f32[1536]{0:T(1024)S(1)} %concatenate.98), channel_id=1, replica_groups=mesh['wide'=8,'narrow'=4] {'wide'}, use_global_device_ids=true, to_apply=%region_31.33 | all-reduce | flops 1536 | bytes 12288 | tf_op jit(solution)/shard_map/psum | solution.py:562
  1311.1 6.5 gather_fusion.7
  (824 shorter events, 446.2 us)
Async XLA Ops:
  7.2 102.4 %all-gather.21.cloned.1.call-start = ((), (), s32[]{:S(2)}) async-start(), calls=%async_computation.15 | async-start | bytes 1990656 | tf_op jit(solution)/shard_map/all_gather | solution.py:363
  9.0 140.3 %all-gather.19.cloned.1.call-start = ((), (), s32[]{:S(2)}) async-start(), calls=%async_computation.14 | async-start | bytes 2949120 | tf_op jit(solution)/shard_map/all_gather | solution.py:364
  10.8 159.0 %all-gather.11.cloned.1.call-start = ((), (), s32[]{:S(2)}) async-start(), calls=%async_computation.10 | async-start | bytes 3686400 | tf_op jit(solution)/shard_map/all_gather | solution.py:367
  11.6 358.4 %all-gather.17.cloned.1.call-start = ((), (), s32[]{:S(2)}) async-start(), calls=%async_computation.13 | async-start | bytes 9584640 | tf_op jit(solution)/shard_map/all_gather | solution.py:370
  12.2 368.2 %all-gather.13.cloned.1.call-start = ((), (), s32[]{:S(2)}) async-start(), calls=%async_computation.11 | async-start | bytes 9584640 | tf_op jit(solution)/shard_map/all_gather | solution.py:368
  15.7 19.2 %all-to-all-start = ((bf16[8,64,640]{2,1,0:T(8,128)(2,1)}), bf16[8,64,640]{2,1,0:T(8,128)(2,1)}, u32[]{:S(2)}, u32[]{:S(2)}) async-start(bf16[8,64,640]{2,1,0:T(8,128)(2,1)} %gather_fusion), calls=%async_computation | async-start | bytes 1310720 | tf_op jit(solution)/shard_map/all_to_all | solution.py:341
  20.6 370.3 %all-gather.15.cloned.1.call-start = ((), (), s32[]{:S(2)}) async-start(), calls=%async_computation.12 | async-start | bytes 9584640 | tf_op jit(solution)/shard_map/all_gather | solution.py:369
  34.8 145.3 %all-to-all-start.2 = ((bf16[8,64,640]{2,1,0:T(8,128)(2,1)}), bf16[8,64,640]{2,1,0:T(8,128)(2,1)S(1)}, u32[]{:S(2)}, u32[]{:S(2)}) async-start(bf16[8,64,640]{2,1,0:T(8,128)(2,1)} %gather_fusion.2), calls=%async_computation.2 | async-start | bytes 1310720 | tf_op jit(solution)/shard_map/all_to_all | solution.py:341
  42.0 56.5 %collective-permute-start.1 = (bf16[512,640]{1,0:T(8,128)(2,1)}, bf16[512,640]{1,0:T(8,128)(2,1)}, u32[]{:S(2)}, u32[]{:S(2)}) collective-permute-start(bf16[512,640]{1,0:T(8,128)(2,1)} %bitcast.2), channel_id=1, source_target_pairs={{0,2},{1,3},{2,0},{3,1},{4,6},{5,7},{6,4},{7,5},{8,10},{9,11},{10,... | collective-permute-start | bytes 1966088 | tf_op jit(solution)/shard_map/ppermute | solution.py:79
  44.2 58.7 %collective-permute-start.2 = (bf16[512,640]{1,0:T(8,128)(2,1)}, bf16[512,640]{1,0:T(8,128)(2,1)}, u32[]{:S(2)}, u32[]{:S(2)}) collective-permute-start(bf16[512,640]{1,0:T(8,128)(2,1)} %bitcast.2), channel_id=1, source_target_pairs={{0,3},{1,0},{2,1},{3,2},{4,7},{5,4},{6,5},{7,6},{8,11},{9,8},{10,9... | collective-permute-start | bytes 1966088 | tf_op jit(solution)/shard_map/ppermute | solution.py:79
  119.7 21.9 %collective-permute-start.4 = (bf16[512,256]{0,1:T(8,128)(2,1)S(1)}, bf16[512,256]{0,1:T(8,128)(2,1)S(1)}, u32[]{:S(2)}, u32[]{:S(2)}) collective-permute-start(bf16[512,256]{0,1:T(8,128)(2,1)S(1)} %get-tuple-element.354), channel_id=1, source_target_pairs={{0,2},{1,3},{2,0},{3,1},{4,6},{5,7},{6,4},{7,5},{8,10},{9,11},{10,... | collective-permute-start | bytes 786440 | tf_op jit(solution)/shard_map/ppermute | solution.py:79
  122.9 23.7 %collective-permute-start.5 = (bf16[512,256]{0,1:T(8,128)(2,1)S(1)}, bf16[512,256]{0,1:T(8,128)(2,1)S(1)}, u32[]{:S(2)}, u32[]{:S(2)}) collective-permute-start(bf16[512,256]{0,1:T(8,128)(2,1)S(1)} %get-tuple-element.354), channel_id=1, source_target_pairs={{0,3},{1,0},{2,1},{3,2},{4,7},{5,4},{6,5},{7,6},{8,11},{9,8},{10,9... | collective-permute-start | bytes 786440 | tf_op jit(solution)/shard_map/ppermute | solution.py:79
  177.0 56.5 %collective-permute-start.7 = (bf16[512,640]{1,0:T(8,128)(2,1)}, bf16[512,640]{1,0:T(8,128)(2,1)S(1)}, u32[]{:S(2)}, u32[]{:S(2)}) collective-permute-start(bf16[512,640]{1,0:T(8,128)(2,1)} %get-tuple-element.381), channel_id=1, source_target_pairs={{0,2},{1,3},{2,0},{3,1},{4,6},{5,7},{6,4},{7,5},{8,10},{9,11},{10,... | collective-permute-start | bytes 1966088 | tf_op jit(solution)/shard_map/ppermute | solution.py:79
  177.0 57.3 %collective-permute-start.8 = (bf16[512,640]{1,0:T(8,128)(2,1)}, bf16[512,640]{1,0:T(8,128)(2,1)}, u32[]{:S(2)}, u32[]{:S(2)}) collective-permute-start(bf16[512,640]{1,0:T(8,128)(2,1)} %get-tuple-element.380), channel_id=1, source_target_pairs={{0,3},{1,0},{2,1},{3,2},{4,7},{5,4},{6,5},{7,6},{8,11},{9,8},{10,9... | collective-permute-start | bytes 1966088 | tf_op jit(solution)/shard_map/ppermute | solution.py:79
  244.2 49.8 %collective-permute-start.16 = (bf16[512,640]{1,0:T(8,128)(2,1)}, bf16[512,640]{1,0:T(8,128)(2,1)}, u32[]{:S(2)}, u32[]{:S(2)}) collective-permute-start(bf16[512,640]{1,0:T(8,128)(2,1)} %get-tuple-element.421), channel_id=1, source_target_pairs={{0,2},{1,3},{2,0},{3,1},{4,6},{5,7},{6,4},{7,5},{8,10},{9,11},{10,... | collective-permute-start | bytes 1966088 | tf_op jit(solution)/shard_map/ppermute | solution.py:79
  247.2 79.6 %collective-permute-start.17 = (bf16[512,640]{1,0:T(8,128)(2,1)}, bf16[512,640]{1,0:T(8,128)(2,1)}, u32[]{:S(2)}, u32[]{:S(2)}) collective-permute-start(bf16[512,640]{1,0:T(8,128)(2,1)} %get-tuple-element.421), channel_id=1, source_target_pairs={{0,3},{1,0},{2,1},{3,2},{4,7},{5,4},{6,5},{7,6},{8,11},{9,8},{10,9... | collective-permute-start | bytes 1966088 | tf_op jit(solution)/shard_map/ppermute | solution.py:79
  248.7 87.3 %collective-permute-start.9 = (bf16[512,640]{1,0:T(8,128)(2,1)S(1)}, bf16[512,640]{1,0:T(8,128)(2,1)}, u32[]{:S(2)}, u32[]{:S(2)}) collective-permute-start(bf16[512,640]{1,0:T(8,128)(2,1)S(1)} %get-tuple-element.351), channel_id=1, source_target_pairs={{0,1},{1,2},{2,3},{3,0},{4,5},{5,6},{6,7},{7,4},{8,9},{9,10},{10,1... | collective-permute-start | bytes 1966088 | tf_op jit(solution)/shard_map/ppermute | solution.py:79
  248.7 101.4 %collective-permute-start.10 = (bf16[512,640]{1,0:T(8,128)(2,1)S(1)}, bf16[512,640]{1,0:T(8,128)(2,1)}, u32[]{:S(2)}, u32[]{:S(2)}) collective-permute-start(bf16[512,640]{1,0:T(8,128)(2,1)S(1)} %get-tuple-element.351), channel_id=1, source_target_pairs={{0,2},{1,3},{2,0},{3,1},{4,6},{5,7},{6,4},{7,5},{8,10},{9,11},{10,... | collective-permute-start | bytes 1966088 | tf_op jit(solution)/shard_map/ppermute | solution.py:79
  253.7 101.3 %collective-permute-start.11 = (bf16[512,640]{1,0:T(8,128)(2,1)S(1)}, bf16[512,640]{1,0:T(8,128)(2,1)}, u32[]{:S(2)}, u32[]{:S(2)}) collective-permute-start(bf16[512,640]{1,0:T(8,128)(2,1)S(1)} %get-tuple-element.351), channel_id=1, source_target_pairs={{0,3},{1,0},{2,1},{3,2},{4,7},{5,4},{6,5},{7,6},{8,11},{9,8},{10,9... | collective-permute-start | bytes 1966088 | tf_op jit(solution)/shard_map/ppermute | solution.py:79
  405.5 33.6 %collective-permute-start.21 = (f32[512]{0:T(512)S(1)}, f32[512]{0:T(512)S(1)}, u32[]{:S(2)}, u32[]{:S(2)}) collective-permute-start(f32[512]{0:T(512)S(1)} %get-tuple-element.348), channel_id=1, source_target_pairs={{0,1},{1,2},{2,3},{3,0},{4,5},{5,6},{6,7},{7,4},{8,9},{9,10},{10,1... | collective-permute-start | bytes 6152 | tf_op jit(solution)/shard_map/ppermute | solution.py:79
  405.5 33.6 %collective-permute-start.22 = (f32[512]{0:T(512)S(1)}, f32[512]{0:T(512)S(1)}, u32[]{:S(2)}, u32[]{:S(2)}) collective-permute-start(f32[512]{0:T(512)S(1)} %get-tuple-element.348), channel_id=1, source_target_pairs={{0,2},{1,3},{2,0},{3,1},{4,6},{5,7},{6,4},{7,5},{8,10},{9,11},{10,... | collective-permute-start | bytes 6152 | tf_op jit(solution)/shard_map/ppermute | solution.py:79
  406.0 34.6 %collective-permute-start.23 = (f32[512]{0:T(512)S(1)}, f32[512]{0:T(512)S(1)}, u32[]{:S(2)}, u32[]{:S(2)}) collective-permute-start(f32[512]{0:T(512)S(1)} %get-tuple-element.348), channel_id=1, source_target_pairs={{0,3},{1,0},{2,1},{3,2},{4,7},{5,4},{6,5},{7,6},{8,11},{9,8},{10,9... | collective-permute-start | bytes 6152 | tf_op jit(solution)/shard_map/ppermute | solution.py:79
  427.2 54.8 %collective-permute-start.19 = (bf16[512,640]{1,0:T(8,128)(2,1)S(1)}, bf16[512,640]{1,0:T(8,128)(2,1)S(1)}, u32[]{:S(2)}, u32[]{:S(2)}) collective-permute-start(bf16[512,640]{1,0:T(8,128)(2,1)S(1)} %get-tuple-element.375), channel_id=1, source_target_pairs={{0,2},{1,3},{2,0},{3,1},{4,6},{5,7},{6,4},{7,5},{8,10},{9,11},{10,... | collective-permute-start | bytes 1966088 | tf_op jit(solution)/shard_map/ppermute | solution.py:79
  439.1 74.8 %collective-permute-start.20 = (bf16[512,640]{1,0:T(8,128)(2,1)S(1)}, bf16[512,640]{1,0:T(8,128)(2,1)S(1)}, u32[]{:S(2)}, u32[]{:S(2)}) collective-permute-start(bf16[512,640]{1,0:T(8,128)(2,1)S(1)} %get-tuple-element.374), channel_id=1, source_target_pairs={{0,3},{1,0},{2,1},{3,2},{4,7},{5,4},{6,5},{7,6},{8,11},{9,8},{10,9... | collective-permute-start | bytes 1966088 | tf_op jit(solution)/shard_map/ppermute | solution.py:79
  439.2 85.0 %collective-permute-start.12 = (bf16[512,640]{1,0:T(8,128)(2,1)S(1)}, bf16[512,640]{1,0:T(8,128)(2,1)S(1)}, u32[]{:S(2)}, u32[]{:S(2)}) collective-permute-start(bf16[512,640]{1,0:T(8,128)(2,1)S(1)} %get-tuple-element.376), channel_id=1, source_target_pairs={{0,1},{1,2},{2,3},{3,0},{4,5},{5,6},{6,7},{7,4},{8,9},{9,10},{10,1... | collective-permute-start | bytes 1966088 | tf_op jit(solution)/shard_map/ppermute | solution.py:79
  440.6 97.6 %collective-permute-start.13 = (bf16[512,640]{1,0:T(8,128)(2,1)S(1)}, bf16[512,640]{1,0:T(8,128)(2,1)S(1)}, u32[]{:S(2)}, u32[]{:S(2)}) collective-permute-start(bf16[512,640]{1,0:T(8,128)(2,1)S(1)} %get-tuple-element.378), channel_id=1, source_target_pairs={{0,2},{1,3},{2,0},{3,1},{4,6},{5,7},{6,4},{7,5},{8,10},{9,11},{10,... | collective-permute-start | bytes 1966088 | tf_op jit(solution)/shard_map/ppermute | solution.py:79
  442.4 99.6 %collective-permute-start.14 = (bf16[512,640]{1,0:T(8,128)(2,1)S(1)}, bf16[512,640]{1,0:T(8,128)(2,1)S(1)}, u32[]{:S(2)}, u32[]{:S(2)}) collective-permute-start(bf16[512,640]{1,0:T(8,128)(2,1)S(1)} %get-tuple-element.377), channel_id=1, source_target_pairs={{0,3},{1,0},{2,1},{3,2},{4,7},{5,4},{6,5},{7,6},{8,11},{9,8},{10,9... | collective-permute-start | bytes 1966088 | tf_op jit(solution)/shard_map/ppermute | solution.py:79
  545.2 55.1 %collective-permute-start.25 = (bf16[512,640]{1,0:T(8,128)(2,1)S(1)}, bf16[512,640]{1,0:T(8,128)(2,1)S(1)}, u32[]{:S(2)}, u32[]{:S(2)}) collective-permute-start(bf16[512,640]{1,0:T(8,128)(2,1)S(1)} %get-tuple-element.346), channel_id=1, source_target_pairs={{0,2},{1,3},{2,0},{3,1},{4,6},{5,7},{6,4},{7,5},{8,10},{9,11},{10,... | collective-permute-start | bytes 1966088 | tf_op jit(solution)/shard_map/ppermute | solution.py:79
  545.3 57.0 %collective-permute-start.26 = (bf16[512,640]{1,0:T(8,128)(2,1)S(1)}, bf16[512,640]{1,0:T(8,128)(2,1)S(1)}, u32[]{:S(2)}, u32[]{:S(2)}) collective-permute-start(bf16[512,640]{1,0:T(8,128)(2,1)S(1)} %get-tuple-element.346), channel_id=1, source_target_pairs={{0,3},{1,0},{2,1},{3,2},{4,7},{5,4},{6,5},{7,6},{8,11},{9,8},{10,9... | collective-permute-start | bytes 1966088 | tf_op jit(solution)/shard_map/ppermute | solution.py:79
  630.7 86.9 %collective-permute-start.30 = (f32[2,512]{1,0:T(2,128)}, f32[2,512]{1,0:T(2,128)}, u32[]{:S(2)}, u32[]{:S(2)}) collective-permute-start(f32[2,512]{1,0:T(2,128)} %pad_maximum_fusion.18), channel_id=1, source_target_pairs={{0,1},{1,2},{2,3},{3,0},{4,5},{5,6},{6,7},{7,4},{8,9},{9,10},{10,1... | collective-permute-start | bytes 12296 | tf_op jit(solution)/shard_map/ppermute | solution.py:79
  630.7 86.9 %collective-permute-start.31 = (f32[2,512]{1,0:T(2,128)}, f32[2,512]{1,0:T(2,128)}, u32[]{:S(2)}, u32[]{:S(2)}) collective-permute-start(f32[2,512]{1,0:T(2,128)} %pad_maximum_fusion.18), channel_id=1, source_target_pairs={{0,2},{1,3},{2,0},{3,1},{4,6},{5,7},{6,4},{7,5},{8,10},{9,11},{10,... | collective-permute-start | bytes 12296 | tf_op jit(solution)/shard_map/ppermute | solution.py:79
  633.8 85.3 %collective-permute-start.32 = (f32[2,512]{1,0:T(2,128)}, f32[2,512]{1,0:T(2,128)}, u32[]{:S(2)}, u32[]{:S(2)}) collective-permute-start(f32[2,512]{1,0:T(2,128)} %pad_maximum_fusion.18), channel_id=1, source_target_pairs={{0,3},{1,0},{2,1},{3,2},{4,7},{5,4},{6,5},{7,6},{8,11},{9,8},{10,9... | collective-permute-start | bytes 12296 | tf_op jit(solution)/shard_map/ppermute | solution.py:79
  636.4 85.5 %collective-permute-start.36 = (f32[512,32]{0,1:T(8,128)S(1)}, f32[512,32]{0,1:T(8,128)S(1)}, u32[]{:S(2)}, u32[]{:S(2)}) collective-permute-start(f32[512,32]{0,1:T(8,128)S(1)} %pad_maximum_fusion.16), channel_id=1, source_target_pairs={{0,1},{1,2},{2,3},{3,0},{4,5},{5,6},{6,7},{7,4},{8,9},{9,10},{10,1... | collective-permute-start | bytes 196616 | tf_op jit(solution)/shard_map/ppermute | solution.py:79
  636.4 85.6 %collective-permute-start.37 = (f32[512,32]{0,1:T(8,128)S(1)}, f32[512,32]{0,1:T(8,128)S(1)}, u32[]{:S(2)}, u32[]{:S(2)}) collective-permute-start(f32[512,32]{0,1:T(8,128)S(1)} %pad_maximum_fusion.16), channel_id=1, source_target_pairs={{0,2},{1,3},{2,0},{3,1},{4,6},{5,7},{6,4},{7,5},{8,10},{9,11},{10,... | collective-permute-start | bytes 196616 | tf_op jit(solution)/shard_map/ppermute | solution.py:79
  719.1 21.9 %collective-permute-start.28 = (bf16[512,256]{0,1:T(8,128)(2,1)}, bf16[512,256]{0,1:T(8,128)(2,1)S(1)}, u32[]{:S(2)}, u32[]{:S(2)}) collective-permute-start(bf16[512,256]{0,1:T(8,128)(2,1)} %get-tuple-element.391), channel_id=1, source_target_pairs={{0,2},{1,3},{2,0},{3,1},{4,6},{5,7},{6,4},{7,5},{8,10},{9,11},{10,... | collective-permute-start | bytes 786440 | tf_op jit(solution)/shard_map/ppermute | solution.py:79
  722.0 21.4 %collective-permute-start.29 = (bf16[512,256]{0,1:T(8,128)(2,1)}, bf16[512,256]{0,1:T(8,128)(2,1)S(1)}, u32[]{:S(2)}, u32[]{:S(2)}) collective-permute-start(bf16[512,256]{0,1:T(8,128)(2,1)} %get-tuple-element.390), channel_id=1, source_target_pairs={{0,3},{1,0},{2,1},{3,2},{4,7},{5,4},{6,5},{7,6},{8,11},{9,8},{10,9... | collective-permute-start | bytes 786440 | tf_op jit(solution)/shard_map/ppermute | solution.py:79
  722.0 191.6 %collective-permute-start.72 = (bf16[1280,1600]{0,1:T(8,128)(2,1)}, bf16[1280,1600]{0,1:T(8,128)(2,1)}, u32[]{:S(2)}, u32[]{:S(2)}) collective-permute-start(bf16[1280,1600]{0,1:T(8,128)(2,1)} %convolution_convert_fusion), channel_id=1, source_target_pairs={{0,4},{4,0},{8,12},{12,8},{16,20},{20,16},{24,28},{28,24},{1,5},{5... | collective-permute-start | bytes 12288008 | tf_op jit(solution)/shard_map/ppermute | solution.py:84
  726.2 29.1 %collective-permute-start.52 = (bf16[128,1280]{1,0:T(8,128)(2,1)}, bf16[128,1280]{1,0:T(8,128)(2,1)}, u32[]{:S(2)}, u32[]{:S(2)}) collective-permute-start(bf16[128,1280]{1,0:T(8,128)(2,1)} %convolution_convert_fusion.13), channel_id=1, source_target_pairs={{0,4},{4,0},{8,12},{12,8},{16,20},{20,16},{24,28},{28,24},{1,5},{5... | collective-permute-start | bytes 983048 | tf_op jit(solution)/shard_map/ppermute | solution.py:84
  734.4 66.8 %collective-permute-start.47 = (bf16[384,960]{0,1:T(8,128)(2,1)}, bf16[384,960]{0,1:T(8,128)(2,1)}, u32[]{:S(2)}, u32[]{:S(2)}) collective-permute-start(bf16[384,960]{0,1:T(8,128)(2,1)} %convolution_convert_fusion.16), channel_id=1, source_target_pairs={{0,4},{4,0},{8,12},{12,8},{16,20},{20,16},{24,28},{28,24},{1,5},{5... | collective-permute-start | bytes 2211848 | tf_op jit(solution)/shard_map/ppermute | solution.py:84
  744.9 40.6 %collective-permute-start.39 = (f32[512]{0:T(512)S(1)}, f32[512]{0:T(512)S(1)}, u32[]{:S(2)}, u32[]{:S(2)}) collective-permute-start(f32[512]{0:T(512)S(1)} %multiply_add_fusion.5), channel_id=1, source_target_pairs={{0,1},{1,2},{2,3},{3,0},{4,5},{5,6},{6,7},{7,4},{8,9},{9,10},{10,1... | collective-permute-start | bytes 6152 | tf_op jit(solution)/shard_map/ppermute | solution.py:79
  745.0 40.9 %collective-permute-start.40 = (f32[512]{0:T(512)S(1)}, f32[512]{0:T(512)S(1)}, u32[]{:S(2)}, u32[]{:S(2)}) collective-permute-start(f32[512]{0:T(512)S(1)} %multiply_add_fusion.5), channel_id=1, source_target_pairs={{0,2},{1,3},{2,0},{3,1},{4,6},{5,7},{6,4},{7,5},{8,10},{9,11},{10,... | collective-permute-start | bytes 6152 | tf_op jit(solution)/shard_map/ppermute | solution.py:79
  785.6 144.1 %collective-permute-start.67 = (bf16[1280,1600]{0,1:T(8,128)(2,1)}, bf16[1280,1600]{0,1:T(8,128)(2,1)}, u32[]{:S(2)}, u32[]{:S(2)}) collective-permute-start(bf16[1280,1600]{0,1:T(8,128)(2,1)} %convolution_convert_fusion.2), channel_id=1, source_target_pairs={{0,4},{4,0},{8,12},{12,8},{16,20},{20,16},{24,28},{28,24},{1,5},{5... | collective-permute-start | bytes 12288008 | tf_op jit(solution)/shard_map/ppermute | solution.py:84
  785.9 17.7 %collective-permute-start.33 = (bf16[512,640]{1,0:T(8,128)(2,1)}, bf16[512,640]{1,0:T(8,128)(2,1)}, u32[]{:S(2)}, u32[]{:S(2)}) collective-permute-start(bf16[512,640]{1,0:T(8,128)(2,1)} %get-tuple-element.370), channel_id=1, source_target_pairs={{0,1},{1,2},{2,3},{3,0},{4,5},{5,6},{6,7},{7,4},{8,9},{9,10},{10,1... | collective-permute-start | bytes 1966088 | tf_op jit(solution)/shard_map/ppermute | solution.py:79
  785.9 56.7 %collective-permute-start.34 = (bf16[512,640]{1,0:T(8,128)(2,1)}, bf16[512,640]{1,0:T(8,128)(2,1)}, u32[]{:S(2)}, u32[]{:S(2)}) collective-permute-start(bf16[512,640]{1,0:T(8,128)(2,1)} %get-tuple-element.372), channel_id=1, source_target_pairs={{0,2},{1,3},{2,0},{3,1},{4,6},{5,7},{6,4},{7,5},{8,10},{9,11},{10,... | collective-permute-start | bytes 1966088 | tf_op jit(solution)/shard_map/ppermute | solution.py:79
  789.3 238.0 %all-to-all-start.1 = ((bf16[8,64,640]{2,1,0:T(8,128)(2,1)}), bf16[8,64,640]{2,1,0:T(8,128)(2,1)}, u32[]{:S(2)}, u32[]{:S(2)}) async-start(bf16[8,64,640]{2,1,0:T(8,128)(2,1)} %bitcast.18), calls=%async_computation.1 | async-start | bytes 1310720 | tf_op jit(solution)/shard_map/all_to_all | solution.py:554
  801.3 44.9 %collective-permute-start.35 = (bf16[512,640]{1,0:T(8,128)(2,1)}, bf16[512,640]{1,0:T(8,128)(2,1)}, u32[]{:S(2)}, u32[]{:S(2)}) collective-permute-start(bf16[512,640]{1,0:T(8,128)(2,1)} %get-tuple-element.371), channel_id=1, source_target_pairs={{0,3},{1,0},{2,1},{3,2},{4,7},{5,4},{6,5},{7,6},{8,11},{9,8},{10,9... | collective-permute-start | bytes 1966088 | tf_op jit(solution)/shard_map/ppermute | solution.py:79
  803.7 141.6 %collective-permute-start.62 = (bf16[1280,1600]{0,1:T(8,128)(2,1)}, bf16[1280,1600]{0,1:T(8,128)(2,1)}, u32[]{:S(2)}, u32[]{:S(2)}) collective-permute-start(bf16[1280,1600]{0,1:T(8,128)(2,1)} %convolution_convert_fusion.4), channel_id=1, source_target_pairs={{0,4},{4,0},{8,12},{12,8},{16,20},{20,16},{24,28},{28,24},{1,5},{5... | collective-permute-start | bytes 12288008 | tf_op jit(solution)/shard_map/ppermute | solution.py:84
  857.1 36.3 %collective-permute-start.57 = (bf16[1280,640]{1,0:T(8,128)(2,1)}, bf16[1280,640]{1,0:T(8,128)(2,1)}, u32[]{:S(2)}, u32[]{:S(2)}) collective-permute-start(bf16[1280,640]{1,0:T(8,128)(2,1)} %convolution_convert_fusion.9), channel_id=1, source_target_pairs={{0,4},{4,0},{8,12},{12,8},{16,20},{20,16},{24,28},{28,24},{1,5},{5... | collective-permute-start | bytes 4915208 | tf_op jit(solution)/shard_map/ppermute | solution.py:84
  926.0 31.6 %collective-permute-start.73 = (bf16[2,160,1600]{2,1,0:T(8,128)(2,1)}, bf16[2,160,1600]{2,1,0:T(8,128)(2,1)}, u32[]{:S(2)}, u32[]{:S(2)}) collective-permute-start(bf16[2,160,1600]{2,1,0:T(8,128)(2,1)} %fusion.41), channel_id=1, source_target_pairs={{0,8},{4,12},{8,0},{12,4},{16,24},{20,28},{24,16},{28,20},{1,9},{5... | collective-permute-start | bytes 3072008 | tf_op jit(solution)/shard_map/ppermute | solution.py:84
  927.8 33.4 %collective-permute-start.75 = (bf16[2,160,1600]{2,1,0:T(8,128)(2,1)S(1)}, bf16[2,160,1600]{2,1,0:T(8,128)(2,1)}, u32[]{:S(2)}, u32[]{:S(2)}) collective-permute-start(bf16[2,160,1600]{2,1,0:T(8,128)(2,1)S(1)} %fusion.42), channel_id=1, source_target_pairs={{0,16},{4,20},{8,24},{12,28},{16,0},{20,4},{24,8},{28,12},{1,17},{... | collective-permute-start | bytes 3072008 | tf_op jit(solution)/shard_map/ppermute | solution.py:84
  941.5 25.7 %collective-permute-start.68 = (bf16[2,160,1600]{2,1,0:T(8,128)(2,1)S(1)}, bf16[2,160,1600]{2,1,0:T(8,128)(2,1)}, u32[]{:S(2)}, u32[]{:S(2)}) collective-permute-start(bf16[2,160,1600]{2,1,0:T(8,128)(2,1)S(1)} %fusion.39), channel_id=1, source_target_pairs={{0,8},{4,12},{8,0},{12,4},{16,24},{20,28},{24,16},{28,20},{1,9},{5... | collective-permute-start | bytes 3072008 | tf_op jit(solution)/shard_map/ppermute | solution.py:84
  943.4 26.5 %collective-permute-start.70 = (bf16[2,160,1600]{2,1,0:T(8,128)(2,1)S(1)}, bf16[2,160,1600]{2,1,0:T(8,128)(2,1)}, u32[]{:S(2)}, u32[]{:S(2)}) collective-permute-start(bf16[2,160,1600]{2,1,0:T(8,128)(2,1)S(1)} %fusion.40), channel_id=1, source_target_pairs={{0,16},{4,20},{8,24},{12,28},{16,0},{20,4},{24,8},{28,12},{1,17},{... | collective-permute-start | bytes 3072008 | tf_op jit(solution)/shard_map/ppermute | solution.py:84
  955.3 34.6 %collective-permute-start.63 = (bf16[2,160,1600]{2,1,0:T(8,128)(2,1)S(1)}, bf16[2,160,1600]{2,1,0:T(8,128)(2,1)S(1)}, u32[]{:S(2)}, u32[]{:S(2)}) collective-permute-start(bf16[2,160,1600]{2,1,0:T(8,128)(2,1)S(1)} %fusion.37), channel_id=1, source_target_pairs={{0,8},{4,12},{8,0},{12,4},{16,24},{20,28},{24,16},{28,20},{1,9},{5... | collective-permute-start | bytes 3072008 | tf_op jit(solution)/shard_map/ppermute | solution.py:84
  957.7 34.2 %collective-permute-start.65 = (bf16[2,160,1600]{2,1,0:T(8,128)(2,1)S(1)}, bf16[2,160,1600]{2,1,0:T(8,128)(2,1)S(1)}, u32[]{:S(2)}, u32[]{:S(2)}) collective-permute-start(bf16[2,160,1600]{2,1,0:T(8,128)(2,1)S(1)} %fusion.38), channel_id=1, source_target_pairs={{0,16},{4,20},{8,24},{12,28},{16,0},{20,4},{24,8},{28,12},{1,17},{... | collective-permute-start | bytes 3072008 | tf_op jit(solution)/shard_map/ppermute | solution.py:84
  961.2 42.0 %collective-permute-start.74 = (bf16[160,1600]{1,0:T(8,128)(2,1)S(1)}, bf16[160,1600]{1,0:T(8,128)(2,1)S(1)}, u32[]{:S(2)}, u32[]{:S(2)}) collective-permute-start(bf16[160,1600]{1,0:T(8,128)(2,1)S(1)} %fusion.63), channel_id=1, source_target_pairs={{0,16},{4,20},{8,24},{12,28},{16,0},{20,4},{24,8},{28,12},{1,17},{... | collective-permute-start | bytes 1536008 | tf_op jit(solution)/shard_map/ppermute | solution.py:84
  967.2 37.3 %collective-permute-start.76 = (bf16[160,1600]{1,0:T(8,128)(2,1)S(1)}, bf16[160,1600]{1,0:T(8,128)(2,1)S(1)}, u32[]{:S(2)}, u32[]{:S(2)}) collective-permute-start(bf16[160,1600]{1,0:T(8,128)(2,1)S(1)} %fusion.64), channel_id=1, source_target_pairs={{0,8},{4,12},{8,0},{12,4},{16,24},{20,28},{24,16},{28,20},{1,9},{5... | collective-permute-start | bytes 1536008 | tf_op jit(solution)/shard_map/ppermute | solution.py:84
  969.9 44.8 %collective-permute-start.69 = (bf16[160,1600]{1,0:T(8,128)(2,1)S(1)}, bf16[160,1600]{1,0:T(8,128)(2,1)S(1)}, u32[]{:S(2)}, u32[]{:S(2)}) collective-permute-start(bf16[160,1600]{1,0:T(8,128)(2,1)S(1)} %fusion.61), channel_id=1, source_target_pairs={{0,16},{4,20},{8,24},{12,28},{16,0},{20,4},{24,8},{28,12},{1,17},{... | collective-permute-start | bytes 1536008 | tf_op jit(solution)/shard_map/ppermute | solution.py:84
  989.9 25.8 %collective-permute-start.71 = (bf16[160,1600]{1,0:T(8,128)(2,1)S(1)}, bf16[160,1600]{1,0:T(8,128)(2,1)S(1)}, u32[]{:S(2)}, u32[]{:S(2)}) collective-permute-start(bf16[160,1600]{1,0:T(8,128)(2,1)S(1)} %fusion.62), channel_id=1, source_target_pairs={{0,8},{4,12},{8,0},{12,4},{16,24},{20,28},{24,16},{28,20},{1,9},{5... | collective-permute-start | bytes 1536008 | tf_op jit(solution)/shard_map/ppermute | solution.py:84
  991.9 34.3 %collective-permute-start.64 = (bf16[160,1600]{1,0:T(8,128)(2,1)S(1)}, bf16[160,1600]{1,0:T(8,128)(2,1)S(1)}, u32[]{:S(2)}, u32[]{:S(2)}) collective-permute-start(bf16[160,1600]{1,0:T(8,128)(2,1)S(1)} %fusion.59), channel_id=1, source_target_pairs={{0,16},{4,20},{8,24},{12,28},{16,0},{20,4},{24,8},{28,12},{1,17},{... | collective-permute-start | bytes 1536008 | tf_op jit(solution)/shard_map/ppermute | solution.py:84
  1003.3 36.4 %collective-permute-start.66 = (bf16[160,1600]{1,0:T(8,128)(2,1)}, bf16[160,1600]{1,0:T(8,128)(2,1)}, u32[]{:S(2)}, u32[]{:S(2)}) collective-permute-start(bf16[160,1600]{1,0:T(8,128)(2,1)} %fusion.60), channel_id=1, source_target_pairs={{0,8},{4,12},{8,0},{12,4},{16,24},{20,28},{24,16},{28,20},{1,9},{5... | collective-permute-start | bytes 1536008 | tf_op jit(solution)/shard_map/ppermute | solution.py:84
  1055.5 34.3 %all-to-all-start.3 = ((bf16[8,64,640]{2,1,0:T(8,128)(2,1)}), bf16[8,64,640]{2,1,0:T(8,128)(2,1)S(1)}, u32[]{:S(2)}, u32[]{:S(2)}) async-start(bf16[8,64,640]{2,1,0:T(8,128)(2,1)} %bitcast.36), calls=%async_computation.3 | async-start | bytes 1310720 | tf_op jit(solution)/shard_map/all_to_all | solution.py:554
  1090.7 79.3 %all-to-all-start.4 = ((bf16[8,17,64,320]{3,2,1,0:T(8,128)(2,1)}), bf16[8,17,64,320]{3,2,1,0:T(8,128)(2,1)}, u32[]{:S(2)}, u32[]{:S(2)}) async-start(bf16[8,17,64,320]{3,2,1,0:T(8,128)(2,1)} %bitcast.468), calls=%async_computation.4 | async-start | bytes 13369344 | tf_op jit(solution)/shard_map/all_to_all | solution.py:255
  1170.0 48.5 %all-to-all-start.7 = ((bf16[8,3,64,96]{3,2,1,0:T(8,128)(2,1)}), bf16[8,3,64,96]{3,2,1,0:T(8,128)(2,1)S(1)}, u32[]{:S(2)}, u32[]{:S(2)}) async-start(bf16[8,3,64,96]{3,2,1,0:T(8,128)(2,1)} %copy-done.7), calls=%async_computation.7 | async-start | bytes 786432 | tf_op jit(solution)/shard_map/all_to_all | solution.py:273
  1219.3 91.8 %all-to-all-start.5 = ((bf16[8,17,64,320]{3,2,1,0:T(8,128)(2,1)}), bf16[8,17,64,320]{3,2,1,0:T(8,128)(2,1)}, u32[]{:S(2)}, u32[]{:S(2)}) async-start(bf16[8,17,64,320]{3,2,1,0:T(8,128)(2,1)} %get-tuple-element.50), calls=%async_computation.5 | async-start | bytes 13369344 | tf_op jit(solution)/shard_map/all_to_all | solution.py:273
  (199 other events, 3658.0 us)
Sparse Core Ops, SparseCore 0:
  10.5 31.5 all-gather.20
  44.5 30.0 all-gather.18
  76.6 32.8 all-gather.10
  111.2 54.9 all-gather.16
  167.9 54.9 all-gather.12
  224.6 54.9 all-gather.14

commit v2 on v1

--- a/solution.py
+++ b/solution.py
@@ -1,3 +1,5 @@
+import functools
+
 import jax
 import jax.numpy as jnp
 from jax import lax
@@ -84,76 +86,344 @@
     return lax.ppermute(value, "wide", [(i, i ^ bit) for i in range(count)])
 
 
-def gather_features(features):
+def along_line(value, pairs):
+    return lax.ppermute(value, "narrow", pairs)
+
+
+pairs_next = [(0, 1), (1, 0), (2, 3), (3, 2)]
+pairs_second = [(0, 2), (2, 0), (1, 3), (3, 1)]
+pairs_inner = [(1, 2), (2, 1)]
+pairs_outward = [(1, 0), (2, 3)]
+pairs_inward = [(0, 1), (3, 2)]
+
+
+def gather_features(features, hold=None):
     count = lax.axis_size("narrow")
     index = lax.axis_index("narrow")
     width = features.shape[1]
-    parts = [features] + [shifted(features, step) for step in range(1, count)]
+    second = along_line(features, pairs_second)
+    near = along_line(features, pairs_next)
+    inner = along_line(features, pairs_inner)
+    if hold is not None:
+        second, hold = tie(second, hold)
+    outer = along_line(second, pairs_outward)
+    third = jnp.where((index == 1) | (index == 2), inner, outer)
+    parts = [features, near, second, third]
+    places = [index ^ step for step in range(count)]
     joined = jnp.zeros((features.shape[0], count * width), features.dtype)
-    for step, part in enumerate(parts):
-        joined = lax.dynamic_update_slice(joined, part, (0, ((index - step) % count) * width))
-    return joined
-
-
-def reduce_features(features):
-    count = lax.axis_size("narrow")
+    for place, part in zip(places, parts):
+        joined = lax.dynamic_update_slice(joined, part, (0, place * width))
+    return joined if hold is None else (joined, hold)
+
+
+def line_piece(features, place):
+    width = features.shape[1] // lax.axis_size("narrow")
+    return lax.dynamic_slice_in_dim(features, place * width, width, 1)
+
+
+def reduce_start(features):
     index = lax.axis_index("narrow")
-    width = features.shape[1] // count
-
-    def piece(step):
-        return lax.dynamic_slice_in_dim(features, ((index + step) % count) * width, width, 1)
-
-    arrived = [shifted(piece(step), step) for step in range(1, count)]
-    total = piece(0).astype(f32)
+    far = line_piece(features, index ^ 3)
+    passed = along_line(far, pairs_inward)
+    inner = along_line(far, pairs_inner)
+    near = along_line(line_piece(features, index ^ 1), pairs_next)
+    return passed, inner, near
+
+
+def reduce_relay(features, passed):
+    index = lax.axis_index("narrow")
+    return (line_piece(features, index ^ 2).astype(f32) + passed.astype(f32)).astype(bf16)
+
+
+def reduce_end(features, arrived):
+    index = lax.axis_index("narrow")
+    total = line_piece(features, index).astype(f32)
     for part in arrived:
         total = total + part.astype(f32)
     return total
 
 
+def reduce_features(features):
+    passed, inner, near = reduce_start(features)
+    second = along_line(reduce_relay(features, passed), pairs_second)
+    return reduce_end(features, (inner, near, second))
+
+
+def gather_small(values):
+    count = lax.axis_size("narrow")
+    index = lax.axis_index("narrow")
+    joined = jnp.zeros((count, values.shape[0]), values.dtype)
+    for step in range(count):
+        part = shifted(values, step) if step else values
+        joined = lax.dynamic_update_slice(joined, part[None], ((index - step) % count, 0))
+    return joined
+
+
+def tie(*values):
+    return lax.optimization_barrier(values)
+
+
+def wide_totals(values):
+    bit = 1
+    while bit < lax.axis_size("wide"):
+        values = values + flipped(values, bit)
+        bit *= 2
+    return values
+
+
+def row_parts(values):
+    return [values] + [shifted(values, step) for step in range(1, lax.axis_size("narrow"))]
+
+
 def row_totals(values):
     count = lax.axis_size("narrow")
     return values + sum(shifted(values, step) for step in range(1, count))
 
 
-def relative_chunks(features):
+def halving_orders(count):
+    bits = list(range(1, count.bit_length() - 1))
+    middle = len(bits) // 2
+    return [bits, bits[middle:] + bits[:middle]]
+
+
+def chunk_rows(features):
     count = lax.axis_size("wide")
-    order = lax.axis_index("wide") ^ jnp.arange(count, dtype=jnp.int32)
-    turned = features.T.reshape(count, features.shape[1] // count, features.shape[0])
-    return jnp.take(turned, order, axis=0)
-
-
-def scatter_rows(left_chunks, right_side):
-    count, rows, tokens = left_chunks.shape
-    bits = count.bit_length() - 1
-    columns = right_side.shape[1]
-    near = left_chunks[0::2].reshape(-1, tokens)
-    away = left_chunks[1::2].reshape(-1, tokens)
-    sent = flipped(product(away, right_side).astype(bf16), 1)
-    kept = product(near, right_side).astype(bf16)
-    shape = (2,) * (bits - 1) + (rows, columns)
-    sent = sent.reshape(shape)
-    kept = kept.reshape(shape)
-    first_bits = list(range(1, bits))
-    middle = (bits - 1) // 2
-    half = rows // 2
-    results = []
-    for begin, order in (
-        (0, first_bits),
-        (half, first_bits[middle:] + first_bits[:middle]),
-    ):
-        total = kept[..., begin : begin + half, :].astype(f32) + sent[
-            ..., begin : begin + half, :
-        ].astype(f32)
-        dims = list(range(bits - 1, 0, -1))
-        for bit in order:
-            at = dims.index(bit)
-            dims.pop(at)
-            away_part = lax.index_in_dim(total, 1, at, keepdims=False)
-            near_part = lax.index_in_dim(total, 0, at, keepdims=False)
-            arrived = flipped(away_part.astype(bf16), 1 << bit)
-            total = near_part + arrived.astype(f32)
-        results.append(total)
-    return jnp.concatenate(results, axis=0)
+    tokens, width = features.shape
+    places = []
+    for core in (1, 0):
+        for half, order in enumerate(halving_orders(count)):
+            chunks = [core]
+            for bit in reversed(order):
+                chunks = chunks + [chunk | (1 << bit) for chunk in chunks]
+            places.append([(chunk, half) for chunk in chunks])
+    chunks = jnp.array([chunk for group in places for chunk, _ in group], jnp.int32)
+    halves = jnp.array([half for group in places for _, half in group], jnp.int32)
+    pieces = features.T.reshape(2 * count, width // (2 * count), tokens)
+    order = 2 * (lax.axis_index("wide") ^ chunks) + halves
+    rows = jnp.take(pieces, order, axis=0, mode="clip").reshape(width, tokens)
+    return rows[: width // 2], rows[width // 2 :]
+
+
+def halves_of(rows):
+    half = rows.shape[0] // 2
+    return rows[:half], rows[half:]
+
+
+def summed(values):
+    total = values[0].astype(f32)
+    for value in values[1:]:
+        total = total + value.astype(f32)
+    return total
+
+
+def add_kernel(sizes, rows, *refs):
+    outs = refs[sum(sizes) :]
+    begin = 0
+    for group, size in enumerate(sizes):
+        columns = outs[0].shape[1]
+        total = summed([ref[:, :columns] for ref in refs[begin : begin + size]])
+        begin += size
+        if len(outs) == 1:
+            outs[0][group * rows : (group + 1) * rows, :] = total.astype(outs[0].dtype)
+        else:
+            outs[group][...] = total.astype(outs[group].dtype)
+
+
+def add_rows(groups, place, rows, joined, kept):
+    columns = groups[0][0].shape[1]
+    start = place * rows
+    if rows % 16:
+        totals = [summed([part[start : start + rows] for part in parts]) for parts in groups]
+        if joined:
+            return jnp.concatenate(totals, axis=0)[:, :kept]
+        return [total.astype(bf16) for total in totals]
+    steps = 1 if joined or rows % 32 else 2
+    block = rows // steps
+    source = pl.BlockSpec((block, columns), lambda step: (place * steps + step, 0))
+    if joined:
+        out_specs = [pl.BlockSpec((len(groups) * rows, kept), lambda step: (0, 0))]
+        out_shape = [jax.ShapeDtypeStruct((len(groups) * rows, kept), f32)]
+    else:
+        out_specs = [pl.BlockSpec((block, columns), lambda step: (step, 0))] * len(groups)
+        out_shape = [jax.ShapeDtypeStruct((rows, columns), bf16)] * len(groups)
+    outs = pl.pallas_call(
+        functools.partial(add_kernel, [len(parts) for parts in groups], block),
+        grid=(steps,),
+        in_specs=[source] * sum(len(parts) for parts in groups),
+        out_specs=out_specs,
+        out_shape=out_shape,
+        compiler_params=pltpu.CompilerParams(vmem_limit_bytes=48 * 1024 * 1024),
+    )(*[part for parts in groups for part in parts])
+    return outs[0] if joined else list(outs)
+
+
+class Scatter:
+    def __init__(self, products):
+        near, away = products[:2], products[2:]
+        self.orders = halving_orders(lax.axis_size("wide"))
+        self.parts = [[own, flipped(sent, 1)] for own, sent in zip(near, away)]
+        self.rows = near[0].shape[0]
+        self.stage = 0
+
+    def outgoing(self):
+        return add_rows(self.parts, 1, self.rows // 2, False, None)
+
+    def send(self, sending):
+        for at, value in enumerate(sending):
+            bit = 1 << self.orders[at][self.stage]
+            self.parts[at] = self.parts[at] + [flipped(value, bit)]
+        self.rows //= 2
+        self.stage += 1
+
+    def step(self):
+        self.send(self.outgoing())
+
+    def finish(self, kept):
+        while self.stage < len(self.orders[0]):
+            self.step()
+        return add_rows(self.parts, 0, self.rows, True, kept)
+
+
+def chunk_kernel(order_ref, left_ref, right_ref, near_a, near_b, away_a, away_b, whole_ref):
+    core = order_ref[2 * pl.num_programs(0)]
+    rows = near_a.shape[0]
+    whole_ref[...] = inner_rows(left_ref[...], right_ref[...])
+    near = pl.multiple_of(core * 2 * rows, 2 * rows)
+    away = pl.multiple_of((1 - core) * 2 * rows, 2 * rows)
+    columns = whole_ref.shape[1]
+    for out, start in ((near_a, near), (near_b, near + rows), (away_a, away), (away_b, away + rows)):
+        out[:, :columns] = whole_ref[pl.ds(start, rows), :].astype(bf16)
+        if out.shape[1] > columns:
+            out[:, columns:] = jnp.zeros((rows, out.shape[1] - columns), bf16)
+
+
+def chunk_places(count):
+    table = []
+    for order in halving_orders(count):
+        chips = [0]
+        for bit in reversed(order):
+            chips = chips + [chip | (1 << (bit - 1)) for chip in chips]
+        table.append([chips.index(chip) for chip in range(count // 2)])
+    return table
+
+
+def chunk_products(left, right):
+    count = lax.axis_size("wide")
+    tokens, width = left.shape
+    columns = right.shape[1]
+    chips = count // 2
+    group = width // chips
+    rows = group // 4
+    if group % 128 or rows % 16:
+        away, near = [product(part, right).astype(bf16) for part in chunk_rows(left)]
+        return [*halves_of(near), *halves_of(away)]
+    index = lax.axis_index("wide")
+    relative = (index // 2) ^ jnp.arange(chips, dtype=jnp.int32)
+    order = jnp.concatenate(
+        [jnp.array(table, jnp.int32)[relative] for table in chunk_places(count)]
+        + [(index % 2)[None]]
+    ).astype(jnp.int32)
+    padded = -(-columns // 128) * 128
+    first = pl.BlockSpec((rows, padded), lambda step, at: (at[step], 0))
+    last = pl.BlockSpec((rows, padded), lambda step, at: (at[pl.num_programs(0) + step], 0))
+    return list(
+        pl.pallas_call(
+            chunk_kernel,
+            grid_spec=pltpu.PrefetchScalarGridSpec(
+                num_scalar_prefetch=1,
+                grid=(chips,),
+                in_specs=[
+                    pl.BlockSpec((tokens, group), lambda step, at: (0, step)),
+                    pl.BlockSpec((tokens, columns), lambda step, at: (0, 0)),
+                ],
+                out_specs=[first, last, first, last],
+                scratch_shapes=[pltpu.VMEM((group, columns), f32)],
+            ),
+            out_shape=[jax.ShapeDtypeStruct((chips * rows, padded), bf16)] * 4,
+            compiler_params=pltpu.CompilerParams(vmem_limit_bytes=48 * 1024 * 1024),
+        )(order, left, right)
+    )
+
+
+def pack_kernel(send_ref, *refs):
+    count = len(refs) - 3
+    blocks, outs, turned = refs[:count], refs[count : count + 2], refs[-1]
+    begin = 0
+    for block in blocks:
+        width = block.shape[1]
+        turned[begin : begin + width, :] = block[...].T.astype(bf16)
+        begin += width
+    capacity = outs[0].shape[1] + outs[1].shape[1]
+    for out, offset in zip(outs, (0, outs[0].shape[1])):
+        slots = out.shape[1]
+
+        def place(step, carry, out=out, offset=offset, slots=slots):
+            owner = step // slots
+            slot = step % slots
+            unit = send_ref[owner * capacity + offset + slot]
+            out[owner, slot] = turned[pl.ds(pl.multiple_of(unit * SLAB, SLAB), SLAB), :]
+            return carry
+
+        lax.fori_loop(0, out.shape[0] * slots, place, 0)
+
+
+def pack_units(send, blocks, count, sizes):
+    rows = blocks[0].shape[0]
+    total = sum(block.shape[1] for block in blocks)
+    vmem = pl.BlockSpec(memory_space=pltpu.VMEM)
+    return pl.pallas_call(
+        pack_kernel,
+        in_specs=[pl.BlockSpec(memory_space=pltpu.SMEM)] + [vmem] * len(blocks),
+        out_specs=[vmem] * 2,
+        out_shape=[jax.ShapeDtypeStruct((count, size, SLAB, rows), bf16) for size in sizes],
+        scratch_shapes=[pltpu.VMEM((total, rows), bf16)],
+        compiler_params=pltpu.CompilerParams(vmem_limit_bytes=56 * 1024 * 1024),
+    )(send, *blocks)
+
+
+def unpack_kernel(back_ref, first_ref, last_ref, *refs):
+    count = (len(refs) - 1) // 2
+    weights, outs, turned = refs[:count], refs[count : 2 * count], refs[-1]
+    first = first_ref.shape[1]
+    capacity = first + last_ref.shape[1]
+
+    def place(unit, carry):
+        slot = back_ref[unit]
+        owner = slot // capacity
+        at = slot % capacity
+        rows = pl.ds(pl.multiple_of(unit * SLAB, SLAB), SLAB)
+
+        @pl.when(at < first)
+        def _():
+            turned[rows, :] = first_ref[owner, at]
+
+        @pl.when(at >= first)
+        def _():
+            turned[rows, :] = last_ref[owner, at - first]
+
+        return carry
+
+    lax.fori_loop(0, turned.shape[0] // SLAB, place, 0)
+    begin = 0
+    for weight, out in zip(weights, outs):
+        width = out.shape[1]
+        steps = turned[begin : begin + width, :].astype(f32).T
+        out[...] = weight[...].astype(f32) + steps
+        begin += width
+
+
+def unpack_units(back, first, last, weights):
+    rows = first.shape[3]
+    total = sum(weight.shape[1] for weight in weights)
+    vmem = pl.BlockSpec(memory_space=pltpu.VMEM)
+    return pl.pallas_call(
+        unpack_kernel,
+        in_specs=[pl.BlockSpec(memory_space=pltpu.SMEM)] + [vmem] * (2 + len(weights)),
+        out_specs=[vmem] * len(weights),
+        out_shape=[jax.ShapeDtypeStruct(weight.shape, f32) for weight in weights],
+        scratch_shapes=[pltpu.VMEM((total, rows), bf16)],
+        compiler_params=pltpu.CompilerParams(vmem_limit_bytes=56 * 1024 * 1024),
+    )(back, first, last, *weights)
 
 
 def unit_rates(col_widths, rates):
@@ -165,23 +435,13 @@
     )
 
 
-def slot_kernel(scale_ref, gradient_ref, left_ref, right_ref, moment_ref, square_ref,
-                change_ref, new_moment_ref, new_square_ref, whole_ref, turned_ref):
-    slot = pl.program_id(0)
-    sources, rows = gradient_ref.shape[0], gradient_ref.shape[3]
+def rotated_step(gradient, left_ref, right_ref, moment_ref, square_ref, new_moment_ref,
+                 new_square_ref, turned_ref, occupied, first_scale, second_scale):
     blocks = left_ref.shape[1] // BASIS
     right_basis = right_ref[0].astype(bf16)
-    for source in range(sources):
-        whole_ref[:, source * rows : (source + 1) * rows] = gradient_ref[source, 0].astype(f32)
-    rate = scale_ref[slot]
-    occupied = scale_ref[pl.num_programs(0) + slot]
-    first_scale = scale_ref[2 * pl.num_programs(0)]
-    second_scale = scale_ref[2 * pl.num_programs(0) + 1]
     turned_ref[...] = lax.dot_general(
-        right_basis, whole_ref[...].astype(bf16), (((0,), (0,)), ((), ())),
-        preferred_element_type=f32,
-    )
-
+        right_basis, gradient, (((0,), (0,)), ((), ())), preferred_element_type=f32
+    )
     for block in range(blocks):
         at = slice(block * BASIS, (block + 1) * BASIS)
         left_basis = left_ref[0, at, :].astype(bf16)
@@ -197,87 +457,212 @@
             direction.astype(bf16), left_basis, (((1,), (1,)), ((), ())),
             preferred_element_type=f32,
         )
-    whole_ref[...] = rate * jnp.dot(
-        right_basis, turned_ref[...].astype(bf16), preferred_element_type=f32
-    )
-    for source in range(sources):
-        change_ref[source, 0] = whole_ref[:, source * rows : (source + 1) * rows].astype(bf16)
-
-
-def slot_steps(gradient, left_basis, right_basis, moment, square, scales):
-    sources, capacity, _, rows = gradient.shape
+    return jnp.dot(right_basis, turned_ref[...].astype(bf16), preferred_element_type=f32)
+
+
+def slot_kernel(place_ref, scale_ref, gradient_ref, left_ref, right_ref, moment_ref, square_ref,
+                change_ref, new_moment_ref, new_square_ref, whole_ref, turned_ref):
+    step = pl.program_id(0)
+    steps = pl.num_programs(0)
+    sources, rows = gradient_ref.shape[0], gradient_ref.shape[3]
+    rate = scale_ref[step]
+    occupied = scale_ref[steps + step]
+
+    @pl.when(occupied > 0.5)
+    def _():
+        for source in range(sources):
+            whole_ref[:, source * rows : (source + 1) * rows] = gradient_ref[source, 0].astype(f32)
+        whole_ref[...] = rate * rotated_step(
+            whole_ref[...].astype(bf16), left_ref, right_ref, moment_ref, square_ref,
+            new_moment_ref, new_square_ref, turned_ref, occupied,
+            scale_ref[2 * steps], scale_ref[2 * steps + 1],
+        )
+        for source in range(sources):
+            change_ref[source, 0] = whole_ref[:, source * rows : (source + 1) * rows].astype(bf16)
+
+    @pl.when(occupied <= 0.5)
+    def _():
+        change_ref[...] = jnp.zeros_like(change_ref)
+
+    @pl.when(jnp.logical_and(occupied <= 0.5, place_ref[steps + step] > 0))
+    def _():
+        new_moment_ref[...] = moment_ref[...]
+        new_square_ref[...] = square_ref[...]
+
+
+def slot_call(places, scales, gradient, left_basis, right_basis, moment, square, written):
+    sources, steps, _, rows = gradient.shape
     row_count = sources * rows
     moment = moment.transpose(0, 2, 1)
     square = square.transpose(0, 2, 1)
-    state = pl.BlockSpec((1, SLAB, row_count), lambda slot: (slot, 0, 0))
-    traded = pl.BlockSpec((sources, 1, SLAB, rows), lambda slot: (0, slot, 0, 0))
+    state = pl.BlockSpec((1, SLAB, row_count), lambda step, place: (place[step], 0, 0))
+    traded = pl.BlockSpec((sources, 1, SLAB, rows), lambda step, place: (0, step, 0, 0))
+    operands = [places, scales, gradient, left_basis, right_basis, moment, square]
+    in_specs = [
+        pl.BlockSpec(memory_space=pltpu.SMEM),
+        traded,
+        pl.BlockSpec((1, row_count, BASIS), lambda step, place: (place[step], 0, 0)),
+        pl.BlockSpec((1, SLAB, SLAB), lambda step, place: (place[step], 0, 0)),
+        state,
+        state,
+    ]
+    aliases = {}
+    kernel = slot_kernel
+    if written == "same":
+        aliases = {5: 1, 6: 2}
+    elif written is not None:
+        operands += [value.transpose(0, 2, 1) for value in written]
+        in_specs += [pl.BlockSpec(memory_space=pl.ANY)] * 2
+        aliases = {7: 1, 8: 2}
+
+        def kernel(*refs):
+            slot_kernel(*refs[:7], *refs[9:])
+
     change, new_moment, new_square = pl.pallas_call(
-        slot_kernel,
-        grid=(capacity,),
-        in_specs=[
-            pl.BlockSpec(memory_space=pltpu.SMEM),
-            traded,
-            pl.BlockSpec((1, row_count, BASIS), lambda slot: (slot, 0, 0)),
-            pl.BlockSpec((1, SLAB, SLAB), lambda slot: (slot, 0, 0)),
-            state,
-            state,
-        ],
-        out_specs=[traded, state, state],
+        kernel,
+        grid_spec=pltpu.PrefetchScalarGridSpec(
+            num_scalar_prefetch=1,
+            grid=(steps,),
+            in_specs=in_specs,
+            out_specs=[traded, state, state],
+            scratch_shapes=[
+                pltpu.VMEM((SLAB, row_count), f32),
+                pltpu.VMEM((SLAB, row_count), f32),
+            ],
+        ),
         out_shape=[
             jax.ShapeDtypeStruct(gradient.shape, bf16),
             jax.ShapeDtypeStruct(moment.shape, f32),
             jax.ShapeDtypeStruct(square.shape, f32),
         ],
-        scratch_shapes=[
-            pltpu.VMEM((SLAB, row_count), f32),
-            pltpu.VMEM((SLAB, row_count), f32),
-        ],
+        input_output_aliases=aliases,
         compiler_params=pltpu.CompilerParams(vmem_limit_bytes=48 * 1024 * 1024),
-    )(scales, gradient, left_basis, right_basis, moment, square)
+    )(*operands)
     return change, new_moment.transpose(0, 2, 1), new_square.transpose(0, 2, 1)
 
 
-def owner_step(
-    blocks, owner_ids, left_basis, right_basis, moment, square, rate_table, wide_index, tcount
-):
-    wide_count = lax.axis_size("wide")
+def slot_group(scales, gradient, left_basis, right_basis, moment, square, group, written):
     capacity = moment.shape[0]
-    rows = blocks[0].shape[0]
-    unit_rows = jnp.concatenate([block.T for block in blocks], axis=0).astype(bf16)
-    unit_rows = unit_rows.reshape(-1, SLAB, rows)
-    units = unit_rows.shape[0]
-    slots = jnp.arange(wide_count * capacity, dtype=jnp.int32)
-    matches = slots[:, None] == owner_ids[None, :]
+    count = group.stop - group.start
+    places = jnp.concatenate(
+        [
+            jnp.arange(group.start, group.stop, dtype=jnp.int32),
+            jnp.ones((count,), jnp.int32),
+        ]
+    )
+    scales = jnp.concatenate(
+        [
+            scales[group],
+            scales[capacity + group.start : capacity + group.stop],
+            scales[2 * capacity :],
+        ]
+    )
+    return slot_call(places, scales, gradient, left_basis, right_basis, moment, square, written)
+
+
+def all_slots(scales, gradient, left_basis, right_basis, moment, square):
+    group = slice(0, moment.shape[0])
+    return slot_group(
+        scales, gradient, left_basis, right_basis, moment, square, group, None
+    )
+
+
+def late_steps(places, scales, gradient, left_basis, right_basis, moment, square):
+    return slot_call(places, scales, gradient, left_basis, right_basis, moment, square, "same")
+
+
+def correction_scales(tcount):
+    return jnp.stack([1.0 / (1.0 - beta_one**tcount), 1.0 / (1.0 - beta_two**tcount)])
+
+
+def slot_scales(owners, rates, capacity, wide_index, tcount):
+    slot_ids = wide_index * capacity + jnp.arange(capacity, dtype=jnp.int32)
+    own = (owners[None, :] == slot_ids[:, None]).astype(f32)
+    return jnp.concatenate(
+        [
+            -jnp.sum(own * rates[None, :], axis=1),
+            jnp.sum(own, axis=1),
+            correction_scales(tcount),
+        ]
+    )
+
+
+def ranks_within(owners, capacity):
+    device = owners // capacity
+    units = owners.shape[0]
+    earlier = jnp.arange(units)[None, :] < jnp.arange(units)[:, None]
+    return jnp.sum(
+        jnp.where(earlier & (device[None, :] == device[:, None]), 1, 0).astype(jnp.int32), axis=1
+    )
+
+
+def routes(owners, capacity, room, wide_count):
+    units = owners.shape[0]
+    if room == capacity:
+        places = owners
+    else:
+        places = owners // capacity * room + ranks_within(owners, capacity)
+    slots = jnp.arange(wide_count * room, dtype=jnp.int32)
+    matches = slots[:, None] == places[None, :]
     unit_of = jnp.sum(
         jnp.where(matches, jnp.arange(units, dtype=jnp.int32)[None, :], 0), axis=1
     )
-    sending = jnp.take(unit_rows, unit_of, axis=0, mode="clip")
-    owned = lax.all_to_all(
-        sending.reshape(wide_count, capacity, SLAB, rows), "wide", split_axis=0, concat_axis=0,
-        tiled=True,
-    )
-    slot_ids = wide_index * capacity + jnp.arange(capacity, dtype=jnp.int32)
-    own = (owner_ids[None, :] == slot_ids[:, None]).astype(f32)
-    slot_rate = -jnp.sum(own * rate_table[None, :], axis=1)
+    return jnp.minimum(unit_of, units - 1), places
+
+
+def late_places(owners, rates, capacity, room, wide_index, tcount):
+    ranks = ranks_within(owners, capacity)
+    mine = owners // capacity == wide_index
+    own = mine[None, :] & (ranks[None, :] == jnp.arange(room, dtype=jnp.int32)[:, None])
+    slot = jnp.sum(jnp.where(own, (owners % capacity)[None, :], 0), axis=1)
+    filled = jnp.sum(own.astype(jnp.int32), axis=1)
+    last = jnp.maximum(jnp.sum(filled) - 1, 0)
+    last_slot = jnp.sum(jnp.where(jnp.arange(room) == last, slot, 0))
+    places = jnp.where(filled > 0, slot, last_slot)
+    untouched = jnp.where((jnp.arange(room) == 0) & (filled == 0), 1, 0)
     scales = jnp.concatenate(
         [
-            slot_rate,
-            jnp.sum(own, axis=1),
-            (1.0 / (1.0 - beta_one**tcount))[None],
-            (1.0 / (1.0 - beta_two**tcount))[None],
+            -jnp.sum(own.astype(f32) * rates[None, :], axis=1),
+            filled.astype(f32),
+            correction_scales(tcount),
         ]
     )
-    change, new_moment, new_square = slot_steps(
-        owned, left_basis, right_basis, moment, square, scales
-    )
-    back = lax.all_to_all(change, "wide", split_axis=0, concat_axis=0, tiled=True)
-    back = back.reshape(wide_count * capacity, SLAB, rows)
-    steps = jnp.take(back, owner_ids, axis=0, mode="clip").reshape(units * SLAB, rows)
+    return jnp.concatenate([places, untouched]).astype(jnp.int32), scales
+
+
+def unit_rows(blocks):
+    joined = jnp.concatenate([block.T for block in blocks], axis=0).astype(bf16)
+    return joined.reshape(-1, SLAB, joined.shape[1])
+
+
+def unit_columns(units, blocks):
+    joined = units.reshape(-1, units.shape[2])
     pieces, begin = ([], 0)
     for block in blocks:
-        pieces.append(steps[begin : begin + block.shape[1]].T.astype(f32))
+        pieces.append(joined[begin : begin + block.shape[1]].T.astype(f32))
         begin += block.shape[1]
-    return pieces, new_moment, new_square
+    return pieces
+
+
+def trade_joined(parts, count):
+    steps = [part.shape[0] // count for part in parts]
+    widths = [part.shape[2] for part in parts]
+    room = max(steps)
+    joined = jnp.concatenate(
+        [
+            jnp.pad(
+                part.reshape(count, own, SLAB, width), ((0, 0), (0, room - own), (0, 0), (0, 0))
+            )
+            for part, own, width in zip(parts, steps, widths)
+        ],
+        axis=3,
+    )
+    traded = lax.all_to_all(joined, "wide", split_axis=0, concat_axis=0, tiled=True)
+    pieces, begin = ([], 0)
+    for own, width in zip(steps, widths):
+        pieces.append(traded[:, :own, :, begin : begin + width])
+        begin += width
+    return pieces
 
 
 def body(
@@ -342,9 +727,7 @@
         return dealt.reshape(row_count, -1)
 
     token_in = to_working(x_in)
-    token_grad = to_working(grad_out)
     residual = token_in.astype(f32)
-    grad_top = token_grad.astype(f32)
     seq_lengths = lengths[0]
     seq_ends = jnp.cumsum(seq_lengths)
     row_ids = jnp.arange(row_count, dtype=jnp.int32)
@@ -368,9 +751,7 @@
     full_gate = lax.all_gather(w_gate, "wide", axis=0, tiled=True)
     full_up = lax.all_gather(w_up, "wide", axis=0, tiled=True)
     full_down = lax.all_gather(w_down, "wide", axis=0, tiled=True)
-    gains_all = lax.all_gather(
-        jnp.concatenate([norm_gains[0], norm_gains[1], q_gain, kv_gain]), "narrow"
-    )
+    gains_all = gather_small(jnp.concatenate([norm_gains[0], norm_gains[1], q_gain, kv_gain]))
     first_gain = gains_all[:, :local_width].reshape(1, -1)
     second_gain = gains_all[:, local_width : 2 * local_width].reshape(1, -1)
     q_width = q_gain.shape[0]
@@ -391,6 +772,7 @@
     key_rot = latents[:, q_width + kv_width :]
     narrow_count = lax.axis_size("narrow")
     latents_all = gather_features(latents[:, : q_width + kv_width].astype(bf16))
+    latents_all, grad_out = tie(latents_all, grad_out)
     latents_all = latents_all.reshape(row_count, narrow_count, q_width + kv_width)
     q_latent_all = latents_all[:, :, :q_width].reshape(row_count, QR).astype(f32)
     kv_latent_all = latents_all[:, :, q_width:].reshape(row_count, KVR).astype(f32)
@@ -431,10 +813,16 @@
 
     scores = all_scores()
     row_max = jnp.max(scores, axis=-1, keepdims=True)
+    grad_all, row_max = gather_features(grad_out, row_max)
+    token_grad_all = to_working(grad_all)
+    grad_top = lax.dynamic_slice_in_dim(
+        token_grad_all, narrow_index * local_width, local_width, 1
+    ).astype(f32)
     exp_scores = jnp.exp(scores - row_max)
     row_total = jnp.sum(exp_scores, axis=-1, keepdims=True)
     prob_rows = (exp_scores / row_total).astype(bf16)
     heads_out = jnp.einsum("hqk,khd->qhd", prob_rows, values, preferred_element_type=f32)
+    mlp_grad = (residual_scale * live_rows * token_grad_all.astype(f32)).astype(bf16)
     heads_out = heads_out.astype(bf16).reshape(row_count, heads_here * VH)
     log_totals = row_max + jnp.log(row_total)
     attn_out = reduce_features(against_rows(heads_out, full_o).astype(bf16))
@@ -447,26 +835,37 @@
     sigmoid_gate = jax.nn.sigmoid(gate_act)
     silu_gate = gate_act * sigmoid_gate
     active = (silu_gate * upward).astype(bf16)
-    mlp_out = reduce_features(against_rows(active, full_down).astype(bf16))
-    layer_out = middle + residual_scale * live_rows * mlp_out
-
-    mlp_grad = gather_features((residual_scale * live_rows * grad_top).astype(bf16))
+    mlp_part = against_rows(active, full_down).astype(bf16)
+    mlp_passed, mlp_inner, mlp_near = reduce_start(mlp_part)
+    down_products = chunk_products(mlp_grad, active)
     active_grad = product(mlp_grad, full_down)
     gate_grad = (
         active_grad * upward * (sigmoid_gate + silu_gate * (1.0 - sigmoid_gate))
     ).astype(bf16)
     up_grad = (active_grad * silu_gate).astype(bf16)
+    gate_grad, up_grad, down_products = tie(gate_grad, up_grad, down_products)
+    down_sum = Scatter(down_products)
     normed_two_part = (
         against_rows(gate_grad, full_gate) + against_rows(up_grad, full_up)
     ).astype(bf16)
-    second_dot = row_totals(
-        jnp.sum(gate_grad.astype(f32) * gate_act + up_grad.astype(f32) * upward, axis=1)
-    )[:, None]
-    normed_two_grad = reduce_features(normed_two_part)
-    block_down = scatter_rows(relative_chunks(mlp_grad), active)
-    chunks_two = relative_chunks(normed_two)
-    block_gate = scatter_rows(chunks_two, gate_grad)
-    block_up = scatter_rows(chunks_two, up_grad)
+    second_dot = jnp.sum(gate_grad.astype(f32) * gate_act + up_grad.astype(f32) * upward, axis=1)
+    passed, inner, near = reduce_start(normed_two_part)
+    gate_products = chunk_products(normed_two, gate_grad)
+    passed, gate_products, up_grad = tie(passed, gate_products, up_grad)
+    gate_sum = Scatter(gate_products)
+    relayed = reduce_relay(normed_two_part, passed)
+    relayed, up_grad = tie(relayed, up_grad)
+    second = along_line(relayed, pairs_second)
+    up_sum = Scatter(chunk_products(normed_two, up_grad))
+    second_dot, up_sum.parts = tie(second_dot, up_sum.parts)
+    second_dot = row_parts(second_dot)
+    second, down_sending, gate_sending, up_sum.parts = tie(
+        second, down_sum.outgoing(), gate_sum.outgoing(), up_sum.parts
+    )
+    second_dot = sum(second_dot)[:, None]
+    down_sum.send(down_sending)
+    gate_sum.send(gate_sending)
+    normed_two_grad = reduce_end(normed_two_part, (inner, near, second))
     post_gain_grad = jnp.sum(normed_two_grad * middle * inv_second, axis=0)
     middle_grad = (
         grad_top
@@ -474,7 +873,18 @@
         - middle * inv_second**2 * second_dot / D
     )
     attn_grad = gather_features((residual_scale * live_rows * middle_grad).astype(bf16))
-    block_o = scatter_rows(relative_chunks(attn_grad), heads_out)
+    up_sum.step()
+    attn_grad, down_sending, gate_sending = tie(
+        attn_grad, down_sum.outgoing(), gate_sum.outgoing()
+    )
+    down_sum.send(down_sending)
+    gate_sum.send(gate_sending)
+    o_products = chunk_products(attn_grad, heads_out)
+    attn_grad, o_products, up_sending = tie(attn_grad, o_products, up_sum.outgoing())
+    up_sum.send(up_sending)
+    mlp_passed, attn_grad = tie(mlp_passed, attn_grad)
+    mlp_second = along_line(reduce_relay(mlp_part, mlp_passed), pairs_second)
+    o_sum = Scatter(o_products)
     heads_grad = product(attn_grad, full_o).astype(bf16).reshape(row_count, heads_here, VH)
 
     prob_rows = jnp.exp(all_scores() - log_totals)
@@ -483,6 +893,8 @@
     )
     prob_grad = jnp.einsum("qhd,khd->hqk", heads_grad, values, preferred_element_type=f32)
     delta_rows = jnp.sum(prob_rows * prob_grad, axis=-1, keepdims=True)
+    delta_rows, o_sending = tie(delta_rows, o_sum.outgoing())
+    o_sum.send(o_sending)
     score_grad = (prob_rows * (prob_grad - delta_rows)).astype(bf16)
     query_grad = score_scale * jnp.einsum(
         "hqk,khd->qhd", score_grad, key_heads, preferred_element_type=f32
@@ -490,6 +902,14 @@
     key_grad = score_scale * jnp.einsum(
         "hqk,qhd->khd", score_grad, queries, preferred_element_type=f32
     )
+    mlp_arrived = (mlp_inner, mlp_near, mlp_second)
+    query_grad, o_sending = tie(query_grad, o_sum.outgoing())
+    o_sum.send(o_sending)
+    query_grad, key_grad, value_grad, mlp_arrived = tie(
+        query_grad, key_grad, value_grad, mlp_arrived
+    )
+    mlp_out = reduce_end(mlp_part, mlp_arrived)
+    layer_out = middle + residual_scale * live_rows * mlp_out
     q_pre_grad = jnp.concatenate(
         [query_grad[..., :NOPE], rotate(query_grad[..., NOPE:], cos_heads, sin_heads, -1.0)],
         axis=-1,
@@ -498,12 +918,9 @@
     kv_pre_grad = jnp.concatenate([key_grad[..., :NOPE], value_grad], axis=-1)
     kv_pre_grad = kv_pre_grad.reshape(row_count, -1).astype(bf16)
     rot_partial = rotate(jnp.sum(key_grad[..., NOPE:], axis=1), cosine_table, sine_table, -1.0)
-    rot_grad = row_totals(rot_partial).astype(bf16)
     q_dot = jnp.sum(q_pre_grad.astype(f32) * q_pre, axis=1)
     kv_dot = jnp.sum(kv_pre_grad.astype(f32) * kv_pre, axis=1)
-    dots = row_totals(jnp.stack([q_dot, kv_dot]))
-    q_dot = dots[0][:, None]
-    kv_dot = dots[1][:, None]
+    dots = row_parts(jnp.concatenate([jnp.stack([q_dot, kv_dot]), rot_partial.T], axis=0))
     q_part = against_rows(q_pre_grad, full_qb).astype(bf16)
     kv_part = against_rows(kv_pre_grad, full_kvb).astype(bf16)
     both_part = jnp.concatenate(
@@ -513,11 +930,60 @@
         ],
         axis=-1,
     ).reshape(row_count, -1)
-    both_grad = reduce_features(both_part)
+    passed, inner, near = reduce_start(both_part)
+    extra = kv_pre_grad.shape[1] - q_pre_grad.shape[1]
+    tcount = step_count[0].astype(f32)
+    wide_rate = D ** (-0.5)
+    block_down = down_sum.finish(w_down.shape[1])
+    block_gate = gate_sum.finish(w_gate.shape[1])
+    block_up = up_sum.finish(w_up.shape[1])
+    block_o = o_sum.finish(w_o.shape[1])
+    passed, q_pre_late, kv_pre_late, block_down, block_gate, block_up = tie(
+        passed, q_pre_grad, kv_pre_grad, block_down, block_gate, block_up
+    )
+    main_blocks = [block_o, block_gate, block_up, block_down]
+    late_blocks_widths = [q_width, kv_width]
+    late_units = sum(late_blocks_widths) // SLAB
+    main_rates = unit_rates(
+        [block.shape[1] for block in main_blocks], [1.0, wide_rate, wide_rate, 0.125]
+    )
+    late_rates = unit_rates(late_blocks_widths, [wide_rate, wide_rate])
+    late_owners, main_owners = owner_a[0, :late_units], owner_a[0, late_units:]
+    capacity_a = mom_a.shape[0]
+    main_send, main_back = routes(main_owners, capacity_a, capacity_a, wide_count)
+    main_scales = slot_scales(main_owners, main_rates, capacity_a, wide_index, tcount)
+    first_slots = (capacity_a + 1) // 2
+    groups = [slice(0, first_slots), slice(first_slots, capacity_a)]
+    main_sent = pack_units(
+        main_send, main_blocks, wide_count, [group.stop - group.start for group in groups]
+    )
+    second = along_line(reduce_relay(both_part, passed), pairs_second)
+    head_columns = w_kvb.shape[1]
+    chips = wide_count // 2
+    head_products = [
+        jnp.concatenate(
+            [
+                jnp.pad(first, ((0, 0), (0, extra))).reshape(chips, -1, head_columns),
+                last.reshape(chips, -1, head_columns),
+            ],
+            axis=1,
+        ).reshape(-1, head_columns)
+        for first, last in zip(
+            chunk_products(q_normed, q_pre_late), chunk_products(kv_normed, kv_pre_late)
+        )
+    ]
+    second, dots, main_sent, head_products = tie(second, dots, main_sent, head_products)
+    main_owned = [
+        lax.all_to_all(part, "wide", split_axis=0, concat_axis=0, tiled=True)
+        for part in main_sent
+    ]
+    dots = sum(dots).T
+    q_dot, kv_dot = dots[:, :1], dots[:, 1:2]
+    rot_grad = dots[:, 2:].astype(bf16)
+    heads_sum = Scatter(head_products)
+    both_grad = reduce_end(both_part, (inner, near, second))
     q_normed_grad = both_grad[:, :q_width]
     kv_normed_grad = both_grad[:, q_width:]
-    block_qb = scatter_rows(relative_chunks(q_normed), q_pre_grad)
-    block_kvb = scatter_rows(relative_chunks(kv_normed), kv_pre_grad)
     q_gain_grad = jnp.sum(q_normed_grad * q_latent * inv_q, axis=0)
     kv_gain_grad = jnp.sum(kv_normed_grad * kv_latent * inv_kv, axis=0)
     q_latent_grad = (
@@ -533,16 +999,29 @@
         + share * jnp.sum(rot_grad.astype(f32) * key_rot, axis=1)
     )[:, None]
     latent_grad = jnp.concatenate([q_latent_grad, kv_latent_grad, rot_grad], axis=1)
-    block_latent = scatter_rows(relative_chunks(normed), latent_grad)
-    block_qa = block_latent[:, :q_width]
-    block_kv = block_latent[:, q_width : q_width + kv_width]
-    block_kr = block_latent[:, q_width + kv_width :]
     full_kr = full_latent[:, q_width + kv_width :]
     own_kr = lax.dynamic_slice_in_dim(full_kr, narrow_index * local_width, local_width, 0)
     normed_part = against_rows(
         latent_grad[:, : q_width + kv_width], full_latent[:, : q_width + kv_width]
     ).astype(bf16)
-    normed_grad = reduce_features(normed_part) + against_rows(rot_grad, own_kr)
+    normed_passed, normed_inner, normed_near = reduce_start(normed_part)
+    latent_sum = Scatter(chunk_products(normed, latent_grad))
+    head_sending = heads_sum.outgoing()
+    latent_sum.parts, head_sending = tie(latent_sum.parts, head_sending)
+    heads_sum.send(head_sending)
+    normed_passed, latent_sending = tie(normed_passed, latent_sum.outgoing())
+    latent_sum.send(latent_sending)
+    normed_second = along_line(reduce_relay(normed_part, normed_passed), pairs_second)
+    head_sending, latent_sending = heads_sum.outgoing(), latent_sum.outgoing()
+    normed_second, head_sending, latent_sending = tie(
+        normed_second, head_sending, latent_sending
+    )
+    heads_sum.send(head_sending)
+    latent_sum.send(latent_sending)
+    normed_second, first_owned = tie(normed_second, main_owned[0])
+    normed_grad = reduce_end(normed_part, (normed_inner, normed_near, normed_second)) + (
+        against_rows(rot_grad, own_kr)
+    )
     in_gain_grad = jnp.sum(normed_grad * residual * inv_first, axis=0)
     input_grad = (
         middle_grad
@@ -550,39 +1029,89 @@
         - residual * inv_first**2 * first_dot / D
     )
 
-    def to_input(features):
-        returned = lax.all_to_all(
-            features.astype(bf16).reshape(wide_count, piece_rows, -1), "wide", split_axis=0,
-            concat_axis=0, tiled=True,
-        )
-        return jnp.take(returned, deal_row, axis=0, mode="clip").astype(f32).reshape(row_count, -1)
-
-    final_out = to_input(layer_out)
-    final_grad = to_input(input_grad)
-    gain_grads = lax.psum(
-        jnp.concatenate([in_gain_grad, post_gain_grad, q_gain_grad, kv_gain_grad]), "wide"
+    gain_grads = wide_totals(
+        jnp.concatenate([in_gain_grad, post_gain_grad, q_gain_grad, kv_gain_grad])
     )
     gains_total = gain_grads[: 2 * local_width].reshape(2, local_width)
     qgain_total = gain_grads[2 * local_width : 2 * local_width + q_width]
     kvgain_total = gain_grads[2 * local_width + q_width :]
-    tcount = step_count[0].astype(f32)
-    wide_rate = D ** (-0.5)
-    class_a = [block_qa, block_kv, block_o, block_gate, block_up, block_down]
-    widths_a = [block.shape[1] for block in class_a]
-    rates_a = unit_rates(widths_a, [wide_rate, wide_rate, 1.0, wide_rate, wide_rate, 0.125])
-    rates_b = unit_rates([block_qb.shape[1]], [QR ** (-0.5)])
-    rates_c = unit_rates([block_kvb.shape[1]], [KVR ** (-0.5)])
-    updates_a, new_mom_a, new_sq_a = owner_step(
-        class_a, owner_a[0], basis_la, basis_ra, mom_a, sq_a, rates_a, wide_index, tcount
-    )
-    updates_b, new_mom_b, new_sq_b = owner_step(
-        [block_qb], owner_b[0], basis_lb, basis_rb, mom_b, sq_b, rates_b, wide_index, tcount
-    )
-    updates_c, new_mom_c, new_sq_c = owner_step(
-        [block_kvb], owner_c[0], basis_lc, basis_rc, mom_c, sq_c, rates_c, wide_index, tcount
-    )
-    update_qb = updates_b[0]
-    update_kvb = updates_c[0]
+    change_one, mid_mom_a, mid_sq_a = slot_group(
+        main_scales, first_owned, basis_la, basis_ra, mom_a, sq_a, groups[0], None
+    )
+    last_owned, input_grad = tie(main_owned[1], input_grad)
+    change_one, latent_sum.parts, heads_sum.parts = tie(
+        change_one, latent_sum.parts, heads_sum.parts
+    )
+    back_one = lax.all_to_all(change_one, "wide", split_axis=0, concat_axis=0, tiled=True)
+    block_heads = heads_sum.finish(w_kvb.shape[1]).reshape(2, -1, w_kvb.shape[1])
+    half_qb = w_qb.shape[0] // 2
+    block_qb = block_heads[:, :half_qb, : w_qb.shape[1]].reshape(w_qb.shape)
+    block_kvb = block_heads[:, half_qb:].reshape(w_kvb.shape)
+    block_latent = latent_sum.finish(latent_grad.shape[1])
+    block_qa = block_latent[:, :q_width]
+    block_kv = block_latent[:, q_width : q_width + kv_width]
+    block_kr = block_latent[:, q_width + kv_width :]
+    late_blocks = [block_qa, block_kv]
+    change_two, mid_mom_a, mid_sq_a = slot_group(
+        main_scales, last_owned, basis_la, basis_ra, mom_a, sq_a, groups[1],
+        (mid_mom_a, mid_sq_a),
+    )
+    back_two = lax.all_to_all(change_two, "wide", split_axis=0, concat_axis=0, tiled=True)
+    late_capacity = min(late_units, capacity_a)
+    late_send, late_back = routes(late_owners, capacity_a, late_capacity, wide_count)
+    late_slots, late_scales = late_places(
+        late_owners, late_rates, capacity_a, late_capacity, wide_index, tcount
+    )
+    owners_b, owners_c = owner_b[0], owner_c[0]
+    capacity_b, capacity_c = mom_b.shape[0], mom_c.shape[0]
+    b_send, b_back = routes(owners_b, capacity_b, capacity_b, wide_count)
+    c_send, c_back = routes(owners_c, capacity_c, capacity_c, wide_count)
+    sent_parts = [
+        jnp.take(unit_rows(blocks), send, axis=0, mode="clip")
+        for blocks, send in (
+            (late_blocks, late_send),
+            ([block_qb], b_send),
+            ([block_kvb], c_send),
+        )
+    ]
+    late_owned, owned_b, owned_c = trade_joined(sent_parts, wide_count)
+    late_owned, back_one = tie(late_owned, back_one)
+
+    def to_input(*features):
+        joined = jnp.stack([value.astype(bf16) for value in features], axis=0)
+        joined = joined.reshape(len(features), wide_count, piece_rows, -1).transpose(1, 0, 2, 3)
+        returned = lax.all_to_all(joined, "wide", split_axis=0, concat_axis=0, tiled=True)
+        placed = jnp.take(returned, deal_row, axis=0, mode="clip").astype(f32)
+        return [placed[:, at].reshape(row_count, -1) for at in range(len(features))]
+
+    final_out, final_grad = to_input(layer_out, input_grad)
+    late_change, new_mom_a, new_sq_a = late_steps(
+        late_slots, late_scales, late_owned, basis_la, basis_ra, mid_mom_a, mid_sq_a
+    )
+    change_b, new_mom_b, new_sq_b = all_slots(
+        slot_scales(owners_b, unit_rates([block_qb.shape[1]], [QR ** (-0.5)]), capacity_b,
+                    wide_index, tcount),
+        owned_b, basis_lb, basis_rb, mom_b, sq_b,
+    )
+    change_c, new_mom_c, new_sq_c = all_slots(
+        slot_scales(owners_c, unit_rates([block_kvb.shape[1]], [KVR ** (-0.5)]), capacity_c,
+                    wide_index, tcount),
+        owned_c, basis_lc, basis_rc, mom_c, sq_c,
+    )
+    returned = trade_joined(
+        [change.reshape((-1,) + change.shape[2:]) for change in (late_change, change_b, change_c)],
+        wide_count,
+    )
+    late_result, result_b, result_c = [
+        jnp.take(part.reshape((-1,) + part.shape[2:]), back, axis=0, mode="clip")
+        for part, back in zip(returned, (late_back, b_back, c_back))
+    ]
+    new_o, new_gate, new_up, new_down = unpack_units(
+        main_back, back_one, back_two, [w_o, w_gate, w_up, w_down]
+    )
+    update_qa, update_kv = unit_columns(late_result, late_blocks)
+    update_qb = unit_columns(result_b, [block_qb])[0]
+    update_kvb = unit_columns(result_c, [block_kvb])[0]
     update_kr, new_kr_mom, new_kr_sq = plain_adam(block_kr, kr_mom, kr_sq, wide_rate, tcount)
     update_gains, new_gain_mom, new_gain_sq = plain_adam(
         gains_total, gain_mom, gain_sq, gain_rate, tcount
@@ -604,14 +1133,14 @@
         block_gate,
         block_up,
         block_down,
-        w_qa.astype(f32) + updates_a[0],
-        w_kv.astype(f32) + updates_a[1],
+        w_qa.astype(f32) + update_qa,
+        w_kv.astype(f32) + update_kv,
         w_qb.astype(f32) + update_qb,
         w_kvb.astype(f32) + update_kvb,
-        w_o.astype(f32) + updates_a[2],
-        w_gate.astype(f32) + updates_a[3],
-        w_up.astype(f32) + updates_a[4],
-        w_down.astype(f32) + updates_a[5],
+        new_o,
+        new_gate,
+        new_up,
+        new_down,
         block_kr,
         w_kr.astype(f32) + update_kr,
         new_kr_mom,

time: 1360 us -> 1050 us (0.77)
  waiting for transfers between devices: 556 us -> 318 us
  Pallas kernels: 52.3 us -> 155 us
  local copies, waits for them, and re-layouts: 232 us -> 131 us
  blocking collectives: 79.8 us -> 30.7 us
  matrix products: 143 us -> 105 us
  starting transfers between devices: 158 us -> 179 us
    ppermute x42 -> x12, waiting for transfers between devices: 382 us -> 0.03 us  [shifted(): lax.ppermute(value, 'narrow', [(i, (i + step) % count) for i in range(cou...]
    ppermute x0 -> x40, waiting for transfers between devices: none -> 196 us  [along_line(): return lax.ppermute(value, 'narrow', pairs)]
    pallas_call x3 -> x30, Pallas kernels: 52.3 us -> 155 us  [the longest x5 59.5 us: slot_call(): pl.pallas_call(kernel, grid_spec=pltpu.PrefetchScalarGridSpec(num_scalar_...]
    ppermute x0 -> x40, starting transfers between devices: none -> 83.6 us  [along_line(): return lax.ppermute(value, 'narrow', pairs)]
    psum x1 -> x0, blocking collectives: 69.3 us -> none  [body(): lax.psum(jnp.concatenate([in_gain_grad, post_gain_grad, q_gain_grad, kv_g...]
    ppermute x16 -> x0, local copies, waits for them, and re-layouts: 41.8 us -> none  [the longest x4 22.2 us: flipped(): return lax.ppermute(value, 'wide', [(i, i ^ bit) for i in range(count)])]
    dot_general x21 -> x11, matrix products: 87 us -> 45.9 us  [product(): return jnp.dot(left_side, right_side, preferred_element_type=jnp.float32)]
    ppermute x35 -> x39, waiting for transfers between devices: 96.9 us -> 64.1 us  [flipped(): return lax.ppermute(value, 'wide', [(i, i ^ bit) for i in range(count)])]
  transfers between devices with their start and end apart: 93 -> 105, of which waited for: 48 -> 34; matrix products, arithmetic and copies ran while one was open for 29% -> 26% of each run, Pallas kernels for 4% -> 14%
where the time goes in v2:
time: 1050 us; the launch traced here: 1030 us
  waiting for transfers between devices  318 us (30%)
  starting transfers between devices  179 us (17%)
  Pallas kernels  155 us (15%)
  local copies, waits for them, and re-layouts  131 us (12%)
  matrix products  105 us (10%)
  other arithmetic  95.2 us (9%)
  blocking collectives  30.7 us (3%)
  between operations  19.5 us (2%)
    ppermute x40, waiting for transfers between devices, along_line(): return lax.ppermute(value, 'narrow', pairs)  196 us
    ppermute x40, starting transfers between devices, along_line(): return lax.ppermute(value, 'narrow', pairs)  83.6 us
    ppermute x39, waiting for transfers between devices, flipped(): return lax.ppermute(value, 'wide', [(i, i ^ bit) for i in range(count)])  64.1 us
    pallas_call x5, Pallas kernels, slot_call(): pl.pallas_call(kernel, grid_spec=pltpu.PrefetchScalarGridSpec(num_scalar_...  59.5 us
    unnamed x476, local copies, waits for them, and re-layouts  50.3 us
    dot_general x11, matrix products, product(): return jnp.dot(left_side, right_side, preferred_element_type=jnp.float32)  45.9 us
    dot_general x8, matrix products, against_rows(): lax.dot_general(left_side, right_side, (((1,), (1,)), ((), ())), preferre...  37.5 us
    pallas_call x18, Pallas kernels, add_rows(): pl.pallas_call(functools.partial(add_kernel, [len(parts) for parts in gro...  37.2 us
  transfers between devices with their start and end apart: 105, of which 34 were waited for; matrix products, arithmetic and copies ran while one was open for 26% of the time, Pallas kernels for 14%

profile of v2, /device:TPU:11, one launch (start us, length us, event | category | flops | bytes accessed | tf_op | source)
XLA Modules:
  0.0 1033.6 jit_solution(833361946832196018)
XLA Ops:
  15.1 4.6 all-to-all-start
  24.7 6.8 all-to-all-done
  37.2 25.0 %collective-permute-done.1 = bf16[512,640]{1,0:T(8,128)(2,1)S(1)} collective-permute-done((bf16[512,640]{1,0:T(8,128)(2,1)S(1)}, bf16[512,640]{1,0:T(8,128)(2,1)S(1)}, u32[]{:S(2)}, u32[]{:S(2)}) %collective-permute-start.1) | collective-permute-done | bytes 655392 | tf_op jit(solution)/shard_map/ppermute | solution.py:90
  66.5 9.8 collective-permute-done.2
  78.6 4.2 copy.340
  82.9 3.9 reshape.797
  90.1 6.3 collective-permute-start.8
  100.5 6.5 collective-permute-done.8
  112.7 6.8 collective-permute-start.22
  127.7 6.8 collective-permute-done.21
  150.0 10.4 %collective-permute-done.11 = bf16[512,640]{1,0:T(8,128)(2,1)} collective-permute-done((bf16[512,640]{1,0:T(8,128)(2,1)}, bf16[512,640]{1,0:T(8,128)(2,1)}, u32[]{:S(2)}, u32[]{:S(2)}) %collective-permute-start.11) | collective-permute-done | bytes 655392 | tf_op jit(solution)/shard_map/ppermute | solution.py:90
  160.3 5.0 collective-permute-start.23
  169.6 4.4 convolution_convert_fusion.1
  184.8 5.4 all-to-all-start.1
  196.6 11.9 %collective-permute-done.13 = bf16[512,640]{1,0:T(8,128)(2,1)S(1)} collective-permute-done((bf16[512,640]{1,0:T(8,128)(2,1)}, bf16[512,640]{1,0:T(8,128)(2,1)S(1)}, u32[]{:S(2)}, u32[]{:S(2)}) %collective-permute-start.13) | collective-permute-done | bytes 655392 | tf_op jit(solution)/shard_map/ppermute | solution.py:90
  208.5 26.0 %collective-permute-done.15 = bf16[512,640]{1,0:T(8,128)(2,1)S(1)} collective-permute-done((bf16[512,640]{1,0:T(8,128)(2,1)S(1)}, bf16[512,640]{1,0:T(8,128)(2,1)S(1)}, u32[]{:S(2)}, u32[]{:S(2)}) %collective-permute-start.15) | collective-permute-done | bytes 655392 | tf_op jit(solution)/shard_map/ppermute | solution.py:90
  244.4 23.8 %collective-permute-done.17 = bf16[512,640]{1,0:T(8,128)(2,1)} collective-permute-done((bf16[512,640]{1,0:T(8,128)(2,1)}, bf16[512,640]{1,0:T(8,128)(2,1)}, u32[]{:S(2)}, u32[]{:S(2)}) %collective-permute-start.17) | collective-permute-done | bytes 655392 | tf_op jit(solution)/shard_map/ppermute | solution.py:90
  268.2 6.1 collective-permute-start.19
  291.4 10.1 fusion.110
  301.5 9.2 fusion.109
  310.7 11.8 %multiply_convert_fusion.2 = (bf16[512,1600]{1,0:T(8,128)(2,1)S(1)}, bf16[512,1600]{1,0:T(8,128)(2,1)S(1)}, bf16[512,1600]{1,0:T(8,128)(2,1)S(1)}) fusion(f32[512,1600]{1,0:T(8,128)} %fusion.109, f32[512,1600]{1,0:T(8,128)} %fusion.110, bf16[512,2560]{1,0:T(8,128)(2,1)} %multiply_convert_fusion.1.left_ref, bf16[2560,1600]{1,0:T(8,128)(2,1)} %all-gather.15.cloned.1.call-done), kind=kOutput, calls=%fused_computation.43 | convolution fusion | flops 4205772800 | bytes 22282240 | tf_op jit(solution)/shard_map/dot_general | solution.py:32
  322.5 9.7 shard_map.813
  336.1 10.1 fusion.111
  346.2 9.6 add_convert_fusion
  359.4 9.1 shard_map.814
  371.2 5.5 collective-permute-done.26
  378.4 9.1 shard_map.817
  391.5 14.5 %collective-permute-done.27 = bf16[512,640]{1,0:T(8,128)(2,1)} collective-permute-done((bf16[512,640]{1,0:T(8,128)(2,1)}, bf16[512,640]{1,0:T(8,128)(2,1)}, u32[]{:S(2)}, u32[]{:S(2)}) %collective-permute-start.27) | collective-permute-done | bytes 655392 | tf_op jit(solution)/shard_map/ppermute | solution.py:90
  414.9 4.3 add_reduce_fusion
  435.3 4.2 constant_dynamic-update-slice_fusion.2
  454.6 15.0 %collective-permute-done.38 = bf16[512,640]{1,0:T(8,128)(2,1)} collective-permute-done((bf16[512,640]{1,0:T(8,128)(2,1)}, bf16[512,640]{1,0:T(8,128)(2,1)}, u32[]{:S(2)}, u32[]{:S(2)}) %collective-permute-start.38) | collective-permute-done | bytes 655392 | tf_op jit(solution)/shard_map/ppermute | solution.py:90
  476.4 4.5 collective-permute-start.40
  480.9 8.8 convolution_convert_fusion.2
  504.7 12.3 %collective-permute-done.46.refs_5_.refs_6_ = bf16[320,1664]{1,0:T(8,128)(2,1)S(1)} collective-permute-done((bf16[320,1664]{1,0:T(8,128)(2,1)}, bf16[320,1664]{1,0:T(8,128)(2,1)S(1)}, u32[]{:S(2)}, u32[]{:S(2)}) %collective-permute-start.46) | collective-permute-done | bytes 1064992 | tf_op jit(solution)/shard_map/ppermute | solution.py:86
  522.6 5.2 shard_map.820
  530.6 4.8 convolution_convert_fusion.8
  539.7 10.7 %multiply_reduce_fusion = (f32[10,512]{1,0:T(8,128)S(1)}, f32[10,512,512]{1,2,0:T(8,128)}) fusion(f32[10,512,512]{1,2,0:T(8,128)} %copy-done.71, f32[10,512]{1,0:T(8,128)S(1)} %fusion.60, bf16[512,10,64]{0,2,1:T(8,128)(2,1)} %bitcast.296, bf16[512,10,128]{0,2,1:T(8,128)(2,1)} %bitcast.301), kind=kOutput, calls=%fused_computation.14 | convolution fusion | flops 343403520 | bytes 22323200 | tf_op jit(solution)/shard_map/qhd,khd->hqk/dot_general | solution.py:894
  557.4 4.0 shard_map.825.refs_3_
  561.4 4.8 collective-permute-done.58.refs_7_
  577.6 4.2 collective-permute-start.53
  586.5 8.6 multiply_convert_fusion
  600.0 10.8 %collective-permute-done.53 = bf16[512,640]{1,0:T(8,128)(2,1)S(1)} collective-permute-done((bf16[512,640]{1,0:T(8,128)(2,1)}, bf16[512,640]{1,0:T(8,128)(2,1)S(1)}, u32[]{:S(2)}, u32[]{:S(2)}) %collective-permute-start.53) | collective-permute-done | bytes 655392 | tf_op jit(solution)/shard_map/ppermute | solution.py:90
  656.7 10.3 %shard_map.829 = (bf16[8,9,64,320]{3,2,1,0:T(8,128)(2,1)}, bf16[8,8,64,320]{3,2,1,0:T(8,128)(2,1)}) custom-call(s32[136]{0:T(256)} %broadcast_minimum_fusion.send_ref, f32[320,640]{1,0:T(8,128)} %shard_map.828.refs_0_, f32[320,1600]{1,0:T(8,128)} %shard_map.826.refs_1_, f32[320,1600]{1,0:T(8,128)} %shard_map.827.refs_2_, f32[320,1600]{1,0:T(8,128)} %shard_map.825.refs_3_), custom_call_target="tpu_custom_call" | custom-call | tf_op jit(solution)/shard_map/pallas_call | solution.py:374
  670.1 6.7 all-to-all-start.3
  682.6 5.4 collective-permute-done.68
  694.7 22.8 %all-to-all-done.3.gradient_ref = bf16[8,9,64,320]{3,2,1,0:T(8,128)(2,1)} async-done(((bf16[8,9,64,320]{3,2,1,0:T(8,128)(2,1)}), bf16[8,9,64,320]{3,2,1,0:T(8,128)(2,1)}, u32[]{:S(2)}, u32[]{:S(2)}) %all-to-all-start.3) | async-done | bytes 2949152 | tf_op jit(solution)/shard_map/all_to_all | solution.py:977
  717.5 6.0 all-to-all-start.2
  724.6 4.0 shard_map.830
  747.8 16.0 %collective-permute-done.79.refs_2_ = bf16[320,384]{1,0:T(8,128)(2,1)S(1)} collective-permute-done((bf16[320,384]{1,0:T(8,128)(2,1)S(1)}, bf16[320,384]{1,0:T(8,128)(2,1)S(1)}, u32[]{:S(2)}, u32[]{:S(2)}) %collective-permute-start.79) | collective-permute-done | bytes 245792 | tf_op jit(solution)/shard_map/ppermute | solution.py:86
  775.0 10.7 %collective-permute-done.76 = bf16[512,640]{1,0:T(8,128)(2,1)S(1)} collective-permute-done((bf16[512,640]{1,0:T(8,128)(2,1)S(1)}, bf16[512,640]{1,0:T(8,128)(2,1)S(1)}, u32[]{:S(2)}, u32[]{:S(2)}) %collective-permute-start.76) | collective-permute-done | bytes 655392 | tf_op jit(solution)/shard_map/ppermute | solution.py:90
  793.1 8.8 all-to-all-start.4
  802.0 23.2 %shard_map.835 = (bf16[8,9,64,320]{3,2,1,0:T(8,128)(2,1)S(1)}, f32[17,64,2560]{2,1,0:T(8,128)}, f32[17,64,2560]{2,1,0:T(8,128)}) custom-call(s32[18]{0:T(128)S(1)} %copy-done.64, f32[20]{0:T(128)S(1)} %pad_maximum_fusion.14.scale_ref, bf16[8,9,64,320]{3,2,1,0:T(8,128)(2,1)} %all-to-all-done.3.gradient_ref, f32[17,2560,128]{2,1,0:T(8,128)} %left_ref.5, ...), custom_call_target="tpu_custom_call" | custom-call | tf_op jit(solution)/shard_map/pallas_call | solution.py:521
  837.9 30.7 %all_to_all.45 = bf16[8,4,64,448]{3,2,1,0:T(8,128)(2,1)} all-to-all(bf16[8,4,64,448]{3,2,1,0:T(8,128)(2,1)S(1)} %fusion.17), channel_id=1, replica_groups=mesh['wide'=8,'narrow'=4] {'wide'}, dimensions={0} | all-to-all | bytes 3670016 | tf_op jit(solution)/shard_map/all_to_all | solution.py:660
  868.7 6.2 all-to-all-start.6
  875.1 21.6 %shard_map.838 = (bf16[8,8,64,320]{3,2,1,0:T(8,128)(2,1)S(1)}, f32[17,64,2560]{2,1,0:T(8,128)}, f32[17,64,2560]{2,1,0:T(8,128)}) custom-call(s32[16]{0:T(128)S(1)} %concatenate.135.refs_0_, f32[18]{0:T(128)S(1)} %pad_maximum_fusion.15.refs_1_, bf16[8,8,64,320]{3,2,1,0:T(8,128)(2,1)} %all-to-all-done.2.refs_2_, ...), custom_call_target="tpu_custom_call", output_to_operand_aliasing={{1}: (7, {}), {2}: (8, {})} | custom-call | tf_op jit(solution)/shard_map/pallas_call | solution.py:521
  898.3 17.1 %all-to-all-done.6.first_ref = bf16[8,9,64,320]{3,2,1,0:T(8,128)(2,1)} async-done(((bf16[8,9,64,320]{3,2,1,0:T(8,128)(2,1)}), bf16[8,9,64,320]{3,2,1,0:T(8,128)(2,1)}, u32[]{:S(2)}, u32[]{:S(2)}) %all-to-all-start.6) | async-done | bytes 2949152 | tf_op jit(solution)/shard_map/all_to_all | solution.py:1045
  915.6 6.4 all-to-all-start.8
  929.6 5.1 shard_map.841
  937.0 5.3 shard_map.840
  942.5 4.3 shard_map.839
  948.8 9.5 all-to-all-done.8.last_ref
  958.3 5.1 all-to-all-start.7
  967.4 20.1 %collective-permute-done.89 = f32[1536]{0:T(1024)S(1)} collective-permute-done((f32[1536]{0:T(1024)S(1)}, f32[1536]{0:T(1024)S(1)}, u32[]{:S(2)}, u32[]{:S(2)}) %collective-permute-start.89) | collective-permute-done | bytes 6176 | tf_op jit(solution)/shard_map/ppermute | solution.py:86
  1004.5 10.3 %shard_map.842 = (f32[320,640]{1,0:T(8,128)}, f32[320,1600]{1,0:T(8,128)}, f32[320,1600]{1,0:T(8,128)}, f32[320,1600]{1,0:T(8,128)}) custom-call(s32[85]{0:T(128)} %copy-done.196, bf16[8,9,64,320]{3,2,1,0:T(8,128)(2,1)} %all-to-all-done.6.first_ref, bf16[8,8,64,320]{3,2,1,0:T(8,128)(2,1)} %all-to-all-done.8.last_ref, bf16[320,640]{1,0:T(8,128)(2,1)} %refs_0_.1, ...), custom_call_target="tpu_custom_call" | custom-call | tf_op jit(solution)/shard_map/pallas_call | solution.py:419
  (946 shorter events, 384.2 us)
Async XLA Ops:
  7.2 71.4 %all-gather.19.cloned.1.call-start = ((), (), s32[]{:S(2)}) async-start(), calls=%async_computation.14 | async-start | bytes 1990656 | tf_op jit(solution)/shard_map/all_gather | solution.py:746
  9.0 126.4 %all-gather.17.cloned.1.call-start = ((), (), s32[]{:S(2)}) async-start(), calls=%async_computation.13 | async-start | bytes 2949120 | tf_op jit(solution)/shard_map/all_gather | solution.py:747
  10.8 158.8 %all-gather.9.cloned.1.call-start = ((), (), s32[]{:S(2)}) async-start(), calls=%async_computation.9 | async-start | bytes 3686400 | tf_op jit(solution)/shard_map/all_gather | solution.py:750
  11.6 279.8 %all-gather.13.cloned.1.call-start = ((), (), s32[]{:S(2)}) async-start(), calls=%async_computation.11 | async-start | bytes 9584640 | tf_op jit(solution)/shard_map/all_gather | solution.py:752
  12.2 289.3 %all-gather.11.cloned.1.call-start = ((), (), s32[]{:S(2)}) async-start(), calls=%async_computation.10 | async-start | bytes 9584640 | tf_op jit(solution)/shard_map/all_gather | solution.py:751
  19.6 291.0 %all-gather.15.cloned.1.call-start = ((), (), s32[]{:S(2)}) async-start(), calls=%async_computation.12 | async-start | bytes 9584640 | tf_op jit(solution)/shard_map/all_gather | solution.py:753
  19.8 45.4 %collective-permute-start.6 = (f32[1536]{0:T(1024)S(1)}, f32[1536]{0:T(1024)S(1)}, u32[]{:S(2)}, u32[]{:S(2)}) collective-permute-start(f32[1536]{0:T(1024)S(1)} %concatenate.108), channel_id=1, source_target_pairs={{0,3},{1,0},{2,1},{3,2},{4,7},{5,4},{6,5},{7,6},{8,11},{9,8},{10,9... | collective-permute-start | bytes 18440 | tf_op jit(solution)/shard_map/ppermute | solution.py:81
  20.0 45.1 %collective-permute-start.5 = (f32[1536]{0:T(1024)S(1)}, f32[1536]{0:T(1024)S(1)}, u32[]{:S(2)}, u32[]{:S(2)}) collective-permute-start(f32[1536]{0:T(1024)S(1)} %concatenate.108), channel_id=1, source_target_pairs={{0,2},{1,3},{2,0},{3,1},{4,6},{5,7},{6,4},{7,5},{8,10},{9,11},{10,... | collective-permute-start | bytes 18440 | tf_op jit(solution)/shard_map/ppermute | solution.py:81
  31.5 30.6 %collective-permute-start.1 = (bf16[512,640]{1,0:T(8,128)(2,1)S(1)}, bf16[512,640]{1,0:T(8,128)(2,1)S(1)}, u32[]{:S(2)}, u32[]{:S(2)}) collective-permute-start(bf16[512,640]{1,0:T(8,128)(2,1)S(1)} %bitcast.287), channel_id=1, source_target_pairs={{0,2},{2,0},{1,3},{3,1},{4,6},{6,4},{5,7},{7,5},{8,10},{10,8},{9,1... | collective-permute-start | bytes 1966088 | tf_op jit(solution)/shard_map/ppermute | solution.py:90
  34.7 31.5 %collective-permute-start = (bf16[512,640]{1,0:T(8,128)(2,1)S(1)}, bf16[512,640]{1,0:T(8,128)(2,1)S(1)}, u32[]{:S(2)}, u32[]{:S(2)}) collective-permute-start(bf16[512,640]{1,0:T(8,128)(2,1)S(1)} %bitcast.288), channel_id=1, source_target_pairs={{0,1},{1,0},{2,3},{3,2},{4,5},{5,4},{6,7},{7,6},{8,9},{9,8},{10,11... | collective-permute-start | bytes 1966088 | tf_op jit(solution)/shard_map/ppermute | solution.py:90
  35.0 41.2 %collective-permute-start.2 = (bf16[512,640]{1,0:T(8,128)(2,1)S(1)}, bf16[512,640]{1,0:T(8,128)(2,1)S(1)}, u32[]{:S(2)}, u32[]{:S(2)}) collective-permute-start(bf16[512,640]{1,0:T(8,128)(2,1)S(1)} %bitcast.289), channel_id=1, source_target_pairs={{1,2},{2,1},{5,6},{6,5},{9,10},{10,9},{13,14},{14,13},{17,18},{18,... | collective-permute-start | bytes 1966088 | tf_op jit(solution)/shard_map/ppermute | solution.py:90
  112.7 66.0 %collective-permute-start.22 = (bf16[512,640]{1,0:T(8,128)(2,1)}, bf16[512,640]{1,0:T(8,128)(2,1)}, u32[]{:S(2)}, u32[]{:S(2)}) collective-permute-start(bf16[512,640]{1,0:T(8,128)(2,1)} %param.55), channel_id=1, source_target_pairs={{1,2},{2,1},{5,6},{6,5},{9,10},{10,9},{13,14},{14,13},{17,18},{18,... | collective-permute-start | bytes 1966088 | tf_op jit(solution)/shard_map/ppermute | solution.py:90
  119.7 40.7 %collective-permute-start.11 = (bf16[512,640]{1,0:T(8,128)(2,1)}, bf16[512,640]{1,0:T(8,128)(2,1)}, u32[]{:S(2)}, u32[]{:S(2)}) collective-permute-start(bf16[512,640]{1,0:T(8,128)(2,1)} %param.55), channel_id=1, source_target_pairs={{0,2},{2,0},{1,3},{3,1},{4,6},{6,4},{5,7},{7,5},{8,10},{10,8},{9,1... | collective-permute-start | bytes 1966088 | tf_op jit(solution)/shard_map/ppermute | solution.py:90
  184.8 89.5 %all-to-all-start.1 = ((bf16[8,64,2560]{2,1,0:T(8,128)(2,1)}), bf16[8,64,2560]{2,1,0:T(8,128)(2,1)}, u32[]{:S(2)}, u32[]{:S(2)}) async-start(bf16[8,64,2560]{2,1,0:T(8,128)(2,1)} %gather_fusion.1), calls=%async_computation.1 | async-start | bytes 5242880 | tf_op jit(solution)/shard_map/all_to_all | solution.py:726
  195.3 39.2 %collective-permute-start.15 = (bf16[512,640]{1,0:T(8,128)(2,1)S(1)}, bf16[512,640]{1,0:T(8,128)(2,1)S(1)}, u32[]{:S(2)}, u32[]{:S(2)}) collective-permute-start(bf16[512,640]{1,0:T(8,128)(2,1)S(1)} %add_convert_fusion.5), channel_id=1, source_target_pairs={{0,2},{2,0},{1,3},{3,1},{4,6},{6,4},{5,7},{7,5},{8,10},{10,8},{9,1... | collective-permute-start | bytes 1966088 | tf_op jit(solution)/shard_map/ppermute | solution.py:90
  237.7 30.6 %collective-permute-start.17 = (bf16[512,640]{1,0:T(8,128)(2,1)}, bf16[512,640]{1,0:T(8,128)(2,1)}, u32[]{:S(2)}, u32[]{:S(2)}) collective-permute-start(bf16[512,640]{1,0:T(8,128)(2,1)} %get-tuple-element.680), channel_id=1, source_target_pairs={{0,2},{2,0},{1,3},{3,1},{4,6},{6,4},{5,7},{7,5},{8,10},{10,8},{9,1... | collective-permute-start | bytes 1966088 | tf_op jit(solution)/shard_map/ppermute | solution.py:90
  242.2 35.9 %collective-permute-start.16 = (bf16[512,640]{1,0:T(8,128)(2,1)}, bf16[512,640]{1,0:T(8,128)(2,1)}, u32[]{:S(2)}, u32[]{:S(2)}) collective-permute-start(bf16[512,640]{1,0:T(8,128)(2,1)} %get-tuple-element.680), channel_id=1, source_target_pairs={{0,1},{1,0},{2,3},{3,2},{4,5},{5,4},{6,7},{7,6},{8,9},{9,8},{10,11... | collective-permute-start | bytes 1966088 | tf_op jit(solution)/shard_map/ppermute | solution.py:90
  242.2 42.2 %collective-permute-start.18 = (bf16[512,640]{1,0:T(8,128)(2,1)}, bf16[512,640]{1,0:T(8,128)(2,1)S(1)}, u32[]{:S(2)}, u32[]{:S(2)}) collective-permute-start(bf16[512,640]{1,0:T(8,128)(2,1)} %get-tuple-element.680), channel_id=1, source_target_pairs={{1,2},{2,1},{5,6},{6,5},{9,10},{10,9},{13,14},{14,13},{17,18},{18,... | collective-permute-start | bytes 1966088 | tf_op jit(solution)/shard_map/ppermute | solution.py:90
  334.7 72.4 %collective-permute-start.28 = (bf16[640,1664]{1,0:T(8,128)(2,1)}, bf16[640,1664]{1,0:T(8,128)(2,1)}, u32[]{:S(2)}, u32[]{:S(2)}) collective-permute-start(bf16[640,1664]{1,0:T(8,128)(2,1)} %get-tuple-element.235), channel_id=1, source_target_pairs={{0,4},{4,0},{8,12},{12,8},{16,20},{20,16},{24,28},{28,24},{1,5},{5... | collective-permute-start | bytes 6389768 | tf_op jit(solution)/shard_map/ppermute | solution.py:86
  377.8 28.2 %collective-permute-start.27 = (bf16[512,640]{1,0:T(8,128)(2,1)}, bf16[512,640]{1,0:T(8,128)(2,1)}, u32[]{:S(2)}, u32[]{:S(2)}) collective-permute-start(bf16[512,640]{1,0:T(8,128)(2,1)} %add_convert_fusion.4), channel_id=1, source_target_pairs={{0,2},{2,0},{1,3},{3,1},{4,6},{6,4},{5,7},{7,5},{8,10},{10,8},{9,1... | collective-permute-start | bytes 1966088 | tf_op jit(solution)/shard_map/ppermute | solution.py:90
  391.0 28.3 %collective-permute-start.29 = (bf16[640,1664]{1,0:T(8,128)(2,1)}, bf16[640,1664]{1,0:T(8,128)(2,1)}, u32[]{:S(2)}, u32[]{:S(2)}) collective-permute-start(bf16[640,1664]{1,0:T(8,128)(2,1)} %get-tuple-element.237), channel_id=1, source_target_pairs={{0,4},{4,0},{8,12},{12,8},{16,20},{20,16},{24,28},{28,24},{1,5},{5... | collective-permute-start | bytes 6389768 | tf_op jit(solution)/shard_map/ppermute | solution.py:86
  410.9 22.7 %collective-permute-start.24 = (bf16[512,640]{1,0:T(8,128)(2,1)}, bf16[512,640]{1,0:T(8,128)(2,1)}, u32[]{:S(2)}, u32[]{:S(2)}) collective-permute-start(bf16[512,640]{1,0:T(8,128)(2,1)} %get-tuple-element.691), channel_id=1, source_target_pairs={{1,2},{2,1},{5,6},{6,5},{9,10},{10,9},{13,14},{14,13},{17,18},{18,... | collective-permute-start | bytes 1966088 | tf_op jit(solution)/shard_map/ppermute | solution.py:90
  429.9 40.6 %collective-permute-start.41 = (bf16[320,1664]{1,0:T(8,128)(2,1)}, bf16[320,1664]{1,0:T(8,128)(2,1)}, u32[]{:S(2)}, u32[]{:S(2)}) collective-permute-start(bf16[320,1664]{1,0:T(8,128)(2,1)} %get-tuple-element.257), channel_id=1, source_target_pairs={{0,8},{4,12},{8,0},{12,4},{16,24},{20,28},{24,16},{28,20},{1,9},{5... | collective-permute-start | bytes 3194888 | tf_op jit(solution)/shard_map/ppermute | solution.py:86
  431.6 39.9 %collective-permute-start.42 = (bf16[320,1664]{1,0:T(8,128)(2,1)}, bf16[320,1664]{1,0:T(8,128)(2,1)}, u32[]{:S(2)}, u32[]{:S(2)}) collective-permute-start(bf16[320,1664]{1,0:T(8,128)(2,1)} %get-tuple-element.258), channel_id=1, source_target_pairs={{0,16},{4,20},{8,24},{12,28},{16,0},{20,4},{24,8},{28,12},{1,17},{... | collective-permute-start | bytes 3194888 | tf_op jit(solution)/shard_map/ppermute | solution.py:86
  432.5 43.9 %collective-permute-start.43 = (bf16[320,1664]{1,0:T(8,128)(2,1)}, bf16[320,1664]{1,0:T(8,128)(2,1)S(1)}, u32[]{:S(2)}, u32[]{:S(2)}) collective-permute-start(bf16[320,1664]{1,0:T(8,128)(2,1)} %get-tuple-element.261), channel_id=1, source_target_pairs={{0,8},{4,12},{8,0},{12,4},{16,24},{20,28},{24,16},{28,20},{1,9},{5... | collective-permute-start | bytes 3194888 | tf_op jit(solution)/shard_map/ppermute | solution.py:86
  439.5 30.1 %collective-permute-start.38 = (bf16[512,640]{1,0:T(8,128)(2,1)}, bf16[512,640]{1,0:T(8,128)(2,1)}, u32[]{:S(2)}, u32[]{:S(2)}) collective-permute-start(bf16[512,640]{1,0:T(8,128)(2,1)} %get-tuple-element.677), channel_id=1, source_target_pairs={{0,2},{2,0},{1,3},{3,1},{4,6},{6,4},{5,7},{7,5},{8,10},{10,8},{9,1... | collective-permute-start | bytes 1966088 | tf_op jit(solution)/shard_map/ppermute | solution.py:90
  441.3 28.4 %collective-permute-start.37 = (bf16[512,640]{1,0:T(8,128)(2,1)}, bf16[512,640]{1,0:T(8,128)(2,1)}, u32[]{:S(2)}, u32[]{:S(2)}) collective-permute-start(bf16[512,640]{1,0:T(8,128)(2,1)} %get-tuple-element.677), channel_id=1, source_target_pairs={{0,1},{1,0},{2,3},{3,2},{4,5},{5,4},{6,7},{7,6},{8,9},{9,8},{10,11... | collective-permute-start | bytes 1966088 | tf_op jit(solution)/shard_map/ppermute | solution.py:90
  469.6 24.6 %collective-permute-start.44 = (bf16[320,1664]{1,0:T(8,128)(2,1)S(1)}, bf16[320,1664]{1,0:T(8,128)(2,1)S(1)}, u32[]{:S(2)}, u32[]{:S(2)}) collective-permute-start(bf16[320,1664]{1,0:T(8,128)(2,1)S(1)} %copy-done.67), channel_id=1, source_target_pairs={{0,16},{4,20},{8,24},{12,28},{16,0},{20,4},{24,8},{28,12},{1,17},{... | collective-permute-start | bytes 3194888 | tf_op jit(solution)/shard_map/ppermute | solution.py:86
  469.7 35.1 %collective-permute-start.45 = (bf16[320,1664]{1,0:T(8,128)(2,1)}, bf16[320,1664]{1,0:T(8,128)(2,1)S(1)}, u32[]{:S(2)}, u32[]{:S(2)}) collective-permute-start(bf16[320,1664]{1,0:T(8,128)(2,1)} %get-tuple-element.274), channel_id=1, source_target_pairs={{0,8},{4,12},{8,0},{12,4},{16,24},{20,28},{24,16},{28,20},{1,9},{5... | collective-permute-start | bytes 3194888 | tf_op jit(solution)/shard_map/ppermute | solution.py:86
  470.5 46.5 %collective-permute-start.46 = (bf16[320,1664]{1,0:T(8,128)(2,1)}, bf16[320,1664]{1,0:T(8,128)(2,1)S(1)}, u32[]{:S(2)}, u32[]{:S(2)}) collective-permute-start(bf16[320,1664]{1,0:T(8,128)(2,1)} %get-tuple-element.275), channel_id=1, source_target_pairs={{0,16},{4,20},{8,24},{12,28},{16,0},{20,4},{24,8},{28,12},{1,17},{... | collective-permute-start | bytes 3194888 | tf_op jit(solution)/shard_map/ppermute | solution.py:86
  471.5 48.2 %collective-permute-start.39 = (bf16[512,640]{1,0:T(8,128)(2,1)}, bf16[512,640]{1,0:T(8,128)(2,1)S(1)}, u32[]{:S(2)}, u32[]{:S(2)}) collective-permute-start(bf16[512,640]{1,0:T(8,128)(2,1)} %get-tuple-element.677), channel_id=1, source_target_pairs={{1,2},{2,1},{5,6},{6,5},{9,10},{10,9},{13,14},{14,13},{17,18},{18,... | collective-permute-start | bytes 1966088 | tf_op jit(solution)/shard_map/ppermute | solution.py:90
  476.4 43.3 %collective-permute-start.40 = (bf16[512,640]{1,0:T(8,128)(2,1)}, bf16[512,640]{1,0:T(8,128)(2,1)}, u32[]{:S(2)}, u32[]{:S(2)}) collective-permute-start(bf16[512,640]{1,0:T(8,128)(2,1)} %collective-permute-done.38), channel_id=1, source_target_pairs={{1,0},{2,3},{5,4},{6,7},{9,8},{10,11},{13,12},{14,15},{17,16},{18,... | collective-permute-start | bytes 1966088 | tf_op jit(solution)/shard_map/ppermute | solution.py:90
  494.2 36.4 %collective-permute-start.20 = (bf16[512,640]{1,0:T(8,128)(2,1)S(1)}, bf16[512,640]{1,0:T(8,128)(2,1)}, u32[]{:S(2)}, u32[]{:S(2)}) collective-permute-start(bf16[512,640]{1,0:T(8,128)(2,1)S(1)} %get-tuple-element.689), channel_id=1, source_target_pairs={{0,1},{3,2},{4,5},{7,6},{8,9},{11,10},{12,13},{15,14},{16,17},{19,... | collective-permute-start | bytes 1966088 | tf_op jit(solution)/shard_map/ppermute | solution.py:90
  520.7 32.0 %collective-permute-start.55 = (bf16[160,1664]{1,0:T(8,128)(2,1)}, bf16[160,1664]{1,0:T(8,128)(2,1)}, u32[]{:S(2)}, u32[]{:S(2)}) collective-permute-start(bf16[160,1664]{1,0:T(8,128)(2,1)} %get-tuple-element.299), channel_id=1, source_target_pairs={{0,16},{4,20},{8,24},{12,28},{16,0},{20,4},{24,8},{28,12},{1,17},{... | collective-permute-start | bytes 1597448 | tf_op jit(solution)/shard_map/ppermute | solution.py:86
  520.8 33.0 %collective-permute-start.56 = (bf16[160,1664]{1,0:T(8,128)(2,1)}, bf16[160,1664]{1,0:T(8,128)(2,1)}, u32[]{:S(2)}, u32[]{:S(2)}) collective-permute-start(bf16[160,1664]{1,0:T(8,128)(2,1)} %get-tuple-element.300), channel_id=1, source_target_pairs={{0,8},{4,12},{8,0},{12,4},{16,24},{20,28},{24,16},{28,20},{1,9},{5... | collective-permute-start | bytes 1597448 | tf_op jit(solution)/shard_map/ppermute | solution.py:86
  521.6 32.3 %collective-permute-start.57 = (bf16[160,1664]{1,0:T(8,128)(2,1)}, bf16[160,1664]{1,0:T(8,128)(2,1)S(1)}, u32[]{:S(2)}, u32[]{:S(2)}) collective-permute-start(bf16[160,1664]{1,0:T(8,128)(2,1)} %get-tuple-element.301), channel_id=1, source_target_pairs={{0,16},{4,20},{8,24},{12,28},{16,0},{20,4},{24,8},{28,12},{1,17},{... | collective-permute-start | bytes 1597448 | tf_op jit(solution)/shard_map/ppermute | solution.py:86
  537.5 47.4 %collective-permute-start.47 = (bf16[640,640]{1,0:T(8,128)(2,1)}, bf16[640,640]{1,0:T(8,128)(2,1)S(1)}, u32[]{:S(2)}, u32[]{:S(2)}) collective-permute-start(bf16[640,640]{1,0:T(8,128)(2,1)} %copy-done.69), channel_id=1, source_target_pairs={{0,4},{4,0},{8,12},{12,8},{16,20},{20,16},{24,28},{28,24},{1,5},{5... | collective-permute-start | bytes 2457608 | tf_op jit(solution)/shard_map/ppermute | solution.py:86
  539.7 45.3 %collective-permute-start.48 = (bf16[640,640]{1,0:T(8,128)(2,1)}, bf16[640,640]{1,0:T(8,128)(2,1)S(1)}, u32[]{:S(2)}, u32[]{:S(2)}) collective-permute-start(bf16[640,640]{1,0:T(8,128)(2,1)} %copy-done.68), channel_id=1, source_target_pairs={{0,4},{4,0},{8,12},{12,8},{16,20},{20,16},{24,28},{28,24},{1,5},{5... | collective-permute-start | bytes 2457608 | tf_op jit(solution)/shard_map/ppermute | solution.py:86
  553.9 23.6 %collective-permute-start.60 = (bf16[160,1664]{1,0:T(8,128)(2,1)}, bf16[160,1664]{1,0:T(8,128)(2,1)S(1)}, u32[]{:S(2)}, u32[]{:S(2)}) collective-permute-start(bf16[160,1664]{1,0:T(8,128)(2,1)} %get-tuple-element.304), channel_id=1, source_target_pairs={{0,8},{4,12},{8,0},{12,4},{16,24},{20,28},{24,16},{28,20},{1,9},{5... | collective-permute-start | bytes 1597448 | tf_op jit(solution)/shard_map/ppermute | solution.py:86
  566.1 33.9 %collective-permute-start.51 = (bf16[512,640]{1,0:T(8,128)(2,1)}, bf16[512,640]{1,0:T(8,128)(2,1)S(1)}, u32[]{:S(2)}, u32[]{:S(2)}) collective-permute-start(bf16[512,640]{1,0:T(8,128)(2,1)} %copy-done.135), channel_id=1, source_target_pairs={{1,2},{2,1},{5,6},{6,5},{9,10},{10,9},{13,14},{14,13},{17,18},{18,... | collective-permute-start | bytes 1966088 | tf_op jit(solution)/shard_map/ppermute | solution.py:90
  572.8 27.2 %collective-permute-start.52 = (bf16[512,640]{1,0:T(8,128)(2,1)}, bf16[512,640]{1,0:T(8,128)(2,1)S(1)}, u32[]{:S(2)}, u32[]{:S(2)}) collective-permute-start(bf16[512,640]{1,0:T(8,128)(2,1)} %get-tuple-element.688), channel_id=1, source_target_pairs={{0,1},{1,0},{2,3},{3,2},{4,5},{5,4},{6,7},{7,6},{8,9},{9,8},{10,11... | collective-permute-start | bytes 1966088 | tf_op jit(solution)/shard_map/ppermute | solution.py:90
  577.6 33.3 %collective-permute-start.53 = (bf16[512,640]{1,0:T(8,128)(2,1)}, bf16[512,640]{1,0:T(8,128)(2,1)S(1)}, u32[]{:S(2)}, u32[]{:S(2)}) collective-permute-start(bf16[512,640]{1,0:T(8,128)(2,1)} %add_convert_fusion.3), channel_id=1, source_target_pairs={{0,2},{2,0},{1,3},{3,1},{4,6},{6,4},{5,7},{7,5},{8,10},{10,8},{9,1... | collective-permute-start | bytes 1966088 | tf_op jit(solution)/shard_map/ppermute | solution.py:90
  617.1 23.8 %collective-permute-start.66 = (bf16[160,640]{1,0:T(8,128)(2,1)}, bf16[160,640]{1,0:T(8,128)(2,1)}, u32[]{:S(2)}, u32[]{:S(2)}) collective-permute-start(bf16[160,640]{1,0:T(8,128)(2,1)} %get-tuple-element.307), channel_id=1, source_target_pairs={{0,8},{4,12},{8,0},{12,4},{16,24},{20,28},{24,16},{28,20},{1,9},{5... | collective-permute-start | bytes 614408 | tf_op jit(solution)/shard_map/ppermute | solution.py:86
  633.0 34.1 %collective-permute-start.64 = (f32[34,512]{0,1:T(8,128)}, f32[34,512]{0,1:T(8,128)}, u32[]{:S(2)}, u32[]{:S(2)}) collective-permute-start(f32[34,512]{0,1:T(8,128)} %copy.359), channel_id=1, source_target_pairs={{0,3},{1,0},{2,1},{3,2},{4,7},{5,4},{6,5},{7,6},{8,11},{9,8},{10,9... | collective-permute-start | bytes 208904 | tf_op jit(solution)/shard_map/ppermute | solution.py:81
  635.9 31.1 %collective-permute-start.63 = (f32[34,512]{0,1:T(8,128)}, f32[34,512]{0,1:T(8,128)}, u32[]{:S(2)}, u32[]{:S(2)}) collective-permute-start(f32[34,512]{0,1:T(8,128)} %copy.359), channel_id=1, source_target_pairs={{0,2},{1,3},{2,0},{3,1},{4,6},{5,7},{6,4},{7,5},{8,10},{9,11},{10,... | collective-permute-start | bytes 208904 | tf_op jit(solution)/shard_map/ppermute | solution.py:81
  638.5 28.6 %collective-permute-start.62 = (f32[34,512]{0,1:T(8,128)}, f32[34,512]{0,1:T(8,128)}, u32[]{:S(2)}, u32[]{:S(2)}) collective-permute-start(f32[34,512]{0,1:T(8,128)} %copy.359), channel_id=1, source_target_pairs={{0,1},{1,2},{2,3},{3,0},{4,5},{5,6},{6,7},{7,4},{8,9},{9,10},{10,1... | collective-permute-start | bytes 208904 | tf_op jit(solution)/shard_map/ppermute | solution.py:81
  670.1 47.3 %all-to-all-start.3 = ((bf16[8,9,64,320]{3,2,1,0:T(8,128)(2,1)}), bf16[8,9,64,320]{3,2,1,0:T(8,128)(2,1)}, u32[]{:S(2)}, u32[]{:S(2)}) async-start(bf16[8,9,64,320]{3,2,1,0:T(8,128)(2,1)} %get-tuple-element.347), calls=%async_computation.3 | async-start | bytes 7077888 | tf_op jit(solution)/shard_map/all_to_all | solution.py:977
  680.6 51.1 %collective-permute-start.74 = (bf16[256,1280]{1,0:T(8,128)(2,1)}, bf16[256,1280]{1,0:T(8,128)(2,1)}, u32[]{:S(2)}, u32[]{:S(2)}) collective-permute-start(bf16[256,1280]{1,0:T(8,128)(2,1)} %bitcast.339), channel_id=1, source_target_pairs={{0,4},{4,0},{8,12},{12,8},{16,20},{20,16},{24,28},{28,24},{1,5},{5... | collective-permute-start | bytes 1966088 | tf_op jit(solution)/shard_map/ppermute | solution.py:86
  681.0 50.7 %collective-permute-start.75 = (bf16[256,1280]{1,0:T(8,128)(2,1)}, bf16[256,1280]{1,0:T(8,128)(2,1)}, u32[]{:S(2)}, u32[]{:S(2)}) collective-permute-start(bf16[256,1280]{1,0:T(8,128)(2,1)} %bitcast.338), channel_id=1, source_target_pairs={{0,4},{4,0},{8,12},{12,8},{16,20},{20,16},{24,28},{28,24},{1,5},{5... | collective-permute-start | bytes 1966088 | tf_op jit(solution)/shard_map/ppermute | solution.py:86
  693.2 46.9 %collective-permute-start.71 = (bf16[512,640]{1,0:T(8,128)(2,1)}, bf16[512,640]{1,0:T(8,128)(2,1)}, u32[]{:S(2)}, u32[]{:S(2)}) collective-permute-start(bf16[512,640]{1,0:T(8,128)(2,1)} %get-tuple-element.687), channel_id=1, source_target_pairs={{0,1},{3,2},{4,5},{7,6},{8,9},{11,10},{12,13},{15,14},{16,17},{19,... | collective-permute-start | bytes 1966088 | tf_op jit(solution)/shard_map/ppermute | solution.py:90
  717.5 73.1 %all-to-all-start.2 = ((bf16[8,8,64,320]{3,2,1,0:T(8,128)(2,1)}), bf16[8,8,64,320]{3,2,1,0:T(8,128)(2,1)}, u32[]{:S(2)}, u32[]{:S(2)}) async-start(bf16[8,8,64,320]{3,2,1,0:T(8,128)(2,1)} %get-tuple-element.315), calls=%async_computation.2 | async-start | bytes 6291456 | tf_op jit(solution)/shard_map/all_to_all | solution.py:977
  740.1 23.7 %collective-permute-start.79 = (bf16[320,384]{1,0:T(8,128)(2,1)S(1)}, bf16[320,384]{1,0:T(8,128)(2,1)S(1)}, u32[]{:S(2)}, u32[]{:S(2)}) collective-permute-start(bf16[320,384]{1,0:T(8,128)(2,1)S(1)} %get-tuple-element.342), channel_id=1, source_target_pairs={{0,8},{4,12},{8,0},{12,4},{16,24},{20,28},{24,16},{28,20},{1,9},{5... | collective-permute-start | bytes 737288 | tf_op jit(solution)/shard_map/ppermute | solution.py:86
  740.2 24.8 %collective-permute-start.80 = (bf16[320,384]{1,0:T(8,128)(2,1)S(1)}, bf16[320,384]{1,0:T(8,128)(2,1)S(1)}, u32[]{:S(2)}, u32[]{:S(2)}) collective-permute-start(bf16[320,384]{1,0:T(8,128)(2,1)S(1)} %get-tuple-element.343), channel_id=1, source_target_pairs={{0,16},{4,20},{8,24},{12,28},{16,0},{20,4},{24,8},{28,12},{1,17},{... | collective-permute-start | bytes 737288 | tf_op jit(solution)/shard_map/ppermute | solution.py:86
  742.9 45.7 %collective-permute-start.69 = (bf16[512,640]{1,0:T(8,128)(2,1)}, bf16[512,640]{1,0:T(8,128)(2,1)S(1)}, u32[]{:S(2)}, u32[]{:S(2)}) collective-permute-start(bf16[512,640]{1,0:T(8,128)(2,1)} %get-tuple-element.687), channel_id=1, source_target_pairs={{1,2},{2,1},{5,6},{6,5},{9,10},{10,9},{13,14},{14,13},{17,18},{18,... | collective-permute-start | bytes 1966088 | tf_op jit(solution)/shard_map/ppermute | solution.py:90
  745.0 43.3 %collective-permute-start.70 = (bf16[512,640]{1,0:T(8,128)(2,1)}, bf16[512,640]{1,0:T(8,128)(2,1)S(1)}, u32[]{:S(2)}, u32[]{:S(2)}) collective-permute-start(bf16[512,640]{1,0:T(8,128)(2,1)} %get-tuple-element.686), channel_id=1, source_target_pairs={{0,1},{1,0},{2,3},{3,2},{4,5},{5,4},{6,7},{7,6},{8,9},{9,8},{10,11... | collective-permute-start | bytes 1966088 | tf_op jit(solution)/shard_map/ppermute | solution.py:90
  745.1 40.5 %collective-permute-start.76 = (bf16[512,640]{1,0:T(8,128)(2,1)S(1)}, bf16[512,640]{1,0:T(8,128)(2,1)S(1)}, u32[]{:S(2)}, u32[]{:S(2)}) collective-permute-start(bf16[512,640]{1,0:T(8,128)(2,1)S(1)} %add_convert_fusion.1), channel_id=1, source_target_pairs={{0,2},{2,0},{1,3},{3,1},{4,6},{6,4},{5,7},{7,5},{8,10},{10,8},{9,1... | collective-permute-start | bytes 1966088 | tf_op jit(solution)/shard_map/ppermute | solution.py:90
  785.6 41.3 %collective-permute-start.84 = (bf16[160,384]{1,0:T(8,128)(2,1)}, bf16[160,384]{1,0:T(8,128)(2,1)}, u32[]{:S(2)}, u32[]{:S(2)}) collective-permute-start(bf16[160,384]{1,0:T(8,128)(2,1)} %get-tuple-element.352), channel_id=1, source_target_pairs={{0,16},{4,20},{8,24},{12,28},{16,0},{20,4},{24,8},{28,12},{1,17},{... | collective-permute-start | bytes 368648 | tf_op jit(solution)/shard_map/ppermute | solution.py:86
  786.9 40.1 %collective-permute-start.85 = (bf16[160,384]{1,0:T(8,128)(2,1)}, bf16[160,384]{1,0:T(8,128)(2,1)}, u32[]{:S(2)}, u32[]{:S(2)}) collective-permute-start(bf16[160,384]{1,0:T(8,128)(2,1)} %get-tuple-element.353), channel_id=1, source_target_pairs={{0,8},{4,12},{8,0},{12,4},{16,24},{20,28},{24,16},{28,20},{1,9},{5... | collective-permute-start | bytes 368648 | tf_op jit(solution)/shard_map/ppermute | solution.py:86
  787.1 39.9 %collective-permute-start.86 = (bf16[64,1280]{1,0:T(8,128)(2,1)}, bf16[64,1280]{1,0:T(8,128)(2,1)}, u32[]{:S(2)}, u32[]{:S(2)}) collective-permute-start(bf16[64,1280]{1,0:T(8,128)(2,1)} %get-tuple-element.354), channel_id=1, source_target_pairs={{0,16},{4,20},{8,24},{12,28},{16,0},{20,4},{24,8},{28,12},{1,17},{... | collective-permute-start | bytes 491528 | tf_op jit(solution)/shard_map/ppermute | solution.py:86
  788.3 38.7 %collective-permute-start.87 = (bf16[64,1280]{1,0:T(8,128)(2,1)}, bf16[64,1280]{1,0:T(8,128)(2,1)}, u32[]{:S(2)}, u32[]{:S(2)}) collective-permute-start(bf16[64,1280]{1,0:T(8,128)(2,1)} %get-tuple-element.355), channel_id=1, source_target_pairs={{0,8},{4,12},{8,0},{12,4},{16,24},{20,28},{24,16},{28,20},{1,9},{5... | collective-permute-start | bytes 491528 | tf_op jit(solution)/shard_map/ppermute | solution.py:86
  793.1 44.8 %all-to-all-start.4 = ((bf16[8,2,64,640]{3,2,1,0:T(8,128)(2,1)}), bf16[8,2,64,640]{3,2,1,0:T(8,128)(2,1)}, u32[]{:S(2)}, u32[]{:S(2)}) async-start(bf16[8,2,64,640]{3,2,1,0:T(8,128)(2,1)} %maximum_bitcast_fusion), calls=%async_computation.4 | async-start | bytes 2621440 | tf_op jit(solution)/shard_map/all_to_all | solution.py:1083
  868.7 46.8 %all-to-all-start.6 = ((bf16[8,9,64,320]{3,2,1,0:T(8,128)(2,1)}), bf16[8,9,64,320]{3,2,1,0:T(8,128)(2,1)}, u32[]{:S(2)}, u32[]{:S(2)}) async-start(bf16[8,9,64,320]{3,2,1,0:T(8,128)(2,1)} %copy-done.46), calls=%async_computation.6 | async-start | bytes 7077888 | tf_op jit(solution)/shard_map/all_to_all | solution.py:1045
  915.6 42.8 %all-to-all-start.8 = ((bf16[8,8,64,320]{3,2,1,0:T(8,128)(2,1)}), bf16[8,8,64,320]{3,2,1,0:T(8,128)(2,1)}, u32[]{:S(2)}, u32[]{:S(2)}) async-start(bf16[8,8,64,320]{3,2,1,0:T(8,128)(2,1)} %copy-done.47), calls=%async_computation.8 | async-start | bytes 6291456 | tf_op jit(solution)/shard_map/all_to_all | solution.py:1059
  958.3 56.5 %all-to-all-start.7 = ((bf16[8,4,64,448]{3,2,1,0:T(8,128)(2,1)}), bf16[8,4,64,448]{3,2,1,0:T(8,128)(2,1)S(1)}, u32[]{:S(2)}, u32[]{:S(2)}) async-start(bf16[8,4,64,448]{3,2,1,0:T(8,128)(2,1)} %fusion.19), calls=%async_computation.7 | async-start | bytes 4194304 | tf_op jit(solution)/shard_map/all_to_all | solution.py:660
  (274 other events, 3489.4 us)
Sparse Core Ops, SparseCore 0:
  10.5 34.0 all-gather.18
  47.0 30.0 all-gather.16
  79.1 32.8 all-gather.8
  113.7 54.9 all-gather.12
  170.4 75.5 all-gather.10
  247.7 57.0 all-gather.14

commit v3 on v2

--- a/solution.py
+++ b/solution.py
@@ -345,13 +345,40 @@
     )
 
 
+def weight_kernel(left_ref, right_ref, out_ref):
+    out_ref[...] = inner_rows(left_ref[...], right_ref[...]).astype(bf16)
+
+
+def weight_product(left, right):
+    tokens, width = left.shape
+    columns = right.shape[1]
+    group = width // 4
+    if group % 128:
+        return inner_rows(left, right).astype(bf16)
+    return pl.pallas_call(
+        weight_kernel,
+        grid=(4,),
+        in_specs=[
+            pl.BlockSpec((tokens, group), lambda step: (0, step)),
+            pl.BlockSpec((tokens, columns), lambda step: (0, 0)),
+        ],
+        out_specs=pl.BlockSpec((group, columns), lambda step: (step, 0)),
+        out_shape=jax.ShapeDtypeStruct((width, columns), bf16),
+        compiler_params=pltpu.CompilerParams(vmem_limit_bytes=48 * 1024 * 1024),
+    )(left, right)
+
+
+def scatter_rows(partial):
+    return lax.psum_scatter(partial, "wide", scatter_dimension=0, tiled=True)
+
+
 def pack_kernel(send_ref, *refs):
     count = len(refs) - 3
     blocks, outs, turned = refs[:count], refs[count : count + 2], refs[-1]
     begin = 0
     for block in blocks:
         width = block.shape[1]
-        turned[begin : begin + width, :] = block[...].T.astype(bf16)
+        turned[begin : begin + width, :] = block[...].astype(f32).T.astype(bf16)
         begin += width
     capacity = outs[0].shape[1] + outs[1].shape[1]
     for out, offset in zip(outs, (0, outs[0].shape[1])):
@@ -594,6 +621,111 @@
     return jnp.sum(
         jnp.where(earlier & (device[None, :] == device[:, None]), 1, 0).astype(jnp.int32), axis=1
     )
+
+
+def turned_lanes(value, tables, sign):
+    near = pltpu.roll(value, 112, 1) * tables[1]
+    far = pltpu.roll(value, 16, 1) * tables[2]
+    return value * tables[0] + sign * (near + far)
+
+
+def lane_ids(shape):
+    return lax.broadcasted_iota(jnp.int32, shape, 1)
+
+
+def head_inputs(head, query_ref, key_value_ref, rotary_ref, tables, bias_ref):
+    at = slice(head * 128, (head + 1) * 128)
+    query = turned_lanes(query_ref[:, at], tables, 1.0).astype(bf16)
+    key_value = key_value_ref[:, at].astype(bf16)
+    key = jnp.where(lane_ids(key_value.shape) < NOPE, key_value, rotary_ref[...])
+    scores = against_rows(query, key) * (NOPE + ROPE) ** (-0.5) + bias_ref[...]
+    exp_scores = jnp.exp(scores - jnp.max(scores, axis=1, keepdims=True))
+    probs = exp_scores / jnp.sum(exp_scores, axis=1, keepdims=True)
+    return query, key_value, key, probs
+
+
+def attend_kernel(query_ref, key_value_ref, rotary_ref, table_ref, bias_ref, out_ref):
+    tables = [table_ref[at] for at in range(3)]
+    mixed = []
+    for head in range(2):
+        _, key_value, _, probs = head_inputs(
+            head, query_ref, key_value_ref, rotary_ref, tables, bias_ref
+        )
+        mixed.append(product(probs.astype(bf16), key_value))
+    lower = pltpu.roll(mixed[0], 64, 1)
+    out_ref[...] = jnp.where(lane_ids(lower.shape) < VH, lower, mixed[1]).astype(bf16)
+
+
+def attend_back_kernel(query_ref, key_value_ref, rotary_ref, table_ref, bias_ref, grad_ref,
+                       query_grad_ref, key_value_grad_ref, sums_ref):
+    tables = [table_ref[at] for at in range(3)]
+    scale = (NOPE + ROPE) ** (-0.5)
+
+    @pl.when(pl.program_id(0) == 0)
+    def _():
+        sums_ref[...] = jnp.zeros_like(sums_ref)
+
+    for head in range(2):
+        at = slice(head * 128, (head + 1) * 128)
+        query, key_value, key, probs = head_inputs(
+            head, query_ref, key_value_ref, rotary_ref, tables, bias_ref
+        )
+        grad = grad_ref[...].astype(f32)
+        lanes = lane_ids(grad.shape)
+        if head == 0:
+            grad = pltpu.roll(grad, 64, 1)
+        grad = jnp.where(lanes < NOPE, 0.0, grad).astype(bf16)
+        value_grad = inner_rows(probs.astype(bf16), grad)
+        prob_grad = against_rows(grad, key_value)
+        delta = jnp.sum(probs * prob_grad, axis=1, keepdims=True)
+        score_grad = (probs * (prob_grad - delta)).astype(bf16)
+        query_grad = turned_lanes(scale * product(score_grad, key), tables, -1.0).astype(bf16)
+        key_grad = scale * inner_rows(score_grad, query)
+        key_value_grad = jnp.where(lanes < NOPE, key_grad, value_grad).astype(bf16)
+        query_grad_ref[:, at] = query_grad
+        key_value_grad_ref[:, at] = key_value_grad
+        sums_ref[0] += query_grad.astype(f32) * query_ref[:, at]
+        sums_ref[1] += key_value_grad.astype(f32) * key_value_ref[:, at]
+        sums_ref[2] += key_grad
+
+
+def attend_specs(tokens):
+    pair = pl.BlockSpec((tokens, 256), lambda step: (0, step))
+    single = pl.BlockSpec((tokens, 128), lambda step: (0, step))
+    shared = pl.BlockSpec((tokens, 128), lambda step: (0, 0))
+    tables = pl.BlockSpec((3, tokens, 128), lambda step: (0, 0, 0))
+    bias = pl.BlockSpec((tokens, tokens), lambda step: (0, 0))
+    return pair, single, shared, tables, bias
+
+
+def attend(queries, keys_values, rotary, tables, bias):
+    tokens, width = queries.shape
+    pair, single, shared, table_spec, bias_spec = attend_specs(tokens)
+    return pl.pallas_call(
+        attend_kernel,
+        grid=(width // 256,),
+        in_specs=[pair, pair, shared, table_spec, bias_spec],
+        out_specs=single,
+        out_shape=jax.ShapeDtypeStruct((tokens, width // 2), bf16),
+        compiler_params=pltpu.CompilerParams(vmem_limit_bytes=48 * 1024 * 1024),
+    )(queries, keys_values, rotary, tables, bias)
+
+
+def attend_back(queries, keys_values, rotary, tables, bias, grad):
+    tokens, width = queries.shape
+    pair, single, shared, table_spec, bias_spec = attend_specs(tokens)
+    return pl.pallas_call(
+        attend_back_kernel,
+        grid=(width // 256,),
+        in_specs=[pair, pair, shared, table_spec, bias_spec, single],
+        out_specs=[pair, pair, table_spec],
+        out_shape=[
+            jax.ShapeDtypeStruct((tokens, width), bf16),
+            jax.ShapeDtypeStruct((tokens, width), bf16),
+            jax.ShapeDtypeStruct((3, tokens, 128), f32),
+        ],
+        compiler_params=pltpu.CompilerParams(vmem_limit_bytes=48 * 1024 * 1024),
+    )(queries, keys_values, rotary, tables, bias, grad)
 
 
 def routes(owners, capacity, room, wide_count):
@@ -740,13 +872,14 @@
     sin_heads = sine_table[:, None, :]
 
     latent_own = jnp.concatenate([w_qa, w_kv, w_kr], axis=1)
-    head_rows = jnp.concatenate(
-        [jnp.pad(w_qb, ((0, 0), (0, w_kvb.shape[1] - w_qb.shape[1]))), w_kvb], axis=0
-    )
+    heads_here = w_o.shape[1] // VH
+    padded_qb = jnp.pad(
+        w_qb.reshape(w_qb.shape[0], heads_here, NOPE + ROPE),
+        ((0, 0), (0, 0), (0, 128 - NOPE - ROPE)),
+    ).reshape(w_qb.shape[0], -1)
     full_latent = lax.all_gather(latent_own, "wide", axis=0, tiled=True)
-    full_heads = lax.all_gather(head_rows, "wide", axis=0)
-    full_qb = full_heads[:, : w_qb.shape[0], : w_qb.shape[1]].reshape(-1, w_qb.shape[1])
-    full_kvb = full_heads[:, w_qb.shape[0] :, :].reshape(-1, w_kvb.shape[1])
+    full_qb = lax.all_gather(padded_qb, "wide", axis=0, tiled=True)
+    full_kvb = lax.all_gather(w_kvb, "wide", axis=0, tiled=True)
     full_o = lax.all_gather(w_o, "wide", axis=0, tiled=True)
     full_gate = lax.all_gather(w_gate, "wide", axis=0, tiled=True)
     full_up = lax.all_gather(w_up, "wide", axis=0, tiled=True)
@@ -763,7 +896,7 @@
         wide = features.astype(f32)
         return lax.rsqrt(jnp.sum(wide * wide, axis=1, keepdims=True) / width + norm_eps)
 
-    token_all = gather_features(token_in)
+    token_all, full_latent = gather_features(token_in, full_latent)
     inv_first = inverse_rms(token_all, D)
     normed = (token_all.astype(f32) * inv_first * first_gain).astype(bf16)
     latents = product(normed, full_latent)
@@ -772,7 +905,6 @@
     key_rot = latents[:, q_width + kv_width :]
     narrow_count = lax.axis_size("narrow")
     latents_all = gather_features(latents[:, : q_width + kv_width].astype(bf16))
-    latents_all, grad_out = tie(latents_all, grad_out)
     latents_all = latents_all.reshape(row_count, narrow_count, q_width + kv_width)
     q_latent_all = latents_all[:, :, :q_width].reshape(row_count, QR).astype(f32)
     kv_latent_all = latents_all[:, :, q_width:].reshape(row_count, KVR).astype(f32)
@@ -780,51 +912,36 @@
     inv_kv = inverse_rms(kv_latent_all, KVR)
     q_normed = (q_latent_all * inv_q * q_gain_all).astype(bf16)
     kv_normed = (kv_latent_all * inv_kv * kv_gain_all).astype(bf16)
-    heads_here = w_o.shape[1] // VH
     q_pre = product(q_normed, full_qb)
     kv_pre = product(kv_normed, full_kvb)
-    q_pre_heads = q_pre.reshape(row_count, heads_here, NOPE + ROPE)
-    kv_pre_heads = kv_pre.reshape(row_count, heads_here, NOPE + VH)
-    queries = jnp.concatenate(
+    key_turned = rotate(key_rot, cosine_table, sine_table, 1.0)
+    rotary = jnp.pad(key_turned, ((0, 0), (NOPE, 128 - NOPE - ROPE))).astype(bf16)
+    allowed = (segment[:, None] == segment[None, :]) & (row_ids[None, :] <= row_ids[:, None])
+    bias = jnp.where(allowed, 0.0, masked_value).astype(f32)
+    half_pads = ((NOPE, 128 - NOPE - ROPE // 2), (NOPE + ROPE // 2, 128 - NOPE - ROPE))
+
+    def lane_table(lower, upper):
+        return sum(
+            jnp.pad(part, ((0, 0), pads)) for part, pads in zip((lower, upper), half_pads)
+        )
+
+    empty = jnp.zeros_like(sine_table)
+    tables = jnp.stack(
         [
-            q_pre_heads[..., :NOPE],
-            rotate(q_pre_heads[..., NOPE:], cos_heads, sin_heads, 1.0),
-        ],
-        axis=-1,
-    ).astype(bf16)
-    key_turned = rotate(key_rot, cosine_table, sine_table, 1.0)
-    key_heads = jnp.concatenate(
-        [
-            kv_pre_heads[..., :NOPE],
-            jnp.broadcast_to(key_turned[:, None, :], (row_count, heads_here, ROPE)),
-        ],
-        axis=-1,
-    ).astype(bf16)
-    values = kv_pre_heads[..., NOPE:].astype(bf16)
-    score_scale = (NOPE + ROPE) ** (-0.5)
-    allowed = (segment[:, None] == segment[None, :]) & (row_ids[None, :] <= row_ids[:, None])
-
-    def all_scores():
-        scores = (
-            jnp.einsum("qhd,khd->hqk", queries, key_heads, preferred_element_type=f32)
-            * score_scale
-        )
-        return jnp.where(allowed[None], scores, masked_value)
-
-    scores = all_scores()
-    row_max = jnp.max(scores, axis=-1, keepdims=True)
-    grad_all, row_max = gather_features(grad_out, row_max)
+            lane_table(cosine_table, cosine_table)
+            + jnp.where(jnp.arange(128) < NOPE, 1.0, 0.0)[None, :],
+            lane_table(-sine_table, empty),
+            lane_table(empty, sine_table),
+        ]
+    )
+    latents_all, grad_out = tie(latents_all, grad_out)
+    heads_out = attend(q_pre, kv_pre, rotary, tables, bias)
+    grad_all, heads_out = gather_features(grad_out, heads_out)
     token_grad_all = to_working(grad_all)
     grad_top = lax.dynamic_slice_in_dim(
         token_grad_all, narrow_index * local_width, local_width, 1
     ).astype(f32)
-    exp_scores = jnp.exp(scores - row_max)
-    row_total = jnp.sum(exp_scores, axis=-1, keepdims=True)
-    prob_rows = (exp_scores / row_total).astype(bf16)
-    heads_out = jnp.einsum("hqk,khd->qhd", prob_rows, values, preferred_element_type=f32)
     mlp_grad = (residual_scale * live_rows * token_grad_all.astype(f32)).astype(bf16)
-    heads_out = heads_out.astype(bf16).reshape(row_count, heads_here * VH)
-    log_totals = row_max + jnp.log(row_total)
     attn_out = reduce_features(against_rows(heads_out, full_o).astype(bf16))
     middle = residual + residual_scale * live_rows * attn_out
     middle_all = gather_features(middle.astype(bf16)).astype(f32)
@@ -848,78 +965,59 @@
     normed_two_part = (
         against_rows(gate_grad, full_gate) + against_rows(up_grad, full_up)
     ).astype(bf16)
-    second_dot = jnp.sum(gate_grad.astype(f32) * gate_act + up_grad.astype(f32) * upward, axis=1)
     passed, inner, near = reduce_start(normed_two_part)
     gate_products = chunk_products(normed_two, gate_grad)
-    passed, gate_products, up_grad = tie(passed, gate_products, up_grad)
+    passed, gate_products, up_grad, down_sending = tie(
+        passed, gate_products, up_grad, down_sum.outgoing()
+    )
+    down_sum.send(down_sending)
     gate_sum = Scatter(gate_products)
     relayed = reduce_relay(normed_two_part, passed)
     relayed, up_grad = tie(relayed, up_grad)
     second = along_line(relayed, pairs_second)
     up_sum = Scatter(chunk_products(normed_two, up_grad))
-    second_dot, up_sum.parts = tie(second_dot, up_sum.parts)
-    second_dot = row_parts(second_dot)
-    second, down_sending, gate_sending, up_sum.parts = tie(
-        second, down_sum.outgoing(), gate_sum.outgoing(), up_sum.parts
-    )
-    second_dot = sum(second_dot)[:, None]
-    down_sum.send(down_sending)
-    gate_sum.send(gate_sending)
+    second, up_sum.parts = tie(second, up_sum.parts)
     normed_two_grad = reduce_end(normed_two_part, (inner, near, second))
     post_gain_grad = jnp.sum(normed_two_grad * middle * inv_second, axis=0)
-    middle_grad = (
-        grad_top
-        + inv_second * norm_gains[1] * normed_two_grad
-        - middle * inv_second**2 * second_dot / D
-    )
-    attn_grad = gather_features((residual_scale * live_rows * middle_grad).astype(bf16))
-    up_sum.step()
-    attn_grad, down_sending, gate_sending = tie(
-        attn_grad, down_sum.outgoing(), gate_sum.outgoing()
-    )
-    down_sum.send(down_sending)
-    gate_sum.send(gate_sending)
-    o_products = chunk_products(attn_grad, heads_out)
-    attn_grad, o_products, up_sending = tie(attn_grad, o_products, up_sum.outgoing())
-    up_sum.send(up_sending)
+    direct_grad = grad_top + inv_second * norm_gains[1] * normed_two_grad
+    direct_all, sendings = gather_features(
+        direct_grad.astype(bf16),
+        (gate_sum.outgoing(), up_sum.outgoing(), down_sum.outgoing()),
+    )
+    direct_all = direct_all.astype(f32)
+    top_all = token_grad_all.astype(f32)
+    second_dot = jnp.sum((direct_all - top_all) * middle_all, axis=1, keepdims=True)
+    attn_grad = (
+        residual_scale
+        * live_rows
+        * (direct_all - middle_all * (inv_second**2 * second_dot / D))
+    ).astype(bf16)
+    middle_grad = direct_grad - middle * (inv_second**2 * second_dot / D)
+    for weight_sum, sending in zip((gate_sum, up_sum, down_sum), sendings):
+        weight_sum.send(sending)
+    o_full = weight_product(attn_grad, heads_out)
+    attn_grad, o_full = tie(attn_grad, o_full)
+    block_o = scatter_rows(o_full)
     mlp_passed, attn_grad = tie(mlp_passed, attn_grad)
     mlp_second = along_line(reduce_relay(mlp_part, mlp_passed), pairs_second)
-    o_sum = Scatter(o_products)
-    heads_grad = product(attn_grad, full_o).astype(bf16).reshape(row_count, heads_here, VH)
-
-    prob_rows = jnp.exp(all_scores() - log_totals)
-    value_grad = jnp.einsum(
-        "hqk,qhd->khd", prob_rows.astype(bf16), heads_grad, preferred_element_type=f32
-    )
-    prob_grad = jnp.einsum("qhd,khd->hqk", heads_grad, values, preferred_element_type=f32)
-    delta_rows = jnp.sum(prob_rows * prob_grad, axis=-1, keepdims=True)
-    delta_rows, o_sending = tie(delta_rows, o_sum.outgoing())
-    o_sum.send(o_sending)
-    score_grad = (prob_rows * (prob_grad - delta_rows)).astype(bf16)
-    query_grad = score_scale * jnp.einsum(
-        "hqk,khd->qhd", score_grad, key_heads, preferred_element_type=f32
-    )
-    key_grad = score_scale * jnp.einsum(
-        "hqk,qhd->khd", score_grad, queries, preferred_element_type=f32
+    heads_grad = product(attn_grad, full_o).astype(bf16)
+
+    q_pre_grad, kv_pre_grad, head_sums = attend_back(
+        q_pre, kv_pre, rotary, tables, bias, heads_grad
     )
     mlp_arrived = (mlp_inner, mlp_near, mlp_second)
-    query_grad, o_sending = tie(query_grad, o_sum.outgoing())
-    o_sum.send(o_sending)
-    query_grad, key_grad, value_grad, mlp_arrived = tie(
-        query_grad, key_grad, value_grad, mlp_arrived
-    )
+    head_sums, q_pre_grad, gate_sending, up_sending = tie(
+        head_sums, q_pre_grad, gate_sum.outgoing(), up_sum.outgoing()
+    )
+    gate_sum.send(gate_sending)
+    up_sum.send(up_sending)
     mlp_out = reduce_end(mlp_part, mlp_arrived)
     layer_out = middle + residual_scale * live_rows * mlp_out
-    q_pre_grad = jnp.concatenate(
-        [query_grad[..., :NOPE], rotate(query_grad[..., NOPE:], cos_heads, sin_heads, -1.0)],
-        axis=-1,
-    )
-    q_pre_grad = q_pre_grad.reshape(row_count, -1).astype(bf16)
-    kv_pre_grad = jnp.concatenate([key_grad[..., :NOPE], value_grad], axis=-1)
-    kv_pre_grad = kv_pre_grad.reshape(row_count, -1).astype(bf16)
-    rot_partial = rotate(jnp.sum(key_grad[..., NOPE:], axis=1), cosine_table, sine_table, -1.0)
-    q_dot = jnp.sum(q_pre_grad.astype(f32) * q_pre, axis=1)
-    kv_dot = jnp.sum(kv_pre_grad.astype(f32) * kv_pre, axis=1)
+    rot_partial = rotate(
+        head_sums[2, :, NOPE : NOPE + ROPE], cosine_table, sine_table, -1.0
+    )
+    q_dot = jnp.sum(head_sums[0], axis=1)
+    kv_dot = jnp.sum(head_sums[1], axis=1)
     dots = row_parts(jnp.concatenate([jnp.stack([q_dot, kv_dot]), rot_partial.T], axis=0))
     q_part = against_rows(q_pre_grad, full_qb).astype(bf16)
     kv_part = against_rows(kv_pre_grad, full_kvb).astype(bf16)
@@ -931,13 +1029,11 @@
         axis=-1,
     ).reshape(row_count, -1)
     passed, inner, near = reduce_start(both_part)
-    extra = kv_pre_grad.shape[1] - q_pre_grad.shape[1]
     tcount = step_count[0].astype(f32)
     wide_rate = D ** (-0.5)
     block_down = down_sum.finish(w_down.shape[1])
     block_gate = gate_sum.finish(w_gate.shape[1])
     block_up = up_sum.finish(w_up.shape[1])
-    block_o = o_sum.finish(w_o.shape[1])
     passed, q_pre_late, kv_pre_late, block_down, block_gate, block_up = tie(
         passed, q_pre_grad, kv_pre_grad, block_down, block_gate, block_up
     )
@@ -959,19 +1055,15 @@
     )
     second = along_line(reduce_relay(both_part, passed), pairs_second)
     head_columns = w_kvb.shape[1]
-    chips = wide_count // 2
-    head_products = [
-        jnp.concatenate(
-            [
-                jnp.pad(first, ((0, 0), (0, extra))).reshape(chips, -1, head_columns),
-                last.reshape(chips, -1, head_columns),
-            ],
-            axis=1,
-        ).reshape(-1, head_columns)
-        for first, last in zip(
-            chunk_products(q_normed, q_pre_late), chunk_products(kv_normed, kv_pre_late)
-        )
-    ]
+    qb_full = inner_rows(q_normed, q_pre_late).astype(bf16)
+    kvb_full = inner_rows(kv_normed, kv_pre_late).astype(bf16)
+    head_products = jnp.concatenate(
+        [
+            qb_full.reshape(wide_count, -1, head_columns),
+            kvb_full.reshape(wide_count, -1, head_columns),
+        ],
+        axis=1,
+    ).reshape(-1, head_columns)
     second, dots, main_sent, head_products = tie(second, dots, main_sent, head_products)
     main_owned = [
         lax.all_to_all(part, "wide", split_axis=0, concat_axis=0, tiled=True)
@@ -980,7 +1072,8 @@
     dots = sum(dots).T
     q_dot, kv_dot = dots[:, :1], dots[:, 1:2]
     rot_grad = dots[:, 2:].astype(bf16)
-    heads_sum = Scatter(head_products)
+    head_products, block_o = tie(head_products, block_o)
+    block_heads = scatter_rows(head_products)
     both_grad = reduce_end(both_part, (inner, near, second))
     q_normed_grad = both_grad[:, :q_width]
     kv_normed_grad = both_grad[:, q_width:]
@@ -993,11 +1086,11 @@
         inv_kv * kv_gain * kv_normed_grad - kv_latent * inv_kv**2 * kv_dot / KVR
     ).astype(bf16)
     share = (narrow_index == 0).astype(f32)
-    first_dot = row_totals(
+    first_dot = row_parts(
         jnp.sum(q_latent_grad.astype(f32) * q_latent, axis=1)
         + jnp.sum(kv_latent_grad.astype(f32) * kv_latent, axis=1)
         + share * jnp.sum(rot_grad.astype(f32) * key_rot, axis=1)
-    )[:, None]
+    )
     latent_grad = jnp.concatenate([q_latent_grad, kv_latent_grad, rot_grad], axis=1)
     full_kr = full_latent[:, q_width + kv_width :]
     own_kr = lax.dynamic_slice_in_dim(full_kr, narrow_index * local_width, local_width, 0)
@@ -1005,20 +1098,18 @@
         latent_grad[:, : q_width + kv_width], full_latent[:, : q_width + kv_width]
     ).astype(bf16)
     normed_passed, normed_inner, normed_near = reduce_start(normed_part)
-    latent_sum = Scatter(chunk_products(normed, latent_grad))
-    head_sending = heads_sum.outgoing()
-    latent_sum.parts, head_sending = tie(latent_sum.parts, head_sending)
-    heads_sum.send(head_sending)
-    normed_passed, latent_sending = tie(normed_passed, latent_sum.outgoing())
-    latent_sum.send(latent_sending)
+    latent_full = weight_product(normed, latent_grad)
+    normed_passed, latent_full = tie(normed_passed, latent_full)
+    latent_late, first_owned, first_dot = tie(latent_full, main_owned[0], first_dot)
+    first_dot = sum(first_dot)[:, None]
+    block_latent = scatter_rows(latent_late)
     normed_second = along_line(reduce_relay(normed_part, normed_passed), pairs_second)
-    head_sending, latent_sending = heads_sum.outgoing(), latent_sum.outgoing()
-    normed_second, head_sending, latent_sending = tie(
-        normed_second, head_sending, latent_sending
-    )
-    heads_sum.send(head_sending)
-    latent_sum.send(latent_sending)
-    normed_second, first_owned = tie(normed_second, main_owned[0])
+    normed_second, first_owned = tie(normed_second, first_owned)
+    change_one, mid_mom_a, mid_sq_a = slot_group(
+        main_scales, first_owned, basis_la, basis_ra, mom_a, sq_a, groups[0], None
+    )
+    change_one, last_owned = tie(change_one, main_owned[1])
+    back_one = lax.all_to_all(change_one, "wide", split_axis=0, concat_axis=0, tiled=True)
     normed_grad = reduce_end(normed_part, (normed_inner, normed_near, normed_second)) + (
         against_rows(rot_grad, own_kr)
     )
@@ -1029,34 +1120,19 @@
         - residual * inv_first**2 * first_dot / D
     )
 
-    gain_grads = wide_totals(
-        jnp.concatenate([in_gain_grad, post_gain_grad, q_gain_grad, kv_gain_grad])
-    )
-    gains_total = gain_grads[: 2 * local_width].reshape(2, local_width)
-    qgain_total = gain_grads[2 * local_width : 2 * local_width + q_width]
-    kvgain_total = gain_grads[2 * local_width + q_width :]
-    change_one, mid_mom_a, mid_sq_a = slot_group(
-        main_scales, first_owned, basis_la, basis_ra, mom_a, sq_a, groups[0], None
-    )
-    last_owned, input_grad = tie(main_owned[1], input_grad)
-    change_one, latent_sum.parts, heads_sum.parts = tie(
-        change_one, latent_sum.parts, heads_sum.parts
-    )
-    back_one = lax.all_to_all(change_one, "wide", split_axis=0, concat_axis=0, tiled=True)
-    block_heads = heads_sum.finish(w_kvb.shape[1]).reshape(2, -1, w_kvb.shape[1])
-    half_qb = w_qb.shape[0] // 2
-    block_qb = block_heads[:, :half_qb, : w_qb.shape[1]].reshape(w_qb.shape)
-    block_kvb = block_heads[:, half_qb:].reshape(w_kvb.shape)
-    block_latent = latent_sum.finish(latent_grad.shape[1])
+    change_two, mid_mom_a, mid_sq_a = slot_group(
+        main_scales, last_owned, basis_la, basis_ra, mom_a, sq_a, groups[1],
+        (mid_mom_a, mid_sq_a),
+    )
+    block_latent, block_heads, change_two = tie(block_latent, block_heads, change_two)
+    back_two = lax.all_to_all(change_two, "wide", split_axis=0, concat_axis=0, tiled=True)
+    block_qb = block_heads[: w_qb.shape[0]].reshape(w_qb.shape[0], heads_here, 128)
+    block_qb = block_qb[:, :, : NOPE + ROPE].reshape(w_qb.shape)
+    block_kvb = block_heads[w_qb.shape[0] :]
     block_qa = block_latent[:, :q_width]
     block_kv = block_latent[:, q_width : q_width + kv_width]
     block_kr = block_latent[:, q_width + kv_width :]
     late_blocks = [block_qa, block_kv]
-    change_two, mid_mom_a, mid_sq_a = slot_group(
-        main_scales, last_owned, basis_la, basis_ra, mom_a, sq_a, groups[1],
-        (mid_mom_a, mid_sq_a),
-    )
-    back_two = lax.all_to_all(change_two, "wide", split_axis=0, concat_axis=0, tiled=True)
     late_capacity = min(late_units, capacity_a)
     late_send, late_back = routes(late_owners, capacity_a, late_capacity, wide_count)
     late_slots, late_scales = late_places(
@@ -1074,17 +1150,39 @@
             ([block_kvb], c_send),
         )
     ]
+    sent_parts, back_two = tie(sent_parts, back_two)
     late_owned, owned_b, owned_c = trade_joined(sent_parts, wide_count)
-    late_owned, back_one = tie(late_owned, back_one)
-
-    def to_input(*features):
-        joined = jnp.stack([value.astype(bf16) for value in features], axis=0)
-        joined = joined.reshape(len(features), wide_count, piece_rows, -1).transpose(1, 0, 2, 3)
-        returned = lax.all_to_all(joined, "wide", split_axis=0, concat_axis=0, tiled=True)
-        placed = jnp.take(returned, deal_row, axis=0, mode="clip").astype(f32)
-        return [placed[:, at].reshape(row_count, -1) for at in range(len(features))]
-
-    final_out, final_grad = to_input(layer_out, input_grad)
+
+    gain_part = jnp.concatenate([in_gain_grad, post_gain_grad, q_gain_grad, kv_gain_grad])
+    gain_high = lax.optimization_barrier(gain_part.astype(bf16))
+    gain_low = (gain_part - gain_high.astype(f32)).astype(bf16)
+    gain_rows = jnp.concatenate([gain_high, gain_low])
+    gain_height = -(-gain_rows.shape[0] // local_width)
+    gain_rows = jnp.pad(gain_rows, (0, gain_height * local_width - gain_rows.shape[0]))
+    gain_rows = jnp.broadcast_to(
+        gain_rows.reshape(1, gain_height, local_width), (wide_count, gain_height, local_width)
+    )
+    leaving = jnp.concatenate(
+        [
+            layer_out.astype(bf16).reshape(wide_count, piece_rows, local_width),
+            input_grad.astype(bf16).reshape(wide_count, piece_rows, local_width),
+            gain_rows,
+        ],
+        axis=1,
+    )
+    leaving, late_owned = tie(leaving, late_owned)
+    returned_rows = lax.all_to_all(leaving, "wide", split_axis=0, concat_axis=0, tiled=True)
+    placed = jnp.take(returned_rows[:, : 2 * piece_rows], deal_row, axis=0, mode="clip")
+    final_out = placed[:, :piece_rows].astype(f32).reshape(row_count, local_width)
+    final_grad = placed[:, piece_rows:].astype(f32).reshape(row_count, local_width)
+    gain_rows = returned_rows[:, 2 * piece_rows :].reshape(wide_count, -1)
+    gain_size = gain_part.shape[0]
+    gain_grads = jnp.sum(gain_rows[:, :gain_size].astype(f32), axis=0) + jnp.sum(
+        gain_rows[:, gain_size : 2 * gain_size].astype(f32), axis=0
+    )
+    gains_total = gain_grads[: 2 * local_width].reshape(2, local_width)
+    qgain_total = gain_grads[2 * local_width : 2 * local_width + q_width]
+    kvgain_total = gain_grads[2 * local_width + q_width :]
     late_change, new_mom_a, new_sq_a = late_steps(
         late_slots, late_scales, late_owned, basis_la, basis_ra, mid_mom_a, mid_sq_a
     )
@@ -1098,6 +1196,7 @@
                     wide_index, tcount),
         owned_c, basis_lc, basis_rc, mom_c, sq_c,
     )
+    late_change, final_grad = tie(late_change, final_grad)
     returned = trade_joined(
         [change.reshape((-1,) + change.shape[2:]) for change in (late_change, change_b, change_c)],
         wide_count,
@@ -1112,6 +1211,7 @@
     update_qa, update_kv = unit_columns(late_result, late_blocks)
     update_qb = unit_columns(result_b, [block_qb])[0]
     update_kvb = unit_columns(result_c, [block_kvb])[0]
+    block_kr = block_kr.astype(f32)
     update_kr, new_kr_mom, new_kr_sq = plain_adam(block_kr, kr_mom, kr_sq, wide_rate, tcount)
     update_gains, new_gain_mom, new_gain_sq = plain_adam(
         gains_total, gain_mom, gain_sq, gain_rate, tcount
@@ -1125,11 +1225,11 @@
     return (
         final_out,
         final_grad,
-        block_qa,
-        block_kv,
-        block_qb,
-        block_kvb,
-        block_o,
+        block_qa.astype(f32),
+        block_kv.astype(f32),
+        block_qb.astype(f32),
+        block_kvb.astype(f32),
+        block_o.astype(f32),
         block_gate,
         block_up,
         block_down,

time: 1050 us -> 985 us (0.938)
  local copies, waits for them, and re-layouts: 131 us -> 105 us
  matrix products: 105 us -> 85.8 us
  blocking collectives: 30.7 us -> 15.1 us
  waiting for transfers between devices: 318 us -> 307 us
    pallas_call x0 -> x4, Pallas kernels: none -> 33.3 us  [the longest x1 15.7 us: attend_back(): pl.pallas_call(attend_back_kernel, grid=(width // 256,), in_specs=[pair,...]
    all_to_all x1 -> x0, blocking collectives: 30.7 us -> none  [trade_joined(): lax.all_to_all(joined, 'wide', split_axis=0, concat_axis=0, tiled=True)]
    ppermute x39 -> x18, waiting for transfers between devices: 64.1 us -> 39.3 us  [flipped(): return lax.ppermute(value, 'wide', [(i, i ^ bit) for i in range(count)])]
    dot_general x6 -> x2, matrix products: 22.1 us -> 1.69 us  [inner_rows(): lax.dot_general(left_side, right_side, (((0,), (0,)), ((), ())), preferre...]
    all_to_all x1, waiting for transfers between devices: 17.1 us -> 1.27 us  [body(): lax.all_to_all(change_one, 'wide', split_axis=0, concat_axis=0, tiled=True)]
    all_gather x0 -> x1, blocking collectives: none -> 15.1 us  [body(): full_kvb = lax.all_gather(w_kvb, 'wide', axis=0, tiled=True)]
    slice x18 -> x7, local copies, waits for them, and re-layouts: 13.4 us -> 1.55 us  [the longest x1 1.18 us: body(): returned_rows[:, :2 * piece_rows]]
    ppermute x39 -> x18, starting transfers between devices: 27.1 us -> 15.3 us  [flipped(): return lax.ppermute(value, 'wide', [(i, i ^ bit) for i in range(count)])]
  transfers between devices with their start and end apart: 105 -> 85, of which waited for: 34 -> 40; matrix products, arithmetic and copies ran while one was open for 26% -> 24% of each run, Pallas kernels for 14% -> 15%
where the time goes in v3:
time: 985 us; the launch traced here: 967 us
  waiting for transfers between devices  307 us (31%)
  starting transfers between devices  175 us (18%)
  Pallas kernels  164 us (17%)
  local copies, waits for them, and re-layouts  105 us (11%)
  other arithmetic  96 us (10%)
  matrix products  85.8 us (9%)
  between operations  18.7 us (2%)
  blocking collectives  15.1 us (2%)
    ppermute x40, waiting for transfers between devices, along_line(): return lax.ppermute(value, 'narrow', pairs)  194 us
    ppermute x40, starting transfers between devices, along_line(): return lax.ppermute(value, 'narrow', pairs)  84.3 us
    pallas_call x5, Pallas kernels, slot_call(): pl.pallas_call(kernel, grid_spec=pltpu.PrefetchScalarGridSpec(num_scalar_...  56.9 us
    dot_general x7, matrix products, product(): return jnp.dot(left_side, right_side, preferred_element_type=jnp.float32)  44.3 us
    dot_general x8, matrix products, against_rows(): lax.dot_general(left_side, right_side, (((1,), (1,)), ((), ())), preferre...  39.8 us
    ppermute x18, waiting for transfers between devices, flipped(): return lax.ppermute(value, 'wide', [(i, i ^ bit) for i in range(count)])  39.3 us
    unnamed x345, local copies, waits for them, and re-layouts  39.2 us
    pallas_call x3, Pallas kernels, chunk_products(): pl.pallas_call(chunk_kernel, grid_spec=pltpu.PrefetchScalarGridSpec(num_s...  27.3 us
  transfers between devices with their start and end apart: 85, of which 40 were waited for; matrix products, arithmetic and copies ran while one was open for 24% of the time, Pallas kernels for 15%

profile of v3, /device:TPU:11, one launch (start us, length us, event | category | flops | bytes accessed | tf_op | source)
XLA Modules:
  0.0 966.8 jit_solution(11945837406345025259)
XLA Ops:
  19.9 5.5 all-to-all-start
  27.4 9.2 all-to-all-done
  40.2 15.1 %all_gather.23 = bf16[256,1280]{1,0:T(8,128)(2,1)} all-gather(bf16[32,1280]{1,0:T(8,128)(2,1)S(1)} %copy-done.106), channel_id=1, replica_groups=mesh['wide'=8,'narrow'=4] {'wide'}, dimensions={0}, use_global_device_ids=true | all-gather | bytes 737280 | tf_op jit(solution)/shard_map/all_gather | solution.py:882
  60.9 3.7 collective-permute-done.1
  64.7 4.7 collective-permute-start.2
  78.2 6.0 collective-permute-done.2
  98.1 4.9 collective-permute-done.8
  103.0 5.9 collective-permute-start.10
  114.5 3.9 collective-permute-start.24
  126.5 11.0 %shard_map.741.right_ref = bf16[512,640]{1,0:T(8,128)(2,1)S(1)} custom-call(f32[512,1280]{1,0:T(8,128)S(1)} %fusion.97.query_ref, f32[512,1280]{1,0:T(8,128)} %fusion.98.key_value_ref, bf16[512,128]{1,0:T(8,128)(2,1)S(1)} %pad.45.rotary_ref, f32[3,512,128]{2,1,0:T(8,128)S(1)} %pad_maximum_fusion.3.table_ref, f32[512,512]{1,0:T(8,128)S(1)} %copy-done.15), custom_call_target="tpu_custom_call" | custom-call | tf_op jit(solution)/shard_map/pallas_call | solution.py:704
  141.8 6.1 collective-permute-start.25
  149.9 4.4 convolution_convert_fusion.1
  162.8 4.2 gather_fusion.1
  167.0 5.6 all-to-all-start.1
  178.7 11.4 %collective-permute-done.13 = bf16[512,640]{1,0:T(8,128)(2,1)S(1)} collective-permute-done((bf16[512,640]{1,0:T(8,128)(2,1)}, bf16[512,640]{1,0:T(8,128)(2,1)S(1)}, u32[]{:S(2)}, u32[]{:S(2)}) %collective-permute-start.13) | collective-permute-done | bytes 655392 | tf_op jit(solution)/shard_map/ppermute | solution.py:90
  190.1 26.0 %collective-permute-done.15 = bf16[512,640]{1,0:T(8,128)(2,1)S(1)} collective-permute-done((bf16[512,640]{1,0:T(8,128)(2,1)S(1)}, bf16[512,640]{1,0:T(8,128)(2,1)S(1)}, u32[]{:S(2)}, u32[]{:S(2)}) %collective-permute-start.15) | collective-permute-done | bytes 655392 | tf_op jit(solution)/shard_map/ppermute | solution.py:90
  228.5 24.0 %collective-permute-done.17 = bf16[512,640]{1,0:T(8,128)(2,1)S(1)} collective-permute-done((bf16[512,640]{1,0:T(8,128)(2,1)}, bf16[512,640]{1,0:T(8,128)(2,1)S(1)}, u32[]{:S(2)}, u32[]{:S(2)}) %collective-permute-start.17) | collective-permute-done | bytes 655392 | tf_op jit(solution)/shard_map/ppermute | solution.py:90
  252.5 4.5 collective-permute-start.19
  257.0 3.8 fusion.3.left_ref
  263.9 3.7 collective-permute-done.18
  273.4 4.0 fusion.8.left_ref
  277.5 11.0 %fusion.100 = f32[512,1600]{1,0:T(8,128)} fusion(bf16[512,2560]{1,0:T(8,128)(2,1)} %fusion.3.left_ref, bf16[2560,1600]{1,0:T(8,128)(2,1)} %all-gather.16.cloned.1.call-done), kind=kOutput, calls=%fused_computation.325 | convolution fusion | flops 4194304000 | bytes 14090240 | tf_op jit(solution)/shard_map/dot_general | solution.py:32
  288.5 10.9 %fusion.99 = f32[512,1600]{1,0:T(8,128)} fusion(bf16[512,2560]{1,0:T(8,128)(2,1)} %fusion.8.left_ref, bf16[2560,1600]{1,0:T(8,128)(2,1)} %all-gather.14.cloned.1.call-done), kind=kOutput, calls=%fused_computation.324 | convolution fusion | flops 4194304000 | bytes 14090240 | tf_op jit(solution)/shard_map/dot_general | solution.py:32
  299.6 12.2 %multiply_convert_fusion = (bf16[512,1600]{1,0:T(8,128)(2,1)S(1)}, bf16[512,1600]{1,0:T(8,128)(2,1)S(1)}, bf16[512,1600]{1,0:T(8,128)(2,1)S(1)}) fusion(f32[512,1600]{1,0:T(8,128)} %fusion.100, f32[512,1600]{1,0:T(8,128)} %fusion.99, bf16[512,2560]{1,0:T(8,128)(2,1)} %fusion.8.left_ref, bf16[2560,1600]{1,0:T(8,128)(2,1)} %all-gather.12.cloned.1.call-done), kind=kOutput, calls=%fused_computation.37 | convolution fusion | flops 4205772800 | bytes 22282240 | tf_op jit(solution)/shard_map/dot_general | solution.py:32
  311.8 9.1 shard_map.742
  324.3 10.1 %fusion.101 = f32[512,2560]{1,0:T(8,128)} fusion(bf16[512,1600]{1,0:T(8,128)(2,1)S(1)} %get-tuple-element.179.right_ref, bf16[2560,1600]{1,0:T(8,128)(2,1)} %all-gather.12.cloned.1.call-done), kind=kOutput, calls=%fused_computation.326 | convolution fusion | flops 4194304000 | bytes 15073280 | tf_op jit(solution)/shard_map/dot_general | solution.py:42
  334.3 9.4 add_convert_fusion
  346.8 9.1 shard_map.743
  364.4 9.1 shard_map.745
  378.5 24.4 %collective-permute-done.27 = bf16[512,640]{1,0:T(8,128)(2,1)S(1)} collective-permute-done((bf16[512,640]{1,0:T(8,128)(2,1)S(1)}, bf16[512,640]{1,0:T(8,128)(2,1)S(1)}, u32[]{:S(2)}, u32[]{:S(2)}) %collective-permute-start.27) | collective-permute-done | bytes 655392 | tf_op jit(solution)/shard_map/ppermute | solution.py:90
  410.8 12.2 %collective-permute-done.26 = bf16[512,640]{1,0:T(8,128)(2,1)S(1)} collective-permute-done((bf16[512,640]{1,0:T(8,128)(2,1)}, bf16[512,640]{1,0:T(8,128)(2,1)S(1)}, u32[]{:S(2)}, u32[]{:S(2)}) %collective-permute-start.26) | collective-permute-done | bytes 655392 | tf_op jit(solution)/shard_map/ppermute | solution.py:90
  426.1 6.0 collective-permute-done.38.refs_2_
  444.1 9.6 collective-permute-done.35
  459.4 8.4 collective-permute-done.40
  475.5 4.1 shard_map.749
  481.2 9.0 convolution_convert_fusion.2
  506.9 4.1 convolution_convert_fusion.6.grad_ref
  511.0 15.7 %shard_map.750 = (bf16[512,1280]{1,0:T(8,128)(2,1)S(1)}, bf16[512,1280]{1,0:T(8,128)(2,1)S(1)}, f32[3,512,128]{2,1,0:T(8,128)S(1)}) custom-call(f32[512,1280]{1,0:T(8,128)} %copy-done.2, f32[512,1280]{1,0:T(8,128)} %fusion.98.key_value_ref, bf16[512,128]{1,0:T(8,128)(2,1)S(1)} %pad.45.rotary_ref, f32[3,512,128]{2,1,0:T(8,128)S(1)} %pad_maximum_fusion.3.table_ref, ...), custom_call_target="tpu_custom_call" | custom-call | tf_op jit(solution)/shard_map/pallas_call | solution.py:717
  528.1 4.3 collective-permute-done.43.refs_2_
  534.8 24.8 %collective-permute-done.45.refs_2_ = bf16[320,1664]{1,0:T(8,128)(2,1)S(1)} collective-permute-done((bf16[320,1664]{1,0:T(8,128)(2,1)}, bf16[320,1664]{1,0:T(8,128)(2,1)S(1)}, u32[]{:S(2)}, u32[]{:S(2)}) %collective-permute-start.45) | collective-permute-done | bytes 1064992 | tf_op jit(solution)/shard_map/ppermute | solution.py:86
  584.8 6.3 collective-permute-start.57
  609.7 10.2 %shard_map.756 = (bf16[8,9,64,320]{3,2,1,0:T(8,128)(2,1)}, bf16[8,8,64,320]{3,2,1,0:T(8,128)(2,1)}) custom-call(s32[136]{0:T(256)} %broadcast_minimum_fusion.send_ref, bf16[320,640]{1,0:T(8,128)(2,1)} %reduce-scatter.4.cloned.1.call-done.refs_0_, f32[320,1600]{1,0:T(8,128)} %shard_map.754.refs_1_, f32[320,1600]{1,0:T(8,128)} %shard_map.755.refs_2_, ...), custom_call_target="tpu_custom_call" | custom-call | tf_op jit(solution)/shard_map/pallas_call | solution.py:401
  622.4 8.3 all-to-all-start.2
  631.1 4.5 collective-permute-start.47
  638.5 4.7 collective-permute-done.48
  649.9 4.7 collective-permute-start.65
  654.5 23.8 %all-to-all-done.2.gradient_ref = bf16[8,9,64,320]{3,2,1,0:T(8,128)(2,1)} async-done(((bf16[8,9,64,320]{3,2,1,0:T(8,128)(2,1)}), bf16[8,9,64,320]{3,2,1,0:T(8,128)(2,1)}, u32[]{:S(2)}, u32[]{:S(2)}) %all-to-all-start.2) | async-done | bytes 2949152 | tf_op jit(solution)/shard_map/all_to_all | solution.py:1069
  678.4 5.9 all-to-all-start.3
  695.2 27.6 %collective-permute-done.63 = bf16[512,640]{1,0:T(8,128)(2,1)S(1)} collective-permute-done((bf16[512,640]{1,0:T(8,128)(2,1)S(1)}, bf16[512,640]{1,0:T(8,128)(2,1)S(1)}, u32[]{:S(2)}, u32[]{:S(2)}) %collective-permute-start.63) | collective-permute-done | bytes 655392 | tf_op jit(solution)/shard_map/ppermute | solution.py:90
  722.8 19.9 %shard_map.758 = (bf16[8,9,64,320]{3,2,1,0:T(8,128)(2,1)S(1)}, f32[17,64,2560]{2,1,0:T(8,128)}, f32[17,64,2560]{2,1,0:T(8,128)}) custom-call(s32[18]{0:T(128)S(1)} %copy-done.50, f32[20]{0:T(128)S(1)} %pad_maximum_fusion.9.scale_ref, bf16[8,9,64,320]{3,2,1,0:T(8,128)(2,1)} %all-to-all-done.2.gradient_ref, f32[17,2560,128]{2,1,0:T(8,128)} %left_ref.5, ...), custom_call_target="tpu_custom_call" | custom-call | tf_op jit(solution)/shard_map/pallas_call | solution.py:548
  744.6 21.8 %shard_map.759 = (bf16[8,8,64,320]{3,2,1,0:T(8,128)(2,1)S(1)}, f32[17,64,2560]{2,1,0:T(8,128)}, f32[17,64,2560]{2,1,0:T(8,128)}) custom-call(s32[16]{0:T(128)S(1)} %concatenate.96.refs_0_, f32[18]{0:T(128)S(1)} %pad_maximum_fusion.8.refs_1_, bf16[8,8,64,320]{3,2,1,0:T(8,128)(2,1)} %all-to-all-done.3.refs_2_, ...), custom_call_target="tpu_custom_call", output_to_operand_aliasing={{1}: (7, {}), {2}: (8, {})} | custom-call | tf_op jit(solution)/shard_map/pallas_call | solution.py:548
  768.2 8.5 all-to-all-start.4
  795.7 17.3 %all-to-all-done.4.last_ref = bf16[8,8,64,320]{3,2,1,0:T(8,128)(2,1)} async-done(((bf16[8,8,64,320]{3,2,1,0:T(8,128)(2,1)}), bf16[8,8,64,320]{3,2,1,0:T(8,128)(2,1)}, u32[]{:S(2)}, u32[]{:S(2)}) %all-to-all-start.4) | async-done | bytes 2621472 | tf_op jit(solution)/shard_map/all_to_all | solution.py:1128
  816.3 6.0 all-to-all-start.5
  825.2 12.1 %collective-permute-done.60 = bf16[512,640]{1,0:T(8,128)(2,1)} collective-permute-done((bf16[512,640]{1,0:T(8,128)(2,1)}, bf16[512,640]{1,0:T(8,128)(2,1)}, u32[]{:S(2)}, u32[]{:S(2)}) %collective-permute-start.60) | collective-permute-done | bytes 655392 | tf_op jit(solution)/shard_map/ppermute | solution.py:90
  842.2 5.3 all-to-all-done.5
  849.1 5.1 all-to-all-start.6
  860.6 11.1 %all-to-all-done.6 = bf16[8,133,640]{2,1,0:T(8,128)(2,1)S(1)} async-done(((bf16[8,133,640]{2,1,0:T(8,128)(2,1)}), bf16[8,133,640]{2,1,0:T(8,128)(2,1)S(1)}, u32[]{:S(2)}, u32[]{:S(2)}) %all-to-all-start.6) | async-done | bytes 1361952 | tf_op jit(solution)/shard_map/all_to_all | solution.py:1174
  871.8 6.0 all-to-all-start.8
  890.8 6.4 shard_map.760
  899.9 3.8 shard_map.761
  905.0 4.9 shard_map.762
  918.4 5.4 all-to-all-start.7
  933.9 10.4 %shard_map.763 = (f32[320,640]{1,0:T(8,128)}, f32[320,1600]{1,0:T(8,128)}, f32[320,1600]{1,0:T(8,128)}, f32[320,1600]{1,0:T(8,128)}) custom-call(s32[85]{0:T(128)} %copy-done.143, bf16[8,9,64,320]{3,2,1,0:T(8,128)(2,1)} %all-to-all-done.8.first_ref, bf16[8,8,64,320]{3,2,1,0:T(8,128)(2,1)} %all-to-all-done.4.last_ref, bf16[320,640]{1,0:T(8,128)(2,1)} %refs_0_.1, ...), custom_call_target="tpu_custom_call" | custom-call | tf_op jit(solution)/shard_map/pallas_call | solution.py:446
  (743 shorter events, 336.7 us)
Async XLA Ops:
  7.3 49.2 %all-gather.18.cloned.1.call-start = ((), (), s32[]{:S(2)}) async-start(), calls=%async_computation.20 | async-start | bytes 1990656 | tf_op jit(solution)/shard_map/all_gather | solution.py:880
  9.1 114.3 %all-gather.8.cloned.1.call-start = ((), (), s32[]{:S(2)}) async-start(), calls=%async_computation.12 | async-start | bytes 2211840 | tf_op jit(solution)/shard_map/all_gather | solution.py:881
  11.2 138.7 %all-gather.10.cloned.1.call-start = ((), (), s32[]{:S(2)}) async-start(), calls=%async_computation.13 | async-start | bytes 3686400 | tf_op jit(solution)/shard_map/all_gather | solution.py:883
  11.9 265.5 %all-gather.16.cloned.1.call-start = ((), (), s32[]{:S(2)}) async-start(), calls=%async_computation.16 | async-start | bytes 9584640 | tf_op jit(solution)/shard_map/all_gather | solution.py:886
  12.5 276.0 %all-gather.14.cloned.1.call-start = ((), (), s32[]{:S(2)}) async-start(), calls=%async_computation.15 | async-start | bytes 9584640 | tf_op jit(solution)/shard_map/all_gather | solution.py:885
  13.3 56.1 %collective-permute-start.4 = (f32[1536]{0:T(1024)S(1)}, f32[1536]{0:T(1024)S(1)}, u32[]{:S(2)}, u32[]{:S(2)}) collective-permute-start(f32[1536]{0:T(1024)S(1)} %concatenate.82), channel_id=1, source_target_pairs={{0,1},{1,2},{2,3},{3,0},{4,5},{5,6},{6,7},{7,4},{8,9},{9,10},{10,1... | collective-permute-start | bytes 18440 | tf_op jit(solution)/shard_map/ppermute | solution.py:81
  14.6 59.2 %collective-permute-start.5 = (f32[1536]{0:T(1024)S(1)}, f32[1536]{0:T(1024)S(1)}, u32[]{:S(2)}, u32[]{:S(2)}) collective-permute-start(f32[1536]{0:T(1024)S(1)} %concatenate.82), channel_id=1, source_target_pairs={{0,2},{1,3},{2,0},{3,1},{4,6},{5,7},{6,4},{7,5},{8,10},{9,11},{10,... | collective-permute-start | bytes 18440 | tf_op jit(solution)/shard_map/ppermute | solution.py:81
  15.6 58.3 %collective-permute-start.6 = (f32[1536]{0:T(1024)S(1)}, f32[1536]{0:T(1024)S(1)}, u32[]{:S(2)}, u32[]{:S(2)}) collective-permute-start(f32[1536]{0:T(1024)S(1)} %concatenate.82), channel_id=1, source_target_pairs={{0,3},{1,0},{2,1},{3,2},{4,7},{5,4},{6,5},{7,6},{8,11},{9,8},{10,9... | collective-permute-start | bytes 18440 | tf_op jit(solution)/shard_map/ppermute | solution.py:81
  25.4 274.2 %all-gather.12.cloned.1.call-start = ((), (), s32[]{:S(2)}) async-start(), calls=%async_computation.14 | async-start | bytes 9584640 | tf_op jit(solution)/shard_map/all_gather | solution.py:884
  36.6 28.1 %collective-permute-start.1 = (bf16[512,640]{1,0:T(8,128)(2,1)S(1)}, bf16[512,640]{1,0:T(8,128)(2,1)}, u32[]{:S(2)}, u32[]{:S(2)}) collective-permute-start(bf16[512,640]{1,0:T(8,128)(2,1)S(1)} %bitcast.228), channel_id=1, source_target_pairs={{0,2},{2,0},{1,3},{3,1},{4,6},{6,4},{5,7},{7,5},{8,10},{10,8},{9,1... | collective-permute-start | bytes 1966088 | tf_op jit(solution)/shard_map/ppermute | solution.py:90
  38.7 37.0 %collective-permute-start = (bf16[512,640]{1,0:T(8,128)(2,1)S(1)}, bf16[512,640]{1,0:T(8,128)(2,1)}, u32[]{:S(2)}, u32[]{:S(2)}) collective-permute-start(bf16[512,640]{1,0:T(8,128)(2,1)S(1)} %bitcast.229), channel_id=1, source_target_pairs={{0,1},{1,0},{2,3},{3,2},{4,5},{5,4},{6,7},{7,6},{8,9},{9,8},{10,11... | collective-permute-start | bytes 1966088 | tf_op jit(solution)/shard_map/ppermute | solution.py:90
  64.7 19.5 %collective-permute-start.2 = (bf16[512,640]{1,0:T(8,128)(2,1)S(1)}, bf16[512,640]{1,0:T(8,128)(2,1)S(1)}, u32[]{:S(2)}, u32[]{:S(2)}) collective-permute-start(bf16[512,640]{1,0:T(8,128)(2,1)S(1)} %bitcast.230), channel_id=1, source_target_pairs={{1,2},{2,1},{5,6},{6,5},{9,10},{10,9},{13,14},{14,13},{17,18},{18,... | collective-permute-start | bytes 1966088 | tf_op jit(solution)/shard_map/ppermute | solution.py:90
  113.5 28.3 %collective-permute-start.11 = (bf16[512,640]{1,0:T(8,128)(2,1)}, bf16[512,640]{1,0:T(8,128)(2,1)}, u32[]{:S(2)}, u32[]{:S(2)}) collective-permute-start(bf16[512,640]{1,0:T(8,128)(2,1)} %param.47), channel_id=1, source_target_pairs={{0,2},{2,0},{1,3},{3,1},{4,6},{6,4},{5,7},{7,5},{8,10},{10,8},{9,1... | collective-permute-start | bytes 1966088 | tf_op jit(solution)/shard_map/ppermute | solution.py:90
  113.6 34.3 %collective-permute-start.23 = (bf16[512,640]{1,0:T(8,128)(2,1)}, bf16[512,640]{1,0:T(8,128)(2,1)}, u32[]{:S(2)}, u32[]{:S(2)}) collective-permute-start(bf16[512,640]{1,0:T(8,128)(2,1)} %param.47), channel_id=1, source_target_pairs={{0,1},{1,0},{2,3},{3,2},{4,5},{5,4},{6,7},{7,6},{8,9},{9,8},{10,11... | collective-permute-start | bytes 1966088 | tf_op jit(solution)/shard_map/ppermute | solution.py:90
  114.5 44.4 %collective-permute-start.24 = (bf16[512,640]{1,0:T(8,128)(2,1)}, bf16[512,640]{1,0:T(8,128)(2,1)}, u32[]{:S(2)}, u32[]{:S(2)}) collective-permute-start(bf16[512,640]{1,0:T(8,128)(2,1)} %param.47), channel_id=1, source_target_pairs={{1,2},{2,1},{5,6},{6,5},{9,10},{10,9},{13,14},{14,13},{17,18},{18,... | collective-permute-start | bytes 1966088 | tf_op jit(solution)/shard_map/ppermute | solution.py:90
  167.0 90.0 %all-to-all-start.1 = ((bf16[8,64,2560]{2,1,0:T(8,128)(2,1)}), bf16[8,64,2560]{2,1,0:T(8,128)(2,1)}, u32[]{:S(2)}, u32[]{:S(2)}) async-start(bf16[8,64,2560]{2,1,0:T(8,128)(2,1)} %gather_fusion.1), calls=%async_computation.1 | async-start | bytes 5242880 | tf_op jit(solution)/shard_map/all_to_all | solution.py:858
  172.6 437.1 %reduce-scatter.4.cloned.1.call-start = ((), (), s32[]{:S(2)}) async-start(), calls=%async_computation.17 | async-start | bytes 3686400 | tf_op jit(solution)/shard_map/reduce_scatter | solution.py:372
  176.0 40.0 %collective-permute-start.15 = (bf16[512,640]{1,0:T(8,128)(2,1)S(1)}, bf16[512,640]{1,0:T(8,128)(2,1)S(1)}, u32[]{:S(2)}, u32[]{:S(2)}) collective-permute-start(bf16[512,640]{1,0:T(8,128)(2,1)S(1)} %add_convert_fusion.5), channel_id=1, source_target_pairs={{0,2},{2,0},{1,3},{3,1},{4,6},{6,4},{5,7},{7,5},{8,10},{10,8},{9,1... | collective-permute-start | bytes 1966088 | tf_op jit(solution)/shard_map/ppermute | solution.py:90
  220.9 31.6 %collective-permute-start.17 = (bf16[512,640]{1,0:T(8,128)(2,1)}, bf16[512,640]{1,0:T(8,128)(2,1)S(1)}, u32[]{:S(2)}, u32[]{:S(2)}) collective-permute-start(bf16[512,640]{1,0:T(8,128)(2,1)} %get-tuple-element.587), channel_id=1, source_target_pairs={{0,2},{2,0},{1,3},{3,1},{4,6},{6,4},{5,7},{7,5},{8,10},{10,8},{9,1... | collective-permute-start | bytes 1966088 | tf_op jit(solution)/shard_map/ppermute | solution.py:90
  225.4 35.4 %collective-permute-start.16 = (bf16[512,640]{1,0:T(8,128)(2,1)}, bf16[512,640]{1,0:T(8,128)(2,1)}, u32[]{:S(2)}, u32[]{:S(2)}) collective-permute-start(bf16[512,640]{1,0:T(8,128)(2,1)} %get-tuple-element.587), channel_id=1, source_target_pairs={{0,1},{1,0},{2,3},{3,2},{4,5},{5,4},{6,7},{7,6},{8,9},{9,8},{10,11... | collective-permute-start | bytes 1966088 | tf_op jit(solution)/shard_map/ppermute | solution.py:90
  225.5 42.1 %collective-permute-start.18 = (bf16[512,640]{1,0:T(8,128)(2,1)}, bf16[512,640]{1,0:T(8,128)(2,1)S(1)}, u32[]{:S(2)}, u32[]{:S(2)}) collective-permute-start(bf16[512,640]{1,0:T(8,128)(2,1)} %get-tuple-element.587), channel_id=1, source_target_pairs={{1,2},{2,1},{5,6},{6,5},{9,10},{10,9},{13,14},{14,13},{17,18},{18,... | collective-permute-start | bytes 1966088 | tf_op jit(solution)/shard_map/ppermute | solution.py:90
  322.2 35.0 %collective-permute-start.29 = (bf16[640,1664]{1,0:T(8,128)(2,1)}, bf16[640,1664]{1,0:T(8,128)(2,1)S(1)}, u32[]{:S(2)}, u32[]{:S(2)}) collective-permute-start(bf16[640,1664]{1,0:T(8,128)(2,1)} %get-tuple-element.186), channel_id=1, source_target_pairs={{0,4},{4,0},{8,12},{12,8},{16,20},{20,16},{24,28},{28,24},{1,5},{5... | collective-permute-start | bytes 6389768 | tf_op jit(solution)/shard_map/ppermute | solution.py:86
  324.3 34.3 %collective-permute-start.30 = (bf16[640,1664]{1,0:T(8,128)(2,1)}, bf16[640,1664]{1,0:T(8,128)(2,1)}, u32[]{:S(2)}, u32[]{:S(2)}) collective-permute-start(bf16[640,1664]{1,0:T(8,128)(2,1)} %get-tuple-element.188), channel_id=1, source_target_pairs={{0,4},{4,0},{8,12},{12,8},{16,20},{20,16},{24,28},{28,24},{1,5},{5... | collective-permute-start | bytes 6389768 | tf_op jit(solution)/shard_map/ppermute | solution.py:86
  373.5 35.0 %collective-permute-start.32 = (bf16[640,1664]{1,0:T(8,128)(2,1)}, bf16[640,1664]{1,0:T(8,128)(2,1)S(1)}, u32[]{:S(2)}, u32[]{:S(2)}) collective-permute-start(bf16[640,1664]{1,0:T(8,128)(2,1)} %get-tuple-element.196), channel_id=1, source_target_pairs={{0,4},{4,0},{8,12},{12,8},{16,20},{20,16},{24,28},{28,24},{1,5},{5... | collective-permute-start | bytes 6389768 | tf_op jit(solution)/shard_map/ppermute | solution.py:86
  375.1 34.4 %collective-permute-start.33 = (bf16[640,1664]{1,0:T(8,128)(2,1)}, bf16[640,1664]{1,0:T(8,128)(2,1)S(1)}, u32[]{:S(2)}, u32[]{:S(2)}) collective-permute-start(bf16[640,1664]{1,0:T(8,128)(2,1)} %get-tuple-element.198), channel_id=1, source_target_pairs={{0,4},{4,0},{8,12},{12,8},{16,20},{20,16},{24,28},{28,24},{1,5},{5... | collective-permute-start | bytes 6389768 | tf_op jit(solution)/shard_map/ppermute | solution.py:86
  375.2 27.8 %collective-permute-start.27 = (bf16[512,640]{1,0:T(8,128)(2,1)S(1)}, bf16[512,640]{1,0:T(8,128)(2,1)S(1)}, u32[]{:S(2)}, u32[]{:S(2)}) collective-permute-start(bf16[512,640]{1,0:T(8,128)(2,1)S(1)} %get-tuple-element.599), channel_id=1, source_target_pairs={{0,1},{1,0},{2,3},{3,2},{4,5},{5,4},{6,7},{7,6},{8,9},{9,8},{10,11... | collective-permute-start | bytes 1966088 | tf_op jit(solution)/shard_map/ppermute | solution.py:90
  375.2 30.8 %collective-permute-start.31 = (bf16[512,640]{1,0:T(8,128)(2,1)S(1)}, bf16[512,640]{1,0:T(8,128)(2,1)S(1)}, u32[]{:S(2)}, u32[]{:S(2)}) collective-permute-start(bf16[512,640]{1,0:T(8,128)(2,1)S(1)} %add_convert_fusion.4), channel_id=1, source_target_pairs={{0,2},{2,0},{1,3},{3,1},{4,6},{6,4},{5,7},{7,5},{8,10},{10,8},{9,1... | collective-permute-start | bytes 1966088 | tf_op jit(solution)/shard_map/ppermute | solution.py:90
  377.5 63.4 %collective-permute-start.36 = (bf16[640,1664]{1,0:T(8,128)(2,1)}, bf16[640,1664]{1,0:T(8,128)(2,1)}, u32[]{:S(2)}, u32[]{:S(2)}) collective-permute-start(bf16[640,1664]{1,0:T(8,128)(2,1)} %get-tuple-element.201), channel_id=1, source_target_pairs={{0,4},{4,0},{8,12},{12,8},{16,20},{20,16},{24,28},{28,24},{1,5},{5... | collective-permute-start | bytes 6389768 | tf_op jit(solution)/shard_map/ppermute | solution.py:86
  403.0 38.0 %collective-permute-start.37 = (bf16[640,1664]{1,0:T(8,128)(2,1)}, bf16[640,1664]{1,0:T(8,128)(2,1)}, u32[]{:S(2)}, u32[]{:S(2)}) collective-permute-start(bf16[640,1664]{1,0:T(8,128)(2,1)} %get-tuple-element.203), channel_id=1, source_target_pairs={{0,4},{4,0},{8,12},{12,8},{16,20},{20,16},{24,28},{28,24},{1,5},{5... | collective-permute-start | bytes 6389768 | tf_op jit(solution)/shard_map/ppermute | solution.py:86
  408.5 23.7 %collective-permute-start.38 = (bf16[320,1664]{1,0:T(8,128)(2,1)}, bf16[320,1664]{1,0:T(8,128)(2,1)S(1)}, u32[]{:S(2)}, u32[]{:S(2)}) collective-permute-start(bf16[320,1664]{1,0:T(8,128)(2,1)} %get-tuple-element.212), channel_id=1, source_target_pairs={{0,8},{4,12},{8,0},{12,4},{16,24},{20,28},{24,16},{28,20},{1,9},{5... | collective-permute-start | bytes 3194888 | tf_op jit(solution)/shard_map/ppermute | solution.py:86
  409.6 23.1 %collective-permute-start.39 = (bf16[320,1664]{1,0:T(8,128)(2,1)S(1)}, bf16[320,1664]{1,0:T(8,128)(2,1)S(1)}, u32[]{:S(2)}, u32[]{:S(2)}) collective-permute-start(bf16[320,1664]{1,0:T(8,128)(2,1)S(1)} %get-tuple-element.213), channel_id=1, source_target_pairs={{0,16},{4,20},{8,24},{12,28},{16,0},{20,4},{24,8},{28,12},{1,17},{... | collective-permute-start | bytes 3194888 | tf_op jit(solution)/shard_map/ppermute | solution.py:86
  426.0 27.7 %collective-permute-start.35 = (bf16[512,640]{1,0:T(8,128)(2,1)}, bf16[512,640]{1,0:T(8,128)(2,1)}, u32[]{:S(2)}, u32[]{:S(2)}) collective-permute-start(bf16[512,640]{1,0:T(8,128)(2,1)} %get-tuple-element.585), channel_id=1, source_target_pairs={{0,2},{2,0},{1,3},{3,1},{4,6},{6,4},{5,7},{7,5},{8,10},{10,8},{9,1... | collective-permute-start | bytes 1966088 | tf_op jit(solution)/shard_map/ppermute | solution.py:90
  432.1 24.9 %collective-permute-start.34 = (bf16[512,640]{1,0:T(8,128)(2,1)}, bf16[512,640]{1,0:T(8,128)(2,1)}, u32[]{:S(2)}, u32[]{:S(2)}) collective-permute-start(bf16[512,640]{1,0:T(8,128)(2,1)} %get-tuple-element.585), channel_id=1, source_target_pairs={{0,1},{1,0},{2,3},{3,2},{4,5},{5,4},{6,7},{7,6},{8,9},{9,8},{10,11... | collective-permute-start | bytes 1966088 | tf_op jit(solution)/shard_map/ppermute | solution.py:90
  434.7 33.1 %collective-permute-start.40 = (bf16[512,640]{1,0:T(8,128)(2,1)}, bf16[512,640]{1,0:T(8,128)(2,1)S(1)}, u32[]{:S(2)}, u32[]{:S(2)}) collective-permute-start(bf16[512,640]{1,0:T(8,128)(2,1)} %get-tuple-element.585), channel_id=1, source_target_pairs={{1,2},{2,1},{5,6},{6,5},{9,10},{10,9},{13,14},{14,13},{17,18},{18,... | collective-permute-start | bytes 1966088 | tf_op jit(solution)/shard_map/ppermute | solution.py:90
  481.1 287.0 %reduce-scatter.8.cloned.1.call-start = ((), (), s32[]{:S(2)}) async-start(), calls=%async_computation.19 | async-start | bytes 2949120 | tf_op jit(solution)/shard_map/reduce_scatter | solution.py:372
  495.6 36.8 %collective-permute-start.43 = (bf16[320,1664]{1,0:T(8,128)(2,1)}, bf16[320,1664]{1,0:T(8,128)(2,1)S(1)}, u32[]{:S(2)}, u32[]{:S(2)}) collective-permute-start(bf16[320,1664]{1,0:T(8,128)(2,1)} %get-tuple-element.222), channel_id=1, source_target_pairs={{0,8},{4,12},{8,0},{12,4},{16,24},{20,28},{24,16},{28,20},{1,9},{5... | collective-permute-start | bytes 3194888 | tf_op jit(solution)/shard_map/ppermute | solution.py:86
  496.8 35.5 %collective-permute-start.44 = (bf16[320,1664]{1,0:T(8,128)(2,1)}, bf16[320,1664]{1,0:T(8,128)(2,1)S(1)}, u32[]{:S(2)}, u32[]{:S(2)}) collective-permute-start(bf16[320,1664]{1,0:T(8,128)(2,1)} %get-tuple-element.223), channel_id=1, source_target_pairs={{0,16},{4,20},{8,24},{12,28},{16,0},{20,4},{24,8},{28,12},{1,17},{... | collective-permute-start | bytes 3194888 | tf_op jit(solution)/shard_map/ppermute | solution.py:86
  499.9 59.7 %collective-permute-start.45 = (bf16[320,1664]{1,0:T(8,128)(2,1)}, bf16[320,1664]{1,0:T(8,128)(2,1)S(1)}, u32[]{:S(2)}, u32[]{:S(2)}) collective-permute-start(bf16[320,1664]{1,0:T(8,128)(2,1)} %get-tuple-element.226), channel_id=1, source_target_pairs={{0,8},{4,12},{8,0},{12,4},{16,24},{20,28},{24,16},{28,20},{1,9},{5... | collective-permute-start | bytes 3194888 | tf_op jit(solution)/shard_map/ppermute | solution.py:86
  500.8 58.8 %collective-permute-start.46 = (bf16[320,1664]{1,0:T(8,128)(2,1)}, bf16[320,1664]{1,0:T(8,128)(2,1)S(1)}, u32[]{:S(2)}, u32[]{:S(2)}) collective-permute-start(bf16[320,1664]{1,0:T(8,128)(2,1)} %get-tuple-element.227), channel_id=1, source_target_pairs={{0,16},{4,20},{8,24},{12,28},{16,0},{20,4},{24,8},{28,12},{1,17},{... | collective-permute-start | bytes 3194888 | tf_op jit(solution)/shard_map/ppermute | solution.py:86
  570.0 33.5 %collective-permute-start.49 = (bf16[512,256]{1,0:T(8,128)(2,1)}, bf16[512,256]{1,0:T(8,128)(2,1)}, u32[]{:S(2)}, u32[]{:S(2)}) collective-permute-start(bf16[512,256]{1,0:T(8,128)(2,1)} %copy.320), channel_id=1, source_target_pairs={{0,1},{3,2},{4,5},{7,6},{8,9},{11,10},{12,13},{15,14},{16,17},{19,... | collective-permute-start | bytes 786440 | tf_op jit(solution)/shard_map/ppermute | solution.py:90
  571.7 19.4 %collective-permute-start.53 = (bf16[160,1664]{1,0:T(8,128)(2,1)}, bf16[160,1664]{1,0:T(8,128)(2,1)}, u32[]{:S(2)}, u32[]{:S(2)}) collective-permute-start(bf16[160,1664]{1,0:T(8,128)(2,1)} %copy-done.60), channel_id=1, source_target_pairs={{0,8},{4,12},{8,0},{12,4},{16,24},{20,28},{24,16},{28,20},{1,9},{5... | collective-permute-start | bytes 1597448 | tf_op jit(solution)/shard_map/ppermute | solution.py:86
  571.9 26.5 %collective-permute-start.54 = (bf16[160,1664]{1,0:T(8,128)(2,1)}, bf16[160,1664]{1,0:T(8,128)(2,1)}, u32[]{:S(2)}, u32[]{:S(2)}) collective-permute-start(bf16[160,1664]{1,0:T(8,128)(2,1)} %copy-done.59), channel_id=1, source_target_pairs={{0,16},{4,20},{8,24},{12,28},{16,0},{20,4},{24,8},{28,12},{1,17},{... | collective-permute-start | bytes 1597448 | tf_op jit(solution)/shard_map/ppermute | solution.py:86
  573.1 26.9 %collective-permute-start.55 = (bf16[160,1664]{1,0:T(8,128)(2,1)}, bf16[160,1664]{1,0:T(8,128)(2,1)}, u32[]{:S(2)}, u32[]{:S(2)}) collective-permute-start(bf16[160,1664]{1,0:T(8,128)(2,1)} %copy-done.56), channel_id=1, source_target_pairs={{0,8},{4,12},{8,0},{12,4},{16,24},{20,28},{24,16},{28,20},{1,9},{5... | collective-permute-start | bytes 1597448 | tf_op jit(solution)/shard_map/ppermute | solution.py:86
  584.8 35.1 %collective-permute-start.57 = (f32[34,512]{0,1:T(8,128)}, f32[34,512]{0,1:T(8,128)}, u32[]{:S(2)}, u32[]{:S(2)}) collective-permute-start(f32[34,512]{0,1:T(8,128)} %copy.288), channel_id=1, source_target_pairs={{0,1},{1,2},{2,3},{3,0},{4,5},{5,6},{6,7},{7,4},{8,9},{9,10},{10,1... | collective-permute-start | bytes 208904 | tf_op jit(solution)/shard_map/ppermute | solution.py:81
  591.1 28.8 %collective-permute-start.58 = (f32[34,512]{0,1:T(8,128)}, f32[34,512]{0,1:T(8,128)}, u32[]{:S(2)}, u32[]{:S(2)}) collective-permute-start(f32[34,512]{0,1:T(8,128)} %copy.288), channel_id=1, source_target_pairs={{0,2},{1,3},{2,0},{3,1},{4,6},{5,7},{6,4},{7,5},{8,10},{9,11},{10,... | collective-permute-start | bytes 208904 | tf_op jit(solution)/shard_map/ppermute | solution.py:81
  598.4 24.0 %collective-permute-start.59 = (f32[34,512]{0,1:T(8,128)}, f32[34,512]{0,1:T(8,128)S(1)}, u32[]{:S(2)}, u32[]{:S(2)}) collective-permute-start(f32[34,512]{0,1:T(8,128)} %copy.288), channel_id=1, source_target_pairs={{0,3},{1,0},{2,1},{3,2},{4,7},{5,4},{6,5},{7,6},{8,11},{9,8},{10,9... | collective-permute-start | bytes 208904 | tf_op jit(solution)/shard_map/ppermute | solution.py:81
  622.4 55.9 %all-to-all-start.2 = ((bf16[8,9,64,320]{3,2,1,0:T(8,128)(2,1)}), bf16[8,9,64,320]{3,2,1,0:T(8,128)(2,1)}, u32[]{:S(2)}, u32[]{:S(2)}) async-start(bf16[8,9,64,320]{3,2,1,0:T(8,128)(2,1)} %get-tuple-element.255), calls=%async_computation.3 | async-start | bytes 7077888 | tf_op jit(solution)/shard_map/all_to_all | solution.py:1069
  647.8 40.5 %collective-permute-start.62 = (bf16[512,640]{1,0:T(8,128)(2,1)}, bf16[512,640]{1,0:T(8,128)(2,1)}, u32[]{:S(2)}, u32[]{:S(2)}) collective-permute-start(bf16[512,640]{1,0:T(8,128)(2,1)} %get-tuple-element.598), channel_id=1, source_target_pairs={{0,1},{3,2},{4,5},{7,6},{8,9},{11,10},{12,13},{15,14},{16,17},{19,... | collective-permute-start | bytes 1966088 | tf_op jit(solution)/shard_map/ppermute | solution.py:90
  649.5 38.8 %collective-permute-start.64 = (f32[512]{0:T(512)S(1)}, f32[512]{0:T(512)S(1)}, u32[]{:S(2)}, u32[]{:S(2)}) collective-permute-start(f32[512]{0:T(512)S(1)} %multiply_add_fusion.5), channel_id=1, source_target_pairs={{0,1},{1,2},{2,3},{3,0},{4,5},{5,6},{6,7},{7,4},{8,9},{9,10},{10,1... | collective-permute-start | bytes 6152 | tf_op jit(solution)/shard_map/ppermute | solution.py:81
  649.9 38.4 %collective-permute-start.65 = (f32[512]{0:T(512)S(1)}, f32[512]{0:T(512)S(1)}, u32[]{:S(2)}, u32[]{:S(2)}) collective-permute-start(f32[512]{0:T(512)S(1)} %multiply_add_fusion.5), channel_id=1, source_target_pairs={{0,2},{1,3},{2,0},{3,1},{4,6},{5,7},{6,4},{7,5},{8,10},{9,11},{10,... | collective-permute-start | bytes 6152 | tf_op jit(solution)/shard_map/ppermute | solution.py:81
  654.5 33.7 %collective-permute-start.66 = (f32[512]{0:T(512)S(1)}, f32[512]{0:T(512)S(1)}, u32[]{:S(2)}, u32[]{:S(2)}) collective-permute-start(f32[512]{0:T(512)S(1)} %multiply_add_fusion.5), channel_id=1, source_target_pairs={{0,3},{1,0},{2,1},{3,2},{4,7},{5,4},{6,5},{7,6},{8,11},{9,8},{10,9... | collective-permute-start | bytes 6152 | tf_op jit(solution)/shard_map/ppermute | solution.py:81
  678.4 66.2 %all-to-all-start.3 = ((bf16[8,8,64,320]{3,2,1,0:T(8,128)(2,1)}), bf16[8,8,64,320]{3,2,1,0:T(8,128)(2,1)}, u32[]{:S(2)}, u32[]{:S(2)}) async-start(bf16[8,8,64,320]{3,2,1,0:T(8,128)(2,1)} %get-tuple-element.267), calls=%async_computation.6 | async-start | bytes 6291456 | tf_op jit(solution)/shard_map/all_to_all | solution.py:1069
  684.3 83.8 %reduce-scatter.6.cloned.1.call-start = ((), (), s32[]{:S(2)}) async-start(), calls=%async_computation.18 | async-start | bytes 2211840 | tf_op jit(solution)/shard_map/reduce_scatter | solution.py:372
  691.8 31.0 %collective-permute-start.63 = (bf16[512,640]{1,0:T(8,128)(2,1)S(1)}, bf16[512,640]{1,0:T(8,128)(2,1)S(1)}, u32[]{:S(2)}, u32[]{:S(2)}) collective-permute-start(bf16[512,640]{1,0:T(8,128)(2,1)S(1)} %add_convert_fusion.1), channel_id=1, source_target_pairs={{0,2},{2,0},{1,3},{3,1},{4,6},{6,4},{5,7},{7,5},{8,10},{10,8},{9,1... | collective-permute-start | bytes 1966088 | tf_op jit(solution)/shard_map/ppermute | solution.py:90
  768.2 44.9 %all-to-all-start.4 = ((bf16[8,8,64,320]{3,2,1,0:T(8,128)(2,1)}), bf16[8,8,64,320]{3,2,1,0:T(8,128)(2,1)}, u32[]{:S(2)}, u32[]{:S(2)}) async-start(bf16[8,8,64,320]{3,2,1,0:T(8,128)(2,1)} %copy-done.32), calls=%async_computation.7 | async-start | bytes 6291456 | tf_op jit(solution)/shard_map/all_to_all | solution.py:1128
  776.9 45.5 %collective-permute-start.20 = (bf16[512,640]{1,0:T(8,128)(2,1)}, bf16[512,640]{1,0:T(8,128)(2,1)}, u32[]{:S(2)}, u32[]{:S(2)}) collective-permute-start(bf16[512,640]{1,0:T(8,128)(2,1)} %get-tuple-element.596), channel_id=1, source_target_pairs={{1,2},{2,1},{5,6},{6,5},{9,10},{10,9},{13,14},{14,13},{17,18},{18,... | collective-permute-start | bytes 1966088 | tf_op jit(solution)/shard_map/ppermute | solution.py:90
  779.6 42.8 %collective-permute-start.21 = (bf16[512,640]{1,0:T(8,128)(2,1)}, bf16[512,640]{1,0:T(8,128)(2,1)}, u32[]{:S(2)}, u32[]{:S(2)}) collective-permute-start(bf16[512,640]{1,0:T(8,128)(2,1)} %get-tuple-element.595), channel_id=1, source_target_pairs={{0,1},{1,0},{2,3},{3,2},{4,5},{5,4},{6,7},{7,6},{8,9},{9,8},{10,11... | collective-permute-start | bytes 1966088 | tf_op jit(solution)/shard_map/ppermute | solution.py:90
  784.2 38.3 %collective-permute-start.42 = (bf16[512,640]{1,0:T(8,128)(2,1)}, bf16[512,640]{1,0:T(8,128)(2,1)}, u32[]{:S(2)}, u32[]{:S(2)}) collective-permute-start(bf16[512,640]{1,0:T(8,128)(2,1)} %add_convert_fusion.3), channel_id=1, source_target_pairs={{0,2},{2,0},{1,3},{3,1},{4,6},{6,4},{5,7},{7,5},{8,10},{10,8},{9,1... | collective-permute-start | bytes 1966088 | tf_op jit(solution)/shard_map/ppermute | solution.py:90
  785.9 51.3 %collective-permute-start.60 = (bf16[512,640]{1,0:T(8,128)(2,1)}, bf16[512,640]{1,0:T(8,128)(2,1)}, u32[]{:S(2)}, u32[]{:S(2)}) collective-permute-start(bf16[512,640]{1,0:T(8,128)(2,1)} %get-tuple-element.598), channel_id=1, source_target_pairs={{1,2},{2,1},{5,6},{6,5},{9,10},{10,9},{13,14},{14,13},{17,18},{18,... | collective-permute-start | bytes 1966088 | tf_op jit(solution)/shard_map/ppermute | solution.py:90
  788.1 37.1 %collective-permute-start.61 = (bf16[512,640]{1,0:T(8,128)(2,1)}, bf16[512,640]{1,0:T(8,128)(2,1)}, u32[]{:S(2)}, u32[]{:S(2)}) collective-permute-start(bf16[512,640]{1,0:T(8,128)(2,1)} %get-tuple-element.597), channel_id=1, source_target_pairs={{0,1},{1,0},{2,3},{3,2},{4,5},{5,4},{6,7},{7,6},{8,9},{9,8},{10,11... | collective-permute-start | bytes 1966088 | tf_op jit(solution)/shard_map/ppermute | solution.py:90
  816.3 31.2 %all-to-all-start.5 = ((bf16[8,4,64,448]{3,2,1,0:T(8,128)(2,1)}), bf16[8,4,64,448]{3,2,1,0:T(8,128)(2,1)}, u32[]{:S(2)}, u32[]{:S(2)}) async-start(bf16[8,4,64,448]{3,2,1,0:T(8,128)(2,1)} %fusion.15), calls=%async_computation.8 | async-start | bytes 4194304 | tf_op jit(solution)/shard_map/all_to_all | solution.py:792
  849.1 22.6 %all-to-all-start.6 = ((bf16[8,133,640]{2,1,0:T(8,128)(2,1)}), bf16[8,133,640]{2,1,0:T(8,128)(2,1)S(1)}, u32[]{:S(2)}, u32[]{:S(2)}) async-start(bf16[8,133,640]{2,1,0:T(8,128)(2,1)} %pad_maximum_fusion.1), calls=%async_computation.9 | async-start | bytes 2785280 | tf_op jit(solution)/shard_map/all_to_all | solution.py:1174
  871.8 46.6 %all-to-all-start.8 = ((bf16[8,9,64,320]{3,2,1,0:T(8,128)(2,1)}), bf16[8,9,64,320]{3,2,1,0:T(8,128)(2,1)}, u32[]{:S(2)}, u32[]{:S(2)}) async-start(bf16[8,9,64,320]{3,2,1,0:T(8,128)(2,1)} %copy-done.31), calls=%async_computation.11 | async-start | bytes 7077888 | tf_op jit(solution)/shard_map/all_to_all | solution.py:1112
  918.4 30.4 %all-to-all-start.7 = ((bf16[8,4,64,448]{3,2,1,0:T(8,128)(2,1)}), bf16[8,4,64,448]{3,2,1,0:T(8,128)(2,1)S(1)}, u32[]{:S(2)}, u32[]{:S(2)}) async-start(bf16[8,4,64,448]{3,2,1,0:T(8,128)(2,1)} %fusion.17), calls=%async_computation.10 | async-start | bytes 4194304 | tf_op jit(solution)/shard_map/all_to_all | solution.py:792
  (187 other events, 2545.5 us)
Sparse Core Ops, SparseCore 0:
  10.6 30.9 all-gather.17
  44.0 26.1 all-gather.7
  72.0 32.8 all-gather.9
  106.7 54.9 all-gather.15
  163.4 79.4 all-gather.13
  244.6 54.9 all-gather.11
  481.2 68.0 reduce-scatter.3
  622.5 64.9 reduce-scatter.7
  691.5 45.6 reduce-scatter.5

commit v4 on v3

--- a/solution.py
+++ b/solution.py
@@ -976,13 +976,14 @@
     relayed, up_grad = tie(relayed, up_grad)
     second = along_line(relayed, pairs_second)
     up_sum = Scatter(chunk_products(normed_two, up_grad))
-    second, up_sum.parts = tie(second, up_sum.parts)
+    second, up_sum.parts, gate_sending = tie(second, up_sum.parts, gate_sum.outgoing())
+    gate_sum.send(gate_sending)
     normed_two_grad = reduce_end(normed_two_part, (inner, near, second))
     post_gain_grad = jnp.sum(normed_two_grad * middle * inv_second, axis=0)
     direct_grad = grad_top + inv_second * norm_gains[1] * normed_two_grad
     direct_all, sendings = gather_features(
         direct_grad.astype(bf16),
-        (gate_sum.outgoing(), up_sum.outgoing(), down_sum.outgoing()),
+        (up_sum.outgoing(), down_sum.outgoing()),
     )
     direct_all = direct_all.astype(f32)
     top_all = token_grad_all.astype(f32)
@@ -993,10 +994,11 @@
         * (direct_all - middle_all * (inv_second**2 * second_dot / D))
     ).astype(bf16)
     middle_grad = direct_grad - middle * (inv_second**2 * second_dot / D)
-    for weight_sum, sending in zip((gate_sum, up_sum, down_sum), sendings):
+    for weight_sum, sending in zip((up_sum, down_sum), sendings):
         weight_sum.send(sending)
     o_full = weight_product(attn_grad, heads_out)
-    attn_grad, o_full = tie(attn_grad, o_full)
+    attn_grad, o_full, gate_sending = tie(attn_grad, o_full, gate_sum.outgoing())
+    gate_sum.send(gate_sending)
     block_o = scatter_rows(o_full)
     mlp_passed, attn_grad = tie(mlp_passed, attn_grad)
     mlp_second = along_line(reduce_relay(mlp_part, mlp_passed), pairs_second)
@@ -1006,13 +1008,8 @@
         q_pre, kv_pre, rotary, tables, bias, heads_grad
     )
     mlp_arrived = (mlp_inner, mlp_near, mlp_second)
-    head_sums, q_pre_grad, gate_sending, up_sending = tie(
-        head_sums, q_pre_grad, gate_sum.outgoing(), up_sum.outgoing()
-    )
-    gate_sum.send(gate_sending)
+    head_sums, q_pre_grad, up_sending = tie(head_sums, q_pre_grad, up_sum.outgoing())
     up_sum.send(up_sending)
-    mlp_out = reduce_end(mlp_part, mlp_arrived)
-    layer_out = middle + residual_scale * live_rows * mlp_out
     rot_partial = rotate(
         head_sums[2, :, NOPE : NOPE + ROPE], cosine_table, sine_table, -1.0
     )
@@ -1085,11 +1082,9 @@
     kv_latent_grad = (
         inv_kv * kv_gain * kv_normed_grad - kv_latent * inv_kv**2 * kv_dot / KVR
     ).astype(bf16)
-    share = (narrow_index == 0).astype(f32)
-    first_dot = row_parts(
-        jnp.sum(q_latent_grad.astype(f32) * q_latent, axis=1)
-        + jnp.sum(kv_latent_grad.astype(f32) * kv_latent, axis=1)
-        + share * jnp.sum(rot_grad.astype(f32) * key_rot, axis=1)
+    first_dot = (
+        norm_eps * (inv_q**2 * q_dot + inv_kv**2 * kv_dot)
+        + jnp.sum(rot_grad.astype(f32) * key_rot, axis=1, keepdims=True)
     )
     latent_grad = jnp.concatenate([q_latent_grad, kv_latent_grad, rot_grad], axis=1)
     full_kr = full_latent[:, q_width + kv_width :]
@@ -1100,16 +1095,12 @@
     normed_passed, normed_inner, normed_near = reduce_start(normed_part)
     latent_full = weight_product(normed, latent_grad)
     normed_passed, latent_full = tie(normed_passed, latent_full)
-    latent_late, first_owned, first_dot = tie(latent_full, main_owned[0], first_dot)
-    first_dot = sum(first_dot)[:, None]
+    latent_late, first_owned = tie(latent_full, main_owned[0])
     block_latent = scatter_rows(latent_late)
     normed_second = along_line(reduce_relay(normed_part, normed_passed), pairs_second)
-    normed_second, first_owned = tie(normed_second, first_owned)
-    change_one, mid_mom_a, mid_sq_a = slot_group(
-        main_scales, first_owned, basis_la, basis_ra, mom_a, sq_a, groups[0], None
-    )
-    change_one, last_owned = tie(change_one, main_owned[1])
-    back_one = lax.all_to_all(change_one, "wide", split_axis=0, concat_axis=0, tiled=True)
+    normed_second, first_owned, mlp_arrived = tie(normed_second, first_owned, mlp_arrived)
+    mlp_out = reduce_end(mlp_part, mlp_arrived)
+    layer_out = middle + residual_scale * live_rows * mlp_out
     normed_grad = reduce_end(normed_part, (normed_inner, normed_near, normed_second)) + (
         against_rows(rot_grad, own_kr)
     )
@@ -1119,13 +1110,36 @@
         + inv_first * norm_gains[0] * normed_grad
         - residual * inv_first**2 * first_dot / D
     )
+    gain_part = jnp.concatenate([in_gain_grad, post_gain_grad, q_gain_grad, kv_gain_grad])
+    gain_high = lax.optimization_barrier(gain_part.astype(bf16))
+    gain_low = (gain_part - gain_high.astype(f32)).astype(bf16)
+    gain_rows = jnp.concatenate([gain_high, gain_low])
+    gain_height = -(-gain_rows.shape[0] // local_width)
+    gain_rows = jnp.pad(gain_rows, (0, gain_height * local_width - gain_rows.shape[0]))
+    gain_rows = jnp.broadcast_to(
+        gain_rows.reshape(1, gain_height, local_width), (wide_count, gain_height, local_width)
+    )
+    leaving = jnp.concatenate(
+        [
+            layer_out.astype(bf16).reshape(wide_count, piece_rows, local_width),
+            input_grad.astype(bf16).reshape(wide_count, piece_rows, local_width),
+            gain_rows,
+        ],
+        axis=1,
+    )
+    leaving, first_owned, last_owned = tie(leaving, first_owned, main_owned[1])
+    returned_rows = lax.all_to_all(leaving, "wide", split_axis=0, concat_axis=0, tiled=True)
+    change_one, mid_mom_a, mid_sq_a = slot_group(
+        main_scales, first_owned, basis_la, basis_ra, mom_a, sq_a, groups[0], None
+    )
+    change_one, last_owned, returned_rows = tie(change_one, last_owned, returned_rows)
+    back_one = lax.all_to_all(change_one, "wide", split_axis=0, concat_axis=0, tiled=True)
 
     change_two, mid_mom_a, mid_sq_a = slot_group(
         main_scales, last_owned, basis_la, basis_ra, mom_a, sq_a, groups[1],
         (mid_mom_a, mid_sq_a),
     )
     block_latent, block_heads, change_two = tie(block_latent, block_heads, change_two)
-    back_two = lax.all_to_all(change_two, "wide", split_axis=0, concat_axis=0, tiled=True)
     block_qb = block_heads[: w_qb.shape[0]].reshape(w_qb.shape[0], heads_here, 128)
     block_qb = block_qb[:, :, : NOPE + ROPE].reshape(w_qb.shape)
     block_kvb = block_heads[w_qb.shape[0] :]
@@ -1150,28 +1164,11 @@
             ([block_kvb], c_send),
         )
     ]
-    sent_parts, back_two = tie(sent_parts, back_two)
+    sent_parts, back_one = tie(sent_parts, back_one)
     late_owned, owned_b, owned_c = trade_joined(sent_parts, wide_count)
-
-    gain_part = jnp.concatenate([in_gain_grad, post_gain_grad, q_gain_grad, kv_gain_grad])
-    gain_high = lax.optimization_barrier(gain_part.astype(bf16))
-    gain_low = (gain_part - gain_high.astype(f32)).astype(bf16)
-    gain_rows = jnp.concatenate([gain_high, gain_low])
-    gain_height = -(-gain_rows.shape[0] // local_width)
-    gain_rows = jnp.pad(gain_rows, (0, gain_height * local_width - gain_rows.shape[0]))
-    gain_rows = jnp.broadcast_to(
-        gain_rows.reshape(1, gain_height, local_width), (wide_count, gain_height, local_width)
-    )
-    leaving = jnp.concatenate(
-        [
-            layer_out.astype(bf16).reshape(wide_count, piece_rows, local_width),
-            input_grad.astype(bf16).reshape(wide_count, piece_rows, local_width),
-            gain_rows,
-        ],
-        axis=1,
-    )
-    leaving, late_owned = tie(leaving, late_owned)
-    returned_rows = lax.all_to_all(leaving, "wide", split_axis=0, concat_axis=0, tiled=True)
+    change_two, late_owned, owned_b, owned_c = tie(change_two, late_owned, owned_b, owned_c)
+    back_two = lax.all_to_all(change_two, "wide", split_axis=0, concat_axis=0, tiled=True)
+
     placed = jnp.take(returned_rows[:, : 2 * piece_rows], deal_row, axis=0, mode="clip")
     final_out = placed[:, :piece_rows].astype(f32).reshape(row_count, local_width)
     final_grad = placed[:, piece_rows:].astype(f32).reshape(row_count, local_width)
@@ -1196,7 +1193,7 @@
                     wide_index, tcount),
         owned_c, basis_lc, basis_rc, mom_c, sq_c,
     )
-    late_change, final_grad = tie(late_change, final_grad)
+    late_change, back_two = tie(late_change, back_two)
     returned = trade_joined(
         [change.reshape((-1,) + change.shape[2:]) for change in (late_change, change_b, change_c)],
         wide_count,

time: 985 us -> 963 us (0.978)
  starting transfers between devices: 175 us -> 164 us
    all_to_all x2, waiting for transfers between devices: 5.73 us -> 23.1 us  [trade_joined(): lax.all_to_all(joined, 'wide', split_axis=0, concat_axis=0, tiled=True)]
    reduce_scatter x3, waiting for transfers between devices: 0.01 us -> 14.3 us  [scatter_rows(): return lax.psum_scatter(partial, 'wide', scatter_dimension=0, tiled=True)]
    ppermute x18, waiting for transfers between devices: 39.3 us -> 27.3 us  [flipped(): return lax.ppermute(value, 'wide', [(i, i ^ bit) for i in range(count)])]
    all_to_all x1, waiting for transfers between devices: 11.1 us -> 0.01 us  [body(): lax.all_to_all(leaving, 'wide', split_axis=0, concat_axis=0, tiled=True)]
    unnamed x345 -> x333, local copies, waits for them, and re-layouts: 39.2 us -> 39.6 us
  transfers between devices with their start and end apart: 85 -> 82, of which waited for: 40 -> 35; matrix products, arithmetic and copies ran while one was open for 24% -> 23% of each run, Pallas kernels for 15% -> 15%
where the time goes in v4:
time: 963 us; the launch traced here: 952 us
  waiting for transfers between devices  301 us (31%)
  starting transfers between devices  164 us (17%)
  Pallas kernels  164 us (17%)
  local copies, waits for them, and re-layouts  109 us (11%)
  other arithmetic  92.9 us (10%)
  matrix products  87.1 us (9%)
  between operations  18.5 us (2%)
  blocking collectives  15.1 us (2%)
    ppermute x40, waiting for transfers between devices, along_line(): return lax.ppermute(value, 'narrow', pairs)  191 us
    ppermute x40, starting transfers between devices, along_line(): return lax.ppermute(value, 'narrow', pairs)  84.2 us
    pallas_call x5, Pallas kernels, slot_call(): pl.pallas_call(kernel, grid_spec=pltpu.PrefetchScalarGridSpec(num_scalar_...  56.3 us
    dot_general x7, matrix products, product(): return jnp.dot(left_side, right_side, preferred_element_type=jnp.float32)  44.4 us
    dot_general x8, matrix products, against_rows(): lax.dot_general(left_side, right_side, (((1,), (1,)), ((), ())), preferre...  41 us
    unnamed x333, local copies, waits for them, and re-layouts  39.6 us
    pallas_call x3, Pallas kernels, chunk_products(): pl.pallas_call(chunk_kernel, grid_spec=pltpu.PrefetchScalarGridSpec(num_s...  27.3 us
    ppermute x18, waiting for transfers between devices, flipped(): return lax.ppermute(value, 'wide', [(i, i ^ bit) for i in range(count)])  27.3 us
  transfers between devices with their start and end apart: 82, of which 35 were waited for; matrix products, arithmetic and copies ran while one was open for 23% of the time, Pallas kernels for 15%

profile of v4, /device:TPU:11, one launch (start us, length us, event | category | flops | bytes accessed | tf_op | source)
XLA Modules:
  0.0 951.6 jit_solution(6248496196532437245)
XLA Ops:
  19.9 5.5 all-to-all-start
  27.4 9.2 all-to-all-done
  40.2 15.1 %all_gather.23 = bf16[256,1280]{1,0:T(8,128)(2,1)} all-gather(bf16[32,1280]{1,0:T(8,128)(2,1)S(1)} %copy-done.104), channel_id=1, replica_groups=mesh['wide'=8,'narrow'=4] {'wide'}, dimensions={0}, use_global_device_ids=true | all-gather | bytes 737280 | tf_op jit(solution)/shard_map/all_gather | solution.py:882
  64.7 4.7 collective-permute-start.2
  78.2 6.0 collective-permute-done.2
  97.9 4.9 collective-permute-done.8
  102.9 5.9 collective-permute-start.10
  114.4 3.8 collective-permute-start.22
  126.3 11.0 %shard_map.741.right_ref = bf16[512,640]{1,0:T(8,128)(2,1)S(1)} custom-call(f32[512,1280]{1,0:T(8,128)S(1)} %fusion.97.query_ref, f32[512,1280]{1,0:T(8,128)} %fusion.98.key_value_ref, bf16[512,128]{1,0:T(8,128)(2,1)S(1)} %pad.45.rotary_ref, f32[3,512,128]{2,1,0:T(8,128)S(1)} %pad_maximum_fusion.3.table_ref, f32[512,512]{1,0:T(8,128)S(1)} %copy-done.15), custom_call_target="tpu_custom_call" | custom-call | tf_op jit(solution)/shard_map/pallas_call | solution.py:704
  141.6 6.2 collective-permute-start.23
  149.8 4.4 convolution_convert_fusion.1
  162.8 4.1 gather_fusion.1
  166.9 5.6 all-to-all-start.1
  178.5 11.4 %collective-permute-done.13 = bf16[512,640]{1,0:T(8,128)(2,1)S(1)} collective-permute-done((bf16[512,640]{1,0:T(8,128)(2,1)}, bf16[512,640]{1,0:T(8,128)(2,1)S(1)}, u32[]{:S(2)}, u32[]{:S(2)}) %collective-permute-start.13) | collective-permute-done | bytes 655392 | tf_op jit(solution)/shard_map/ppermute | solution.py:90
  189.9 26.0 %collective-permute-done.15 = bf16[512,640]{1,0:T(8,128)(2,1)S(1)} collective-permute-done((bf16[512,640]{1,0:T(8,128)(2,1)S(1)}, bf16[512,640]{1,0:T(8,128)(2,1)S(1)}, u32[]{:S(2)}, u32[]{:S(2)}) %collective-permute-start.15) | collective-permute-done | bytes 655392 | tf_op jit(solution)/shard_map/ppermute | solution.py:90
  228.3 24.0 %collective-permute-done.17 = bf16[512,640]{1,0:T(8,128)(2,1)S(1)} collective-permute-done((bf16[512,640]{1,0:T(8,128)(2,1)}, bf16[512,640]{1,0:T(8,128)(2,1)S(1)}, u32[]{:S(2)}, u32[]{:S(2)}) %collective-permute-start.17) | collective-permute-done | bytes 655392 | tf_op jit(solution)/shard_map/ppermute | solution.py:90
  252.3 4.5 collective-permute-start.19
  256.8 3.8 fusion.3.left_ref
  263.5 3.8 collective-permute-done.18
  273.2 4.0 fusion.8.left_ref
  277.2 11.0 %fusion.100 = f32[512,1600]{1,0:T(8,128)} fusion(bf16[512,2560]{1,0:T(8,128)(2,1)} %fusion.3.left_ref, bf16[2560,1600]{1,0:T(8,128)(2,1)} %all-gather.16.cloned.1.call-done), kind=kOutput, calls=%fused_computation.322 | convolution fusion | flops 4194304000 | bytes 14090240 | tf_op jit(solution)/shard_map/dot_general | solution.py:32
  288.2 10.9 %fusion.99 = f32[512,1600]{1,0:T(8,128)} fusion(bf16[512,2560]{1,0:T(8,128)(2,1)} %fusion.8.left_ref, bf16[2560,1600]{1,0:T(8,128)(2,1)} %all-gather.14.cloned.1.call-done), kind=kOutput, calls=%fused_computation.321 | convolution fusion | flops 4194304000 | bytes 14090240 | tf_op jit(solution)/shard_map/dot_general | solution.py:32
  299.3 12.2 %multiply_convert_fusion = (bf16[512,1600]{1,0:T(8,128)(2,1)S(1)}, bf16[512,1600]{1,0:T(8,128)(2,1)S(1)}, bf16[512,1600]{1,0:T(8,128)(2,1)S(1)}) fusion(f32[512,1600]{1,0:T(8,128)} %fusion.100, f32[512,1600]{1,0:T(8,128)} %fusion.99, bf16[512,2560]{1,0:T(8,128)(2,1)} %fusion.8.left_ref, bf16[2560,1600]{1,0:T(8,128)(2,1)} %all-gather.12.cloned.1.call-done), kind=kOutput, calls=%fused_computation.37 | convolution fusion | flops 4205772800 | bytes 22282240 | tf_op jit(solution)/shard_map/dot_general | solution.py:32
  311.6 9.1 shard_map.742
  324.0 10.1 %fusion.101 = f32[512,2560]{1,0:T(8,128)} fusion(bf16[512,1600]{1,0:T(8,128)(2,1)S(1)} %get-tuple-element.184.right_ref, bf16[2560,1600]{1,0:T(8,128)(2,1)} %all-gather.12.cloned.1.call-done), kind=kOutput, calls=%fused_computation.323 | convolution fusion | flops 4194304000 | bytes 15073280 | tf_op jit(solution)/shard_map/dot_general | solution.py:42
  334.1 9.4 add_convert_fusion
  346.5 9.1 shard_map.743
  364.7 9.1 shard_map.745
  378.4 28.0 %collective-permute-done.29 = bf16[512,640]{1,0:T(8,128)(2,1)S(1)} collective-permute-done((bf16[512,640]{1,0:T(8,128)(2,1)}, bf16[512,640]{1,0:T(8,128)(2,1)S(1)}, u32[]{:S(2)}, u32[]{:S(2)}) %collective-permute-start.29) | collective-permute-done | bytes 655392 | tf_op jit(solution)/shard_map/ppermute | solution.py:90
  430.6 4.7 collective-permute-done.36.refs_2_
  446.0 8.9 collective-permute-done.35
  454.9 6.0 collective-permute-start.39
  465.4 6.5 collective-permute-done.38
  476.0 3.8 fusion.9
  482.7 4.1 shard_map.749
  488.4 9.0 convolution_convert_fusion.2
  505.1 7.4 collective-permute-done.47.refs_3_
  516.6 4.2 convolution_convert_fusion.6.grad_ref
  520.9 15.6 %shard_map.751 = (bf16[512,1280]{1,0:T(8,128)(2,1)S(1)}, bf16[512,1280]{1,0:T(8,128)(2,1)S(1)}, f32[3,512,128]{2,1,0:T(8,128)S(1)}) custom-call(f32[512,1280]{1,0:T(8,128)} %copy-done.2, f32[512,1280]{1,0:T(8,128)} %fusion.98.key_value_ref, bf16[512,128]{1,0:T(8,128)(2,1)S(1)} %pad.45.rotary_ref, f32[3,512,128]{2,1,0:T(8,128)S(1)} %pad_maximum_fusion.3.table_ref, ...), custom_call_target="tpu_custom_call" | custom-call | tf_op jit(solution)/shard_map/pallas_call | solution.py:717
  538.6 10.8 %collective-permute-done.42.refs_2_ = bf16[320,1664]{1,0:T(8,128)(2,1)S(1)} collective-permute-done((bf16[320,1664]{1,0:T(8,128)(2,1)S(1)}, bf16[320,1664]{1,0:T(8,128)(2,1)S(1)}, u32[]{:S(2)}, u32[]{:S(2)}) %collective-permute-start.42) | collective-permute-done | bytes 1064992 | tf_op jit(solution)/shard_map/ppermute | solution.py:86
  571.8 5.6 collective-permute-start.55
  591.1 10.2 %shard_map.756 = (bf16[8,9,64,320]{3,2,1,0:T(8,128)(2,1)}, bf16[8,8,64,320]{3,2,1,0:T(8,128)(2,1)}) custom-call(s32[136]{0:T(256)} %broadcast_minimum_fusion.send_ref, bf16[320,640]{1,0:T(8,128)(2,1)} %reduce-scatter.4.cloned.1.call-done.refs_0_, f32[320,1600]{1,0:T(8,128)} %shard_map.754.refs_1_, f32[320,1600]{1,0:T(8,128)} %shard_map.755.refs_2_, ...), custom_call_target="tpu_custom_call" | custom-call | tf_op jit(solution)/shard_map/pallas_call | solution.py:401
  601.3 4.3 collective-permute-done.53
  606.3 10.3 %all-to-all-start.2 = ((bf16[8,9,64,320]{3,2,1,0:T(8,128)(2,1)}), bf16[8,9,64,320]{3,2,1,0:T(8,128)(2,1)}, u32[]{:S(2)}, u32[]{:S(2)}) async-start(bf16[8,9,64,320]{3,2,1,0:T(8,128)(2,1)} %get-tuple-element.259), calls=%async_computation.3 | async-start | bytes 7077888 | tf_op jit(solution)/shard_map/all_to_all | solution.py:1066
  617.7 3.9 collective-permute-start.44
  625.4 4.6 collective-permute-done.45
  642.3 22.0 %all-to-all-done.2.gradient_ref = bf16[8,9,64,320]{3,2,1,0:T(8,128)(2,1)} async-done(((bf16[8,9,64,320]{3,2,1,0:T(8,128)(2,1)}), bf16[8,9,64,320]{3,2,1,0:T(8,128)(2,1)}, u32[]{:S(2)}, u32[]{:S(2)}) %all-to-all-start.2) | async-done | bytes 2949152 | tf_op jit(solution)/shard_map/all_to_all | solution.py:1066
  664.3 6.0 all-to-all-start.3
  682.6 25.7 %collective-permute-done.58 = bf16[512,640]{1,0:T(8,128)(2,1)S(1)} collective-permute-done((bf16[512,640]{1,0:T(8,128)(2,1)S(1)}, bf16[512,640]{1,0:T(8,128)(2,1)S(1)}, u32[]{:S(2)}, u32[]{:S(2)}) %collective-permute-start.58) | collective-permute-done | bytes 655392 | tf_op jit(solution)/shard_map/ppermute | solution.py:90
  708.3 15.1 %collective-permute-done.62 = bf16[512,640]{1,0:T(8,128)(2,1)S(1)} collective-permute-done((bf16[512,640]{1,0:T(8,128)(2,1)}, bf16[512,640]{1,0:T(8,128)(2,1)S(1)}, u32[]{:S(2)}, u32[]{:S(2)}) %collective-permute-start.62) | collective-permute-done | bytes 655392 | tf_op jit(solution)/shard_map/ppermute | solution.py:90
  724.2 4.7 fusion.23
  732.4 5.5 all-to-all-start.4
  739.0 23.5 %shard_map.758 = (bf16[8,9,64,320]{3,2,1,0:T(8,128)(2,1)S(1)}, f32[17,64,2560]{2,1,0:T(8,128)}, f32[17,64,2560]{2,1,0:T(8,128)}) custom-call(s32[18]{0:T(128)S(1)} %copy-done.50, f32[20]{0:T(128)S(1)} %pad_maximum_fusion.8.scale_ref, bf16[8,9,64,320]{3,2,1,0:T(8,128)(2,1)} %all-to-all-done.2.gradient_ref, f32[17,2560,128]{2,1,0:T(8,128)} %left_ref.5, ...), custom_call_target="tpu_custom_call" | custom-call | tf_op jit(solution)/shard_map/pallas_call | solution.py:548
  765.4 6.5 all-to-all-start.5
  772.3 19.7 %shard_map.759 = (bf16[8,8,64,320]{3,2,1,0:T(8,128)(2,1)S(1)}, f32[17,64,2560]{2,1,0:T(8,128)}, f32[17,64,2560]{2,1,0:T(8,128)}) custom-call(s32[16]{0:T(128)S(1)} %concatenate.97.refs_0_, f32[18]{0:T(128)S(1)} %pad_maximum_fusion.9.refs_1_, bf16[8,8,64,320]{3,2,1,0:T(8,128)(2,1)} %all-to-all-done.3.refs_2_, ...), custom_call_target="tpu_custom_call", output_to_operand_aliasing={{1}: (7, {}), {2}: (8, {})} | custom-call | tf_op jit(solution)/shard_map/pallas_call | solution.py:548
  793.6 14.3 %reduce-scatter.6.cloned.1.call-done = bf16[320,288]{1,0:T(8,128)(2,1)} async-done(((bf16[2560,288]{1,0:T(8,128)(2,1)}), bf16[320,288]{1,0:T(8,128)(2,1)}) %reduce-scatter.6.cloned.1.call-update) | async-done | bytes 184336 | tf_op jit(solution)/shard_map/reduce_scatter | solution.py:372
  821.6 4.3 all-to-all-start.6
  827.1 23.1 %all-to-all-done.6 = bf16[8,4,64,448]{3,2,1,0:T(8,128)(2,1)} async-done(((bf16[8,4,64,448]{3,2,1,0:T(8,128)(2,1)}), bf16[8,4,64,448]{3,2,1,0:T(8,128)(2,1)}, u32[]{:S(2)}, u32[]{:S(2)}) %all-to-all-start.6) | async-done | bytes 1835040 | tf_op jit(solution)/shard_map/all_to_all | solution.py:792
  854.5 6.1 all-to-all-start.7
  870.5 4.3 shard_map.760
  876.0 5.3 shard_map.761
  885.5 11.5 %all-to-all-done.7.last_ref = bf16[8,8,64,320]{3,2,1,0:T(8,128)(2,1)} async-done(((bf16[8,8,64,320]{3,2,1,0:T(8,128)(2,1)}), bf16[8,8,64,320]{3,2,1,0:T(8,128)(2,1)}, u32[]{:S(2)}, u32[]{:S(2)}) %all-to-all-start.7) | async-done | bytes 2621472 | tf_op jit(solution)/shard_map/all_to_all | solution.py:1170
  900.0 5.5 all-to-all-start.8
  923.2 10.3 %shard_map.763 = (f32[320,640]{1,0:T(8,128)}, f32[320,1600]{1,0:T(8,128)}, f32[320,1600]{1,0:T(8,128)}, f32[320,1600]{1,0:T(8,128)}) custom-call(s32[85]{0:T(128)} %copy-done.138, bf16[8,9,64,320]{3,2,1,0:T(8,128)(2,1)} %all-to-all-done.5.first_ref, bf16[8,8,64,320]{3,2,1,0:T(8,128)(2,1)} %all-to-all-done.7.last_ref, bf16[320,640]{1,0:T(8,128)(2,1)} %refs_0_.1, ...), custom_call_target="tpu_custom_call" | custom-call | tf_op jit(solution)/shard_map/pallas_call | solution.py:446
  (723 shorter events, 327.1 us)
Async XLA Ops:
  7.3 49.2 %all-gather.18.cloned.1.call-start = ((), (), s32[]{:S(2)}) async-start(), calls=%async_computation.20 | async-start | bytes 1990656 | tf_op jit(solution)/shard_map/all_gather | solution.py:880
  9.1 114.2 %all-gather.8.cloned.1.call-start = ((), (), s32[]{:S(2)}) async-start(), calls=%async_computation.12 | async-start | bytes 2211840 | tf_op jit(solution)/shard_map/all_gather | solution.py:881
  11.2 138.6 %all-gather.10.cloned.1.call-start = ((), (), s32[]{:S(2)}) async-start(), calls=%async_computation.13 | async-start | bytes 3686400 | tf_op jit(solution)/shard_map/all_gather | solution.py:883
  11.9 265.3 %all-gather.16.cloned.1.call-start = ((), (), s32[]{:S(2)}) async-start(), calls=%async_computation.16 | async-start | bytes 9584640 | tf_op jit(solution)/shard_map/all_gather | solution.py:886
  12.5 275.7 %all-gather.14.cloned.1.call-start = ((), (), s32[]{:S(2)}) async-start(), calls=%async_computation.15 | async-start | bytes 9584640 | tf_op jit(solution)/shard_map/all_gather | solution.py:885
  13.3 56.1 %collective-permute-start.4 = (f32[1536]{0:T(1024)S(1)}, f32[1536]{0:T(1024)S(1)}, u32[]{:S(2)}, u32[]{:S(2)}) collective-permute-start(f32[1536]{0:T(1024)S(1)} %concatenate.83), channel_id=1, source_target_pairs={{0,1},{1,2},{2,3},{3,0},{4,5},{5,6},{6,7},{7,4},{8,9},{9,10},{10,1... | collective-permute-start | bytes 18440 | tf_op jit(solution)/shard_map/ppermute | solution.py:81
  14.6 59.2 %collective-permute-start.5 = (f32[1536]{0:T(1024)S(1)}, f32[1536]{0:T(1024)S(1)}, u32[]{:S(2)}, u32[]{:S(2)}) collective-permute-start(f32[1536]{0:T(1024)S(1)} %concatenate.83), channel_id=1, source_target_pairs={{0,2},{1,3},{2,0},{3,1},{4,6},{5,7},{6,4},{7,5},{8,10},{9,11},{10,... | collective-permute-start | bytes 18440 | tf_op jit(solution)/shard_map/ppermute | solution.py:81
  15.6 58.2 %collective-permute-start.6 = (f32[1536]{0:T(1024)S(1)}, f32[1536]{0:T(1024)S(1)}, u32[]{:S(2)}, u32[]{:S(2)}) collective-permute-start(f32[1536]{0:T(1024)S(1)} %concatenate.83), channel_id=1, source_target_pairs={{0,3},{1,0},{2,1},{3,2},{4,7},{5,4},{6,5},{7,6},{8,11},{9,8},{10,9... | collective-permute-start | bytes 18440 | tf_op jit(solution)/shard_map/ppermute | solution.py:81
  25.4 273.9 %all-gather.12.cloned.1.call-start = ((), (), s32[]{:S(2)}) async-start(), calls=%async_computation.14 | async-start | bytes 9584640 | tf_op jit(solution)/shard_map/all_gather | solution.py:884
  36.6 28.1 %collective-permute-start.1 = (bf16[512,640]{1,0:T(8,128)(2,1)S(1)}, bf16[512,640]{1,0:T(8,128)(2,1)}, u32[]{:S(2)}, u32[]{:S(2)}) collective-permute-start(bf16[512,640]{1,0:T(8,128)(2,1)S(1)} %bitcast.231), channel_id=1, source_target_pairs={{0,2},{2,0},{1,3},{3,1},{4,6},{6,4},{5,7},{7,5},{8,10},{10,8},{9,1... | collective-permute-start | bytes 1966088 | tf_op jit(solution)/shard_map/ppermute | solution.py:90
  38.8 37.0 %collective-permute-start = (bf16[512,640]{1,0:T(8,128)(2,1)S(1)}, bf16[512,640]{1,0:T(8,128)(2,1)}, u32[]{:S(2)}, u32[]{:S(2)}) collective-permute-start(bf16[512,640]{1,0:T(8,128)(2,1)S(1)} %bitcast.232), channel_id=1, source_target_pairs={{0,1},{1,0},{2,3},{3,2},{4,5},{5,4},{6,7},{7,6},{8,9},{9,8},{10,11... | collective-permute-start | bytes 1966088 | tf_op jit(solution)/shard_map/ppermute | solution.py:90
  64.7 19.5 %collective-permute-start.2 = (bf16[512,640]{1,0:T(8,128)(2,1)S(1)}, bf16[512,640]{1,0:T(8,128)(2,1)S(1)}, u32[]{:S(2)}, u32[]{:S(2)}) collective-permute-start(bf16[512,640]{1,0:T(8,128)(2,1)S(1)} %bitcast.233), channel_id=1, source_target_pairs={{1,2},{2,1},{5,6},{6,5},{9,10},{10,9},{13,14},{14,13},{17,18},{18,... | collective-permute-start | bytes 1966088 | tf_op jit(solution)/shard_map/ppermute | solution.py:90
  113.4 28.3 %collective-permute-start.11 = (bf16[512,640]{1,0:T(8,128)(2,1)}, bf16[512,640]{1,0:T(8,128)(2,1)}, u32[]{:S(2)}, u32[]{:S(2)}) collective-permute-start(bf16[512,640]{1,0:T(8,128)(2,1)} %param.47), channel_id=1, source_target_pairs={{0,2},{2,0},{1,3},{3,1},{4,6},{6,4},{5,7},{7,5},{8,10},{10,8},{9,1... | collective-permute-start | bytes 1966088 | tf_op jit(solution)/shard_map/ppermute | solution.py:90
  113.5 34.3 %collective-permute-start.21 = (bf16[512,640]{1,0:T(8,128)(2,1)}, bf16[512,640]{1,0:T(8,128)(2,1)}, u32[]{:S(2)}, u32[]{:S(2)}) collective-permute-start(bf16[512,640]{1,0:T(8,128)(2,1)} %param.47), channel_id=1, source_target_pairs={{0,1},{1,0},{2,3},{3,2},{4,5},{5,4},{6,7},{7,6},{8,9},{9,8},{10,11... | collective-permute-start | bytes 1966088 | tf_op jit(solution)/shard_map/ppermute | solution.py:90
  114.4 44.4 %collective-permute-start.22 = (bf16[512,640]{1,0:T(8,128)(2,1)}, bf16[512,640]{1,0:T(8,128)(2,1)}, u32[]{:S(2)}, u32[]{:S(2)}) collective-permute-start(bf16[512,640]{1,0:T(8,128)(2,1)} %param.47), channel_id=1, source_target_pairs={{1,2},{2,1},{5,6},{6,5},{9,10},{10,9},{13,14},{14,13},{17,18},{18,... | collective-permute-start | bytes 1966088 | tf_op jit(solution)/shard_map/ppermute | solution.py:90
  141.6 19.1 %collective-permute-start.23 = (bf16[512,640]{1,0:T(8,128)(2,1)}, bf16[512,640]{1,0:T(8,128)(2,1)S(1)}, u32[]{:S(2)}, u32[]{:S(2)}) collective-permute-start(bf16[512,640]{1,0:T(8,128)(2,1)} %collective-permute-done.11), channel_id=1, source_target_pairs={{1,0},{2,3},{5,4},{6,7},{9,8},{10,11},{13,12},{14,15},{17,16},{18,... | collective-permute-start | bytes 1966088 | tf_op jit(solution)/shard_map/ppermute | solution.py:90
  155.4 19.1 %collective-permute-start.14 = (bf16[512,640]{1,0:T(8,128)(2,1)}, bf16[512,640]{1,0:T(8,128)(2,1)S(1)}, u32[]{:S(2)}, u32[]{:S(2)}) collective-permute-start(bf16[512,640]{1,0:T(8,128)(2,1)} %get-tuple-element.607), channel_id=1, source_target_pairs={{0,1},{3,2},{4,5},{7,6},{8,9},{11,10},{12,13},{15,14},{16,17},{19,... | collective-permute-start | bytes 1966088 | tf_op jit(solution)/shard_map/ppermute | solution.py:90
  166.9 89.9 %all-to-all-start.1 = ((bf16[8,64,2560]{2,1,0:T(8,128)(2,1)}), bf16[8,64,2560]{2,1,0:T(8,128)(2,1)}, u32[]{:S(2)}, u32[]{:S(2)}) async-start(bf16[8,64,2560]{2,1,0:T(8,128)(2,1)} %gather_fusion.1), calls=%async_computation.1 | async-start | bytes 5242880 | tf_op jit(solution)/shard_map/all_to_all | solution.py:858
  172.4 418.7 %reduce-scatter.4.cloned.1.call-start = ((), (), s32[]{:S(2)}) async-start(), calls=%async_computation.17 | async-start | bytes 3686400 | tf_op jit(solution)/shard_map/reduce_scatter | solution.py:372
  175.8 40.0 %collective-permute-start.15 = (bf16[512,640]{1,0:T(8,128)(2,1)S(1)}, bf16[512,640]{1,0:T(8,128)(2,1)S(1)}, u32[]{:S(2)}, u32[]{:S(2)}) collective-permute-start(bf16[512,640]{1,0:T(8,128)(2,1)S(1)} %add_convert_fusion.5), channel_id=1, source_target_pairs={{0,2},{2,0},{1,3},{3,1},{4,6},{6,4},{5,7},{7,5},{8,10},{10,8},{9,1... | collective-permute-start | bytes 1966088 | tf_op jit(solution)/shard_map/ppermute | solution.py:90
  220.7 31.5 %collective-permute-start.17 = (bf16[512,640]{1,0:T(8,128)(2,1)}, bf16[512,640]{1,0:T(8,128)(2,1)S(1)}, u32[]{:S(2)}, u32[]{:S(2)}) collective-permute-start(bf16[512,640]{1,0:T(8,128)(2,1)} %get-tuple-element.592), channel_id=1, source_target_pairs={{0,2},{2,0},{1,3},{3,1},{4,6},{6,4},{5,7},{7,5},{8,10},{10,8},{9,1... | collective-permute-start | bytes 1966088 | tf_op jit(solution)/shard_map/ppermute | solution.py:90
  225.2 35.4 %collective-permute-start.16 = (bf16[512,640]{1,0:T(8,128)(2,1)}, bf16[512,640]{1,0:T(8,128)(2,1)}, u32[]{:S(2)}, u32[]{:S(2)}) collective-permute-start(bf16[512,640]{1,0:T(8,128)(2,1)} %get-tuple-element.592), channel_id=1, source_target_pairs={{0,1},{1,0},{2,3},{3,2},{4,5},{5,4},{6,7},{7,6},{8,9},{9,8},{10,11... | collective-permute-start | bytes 1966088 | tf_op jit(solution)/shard_map/ppermute | solution.py:90
  225.3 42.1 %collective-permute-start.18 = (bf16[512,640]{1,0:T(8,128)(2,1)}, bf16[512,640]{1,0:T(8,128)(2,1)S(1)}, u32[]{:S(2)}, u32[]{:S(2)}) collective-permute-start(bf16[512,640]{1,0:T(8,128)(2,1)} %get-tuple-element.592), channel_id=1, source_target_pairs={{1,2},{2,1},{5,6},{6,5},{9,10},{10,9},{13,14},{14,13},{17,18},{18,... | collective-permute-start | bytes 1966088 | tf_op jit(solution)/shard_map/ppermute | solution.py:90
  322.0 34.9 %collective-permute-start.27 = (bf16[640,1664]{1,0:T(8,128)(2,1)}, bf16[640,1664]{1,0:T(8,128)(2,1)S(1)}, u32[]{:S(2)}, u32[]{:S(2)}) collective-permute-start(bf16[640,1664]{1,0:T(8,128)(2,1)} %get-tuple-element.191), channel_id=1, source_target_pairs={{0,4},{4,0},{8,12},{12,8},{16,20},{20,16},{24,28},{28,24},{1,5},{5... | collective-permute-start | bytes 6389768 | tf_op jit(solution)/shard_map/ppermute | solution.py:86
  324.0 32.9 %collective-permute-start.28 = (bf16[640,1664]{1,0:T(8,128)(2,1)}, bf16[640,1664]{1,0:T(8,128)(2,1)}, u32[]{:S(2)}, u32[]{:S(2)}) collective-permute-start(bf16[640,1664]{1,0:T(8,128)(2,1)} %get-tuple-element.193), channel_id=1, source_target_pairs={{0,4},{4,0},{8,12},{12,8},{16,20},{20,16},{24,28},{28,24},{1,5},{5... | collective-permute-start | bytes 6389768 | tf_op jit(solution)/shard_map/ppermute | solution.py:86
  375.1 33.3 %collective-permute-start.30 = (bf16[640,1664]{1,0:T(8,128)(2,1)}, bf16[640,1664]{1,0:T(8,128)(2,1)S(1)}, u32[]{:S(2)}, u32[]{:S(2)}) collective-permute-start(bf16[640,1664]{1,0:T(8,128)(2,1)} %get-tuple-element.201), channel_id=1, source_target_pairs={{0,4},{4,0},{8,12},{12,8},{16,20},{20,16},{24,28},{28,24},{1,5},{5... | collective-permute-start | bytes 6389768 | tf_op jit(solution)/shard_map/ppermute | solution.py:86
  376.8 35.0 %collective-permute-start.32 = (bf16[640,1664]{1,0:T(8,128)(2,1)}, bf16[640,1664]{1,0:T(8,128)(2,1)S(1)}, u32[]{:S(2)}, u32[]{:S(2)}) collective-permute-start(bf16[640,1664]{1,0:T(8,128)(2,1)} %get-tuple-element.205), channel_id=1, source_target_pairs={{0,4},{4,0},{8,12},{12,8},{16,20},{20,16},{24,28},{28,24},{1,5},{5... | collective-permute-start | bytes 6389768 | tf_op jit(solution)/shard_map/ppermute | solution.py:86
  376.8 36.4 %collective-permute-start.33 = (bf16[640,1664]{1,0:T(8,128)(2,1)}, bf16[640,1664]{1,0:T(8,128)(2,1)S(1)}, u32[]{:S(2)}, u32[]{:S(2)}) collective-permute-start(bf16[640,1664]{1,0:T(8,128)(2,1)} %get-tuple-element.207), channel_id=1, source_target_pairs={{0,4},{4,0},{8,12},{12,8},{16,20},{20,16},{24,28},{28,24},{1,5},{5... | collective-permute-start | bytes 6389768 | tf_op jit(solution)/shard_map/ppermute | solution.py:86
  377.3 42.1 %collective-permute-start.31 = (bf16[640,1664]{1,0:T(8,128)(2,1)}, bf16[640,1664]{1,0:T(8,128)(2,1)S(1)}, u32[]{:S(2)}, u32[]{:S(2)}) collective-permute-start(bf16[640,1664]{1,0:T(8,128)(2,1)} %get-tuple-element.203), channel_id=1, source_target_pairs={{0,4},{4,0},{8,12},{12,8},{16,20},{20,16},{24,28},{28,24},{1,5},{5... | collective-permute-start | bytes 6389768 | tf_op jit(solution)/shard_map/ppermute | solution.py:86
  377.3 29.1 %collective-permute-start.29 = (bf16[512,640]{1,0:T(8,128)(2,1)}, bf16[512,640]{1,0:T(8,128)(2,1)S(1)}, u32[]{:S(2)}, u32[]{:S(2)}) collective-permute-start(bf16[512,640]{1,0:T(8,128)(2,1)} %add_convert_fusion.4), channel_id=1, source_target_pairs={{0,2},{2,0},{1,3},{3,1},{4,6},{6,4},{5,7},{7,5},{8,10},{10,8},{9,1... | collective-permute-start | bytes 1966088 | tf_op jit(solution)/shard_map/ppermute | solution.py:90
  411.8 23.5 %collective-permute-start.36 = (bf16[320,1664]{1,0:T(8,128)(2,1)}, bf16[320,1664]{1,0:T(8,128)(2,1)S(1)}, u32[]{:S(2)}, u32[]{:S(2)}) collective-permute-start(bf16[320,1664]{1,0:T(8,128)(2,1)} %get-tuple-element.217), channel_id=1, source_target_pairs={{0,8},{4,12},{8,0},{12,4},{16,24},{20,28},{24,16},{28,20},{1,9},{5... | collective-permute-start | bytes 3194888 | tf_op jit(solution)/shard_map/ppermute | solution.py:86
  414.5 24.2 %collective-permute-start.37 = (bf16[320,1664]{1,0:T(8,128)(2,1)}, bf16[320,1664]{1,0:T(8,128)(2,1)S(1)}, u32[]{:S(2)}, u32[]{:S(2)}) collective-permute-start(bf16[320,1664]{1,0:T(8,128)(2,1)} %get-tuple-element.218), channel_id=1, source_target_pairs={{0,16},{4,20},{8,24},{12,28},{16,0},{20,4},{24,8},{28,12},{1,17},{... | collective-permute-start | bytes 3194888 | tf_op jit(solution)/shard_map/ppermute | solution.py:86
  428.2 26.8 %collective-permute-start.35 = (bf16[512,640]{1,0:T(8,128)(2,1)}, bf16[512,640]{1,0:T(8,128)(2,1)}, u32[]{:S(2)}, u32[]{:S(2)}) collective-permute-start(bf16[512,640]{1,0:T(8,128)(2,1)} %get-tuple-element.590), channel_id=1, source_target_pairs={{0,2},{2,0},{1,3},{3,1},{4,6},{6,4},{5,7},{7,5},{8,10},{10,8},{9,1... | collective-permute-start | bytes 1966088 | tf_op jit(solution)/shard_map/ppermute | solution.py:90
  428.2 34.0 %collective-permute-start.40 = (bf16[320,1664]{1,0:T(8,128)(2,1)}, bf16[320,1664]{1,0:T(8,128)(2,1)S(1)}, u32[]{:S(2)}, u32[]{:S(2)}) collective-permute-start(bf16[320,1664]{1,0:T(8,128)(2,1)} %get-tuple-element.222), channel_id=1, source_target_pairs={{0,8},{4,12},{8,0},{12,4},{16,24},{20,28},{24,16},{28,20},{1,9},{5... | collective-permute-start | bytes 3194888 | tf_op jit(solution)/shard_map/ppermute | solution.py:86
  429.3 33.0 %collective-permute-start.41 = (bf16[320,1664]{1,0:T(8,128)(2,1)}, bf16[320,1664]{1,0:T(8,128)(2,1)S(1)}, u32[]{:S(2)}, u32[]{:S(2)}) collective-permute-start(bf16[320,1664]{1,0:T(8,128)(2,1)} %get-tuple-element.223), channel_id=1, source_target_pairs={{0,16},{4,20},{8,24},{12,28},{16,0},{20,4},{24,8},{28,12},{1,17},{... | collective-permute-start | bytes 3194888 | tf_op jit(solution)/shard_map/ppermute | solution.py:86
  435.3 25.7 %collective-permute-start.34 = (bf16[512,640]{1,0:T(8,128)(2,1)}, bf16[512,640]{1,0:T(8,128)(2,1)S(1)}, u32[]{:S(2)}, u32[]{:S(2)}) collective-permute-start(bf16[512,640]{1,0:T(8,128)(2,1)} %get-tuple-element.590), channel_id=1, source_target_pairs={{0,1},{1,0},{2,3},{3,2},{4,5},{5,4},{6,7},{7,6},{8,9},{9,8},{10,11... | collective-permute-start | bytes 1966088 | tf_op jit(solution)/shard_map/ppermute | solution.py:90
  441.5 30.4 %collective-permute-start.38 = (bf16[512,640]{1,0:T(8,128)(2,1)}, bf16[512,640]{1,0:T(8,128)(2,1)}, u32[]{:S(2)}, u32[]{:S(2)}) collective-permute-start(bf16[512,640]{1,0:T(8,128)(2,1)} %get-tuple-element.590), channel_id=1, source_target_pairs={{1,2},{2,1},{5,6},{6,5},{9,10},{10,9},{13,14},{14,13},{17,18},{18,... | collective-permute-start | bytes 1966088 | tf_op jit(solution)/shard_map/ppermute | solution.py:90
  454.9 19.8 %collective-permute-start.39 = (bf16[512,640]{1,0:T(8,128)(2,1)}, bf16[512,640]{1,0:T(8,128)(2,1)S(1)}, u32[]{:S(2)}, u32[]{:S(2)}) collective-permute-start(bf16[512,640]{1,0:T(8,128)(2,1)} %collective-permute-done.35), channel_id=1, source_target_pairs={{1,0},{2,3},{5,4},{6,7},{9,8},{10,11},{13,12},{14,15},{17,16},{18,... | collective-permute-start | bytes 1966088 | tf_op jit(solution)/shard_map/ppermute | solution.py:90
  503.0 46.4 %collective-permute-start.42 = (bf16[320,1664]{1,0:T(8,128)(2,1)S(1)}, bf16[320,1664]{1,0:T(8,128)(2,1)S(1)}, u32[]{:S(2)}, u32[]{:S(2)}) collective-permute-start(bf16[320,1664]{1,0:T(8,128)(2,1)S(1)} %copy-done.57), channel_id=1, source_target_pairs={{0,8},{4,12},{8,0},{12,4},{16,24},{20,28},{24,16},{28,20},{1,9},{5... | collective-permute-start | bytes 3194888 | tf_op jit(solution)/shard_map/ppermute | solution.py:86
  504.4 45.0 %collective-permute-start.43 = (bf16[320,1664]{1,0:T(8,128)(2,1)S(1)}, bf16[320,1664]{1,0:T(8,128)(2,1)S(1)}, u32[]{:S(2)}, u32[]{:S(2)}) collective-permute-start(bf16[320,1664]{1,0:T(8,128)(2,1)S(1)} %copy-done.55), channel_id=1, source_target_pairs={{0,16},{4,20},{8,24},{12,28},{16,0},{20,4},{24,8},{28,12},{1,17},{... | collective-permute-start | bytes 3194888 | tf_op jit(solution)/shard_map/ppermute | solution.py:86
  537.3 34.5 %collective-permute-start.49 = (bf16[160,1664]{1,0:T(8,128)(2,1)}, bf16[160,1664]{1,0:T(8,128)(2,1)}, u32[]{:S(2)}, u32[]{:S(2)}) collective-permute-start(bf16[160,1664]{1,0:T(8,128)(2,1)} %get-tuple-element.238), channel_id=1, source_target_pairs={{0,16},{4,20},{8,24},{12,28},{16,0},{20,4},{24,8},{28,12},{1,17},{... | collective-permute-start | bytes 1597448 | tf_op jit(solution)/shard_map/ppermute | solution.py:86
  537.8 34.0 %collective-permute-start.50 = (bf16[160,1664]{1,0:T(8,128)(2,1)}, bf16[160,1664]{1,0:T(8,128)(2,1)}, u32[]{:S(2)}, u32[]{:S(2)}) collective-permute-start(bf16[160,1664]{1,0:T(8,128)(2,1)} %get-tuple-element.239), channel_id=1, source_target_pairs={{0,8},{4,12},{8,0},{12,4},{16,24},{20,28},{24,16},{28,20},{1,9},{5... | collective-permute-start | bytes 1597448 | tf_op jit(solution)/shard_map/ppermute | solution.py:86
  559.9 26.4 %collective-permute-start.46 = (bf16[512,256]{1,0:T(8,128)(2,1)}, bf16[512,256]{1,0:T(8,128)(2,1)}, u32[]{:S(2)}, u32[]{:S(2)}) collective-permute-start(bf16[512,256]{1,0:T(8,128)(2,1)} %copy.335), channel_id=1, source_target_pairs={{0,1},{3,2},{4,5},{7,6},{8,9},{11,10},{12,13},{15,14},{16,17},{19,... | collective-permute-start | bytes 786440 | tf_op jit(solution)/shard_map/ppermute | solution.py:90
  561.2 21.2 %collective-permute-start.51 = (bf16[160,1664]{1,0:T(8,128)(2,1)}, bf16[160,1664]{1,0:T(8,128)(2,1)}, u32[]{:S(2)}, u32[]{:S(2)}) collective-permute-start(bf16[160,1664]{1,0:T(8,128)(2,1)} %copy-done.63), channel_id=1, source_target_pairs={{0,16},{4,20},{8,24},{12,28},{16,0},{20,4},{24,8},{28,12},{1,17},{... | collective-permute-start | bytes 1597448 | tf_op jit(solution)/shard_map/ppermute | solution.py:86
  561.2 21.3 %collective-permute-start.52 = (bf16[160,1664]{1,0:T(8,128)(2,1)}, bf16[160,1664]{1,0:T(8,128)(2,1)}, u32[]{:S(2)}, u32[]{:S(2)}) collective-permute-start(bf16[160,1664]{1,0:T(8,128)(2,1)} %copy-done.62), channel_id=1, source_target_pairs={{0,8},{4,12},{8,0},{12,4},{16,24},{20,28},{24,16},{28,20},{1,9},{5... | collective-permute-start | bytes 1597448 | tf_op jit(solution)/shard_map/ppermute | solution.py:86
  571.8 29.5 %collective-permute-start.54 = (f32[34,512]{0,1:T(8,128)}, f32[34,512]{0,1:T(8,128)}, u32[]{:S(2)}, u32[]{:S(2)}) collective-permute-start(f32[34,512]{0,1:T(8,128)} %copy.300), channel_id=1, source_target_pairs={{0,1},{1,2},{2,3},{3,0},{4,5},{5,6},{6,7},{7,4},{8,9},{9,10},{10,1... | collective-permute-start | bytes 208904 | tf_op jit(solution)/shard_map/ppermute | solution.py:81
  571.8 29.5 %collective-permute-start.55 = (f32[34,512]{0,1:T(8,128)}, f32[34,512]{0,1:T(8,128)}, u32[]{:S(2)}, u32[]{:S(2)}) collective-permute-start(f32[34,512]{0,1:T(8,128)} %copy.300), channel_id=1, source_target_pairs={{0,2},{1,3},{2,0},{3,1},{4,6},{5,7},{6,4},{7,5},{8,10},{9,11},{10,... | collective-permute-start | bytes 208904 | tf_op jit(solution)/shard_map/ppermute | solution.py:81
  582.3 19.0 %collective-permute-start.56 = (f32[34,512]{0,1:T(8,128)}, f32[34,512]{0,1:T(8,128)S(1)}, u32[]{:S(2)}, u32[]{:S(2)}) collective-permute-start(f32[34,512]{0,1:T(8,128)} %copy.300), channel_id=1, source_target_pairs={{0,3},{1,0},{2,1},{3,2},{4,7},{5,4},{6,5},{7,6},{8,11},{9,8},{10,9... | collective-permute-start | bytes 208904 | tf_op jit(solution)/shard_map/ppermute | solution.py:81
  606.3 58.0 %all-to-all-start.2 = ((bf16[8,9,64,320]{3,2,1,0:T(8,128)(2,1)}), bf16[8,9,64,320]{3,2,1,0:T(8,128)(2,1)}, u32[]{:S(2)}, u32[]{:S(2)}) async-start(bf16[8,9,64,320]{3,2,1,0:T(8,128)(2,1)} %get-tuple-element.259), calls=%async_computation.3 | async-start | bytes 7077888 | tf_op jit(solution)/shard_map/all_to_all | solution.py:1066
  616.7 177.0 %reduce-scatter.8.cloned.1.call-start = ((), (), s32[]{:S(2)}) async-start(), calls=%async_computation.19 | async-start | bytes 2949120 | tf_op jit(solution)/shard_map/reduce_scatter | solution.py:372
  634.1 39.8 %collective-permute-start.57 = (bf16[512,640]{1,0:T(8,128)(2,1)}, bf16[512,640]{1,0:T(8,128)(2,1)}, u32[]{:S(2)}, u32[]{:S(2)}) collective-permute-start(bf16[512,640]{1,0:T(8,128)(2,1)} %get-tuple-element.601), channel_id=1, source_target_pairs={{0,1},{3,2},{4,5},{7,6},{8,9},{11,10},{12,13},{15,14},{16,17},{19,... | collective-permute-start | bytes 1966088 | tf_op jit(solution)/shard_map/ppermute | solution.py:90
  635.4 43.4 %collective-permute-start.59 = (bf16[512,640]{1,0:T(8,128)(2,1)}, bf16[512,640]{1,0:T(8,128)(2,1)}, u32[]{:S(2)}, u32[]{:S(2)}) collective-permute-start(bf16[512,640]{1,0:T(8,128)(2,1)} %get-tuple-element.603), channel_id=1, source_target_pairs={{1,2},{2,1},{5,6},{6,5},{9,10},{10,9},{13,14},{14,13},{17,18},{18,... | collective-permute-start | bytes 1966088 | tf_op jit(solution)/shard_map/ppermute | solution.py:90
  637.6 45.0 %collective-permute-start.60 = (bf16[512,640]{1,0:T(8,128)(2,1)}, bf16[512,640]{1,0:T(8,128)(2,1)}, u32[]{:S(2)}, u32[]{:S(2)}) collective-permute-start(bf16[512,640]{1,0:T(8,128)(2,1)} %get-tuple-element.602), channel_id=1, source_target_pairs={{0,1},{1,0},{2,3},{3,2},{4,5},{5,4},{6,7},{7,6},{8,9},{9,8},{10,11... | collective-permute-start | bytes 1966088 | tf_op jit(solution)/shard_map/ppermute | solution.py:90
  642.2 40.4 %collective-permute-start.61 = (bf16[512,640]{1,0:T(8,128)(2,1)}, bf16[512,640]{1,0:T(8,128)(2,1)}, u32[]{:S(2)}, u32[]{:S(2)}) collective-permute-start(bf16[512,640]{1,0:T(8,128)(2,1)} %add_convert_fusion.2), channel_id=1, source_target_pairs={{0,2},{2,0},{1,3},{3,1},{4,6},{6,4},{5,7},{7,5},{8,10},{10,8},{9,1... | collective-permute-start | bytes 1966088 | tf_op jit(solution)/shard_map/ppermute | solution.py:90
  664.3 68.1 %all-to-all-start.3 = ((bf16[8,8,64,320]{3,2,1,0:T(8,128)(2,1)}), bf16[8,8,64,320]{3,2,1,0:T(8,128)(2,1)}, u32[]{:S(2)}, u32[]{:S(2)}) async-start(bf16[8,8,64,320]{3,2,1,0:T(8,128)(2,1)} %get-tuple-element.267), calls=%async_computation.4 | async-start | bytes 6291456 | tf_op jit(solution)/shard_map/all_to_all | solution.py:1066
  675.4 32.9 %collective-permute-start.58 = (bf16[512,640]{1,0:T(8,128)(2,1)S(1)}, bf16[512,640]{1,0:T(8,128)(2,1)S(1)}, u32[]{:S(2)}, u32[]{:S(2)}) collective-permute-start(bf16[512,640]{1,0:T(8,128)(2,1)S(1)} %add_convert_fusion.3), channel_id=1, source_target_pairs={{0,2},{2,0},{1,3},{3,1},{4,6},{6,4},{5,7},{7,5},{8,10},{10,8},{9,1... | collective-permute-start | bytes 1966088 | tf_op jit(solution)/shard_map/ppermute | solution.py:90
  677.8 30.4 %collective-permute-start.63 = (bf16[512,640]{1,0:T(8,128)(2,1)}, bf16[512,640]{1,0:T(8,128)(2,1)S(1)}, u32[]{:S(2)}, u32[]{:S(2)}) collective-permute-start(bf16[512,640]{1,0:T(8,128)(2,1)} %get-tuple-element.600), channel_id=1, source_target_pairs={{0,1},{1,0},{2,3},{3,2},{4,5},{5,4},{6,7},{7,6},{8,9},{9,8},{10,11... | collective-permute-start | bytes 1966088 | tf_op jit(solution)/shard_map/ppermute | solution.py:90
  678.7 44.6 %collective-permute-start.62 = (bf16[512,640]{1,0:T(8,128)(2,1)}, bf16[512,640]{1,0:T(8,128)(2,1)S(1)}, u32[]{:S(2)}, u32[]{:S(2)}) collective-permute-start(bf16[512,640]{1,0:T(8,128)(2,1)} %get-tuple-element.601), channel_id=1, source_target_pairs={{1,2},{2,1},{5,6},{6,5},{9,10},{10,9},{13,14},{14,13},{17,18},{18,... | collective-permute-start | bytes 1966088 | tf_op jit(solution)/shard_map/ppermute | solution.py:90
  732.4 31.9 %all-to-all-start.4 = ((bf16[8,133,640]{2,1,0:T(8,128)(2,1)}), bf16[8,133,640]{2,1,0:T(8,128)(2,1)S(1)}, u32[]{:S(2)}, u32[]{:S(2)}) async-start(bf16[8,133,640]{2,1,0:T(8,128)(2,1)} %pad_maximum_fusion.1), calls=%async_computation.5 | async-start | bytes 2785280 | tf_op jit(solution)/shard_map/all_to_all | solution.py:1131
  738.0 70.0 %reduce-scatter.6.cloned.1.call-start = ((), (), s32[]{:S(2)}) async-start(), calls=%async_computation.18 | async-start | bytes 2211840 | tf_op jit(solution)/shard_map/reduce_scatter | solution.py:372
  765.4 52.9 %all-to-all-start.5 = ((bf16[8,9,64,320]{3,2,1,0:T(8,128)(2,1)}), bf16[8,9,64,320]{3,2,1,0:T(8,128)(2,1)}, u32[]{:S(2)}, u32[]{:S(2)}) async-start(bf16[8,9,64,320]{3,2,1,0:T(8,128)(2,1)} %copy-done.30), calls=%async_computation.8 | async-start | bytes 7077888 | tf_op jit(solution)/shard_map/all_to_all | solution.py:1136
  821.6 28.6 %all-to-all-start.6 = ((bf16[8,4,64,448]{3,2,1,0:T(8,128)(2,1)}), bf16[8,4,64,448]{3,2,1,0:T(8,128)(2,1)}, u32[]{:S(2)}, u32[]{:S(2)}) async-start(bf16[8,4,64,448]{3,2,1,0:T(8,128)(2,1)} %fusion.15), calls=%async_computation.9 | async-start | bytes 4194304 | tf_op jit(solution)/shard_map/all_to_all | solution.py:792
  854.5 42.5 %all-to-all-start.7 = ((bf16[8,8,64,320]{3,2,1,0:T(8,128)(2,1)}), bf16[8,8,64,320]{3,2,1,0:T(8,128)(2,1)}, u32[]{:S(2)}, u32[]{:S(2)}) async-start(bf16[8,8,64,320]{3,2,1,0:T(8,128)(2,1)} %copy-done.31), calls=%async_computation.10 | async-start | bytes 6291456 | tf_op jit(solution)/shard_map/all_to_all | solution.py:1170
  900.0 33.6 %all-to-all-start.8 = ((bf16[8,4,64,448]{3,2,1,0:T(8,128)(2,1)}), bf16[8,4,64,448]{3,2,1,0:T(8,128)(2,1)S(1)}, u32[]{:S(2)}, u32[]{:S(2)}) async-start(bf16[8,4,64,448]{3,2,1,0:T(8,128)(2,1)} %fusion.17), calls=%async_computation.11 | async-start | bytes 4194304 | tf_op jit(solution)/shard_map/all_to_all | solution.py:792
  (177 other events, 2042.8 us)
Sparse Core Ops, SparseCore 0:
  10.6 30.9 all-gather.17
  44.0 26.1 all-gather.7
  72.1 32.8 all-gather.9
  106.7 54.9 all-gather.15
  163.4 79.1 all-gather.13
  244.3 54.9 all-gather.11
  488.5 62.3 reduce-scatter.3
  625.1 60.0 reduce-scatter.7
  742.8 65.1 reduce-scatter.5

commit v5 on v4

--- a/solution.py
+++ b/solution.py
@@ -1139,6 +1139,8 @@
         main_scales, last_owned, basis_la, basis_ra, mom_a, sq_a, groups[1],
         (mid_mom_a, mid_sq_a),
     )
+    leaving_two, back_one = tie(change_two, back_one)
+    back_two = lax.all_to_all(leaving_two, "wide", split_axis=0, concat_axis=0, tiled=True)
     block_latent, block_heads, change_two = tie(block_latent, block_heads, change_two)
     block_qb = block_heads[: w_qb.shape[0]].reshape(w_qb.shape[0], heads_here, 128)
     block_qb = block_qb[:, :, : NOPE + ROPE].reshape(w_qb.shape)
@@ -1164,10 +1166,8 @@
             ([block_kvb], c_send),
         )
     ]
-    sent_parts, back_one = tie(sent_parts, back_one)
+    sent_parts, back_two = tie(sent_parts, back_two)
     late_owned, owned_b, owned_c = trade_joined(sent_parts, wide_count)
-    change_two, late_owned, owned_b, owned_c = tie(change_two, late_owned, owned_b, owned_c)
-    back_two = lax.all_to_all(change_two, "wide", split_axis=0, concat_axis=0, tiled=True)
 
     placed = jnp.take(returned_rows[:, : 2 * piece_rows], deal_row, axis=0, mode="clip")
     final_out = placed[:, :piece_rows].astype(f32).reshape(row_count, local_width)

time: 963 us -> 972 us (level)
  waiting for transfers between devices: 301 us -> 312 us
    all_to_all x1, waiting for transfers between devices: 0.01 us -> 20.1 us  [body(): lax.all_to_all(change_one, 'wide', split_axis=0, concat_axis=0, tiled=True)]
    reduce_scatter x3, waiting for transfers between devices: 14.3 us -> 0.01 us  [scatter_rows(): return lax.psum_scatter(partial, 'wide', scatter_dimension=0, tiled=True)]
    all_to_all x1, waiting for transfers between devices: 11.5 us -> 23.2 us  [body(): lax.all_to_all(leaving_two, 'wide', split_axis=0, concat_axis=0, tiled=True)]
    unnamed x333 -> x343, local copies, waits for them, and re-layouts: 39.6 us -> 38.2 us
  transfers between devices with their start and end apart: 82 -> 82, of which waited for: 35 -> 36; matrix products, arithmetic and copies ran while one was open for 23% -> 23% of each run, Pallas kernels for 15% -> 14%
where the time goes in v5:
time: 972 us; the launch traced here: 960 us
  waiting for transfers between devices  312 us (32%)
  starting transfers between devices  165 us (17%)
  Pallas kernels  165 us (17%)
  local copies, waits for them, and re-layouts  103 us (11%)
  other arithmetic  93.9 us (10%)
  matrix products  87.2 us (9%)
  between operations  18.6 us (2%)
  blocking collectives  15.1 us (2%)
    ppermute x40, waiting for transfers between devices, along_line(): return lax.ppermute(value, 'narrow', pairs)  198 us
    ppermute x40, starting transfers between devices, along_line(): return lax.ppermute(value, 'narrow', pairs)  83.7 us
    pallas_call x5, Pallas kernels, slot_call(): pl.pallas_call(kernel, grid_spec=pltpu.PrefetchScalarGridSpec(num_scalar_...  57.4 us
    dot_general x7, matrix products, product(): return jnp.dot(left_side, right_side, preferred_element_type=jnp.float32)  44.4 us
    dot_general x8, matrix products, against_rows(): lax.dot_general(left_side, right_side, (((1,), (1,)), ((), ())), preferre...  41.2 us
    unnamed x343, local copies, waits for them, and re-layouts  38.2 us
    pallas_call x3, Pallas kernels, chunk_products(): pl.pallas_call(chunk_kernel, grid_spec=pltpu.PrefetchScalarGridSpec(num_s...  27.3 us
    ppermute x18, waiting for transfers between devices, flipped(): return lax.ppermute(value, 'wide', [(i, i ^ bit) for i in range(count)])  27.2 us
  transfers between devices with their start and end apart: 82, of which 36 were waited for; matrix products, arithmetic and copies ran while one was open for 23% of the time, Pallas kernels for 14%

profile of v5, /device:TPU:11, one launch (start us, length us, event | category | flops | bytes accessed | tf_op | source)
XLA Modules:
  0.0 959.6 jit_solution(6755404336659006889)
XLA Ops:
  19.9 5.5 all-to-all-start
  27.4 9.2 all-to-all-done
  40.2 15.1 %all_gather.23 = bf16[256,1280]{1,0:T(8,128)(2,1)} all-gather(bf16[32,1280]{1,0:T(8,128)(2,1)S(1)} %copy-done.107), channel_id=1, replica_groups=mesh['wide'=8,'narrow'=4] {'wide'}, dimensions={0}, use_global_device_ids=true | all-gather | bytes 737280 | tf_op jit(solution)/shard_map/all_gather | solution.py:882
  64.7 4.7 collective-permute-start.2
  78.2 6.0 collective-permute-done.2
  97.9 4.9 collective-permute-done.8
  102.8 5.9 collective-permute-start.10
  114.4 3.8 collective-permute-start.22
  126.3 11.0 %shard_map.741.right_ref = bf16[512,640]{1,0:T(8,128)(2,1)S(1)} custom-call(f32[512,1280]{1,0:T(8,128)S(1)} %fusion.97.query_ref, f32[512,1280]{1,0:T(8,128)} %fusion.98.key_value_ref, bf16[512,128]{1,0:T(8,128)(2,1)S(1)} %pad.45.rotary_ref, f32[3,512,128]{2,1,0:T(8,128)S(1)} %pad_maximum_fusion.3.table_ref, f32[512,512]{1,0:T(8,128)S(1)} %copy-done.15), custom_call_target="tpu_custom_call" | custom-call | tf_op jit(solution)/shard_map/pallas_call | solution.py:704
  141.6 6.2 collective-permute-start.23
  149.8 4.4 convolution_convert_fusion.1
  162.8 4.1 gather_fusion.1
  166.9 5.6 all-to-all-start.1
  178.5 11.4 %collective-permute-done.13 = bf16[512,640]{1,0:T(8,128)(2,1)S(1)} collective-permute-done((bf16[512,640]{1,0:T(8,128)(2,1)}, bf16[512,640]{1,0:T(8,128)(2,1)S(1)}, u32[]{:S(2)}, u32[]{:S(2)}) %collective-permute-start.13) | collective-permute-done | bytes 655392 | tf_op jit(solution)/shard_map/ppermute | solution.py:90
  189.9 26.0 %collective-permute-done.15 = bf16[512,640]{1,0:T(8,128)(2,1)S(1)} collective-permute-done((bf16[512,640]{1,0:T(8,128)(2,1)S(1)}, bf16[512,640]{1,0:T(8,128)(2,1)S(1)}, u32[]{:S(2)}, u32[]{:S(2)}) %collective-permute-start.15) | collective-permute-done | bytes 655392 | tf_op jit(solution)/shard_map/ppermute | solution.py:90
  228.3 24.0 %collective-permute-done.17 = bf16[512,640]{1,0:T(8,128)(2,1)S(1)} collective-permute-done((bf16[512,640]{1,0:T(8,128)(2,1)}, bf16[512,640]{1,0:T(8,128)(2,1)S(1)}, u32[]{:S(2)}, u32[]{:S(2)}) %collective-permute-start.17) | collective-permute-done | bytes 655392 | tf_op jit(solution)/shard_map/ppermute | solution.py:90
  252.3 4.5 collective-permute-start.19
  256.8 3.8 fusion.3.left_ref
  273.2 4.0 fusion.8.left_ref
  277.2 11.0 %fusion.100 = f32[512,1600]{1,0:T(8,128)} fusion(bf16[512,2560]{1,0:T(8,128)(2,1)} %fusion.3.left_ref, bf16[2560,1600]{1,0:T(8,128)(2,1)} %all-gather.16.cloned.1.call-done), kind=kOutput, calls=%fused_computation.322 | convolution fusion | flops 4194304000 | bytes 14090240 | tf_op jit(solution)/shard_map/dot_general | solution.py:32
  288.3 10.9 %fusion.99 = f32[512,1600]{1,0:T(8,128)} fusion(bf16[512,2560]{1,0:T(8,128)(2,1)} %fusion.8.left_ref, bf16[2560,1600]{1,0:T(8,128)(2,1)} %all-gather.14.cloned.1.call-done), kind=kOutput, calls=%fused_computation.321 | convolution fusion | flops 4194304000 | bytes 14090240 | tf_op jit(solution)/shard_map/dot_general | solution.py:32
  299.3 12.2 %multiply_convert_fusion = (bf16[512,1600]{1,0:T(8,128)(2,1)S(1)}, bf16[512,1600]{1,0:T(8,128)(2,1)S(1)}, bf16[512,1600]{1,0:T(8,128)(2,1)S(1)}) fusion(f32[512,1600]{1,0:T(8,128)} %fusion.100, f32[512,1600]{1,0:T(8,128)} %fusion.99, bf16[512,2560]{1,0:T(8,128)(2,1)} %fusion.8.left_ref, bf16[2560,1600]{1,0:T(8,128)(2,1)} %all-gather.12.cloned.1.call-done), kind=kOutput, calls=%fused_computation.37 | convolution fusion | flops 4205772800 | bytes 22282240 | tf_op jit(solution)/shard_map/dot_general | solution.py:32
  311.6 9.1 shard_map.742
  324.1 10.1 %fusion.101 = f32[512,2560]{1,0:T(8,128)} fusion(bf16[512,1600]{1,0:T(8,128)(2,1)S(1)} %get-tuple-element.181.right_ref, bf16[2560,1600]{1,0:T(8,128)(2,1)} %all-gather.12.cloned.1.call-done), kind=kOutput, calls=%fused_computation.323 | convolution fusion | flops 4194304000 | bytes 15073280 | tf_op jit(solution)/shard_map/dot_general | solution.py:42
  334.1 9.4 add_convert_fusion
  346.5 9.1 shard_map.743
  364.7 9.1 shard_map.745
  378.3 27.9 %collective-permute-done.29 = bf16[512,640]{1,0:T(8,128)(2,1)S(1)} collective-permute-done((bf16[512,640]{1,0:T(8,128)(2,1)}, bf16[512,640]{1,0:T(8,128)(2,1)S(1)}, u32[]{:S(2)}, u32[]{:S(2)}) %collective-permute-start.29) | collective-permute-done | bytes 655392 | tf_op jit(solution)/shard_map/ppermute | solution.py:90
  430.4 4.8 collective-permute-done.36.refs_2_
  445.8 8.9 collective-permute-done.35
  454.8 6.1 collective-permute-start.39
  465.3 6.5 collective-permute-done.38
  482.6 4.1 shard_map.749
  488.3 9.0 convolution_convert_fusion.2
  504.9 7.4 collective-permute-done.47.refs_3_
  516.4 4.2 convolution_convert_fusion.6.grad_ref
  520.6 15.6 %shard_map.751 = (bf16[512,1280]{1,0:T(8,128)(2,1)S(1)}, bf16[512,1280]{1,0:T(8,128)(2,1)S(1)}, f32[3,512,128]{2,1,0:T(8,128)S(1)}) custom-call(f32[512,1280]{1,0:T(8,128)} %copy-done.2, f32[512,1280]{1,0:T(8,128)} %fusion.98.key_value_ref, bf16[512,128]{1,0:T(8,128)(2,1)S(1)} %pad.45.rotary_ref, f32[3,512,128]{2,1,0:T(8,128)S(1)} %pad_maximum_fusion.3.table_ref, ...), custom_call_target="tpu_custom_call" | custom-call | tf_op jit(solution)/shard_map/pallas_call | solution.py:717
  538.4 10.7 %collective-permute-done.42.refs_2_ = bf16[320,1664]{1,0:T(8,128)(2,1)S(1)} collective-permute-done((bf16[320,1664]{1,0:T(8,128)(2,1)S(1)}, bf16[320,1664]{1,0:T(8,128)(2,1)S(1)}, u32[]{:S(2)}, u32[]{:S(2)}) %collective-permute-start.42) | collective-permute-done | bytes 1064992 | tf_op jit(solution)/shard_map/ppermute | solution.py:86
  571.6 5.7 collective-permute-start.55
  590.9 10.2 %shard_map.756 = (bf16[8,9,64,320]{3,2,1,0:T(8,128)(2,1)}, bf16[8,8,64,320]{3,2,1,0:T(8,128)(2,1)}) custom-call(s32[136]{0:T(256)} %broadcast_minimum_fusion.send_ref, bf16[320,640]{1,0:T(8,128)(2,1)} %reduce-scatter.4.cloned.1.call-done.refs_0_, f32[320,1600]{1,0:T(8,128)} %shard_map.754.refs_1_, f32[320,1600]{1,0:T(8,128)} %shard_map.755.refs_2_, ...), custom_call_target="tpu_custom_call" | custom-call | tf_op jit(solution)/shard_map/pallas_call | solution.py:401
  601.1 4.3 collective-permute-done.53
  606.1 10.4 %all-to-all-start.2 = ((bf16[8,9,64,320]{3,2,1,0:T(8,128)(2,1)}), bf16[8,9,64,320]{3,2,1,0:T(8,128)(2,1)}, u32[]{:S(2)}, u32[]{:S(2)}) async-start(bf16[8,9,64,320]{3,2,1,0:T(8,128)(2,1)} %get-tuple-element.256), calls=%async_computation.3 | async-start | bytes 7077888 | tf_op jit(solution)/shard_map/all_to_all | solution.py:1066
  618.1 3.9 collective-permute-start.44
  626.3 4.1 collective-permute-done.45
  642.8 14.3 %all-to-all-done.2.gradient_ref = bf16[8,9,64,320]{3,2,1,0:T(8,128)(2,1)} async-done(((bf16[8,9,64,320]{3,2,1,0:T(8,128)(2,1)}), bf16[8,9,64,320]{3,2,1,0:T(8,128)(2,1)}, u32[]{:S(2)}, u32[]{:S(2)}) %all-to-all-start.2) | async-done | bytes 2949152 | tf_op jit(solution)/shard_map/all_to_all | solution.py:1066
  657.2 5.9 all-to-all-start.3
  675.4 4.7 collective-permute-done.61
  680.1 28.9 %collective-permute-done.58 = bf16[512,640]{1,0:T(8,128)(2,1)} collective-permute-done((bf16[512,640]{1,0:T(8,128)(2,1)}, bf16[512,640]{1,0:T(8,128)(2,1)}, u32[]{:S(2)}, u32[]{:S(2)}) %collective-permute-start.58) | collective-permute-done | bytes 655392 | tf_op jit(solution)/shard_map/ppermute | solution.py:90
  708.9 15.1 %collective-permute-done.62 = bf16[512,640]{1,0:T(8,128)(2,1)} collective-permute-done((bf16[512,640]{1,0:T(8,128)(2,1)}, bf16[512,640]{1,0:T(8,128)(2,1)}, u32[]{:S(2)}, u32[]{:S(2)}) %collective-permute-start.62) | collective-permute-done | bytes 655392 | tf_op jit(solution)/shard_map/ppermute | solution.py:90
  724.1 4.8 fusion.23
  732.5 5.6 all-to-all-start.4
  739.3 23.5 %shard_map.758 = (bf16[8,9,64,320]{3,2,1,0:T(8,128)(2,1)S(1)}, f32[17,64,2560]{2,1,0:T(8,128)}, f32[17,64,2560]{2,1,0:T(8,128)}) custom-call(s32[18]{0:T(128)S(1)} %copy-done.47, f32[20]{0:T(128)S(1)} %pad_maximum_fusion.8.scale_ref, bf16[8,9,64,320]{3,2,1,0:T(8,128)(2,1)} %all-to-all-done.2.gradient_ref, f32[17,2560,128]{2,1,0:T(8,128)} %left_ref.5, ...), custom_call_target="tpu_custom_call" | custom-call | tf_op jit(solution)/shard_map/pallas_call | solution.py:548
  765.7 4.7 all-to-all-start.5
  772.6 21.4 %shard_map.759 = (bf16[8,8,64,320]{3,2,1,0:T(8,128)(2,1)S(1)}, f32[17,64,2560]{2,1,0:T(8,128)}, f32[17,64,2560]{2,1,0:T(8,128)}) custom-call(s32[16]{0:T(128)S(1)} %concatenate.97.refs_0_, f32[18]{0:T(128)S(1)} %pad_maximum_fusion.9.refs_1_, bf16[8,8,64,320]{3,2,1,0:T(8,128)(2,1)} %all-to-all-done.3.refs_2_, ...), custom_call_target="tpu_custom_call", output_to_operand_aliasing={{1}: (7, {}), {2}: (8, {})} | custom-call | tf_op jit(solution)/shard_map/pallas_call | solution.py:548
  795.7 20.1 %all-to-all-done.5.first_ref = bf16[8,9,64,320]{3,2,1,0:T(8,128)(2,1)} async-done(((bf16[8,9,64,320]{3,2,1,0:T(8,128)(2,1)}), bf16[8,9,64,320]{3,2,1,0:T(8,128)(2,1)}, u32[]{:S(2)}, u32[]{:S(2)}) %all-to-all-start.5) | async-done | bytes 2949152 | tf_op jit(solution)/shard_map/all_to_all | solution.py:1136
  815.9 6.5 all-to-all-start.6
  835.6 23.2 %all-to-all-done.6.last_ref = bf16[8,8,64,320]{3,2,1,0:T(8,128)(2,1)} async-done(((bf16[8,8,64,320]{3,2,1,0:T(8,128)(2,1)}), bf16[8,8,64,320]{3,2,1,0:T(8,128)(2,1)}, u32[]{:S(2)}, u32[]{:S(2)}) %all-to-all-start.6) | async-done | bytes 2621472 | tf_op jit(solution)/shard_map/all_to_all | solution.py:1143
  862.1 5.3 all-to-all-start.7
  876.0 16.5 %all-to-all-done.7 = bf16[8,4,64,448]{3,2,1,0:T(8,128)(2,1)S(1)} async-done(((bf16[8,4,64,448]{3,2,1,0:T(8,128)(2,1)}), bf16[8,4,64,448]{3,2,1,0:T(8,128)(2,1)S(1)}, u32[]{:S(2)}, u32[]{:S(2)}) %all-to-all-start.7) | async-done | bytes 1835040 | tf_op jit(solution)/shard_map/all_to_all | solution.py:792
  892.7 4.3 shard_map.760
  897.3 3.8 shard_map.761
  901.4 4.4 shard_map.762
  907.8 7.5 all-to-all-start.8
  931.2 10.3 %shard_map.763 = (f32[320,640]{1,0:T(8,128)}, f32[320,1600]{1,0:T(8,128)}, f32[320,1600]{1,0:T(8,128)}, f32[320,1600]{1,0:T(8,128)}) custom-call(s32[85]{0:T(128)} %copy-done.142, bf16[8,9,64,320]{3,2,1,0:T(8,128)(2,1)} %all-to-all-done.5.first_ref, bf16[8,8,64,320]{3,2,1,0:T(8,128)(2,1)} %all-to-all-done.6.last_ref, bf16[320,640]{1,0:T(8,128)(2,1)} %refs_0_.1, ...), custom_call_target="tpu_custom_call" | custom-call | tf_op jit(solution)/shard_map/pallas_call | solution.py:446
  (733 shorter events, 325.3 us)
Async XLA Ops:
  7.3 49.2 %all-gather.18.cloned.1.call-start = ((), (), s32[]{:S(2)}) async-start(), calls=%async_computation.20 | async-start | bytes 1990656 | tf_op jit(solution)/shard_map/all_gather | solution.py:880
  9.1 114.2 %all-gather.8.cloned.1.call-start = ((), (), s32[]{:S(2)}) async-start(), calls=%async_computation.12 | async-start | bytes 2211840 | tf_op jit(solution)/shard_map/all_gather | solution.py:881
  11.2 138.6 %all-gather.10.cloned.1.call-start = ((), (), s32[]{:S(2)}) async-start(), calls=%async_computation.13 | async-start | bytes 3686400 | tf_op jit(solution)/shard_map/all_gather | solution.py:883
  11.9 265.3 %all-gather.16.cloned.1.call-start = ((), (), s32[]{:S(2)}) async-start(), calls=%async_computation.16 | async-start | bytes 9584640 | tf_op jit(solution)/shard_map/all_gather | solution.py:886
  12.5 275.7 %all-gather.14.cloned.1.call-start = ((), (), s32[]{:S(2)}) async-start(), calls=%async_computation.15 | async-start | bytes 9584640 | tf_op jit(solution)/shard_map/all_gather | solution.py:885
  13.3 56.1 %collective-permute-start.4 = (f32[1536]{0:T(1024)S(1)}, f32[1536]{0:T(1024)S(1)}, u32[]{:S(2)}, u32[]{:S(2)}) collective-permute-start(f32[1536]{0:T(1024)S(1)} %concatenate.83), channel_id=1, source_target_pairs={{0,1},{1,2},{2,3},{3,0},{4,5},{5,6},{6,7},{7,4},{8,9},{9,10},{10,1... | collective-permute-start | bytes 18440 | tf_op jit(solution)/shard_map/ppermute | solution.py:81
  14.6 59.2 %collective-permute-start.5 = (f32[1536]{0:T(1024)S(1)}, f32[1536]{0:T(1024)S(1)}, u32[]{:S(2)}, u32[]{:S(2)}) collective-permute-start(f32[1536]{0:T(1024)S(1)} %concatenate.83), channel_id=1, source_target_pairs={{0,2},{1,3},{2,0},{3,1},{4,6},{5,7},{6,4},{7,5},{8,10},{9,11},{10,... | collective-permute-start | bytes 18440 | tf_op jit(solution)/shard_map/ppermute | solution.py:81
  15.6 58.2 %collective-permute-start.6 = (f32[1536]{0:T(1024)S(1)}, f32[1536]{0:T(1024)S(1)}, u32[]{:S(2)}, u32[]{:S(2)}) collective-permute-start(f32[1536]{0:T(1024)S(1)} %concatenate.83), channel_id=1, source_target_pairs={{0,3},{1,0},{2,1},{3,2},{4,7},{5,4},{6,5},{7,6},{8,11},{9,8},{10,9... | collective-permute-start | bytes 18440 | tf_op jit(solution)/shard_map/ppermute | solution.py:81
  25.4 273.9 %all-gather.12.cloned.1.call-start = ((), (), s32[]{:S(2)}) async-start(), calls=%async_computation.14 | async-start | bytes 9584640 | tf_op jit(solution)/shard_map/all_gather | solution.py:884
  36.6 28.1 %collective-permute-start.1 = (bf16[512,640]{1,0:T(8,128)(2,1)S(1)}, bf16[512,640]{1,0:T(8,128)(2,1)}, u32[]{:S(2)}, u32[]{:S(2)}) collective-permute-start(bf16[512,640]{1,0:T(8,128)(2,1)S(1)} %bitcast.231), channel_id=1, source_target_pairs={{0,2},{2,0},{1,3},{3,1},{4,6},{6,4},{5,7},{7,5},{8,10},{10,8},{9,1... | collective-permute-start | bytes 1966088 | tf_op jit(solution)/shard_map/ppermute | solution.py:90
  38.8 37.0 %collective-permute-start = (bf16[512,640]{1,0:T(8,128)(2,1)S(1)}, bf16[512,640]{1,0:T(8,128)(2,1)}, u32[]{:S(2)}, u32[]{:S(2)}) collective-permute-start(bf16[512,640]{1,0:T(8,128)(2,1)S(1)} %bitcast.232), channel_id=1, source_target_pairs={{0,1},{1,0},{2,3},{3,2},{4,5},{5,4},{6,7},{7,6},{8,9},{9,8},{10,11... | collective-permute-start | bytes 1966088 | tf_op jit(solution)/shard_map/ppermute | solution.py:90
  64.7 19.5 %collective-permute-start.2 = (bf16[512,640]{1,0:T(8,128)(2,1)S(1)}, bf16[512,640]{1,0:T(8,128)(2,1)S(1)}, u32[]{:S(2)}, u32[]{:S(2)}) collective-permute-start(bf16[512,640]{1,0:T(8,128)(2,1)S(1)} %bitcast.233), channel_id=1, source_target_pairs={{1,2},{2,1},{5,6},{6,5},{9,10},{10,9},{13,14},{14,13},{17,18},{18,... | collective-permute-start | bytes 1966088 | tf_op jit(solution)/shard_map/ppermute | solution.py:90
  113.4 28.3 %collective-permute-start.11 = (bf16[512,640]{1,0:T(8,128)(2,1)}, bf16[512,640]{1,0:T(8,128)(2,1)}, u32[]{:S(2)}, u32[]{:S(2)}) collective-permute-start(bf16[512,640]{1,0:T(8,128)(2,1)} %param.47), channel_id=1, source_target_pairs={{0,2},{2,0},{1,3},{3,1},{4,6},{6,4},{5,7},{7,5},{8,10},{10,8},{9,1... | collective-permute-start | bytes 1966088 | tf_op jit(solution)/shard_map/ppermute | solution.py:90
  113.5 34.3 %collective-permute-start.21 = (bf16[512,640]{1,0:T(8,128)(2,1)}, bf16[512,640]{1,0:T(8,128)(2,1)}, u32[]{:S(2)}, u32[]{:S(2)}) collective-permute-start(bf16[512,640]{1,0:T(8,128)(2,1)} %param.47), channel_id=1, source_target_pairs={{0,1},{1,0},{2,3},{3,2},{4,5},{5,4},{6,7},{7,6},{8,9},{9,8},{10,11... | collective-permute-start | bytes 1966088 | tf_op jit(solution)/shard_map/ppermute | solution.py:90
  114.4 44.4 %collective-permute-start.22 = (bf16[512,640]{1,0:T(8,128)(2,1)}, bf16[512,640]{1,0:T(8,128)(2,1)}, u32[]{:S(2)}, u32[]{:S(2)}) collective-permute-start(bf16[512,640]{1,0:T(8,128)(2,1)} %param.47), channel_id=1, source_target_pairs={{1,2},{2,1},{5,6},{6,5},{9,10},{10,9},{13,14},{14,13},{17,18},{18,... | collective-permute-start | bytes 1966088 | tf_op jit(solution)/shard_map/ppermute | solution.py:90
  141.6 19.1 %collective-permute-start.23 = (bf16[512,640]{1,0:T(8,128)(2,1)}, bf16[512,640]{1,0:T(8,128)(2,1)S(1)}, u32[]{:S(2)}, u32[]{:S(2)}) collective-permute-start(bf16[512,640]{1,0:T(8,128)(2,1)} %collective-permute-done.11), channel_id=1, source_target_pairs={{1,0},{2,3},{5,4},{6,7},{9,8},{10,11},{13,12},{14,15},{17,16},{18,... | collective-permute-start | bytes 1966088 | tf_op jit(solution)/shard_map/ppermute | solution.py:90
  155.4 19.1 %collective-permute-start.14 = (bf16[512,640]{1,0:T(8,128)(2,1)}, bf16[512,640]{1,0:T(8,128)(2,1)S(1)}, u32[]{:S(2)}, u32[]{:S(2)}) collective-permute-start(bf16[512,640]{1,0:T(8,128)(2,1)} %get-tuple-element.601), channel_id=1, source_target_pairs={{0,1},{3,2},{4,5},{7,6},{8,9},{11,10},{12,13},{15,14},{16,17},{19,... | collective-permute-start | bytes 1966088 | tf_op jit(solution)/shard_map/ppermute | solution.py:90
  166.9 90.0 %all-to-all-start.1 = ((bf16[8,64,2560]{2,1,0:T(8,128)(2,1)}), bf16[8,64,2560]{2,1,0:T(8,128)(2,1)}, u32[]{:S(2)}, u32[]{:S(2)}) async-start(bf16[8,64,2560]{2,1,0:T(8,128)(2,1)} %gather_fusion.1), calls=%async_computation.1 | async-start | bytes 5242880 | tf_op jit(solution)/shard_map/all_to_all | solution.py:858
  172.4 418.5 %reduce-scatter.4.cloned.1.call-start = ((), (), s32[]{:S(2)}) async-start(), calls=%async_computation.17 | async-start | bytes 3686400 | tf_op jit(solution)/shard_map/reduce_scatter | solution.py:372
  175.8 40.0 %collective-permute-start.15 = (bf16[512,640]{1,0:T(8,128)(2,1)S(1)}, bf16[512,640]{1,0:T(8,128)(2,1)S(1)}, u32[]{:S(2)}, u32[]{:S(2)}) collective-permute-start(bf16[512,640]{1,0:T(8,128)(2,1)S(1)} %add_convert_fusion.5), channel_id=1, source_target_pairs={{0,2},{2,0},{1,3},{3,1},{4,6},{6,4},{5,7},{7,5},{8,10},{10,8},{9,1... | collective-permute-start | bytes 1966088 | tf_op jit(solution)/shard_map/ppermute | solution.py:90
  220.8 31.6 %collective-permute-start.17 = (bf16[512,640]{1,0:T(8,128)(2,1)}, bf16[512,640]{1,0:T(8,128)(2,1)S(1)}, u32[]{:S(2)}, u32[]{:S(2)}) collective-permute-start(bf16[512,640]{1,0:T(8,128)(2,1)} %get-tuple-element.586), channel_id=1, source_target_pairs={{0,2},{2,0},{1,3},{3,1},{4,6},{6,4},{5,7},{7,5},{8,10},{10,8},{9,1... | collective-permute-start | bytes 1966088 | tf_op jit(solution)/shard_map/ppermute | solution.py:90
  225.2 35.4 %collective-permute-start.16 = (bf16[512,640]{1,0:T(8,128)(2,1)}, bf16[512,640]{1,0:T(8,128)(2,1)}, u32[]{:S(2)}, u32[]{:S(2)}) collective-permute-start(bf16[512,640]{1,0:T(8,128)(2,1)} %get-tuple-element.586), channel_id=1, source_target_pairs={{0,1},{1,0},{2,3},{3,2},{4,5},{5,4},{6,7},{7,6},{8,9},{9,8},{10,11... | collective-permute-start | bytes 1966088 | tf_op jit(solution)/shard_map/ppermute | solution.py:90
  225.3 42.1 %collective-permute-start.18 = (bf16[512,640]{1,0:T(8,128)(2,1)}, bf16[512,640]{1,0:T(8,128)(2,1)S(1)}, u32[]{:S(2)}, u32[]{:S(2)}) collective-permute-start(bf16[512,640]{1,0:T(8,128)(2,1)} %get-tuple-element.586), channel_id=1, source_target_pairs={{1,2},{2,1},{5,6},{6,5},{9,10},{10,9},{13,14},{14,13},{17,18},{18,... | collective-permute-start | bytes 1966088 | tf_op jit(solution)/shard_map/ppermute | solution.py:90
  322.0 34.9 %collective-permute-start.27 = (bf16[640,1664]{1,0:T(8,128)(2,1)}, bf16[640,1664]{1,0:T(8,128)(2,1)S(1)}, u32[]{:S(2)}, u32[]{:S(2)}) collective-permute-start(bf16[640,1664]{1,0:T(8,128)(2,1)} %get-tuple-element.188), channel_id=1, source_target_pairs={{0,4},{4,0},{8,12},{12,8},{16,20},{20,16},{24,28},{28,24},{1,5},{5... | collective-permute-start | bytes 6389768 | tf_op jit(solution)/shard_map/ppermute | solution.py:86
  324.1 32.9 %collective-permute-start.28 = (bf16[640,1664]{1,0:T(8,128)(2,1)}, bf16[640,1664]{1,0:T(8,128)(2,1)}, u32[]{:S(2)}, u32[]{:S(2)}) collective-permute-start(bf16[640,1664]{1,0:T(8,128)(2,1)} %get-tuple-element.190), channel_id=1, source_target_pairs={{0,4},{4,0},{8,12},{12,8},{16,20},{20,16},{24,28},{28,24},{1,5},{5... | collective-permute-start | bytes 6389768 | tf_op jit(solution)/shard_map/ppermute | solution.py:86
  375.1 33.2 %collective-permute-start.30 = (bf16[640,1664]{1,0:T(8,128)(2,1)}, bf16[640,1664]{1,0:T(8,128)(2,1)S(1)}, u32[]{:S(2)}, u32[]{:S(2)}) collective-permute-start(bf16[640,1664]{1,0:T(8,128)(2,1)} %get-tuple-element.198), channel_id=1, source_target_pairs={{0,4},{4,0},{8,12},{12,8},{16,20},{20,16},{24,28},{28,24},{1,5},{5... | collective-permute-start | bytes 6389768 | tf_op jit(solution)/shard_map/ppermute | solution.py:86
  376.7 35.0 %collective-permute-start.32 = (bf16[640,1664]{1,0:T(8,128)(2,1)}, bf16[640,1664]{1,0:T(8,128)(2,1)S(1)}, u32[]{:S(2)}, u32[]{:S(2)}) collective-permute-start(bf16[640,1664]{1,0:T(8,128)(2,1)} %get-tuple-element.202), channel_id=1, source_target_pairs={{0,4},{4,0},{8,12},{12,8},{16,20},{20,16},{24,28},{28,24},{1,5},{5... | collective-permute-start | bytes 6389768 | tf_op jit(solution)/shard_map/ppermute | solution.py:86
  376.7 36.3 %collective-permute-start.33 = (bf16[640,1664]{1,0:T(8,128)(2,1)}, bf16[640,1664]{1,0:T(8,128)(2,1)S(1)}, u32[]{:S(2)}, u32[]{:S(2)}) collective-permute-start(bf16[640,1664]{1,0:T(8,128)(2,1)} %get-tuple-element.204), channel_id=1, source_target_pairs={{0,4},{4,0},{8,12},{12,8},{16,20},{20,16},{24,28},{28,24},{1,5},{5... | collective-permute-start | bytes 6389768 | tf_op jit(solution)/shard_map/ppermute | solution.py:86
  377.2 42.0 %collective-permute-start.31 = (bf16[640,1664]{1,0:T(8,128)(2,1)}, bf16[640,1664]{1,0:T(8,128)(2,1)S(1)}, u32[]{:S(2)}, u32[]{:S(2)}) collective-permute-start(bf16[640,1664]{1,0:T(8,128)(2,1)} %get-tuple-element.200), channel_id=1, source_target_pairs={{0,4},{4,0},{8,12},{12,8},{16,20},{20,16},{24,28},{28,24},{1,5},{5... | collective-permute-start | bytes 6389768 | tf_op jit(solution)/shard_map/ppermute | solution.py:86
  377.3 29.0 %collective-permute-start.29 = (bf16[512,640]{1,0:T(8,128)(2,1)}, bf16[512,640]{1,0:T(8,128)(2,1)S(1)}, u32[]{:S(2)}, u32[]{:S(2)}) collective-permute-start(bf16[512,640]{1,0:T(8,128)(2,1)} %add_convert_fusion.4), channel_id=1, source_target_pairs={{0,2},{2,0},{1,3},{3,1},{4,6},{6,4},{5,7},{7,5},{8,10},{10,8},{9,1... | collective-permute-start | bytes 1966088 | tf_op jit(solution)/shard_map/ppermute | solution.py:90
  411.7 23.5 %collective-permute-start.36 = (bf16[320,1664]{1,0:T(8,128)(2,1)}, bf16[320,1664]{1,0:T(8,128)(2,1)S(1)}, u32[]{:S(2)}, u32[]{:S(2)}) collective-permute-start(bf16[320,1664]{1,0:T(8,128)(2,1)} %get-tuple-element.214), channel_id=1, source_target_pairs={{0,8},{4,12},{8,0},{12,4},{16,24},{20,28},{24,16},{28,20},{1,9},{5... | collective-permute-start | bytes 3194888 | tf_op jit(solution)/shard_map/ppermute | solution.py:86
  414.4 24.2 %collective-permute-start.37 = (bf16[320,1664]{1,0:T(8,128)(2,1)}, bf16[320,1664]{1,0:T(8,128)(2,1)S(1)}, u32[]{:S(2)}, u32[]{:S(2)}) collective-permute-start(bf16[320,1664]{1,0:T(8,128)(2,1)} %get-tuple-element.215), channel_id=1, source_target_pairs={{0,16},{4,20},{8,24},{12,28},{16,0},{20,4},{24,8},{28,12},{1,17},{... | collective-permute-start | bytes 3194888 | tf_op jit(solution)/shard_map/ppermute | solution.py:86
  428.0 26.8 %collective-permute-start.35 = (bf16[512,640]{1,0:T(8,128)(2,1)}, bf16[512,640]{1,0:T(8,128)(2,1)}, u32[]{:S(2)}, u32[]{:S(2)}) collective-permute-start(bf16[512,640]{1,0:T(8,128)(2,1)} %get-tuple-element.584), channel_id=1, source_target_pairs={{0,2},{2,0},{1,3},{3,1},{4,6},{6,4},{5,7},{7,5},{8,10},{10,8},{9,1... | collective-permute-start | bytes 1966088 | tf_op jit(solution)/shard_map/ppermute | solution.py:90
  428.1 34.1 %collective-permute-start.40 = (bf16[320,1664]{1,0:T(8,128)(2,1)}, bf16[320,1664]{1,0:T(8,128)(2,1)S(1)}, u32[]{:S(2)}, u32[]{:S(2)}) collective-permute-start(bf16[320,1664]{1,0:T(8,128)(2,1)} %get-tuple-element.219), channel_id=1, source_target_pairs={{0,8},{4,12},{8,0},{12,4},{16,24},{20,28},{24,16},{28,20},{1,9},{5... | collective-permute-start | bytes 3194888 | tf_op jit(solution)/shard_map/ppermute | solution.py:86
  429.2 33.0 %collective-permute-start.41 = (bf16[320,1664]{1,0:T(8,128)(2,1)}, bf16[320,1664]{1,0:T(8,128)(2,1)S(1)}, u32[]{:S(2)}, u32[]{:S(2)}) collective-permute-start(bf16[320,1664]{1,0:T(8,128)(2,1)} %get-tuple-element.220), channel_id=1, source_target_pairs={{0,16},{4,20},{8,24},{12,28},{16,0},{20,4},{24,8},{28,12},{1,17},{... | collective-permute-start | bytes 3194888 | tf_op jit(solution)/shard_map/ppermute | solution.py:86
  435.2 25.7 %collective-permute-start.34 = (bf16[512,640]{1,0:T(8,128)(2,1)}, bf16[512,640]{1,0:T(8,128)(2,1)S(1)}, u32[]{:S(2)}, u32[]{:S(2)}) collective-permute-start(bf16[512,640]{1,0:T(8,128)(2,1)} %get-tuple-element.584), channel_id=1, source_target_pairs={{0,1},{1,0},{2,3},{3,2},{4,5},{5,4},{6,7},{7,6},{8,9},{9,8},{10,11... | collective-permute-start | bytes 1966088 | tf_op jit(solution)/shard_map/ppermute | solution.py:90
  441.3 30.4 %collective-permute-start.38 = (bf16[512,640]{1,0:T(8,128)(2,1)}, bf16[512,640]{1,0:T(8,128)(2,1)}, u32[]{:S(2)}, u32[]{:S(2)}) collective-permute-start(bf16[512,640]{1,0:T(8,128)(2,1)} %get-tuple-element.584), channel_id=1, source_target_pairs={{1,2},{2,1},{5,6},{6,5},{9,10},{10,9},{13,14},{14,13},{17,18},{18,... | collective-permute-start | bytes 1966088 | tf_op jit(solution)/shard_map/ppermute | solution.py:90
  454.8 19.9 %collective-permute-start.39 = (bf16[512,640]{1,0:T(8,128)(2,1)}, bf16[512,640]{1,0:T(8,128)(2,1)S(1)}, u32[]{:S(2)}, u32[]{:S(2)}) collective-permute-start(bf16[512,640]{1,0:T(8,128)(2,1)} %collective-permute-done.35), channel_id=1, source_target_pairs={{1,0},{2,3},{5,4},{6,7},{9,8},{10,11},{13,12},{14,15},{17,16},{18,... | collective-permute-start | bytes 1966088 | tf_op jit(solution)/shard_map/ppermute | solution.py:90
  503.0 46.2 %collective-permute-start.42 = (bf16[320,1664]{1,0:T(8,128)(2,1)S(1)}, bf16[320,1664]{1,0:T(8,128)(2,1)S(1)}, u32[]{:S(2)}, u32[]{:S(2)}) collective-permute-start(bf16[320,1664]{1,0:T(8,128)(2,1)S(1)} %copy-done.54), channel_id=1, source_target_pairs={{0,8},{4,12},{8,0},{12,4},{16,24},{20,28},{24,16},{28,20},{1,9},{5... | collective-permute-start | bytes 3194888 | tf_op jit(solution)/shard_map/ppermute | solution.py:86
  504.2 45.0 %collective-permute-start.43 = (bf16[320,1664]{1,0:T(8,128)(2,1)S(1)}, bf16[320,1664]{1,0:T(8,128)(2,1)S(1)}, u32[]{:S(2)}, u32[]{:S(2)}) collective-permute-start(bf16[320,1664]{1,0:T(8,128)(2,1)S(1)} %copy-done.52), channel_id=1, source_target_pairs={{0,16},{4,20},{8,24},{12,28},{16,0},{20,4},{24,8},{28,12},{1,17},{... | collective-permute-start | bytes 3194888 | tf_op jit(solution)/shard_map/ppermute | solution.py:86
  537.1 34.5 %collective-permute-start.49 = (bf16[160,1664]{1,0:T(8,128)(2,1)}, bf16[160,1664]{1,0:T(8,128)(2,1)}, u32[]{:S(2)}, u32[]{:S(2)}) collective-permute-start(bf16[160,1664]{1,0:T(8,128)(2,1)} %get-tuple-element.235), channel_id=1, source_target_pairs={{0,16},{4,20},{8,24},{12,28},{16,0},{20,4},{24,8},{28,12},{1,17},{... | collective-permute-start | bytes 1597448 | tf_op jit(solution)/shard_map/ppermute | solution.py:86
  537.6 34.0 %collective-permute-start.50 = (bf16[160,1664]{1,0:T(8,128)(2,1)}, bf16[160,1664]{1,0:T(8,128)(2,1)}, u32[]{:S(2)}, u32[]{:S(2)}) collective-permute-start(bf16[160,1664]{1,0:T(8,128)(2,1)} %get-tuple-element.236), channel_id=1, source_target_pairs={{0,8},{4,12},{8,0},{12,4},{16,24},{20,28},{24,16},{28,20},{1,9},{5... | collective-permute-start | bytes 1597448 | tf_op jit(solution)/shard_map/ppermute | solution.py:86
  559.6 26.4 %collective-permute-start.46 = (bf16[512,256]{1,0:T(8,128)(2,1)}, bf16[512,256]{1,0:T(8,128)(2,1)}, u32[]{:S(2)}, u32[]{:S(2)}) collective-permute-start(bf16[512,256]{1,0:T(8,128)(2,1)} %copy.335), channel_id=1, source_target_pairs={{0,1},{3,2},{4,5},{7,6},{8,9},{11,10},{12,13},{15,14},{16,17},{19,... | collective-permute-start | bytes 786440 | tf_op jit(solution)/shard_map/ppermute | solution.py:90
  560.9 21.2 %collective-permute-start.51 = (bf16[160,1664]{1,0:T(8,128)(2,1)}, bf16[160,1664]{1,0:T(8,128)(2,1)}, u32[]{:S(2)}, u32[]{:S(2)}) collective-permute-start(bf16[160,1664]{1,0:T(8,128)(2,1)} %copy-done.60), channel_id=1, source_target_pairs={{0,16},{4,20},{8,24},{12,28},{16,0},{20,4},{24,8},{28,12},{1,17},{... | collective-permute-start | bytes 1597448 | tf_op jit(solution)/shard_map/ppermute | solution.py:86
  561.0 21.4 %collective-permute-start.52 = (bf16[160,1664]{1,0:T(8,128)(2,1)}, bf16[160,1664]{1,0:T(8,128)(2,1)}, u32[]{:S(2)}, u32[]{:S(2)}) collective-permute-start(bf16[160,1664]{1,0:T(8,128)(2,1)} %copy-done.59), channel_id=1, source_target_pairs={{0,8},{4,12},{8,0},{12,4},{16,24},{20,28},{24,16},{28,20},{1,9},{5... | collective-permute-start | bytes 1597448 | tf_op jit(solution)/shard_map/ppermute | solution.py:86
  571.6 29.6 %collective-permute-start.54 = (f32[34,512]{0,1:T(8,128)}, f32[34,512]{0,1:T(8,128)}, u32[]{:S(2)}, u32[]{:S(2)}) collective-permute-start(f32[34,512]{0,1:T(8,128)} %copy.300), channel_id=1, source_target_pairs={{0,1},{1,2},{2,3},{3,0},{4,5},{5,6},{6,7},{7,4},{8,9},{9,10},{10,1... | collective-permute-start | bytes 208904 | tf_op jit(solution)/shard_map/ppermute | solution.py:81
  571.6 29.5 %collective-permute-start.55 = (f32[34,512]{0,1:T(8,128)}, f32[34,512]{0,1:T(8,128)}, u32[]{:S(2)}, u32[]{:S(2)}) collective-permute-start(f32[34,512]{0,1:T(8,128)} %copy.300), channel_id=1, source_target_pairs={{0,2},{1,3},{2,0},{3,1},{4,6},{5,7},{6,4},{7,5},{8,10},{9,11},{10,... | collective-permute-start | bytes 208904 | tf_op jit(solution)/shard_map/ppermute | solution.py:81
  582.1 19.0 %collective-permute-start.56 = (f32[34,512]{0,1:T(8,128)}, f32[34,512]{0,1:T(8,128)S(1)}, u32[]{:S(2)}, u32[]{:S(2)}) collective-permute-start(f32[34,512]{0,1:T(8,128)} %copy.300), channel_id=1, source_target_pairs={{0,3},{1,0},{2,1},{3,2},{4,7},{5,4},{6,5},{7,6},{8,11},{9,8},{10,9... | collective-permute-start | bytes 208904 | tf_op jit(solution)/shard_map/ppermute | solution.py:81
  606.1 51.0 %all-to-all-start.2 = ((bf16[8,9,64,320]{3,2,1,0:T(8,128)(2,1)}), bf16[8,9,64,320]{3,2,1,0:T(8,128)(2,1)}, u32[]{:S(2)}, u32[]{:S(2)}) async-start(bf16[8,9,64,320]{3,2,1,0:T(8,128)(2,1)} %get-tuple-element.256), calls=%async_computation.3 | async-start | bytes 7077888 | tf_op jit(solution)/shard_map/all_to_all | solution.py:1066
  634.6 32.1 %collective-permute-start.57 = (bf16[512,640]{1,0:T(8,128)(2,1)}, bf16[512,640]{1,0:T(8,128)(2,1)}, u32[]{:S(2)}, u32[]{:S(2)}) collective-permute-start(bf16[512,640]{1,0:T(8,128)(2,1)} %get-tuple-element.595), channel_id=1, source_target_pairs={{0,1},{3,2},{4,5},{7,6},{8,9},{11,10},{12,13},{15,14},{16,17},{19,... | collective-permute-start | bytes 1966088 | tf_op jit(solution)/shard_map/ppermute | solution.py:90
  635.9 36.5 %collective-permute-start.59 = (bf16[512,640]{1,0:T(8,128)(2,1)}, bf16[512,640]{1,0:T(8,128)(2,1)}, u32[]{:S(2)}, u32[]{:S(2)}) collective-permute-start(bf16[512,640]{1,0:T(8,128)(2,1)} %get-tuple-element.597), channel_id=1, source_target_pairs={{1,2},{2,1},{5,6},{6,5},{9,10},{10,9},{13,14},{14,13},{17,18},{18,... | collective-permute-start | bytes 1966088 | tf_op jit(solution)/shard_map/ppermute | solution.py:90
  638.2 37.2 %collective-permute-start.60 = (bf16[512,640]{1,0:T(8,128)(2,1)}, bf16[512,640]{1,0:T(8,128)(2,1)}, u32[]{:S(2)}, u32[]{:S(2)}) collective-permute-start(bf16[512,640]{1,0:T(8,128)(2,1)} %get-tuple-element.596), channel_id=1, source_target_pairs={{0,1},{1,0},{2,3},{3,2},{4,5},{5,4},{6,7},{7,6},{8,9},{9,8},{10,11... | collective-permute-start | bytes 1966088 | tf_op jit(solution)/shard_map/ppermute | solution.py:90
  642.7 37.3 %collective-permute-start.61 = (bf16[512,640]{1,0:T(8,128)(2,1)}, bf16[512,640]{1,0:T(8,128)(2,1)}, u32[]{:S(2)}, u32[]{:S(2)}) collective-permute-start(bf16[512,640]{1,0:T(8,128)(2,1)} %add_convert_fusion.2), channel_id=1, source_target_pairs={{0,2},{2,0},{1,3},{3,1},{4,6},{6,4},{5,7},{7,5},{8,10},{10,8},{9,1... | collective-permute-start | bytes 1966088 | tf_op jit(solution)/shard_map/ppermute | solution.py:90
  657.2 75.3 %all-to-all-start.3 = ((bf16[8,8,64,320]{3,2,1,0:T(8,128)(2,1)}), bf16[8,8,64,320]{3,2,1,0:T(8,128)(2,1)}, u32[]{:S(2)}, u32[]{:S(2)}) async-start(bf16[8,8,64,320]{3,2,1,0:T(8,128)(2,1)} %get-tuple-element.264), calls=%async_computation.4 | async-start | bytes 6291456 | tf_op jit(solution)/shard_map/all_to_all | solution.py:1066
  663.1 163.0 %reduce-scatter.8.cloned.1.call-start = ((), (), s32[]{:S(2)}) async-start(), calls=%async_computation.19 | async-start | bytes 2949120 | tf_op jit(solution)/shard_map/reduce_scatter | solution.py:372
  669.2 39.7 %collective-permute-start.58 = (bf16[512,640]{1,0:T(8,128)(2,1)}, bf16[512,640]{1,0:T(8,128)(2,1)}, u32[]{:S(2)}, u32[]{:S(2)}) collective-permute-start(bf16[512,640]{1,0:T(8,128)(2,1)} %add_convert_fusion.3), channel_id=1, source_target_pairs={{0,2},{2,0},{1,3},{3,1},{4,6},{6,4},{5,7},{7,5},{8,10},{10,8},{9,1... | collective-permute-start | bytes 1966088 | tf_op jit(solution)/shard_map/ppermute | solution.py:90
  671.4 37.5 %collective-permute-start.63 = (bf16[512,640]{1,0:T(8,128)(2,1)}, bf16[512,640]{1,0:T(8,128)(2,1)}, u32[]{:S(2)}, u32[]{:S(2)}) collective-permute-start(bf16[512,640]{1,0:T(8,128)(2,1)} %get-tuple-element.594), channel_id=1, source_target_pairs={{0,1},{1,0},{2,3},{3,2},{4,5},{5,4},{6,7},{7,6},{8,9},{9,8},{10,11... | collective-permute-start | bytes 1966088 | tf_op jit(solution)/shard_map/ppermute | solution.py:90
  672.4 51.6 %collective-permute-start.62 = (bf16[512,640]{1,0:T(8,128)(2,1)}, bf16[512,640]{1,0:T(8,128)(2,1)}, u32[]{:S(2)}, u32[]{:S(2)}) collective-permute-start(bf16[512,640]{1,0:T(8,128)(2,1)} %get-tuple-element.595), channel_id=1, source_target_pairs={{1,2},{2,1},{5,6},{6,5},{9,10},{10,9},{13,14},{14,13},{17,18},{18,... | collective-permute-start | bytes 1966088 | tf_op jit(solution)/shard_map/ppermute | solution.py:90
  732.5 32.1 %all-to-all-start.4 = ((bf16[8,133,640]{2,1,0:T(8,128)(2,1)}), bf16[8,133,640]{2,1,0:T(8,128)(2,1)S(1)}, u32[]{:S(2)}, u32[]{:S(2)}) async-start(bf16[8,133,640]{2,1,0:T(8,128)(2,1)} %pad_maximum_fusion.1), calls=%async_computation.5 | async-start | bytes 2785280 | tf_op jit(solution)/shard_map/all_to_all | solution.py:1131
  765.7 50.2 %all-to-all-start.5 = ((bf16[8,9,64,320]{3,2,1,0:T(8,128)(2,1)}), bf16[8,9,64,320]{3,2,1,0:T(8,128)(2,1)}, u32[]{:S(2)}, u32[]{:S(2)}) async-start(bf16[8,9,64,320]{3,2,1,0:T(8,128)(2,1)} %copy-done.30), calls=%async_computation.8 | async-start | bytes 7077888 | tf_op jit(solution)/shard_map/all_to_all | solution.py:1136
  770.4 55.8 %reduce-scatter.6.cloned.1.call-start = ((), (), s32[]{:S(2)}) async-start(), calls=%async_computation.18 | async-start | bytes 2211840 | tf_op jit(solution)/shard_map/reduce_scatter | solution.py:372
  815.9 42.9 %all-to-all-start.6 = ((bf16[8,8,64,320]{3,2,1,0:T(8,128)(2,1)}), bf16[8,8,64,320]{3,2,1,0:T(8,128)(2,1)}, u32[]{:S(2)}, u32[]{:S(2)}) async-start(bf16[8,8,64,320]{3,2,1,0:T(8,128)(2,1)} %copy-done.31), calls=%async_computation.9 | async-start | bytes 6291456 | tf_op jit(solution)/shard_map/all_to_all | solution.py:1143
  862.1 30.3 %all-to-all-start.7 = ((bf16[8,4,64,448]{3,2,1,0:T(8,128)(2,1)}), bf16[8,4,64,448]{3,2,1,0:T(8,128)(2,1)S(1)}, u32[]{:S(2)}, u32[]{:S(2)}) async-start(bf16[8,4,64,448]{3,2,1,0:T(8,128)(2,1)} %fusion.15), calls=%async_computation.10 | async-start | bytes 4194304 | tf_op jit(solution)/shard_map/all_to_all | solution.py:792
  907.8 33.8 %all-to-all-start.8 = ((bf16[8,4,64,448]{3,2,1,0:T(8,128)(2,1)}), bf16[8,4,64,448]{3,2,1,0:T(8,128)(2,1)S(1)}, u32[]{:S(2)}, u32[]{:S(2)}) async-start(bf16[8,4,64,448]{3,2,1,0:T(8,128)(2,1)} %fusion.17), calls=%async_computation.11 | async-start | bytes 4194304 | tf_op jit(solution)/shard_map/all_to_all | solution.py:792
  (182 other events, 2217.6 us)
Sparse Core Ops, SparseCore 0:
  10.6 30.9 all-gather.17
  44.0 26.1 all-gather.7
  72.1 32.8 all-gather.9
  106.7 54.9 all-gather.15
  163.4 79.1 all-gather.13
  244.3 54.9 all-gather.11
  488.4 62.2 reduce-scatter.3
  675.5 44.0 reduce-scatter.7
  775.2 48.4 reduce-scatter.5
